TPU v7x, 32 devices: a whole 2x2x4 slice. The times are simulated.
32 devices in a mesh: dp: 2 (over core), seq: 4 (over y, x), head: 4 (over z).
Axes of the slice: x: 2, y: 2, z: 4, core: 2. Of those that a mesh axis runs over, the one named last changes fastest.
Arguments:
- frames: bfloat16 [2, 3072, 1536], P('dp', ('seq', 'head')), may hold values from -600 to 600
- norm_gain: float32 [1536], replicated, may hold values from 0.1 to 1.9
- w_query: bfloat16 [1536, 1536], P('dp', 'head'), may hold values from -1.6 to 1.6
- w_key: bfloat16 [1536, 1536], P('dp', 'head'), may hold values from -16 to 16
- w_value: bfloat16 [1536, 1536], P('dp', 'head'), may hold values from -0.15625 to 0.15625
- w_out: bfloat16 [1536, 1536], P('head', 'dp'), may hold values from -0.4375 to 0.4375
- group_band: int32 [2, 24, 12], P('dp', 'seq'), may hold values 0 or 1
- lengths: int32 [2], P('dp'), may hold values from 1536 to 3072
Outputs:
- update: bfloat16 [2, 3072, 1536], P('dp', ('seq', 'head'))
All inputs are finite; a program needn't handle non-finite values. No bound on the sum of `group_band` on one device may be relied on, other than what follows from the above.
Results may differ from a plain program's by a relative error of at most 0.012.
Values may be sent and summed in bfloat16 or wider, within the bound.
No kernel may reach another device: no remote copies, remote signals or barrier semaphores. Data moves between devices by JAX's collectives and lax.ppermute only.
A program may use at most 128 MiB of HBM per device.

v0:
```python
import math

import jax
import jax.numpy as jnp
from jax import lax
from jax.sharding import PartitionSpec as P

HD = 64
GROUP = 128


epsilon = 1e-05


def from_behind(value, axis, steps):
    count = lax.axis_size(axis)
    first, last = (max(0, -steps), min(count, count - steps))
    return lax.ppermute(value, axis, [(source, source + steps) for source in range(first, last)])


def layer_norm(rows, norm_gain):
    values = rows.astype(jnp.float32)
    center = values - jnp.mean(values, axis=-1, keepdims=True)
    spread = jnp.mean(center * center, axis=-1, keepdims=True)
    return (center * lax.rsqrt(spread + epsilon) * norm_gain).astype(jnp.bfloat16)


def permission(
    query_start,
    key_start,
    query_groups,
    key_groups,
    group_size,
    band_rows,
    length_value,
    total_groups,
):
    query_ids = query_start + jnp.arange(query_groups, dtype=jnp.int32)
    key_ids = key_start + jnp.arange(key_groups, dtype=jnp.int32)
    offsets = key_ids[None, :] - query_ids[:, None]
    reach_groups = band_rows.shape[1] // 2
    column = jnp.where(offsets < 0, offsets + reach_groups, offsets + reach_groups - 1)
    hits = column[:, :, None] == jnp.arange(2 * reach_groups, dtype=jnp.int32)[None, None, :]
    picked = jnp.sum(jnp.where(hits, band_rows[:, None, :], 0), axis=-1)
    inside = (key_ids >= 0) & (key_ids < total_groups)
    linked = (offsets != 0) & (jnp.abs(offsets) <= reach_groups) & inside[None, :] & (picked == 1)
    key_frames = key_start * group_size + jnp.arange(key_groups * group_size, dtype=jnp.int32)
    alive_keys = key_frames < length_value
    linked_rows = (
        jnp.repeat(jnp.repeat(linked, group_size, axis=0), group_size, axis=1) & alive_keys[None, :]
    )
    same_group = jnp.repeat(jnp.repeat(offsets == 0, group_size, axis=0), group_size, axis=1)
    return linked_rows | same_group


def local(frames, norm_gain, w_query, w_key, w_value, w_out, group_band, lengths):
    normalized = layer_norm(frames[0], norm_gain)
    gathered = lax.all_gather(normalized, "head", axis=0, tiled=True)
    rows_here = gathered.shape[0]
    local_width = w_query.shape[1]
    group_dev = group_band.shape[1]
    seq_index = lax.axis_index("seq")
    total_groups = group_dev * lax.axis_size("seq")
    query_sum = jnp.dot(
        gathered,
        lax.all_gather(w_query, "dp", axis=0, tiled=True),
        preferred_element_type=jnp.float32,
    )
    key_sum = jnp.dot(
        gathered,
        lax.all_gather(w_key, "dp", axis=0, tiled=True),
        preferred_element_type=jnp.float32,
    )
    value_sum = jnp.dot(
        gathered,
        lax.all_gather(w_value, "dp", axis=0, tiled=True),
        preferred_element_type=jnp.float32,
    )
    query_rows = query_sum.astype(jnp.bfloat16)
    own_keys = key_sum.astype(jnp.bfloat16)
    own_values = value_sum.astype(jnp.bfloat16)
    sides = []
    for distance in (1, -1):
        sides.append(from_behind((own_keys, own_values), "seq", distance))
    keys_window = jnp.concatenate([sides[0][0], own_keys, sides[1][0]], axis=0)
    values_window = jnp.concatenate([sides[0][1], own_values, sides[1][1]], axis=0)
    allowed = permission(
        seq_index * group_dev,
        seq_index * group_dev - group_dev,
        group_dev,
        3 * group_dev,
        GROUP,
        group_band[0],
        lengths[0],
        total_groups,
    )
    score_scale = 1.0 / math.sqrt(HD)

    def head_context(head_index):
        start_col = head_index * HD
        query_head = lax.dynamic_slice_in_dim(query_rows, start_col, HD, 1)
        key_head = lax.dynamic_slice_in_dim(keys_window, start_col, HD, 1)
        value_head = lax.dynamic_slice_in_dim(values_window, start_col, HD, 1)
        scores = (
            lax.dot_general(
                query_head, key_head, (((1,), (1,)), ((), ())), preferred_element_type=jnp.float32
            )
            * score_scale
        )
        masked = jnp.where(allowed, scores, -jnp.inf)
        row_max = jnp.max(masked, axis=-1, keepdims=True)
        weights = jnp.exp(masked - row_max)
        row_total = jnp.sum(weights, axis=-1, keepdims=True)
        rounded = weights.astype(jnp.bfloat16)
        return jnp.dot(rounded, value_head, preferred_element_type=jnp.float32) / row_total

    per_head = lax.map(head_context, jnp.arange(local_width // HD, dtype=jnp.int32))
    context = (
        jnp.transpose(per_head, (1, 0, 2)).reshape(rows_here, local_width).astype(jnp.bfloat16)
    )
    frame_context = lax.all_to_all(context, "head", split_axis=0, concat_axis=1, tiled=True)
    full_rows = lax.all_gather(w_out, "head", axis=0, tiled=True)
    update = jnp.dot(
        frame_context,
        lax.all_gather(full_rows, "dp", axis=1, tiled=True),
        preferred_element_type=jnp.float32,
    )
    return update.astype(jnp.bfloat16)[None]


def solution(mesh):
    return jax.shard_map(
        local,
        mesh=mesh,
        in_specs=(
            P("dp", ("seq", "head"), None),
            P(),
            P("dp", "head"),
            P("dp", "head"),
            P("dp", "head"),
            P("head", "dp"),
            P("dp", "seq", None),
            P("dp"),
        ),
        out_specs=P("dp", ("seq", "head"), None),
        check_vma=False,
    )
```

profile of v0, /device:TPU:1, one launch (start us, length us, event | category | flops | bytes accessed | tf_op | source)
XLA Modules:
  0.0 267.8 jit_solution(1453503193458749704)
XLA Ops:
  6.5 0.7 all-gather.13.cloned.1.call-update
  7.3 1.2 convert_reduce_fusion
  8.5 1.4 fusion.25
  9.9 1.2 fusion.27
  11.2 0.7 all-gather.11.cloned.1.call-update
  15.8 4.8 %all-gather.13.cloned.1.call-done = bf16[1536,384]{1,0:T(8,128)(2,1)} async-done(((bf16[768,384]{1,0:T(8,128)(2,1)}), bf16[1536,384]{1,0:T(8,128)(2,1)}) %all-gather.13.cloned.1.call-update) | async-done | bytes 1179664 | tf_op jit(solution)/shard_map/all_gather | solution.py:76
  20.6 52.8 %all-gather.7.cloned.1.call-done = bf16[768,1536]{1,0:T(8,128)(2,1)} async-done(((bf16[192,1536]{1,0:T(8,128)(2,1)}), bf16[768,1536]{1,0:T(8,128)(2,1)}) %all-gather.7.cloned.1.call-update) | async-done | bytes 2359312 | tf_op jit(solution)/shard_map/all_gather | solution.py:58
  73.5 3.4 %convolution_convert_fusion.1 = bf16[768,384]{1,0:T(8,128)(2,1)S(1)} fusion(bf16[768,1536]{1,0:T(8,128)(2,1)} %all-gather.7.cloned.1.call-done, bf16[1536,384]{1,0:T(8,128)(2,1)} %all-gather.13.cloned.1.call-done), kind=kOutput, calls=%fused_computation.21 | convolution fusion | flops 906264576 | bytes 4128768 | tf_op jit(solution)/shard_map/dot_general | solution.py:74
  76.8 3.1 %collective-permute-start.2 = (bf16[768,384]{1,0:T(8,128)(2,1)S(1)}, bf16[768,384]{1,0:T(8,128)(2,1)S(1)}, u32[]{:S(2)}, u32[]{:S(2)}) collective-permute-start(bf16[768,384]{1,0:T(8,128)(2,1)S(1)} %convolution_convert_fusion.1), channel_id=1, source_target_pairs={{0,4},{4,8},{8,12},{1,5},{5,9},{9,13},{2,6},{6,10},{10,14},{3,7},{... | collective-permute-start | bytes 1769480 | tf_op jit(solution)/shard_map/ppermute | solution.py:18
  80.0 1.3 collective-permute-start.3
  81.3 2.2 all-gather.11.cloned.1.call-done
  83.5 3.4 %convolution_convert_fusion.2 = bf16[768,384]{1,0:T(8,128)(2,1)S(1)} fusion(bf16[768,1536]{1,0:T(8,128)(2,1)} %all-gather.7.cloned.1.call-done, bf16[1536,384]{1,0:T(8,128)(2,1)} %all-gather.11.cloned.1.call-done), kind=kOutput, calls=%fused_computation.22 | convolution fusion | flops 906264576 | bytes 4128768 | tf_op jit(solution)/shard_map/dot_general | solution.py:69
  86.9 4.3 %collective-permute-start = (bf16[768,384]{1,0:T(8,128)(2,1)S(1)}, bf16[768,384]{1,0:T(8,128)(2,1)}, u32[]{:S(2)}, u32[]{:S(2)}) collective-permute-start(bf16[768,384]{1,0:T(8,128)(2,1)S(1)} %convolution_convert_fusion.2), channel_id=1, source_target_pairs={{0,4},{4,8},{8,12},{1,5},{5,9},{9,13},{2,6},{6,10},{10,14},{3,7},{... | collective-permute-start | bytes 1769480 | tf_op jit(solution)/shard_map/ppermute | solution.py:18
  91.2 1.3 collective-permute-start.1
  92.5 43.7 %all-gather.15.cloned.1.call-done = bf16[1536,768]{1,0:T(8,128)(2,1)} async-done(((bf16[384,768]{1,0:T(8,128)(2,1)}), bf16[1536,768]{1,0:T(8,128)(2,1)}) %all-gather.15.cloned.1.call-update) | async-done | bytes 2359312 | tf_op jit(solution)/shard_map/all_gather | solution.py:122
  136.2 9.8 %all-gather.9.cloned.1.call-done = bf16[1536,384]{1,0:T(8,128)(2,1)} async-done(((bf16[768,384]{1,0:T(8,128)(2,1)}), bf16[1536,384]{1,0:T(8,128)(2,1)}) %all-gather.9.cloned.1.call-update) | async-done | bytes 1179664 | tf_op jit(solution)/shard_map/all_gather | solution.py:66
  146.1 4.2 %convolution_convert_fusion.3 = bf16[768,384]{1,0:T(8,128)(2,1)} fusion(bf16[768,1536]{1,0:T(8,128)(2,1)} %all-gather.7.cloned.1.call-done, bf16[1536,384]{1,0:T(8,128)(2,1)} %all-gather.9.cloned.1.call-done), kind=kOutput, calls=%fused_computation.23 | convolution fusion | flops 906264576 | bytes 4128768 | tf_op jit(solution)/shard_map/dot_general | solution.py:64
  150.3 1.3 pad_maximum_fusion.1
  151.6 1.4 pad_maximum_fusion
  153.1 80.6 %while.11 = (s32[]{:T(128)}, bf16[6,768,64]{1,2,0:T(8,128)(2,1)}, s32[6]{0:T(128)S(1)}, bf16[768,384]{1,0:T(8,128)(2,1)}, bf16[2304,384]{1,0:T(8,128)(2,1)S(1)},...) while((s32[]{:T(128)}, bf16[6,768,64]{1,2,0:T(8,128)(2,1)}, ...), condition=%wide.region_6.7_spmd.clone, body=%wide.region_3.6_spmd.clone.sunk | while | flops 468957696 | bytes 37067480 | solution.py:117
  153.2 0.7 dynamic_slice.34
  154.6 1.2 broadcast_in_dim.77
  155.8 1.9 copy.32
  158.2 1.9 copy.33
  160.1 3.3 %fusion.49 = (f32[768]{0:T(1024)S(1)}, f32[768,2304]{1,0:T(8,128)S(1)}) fusion(bf16[2304,384]{1,0:T(8,128)(2,1)S(1)} %get-tuple-element.177, s32[]{:T(128)S(6)} %select_n.29, bf16[768,384]{1,0:T(8,128)(2,1)} %get-tuple-element.176, pred[768,2304]{1,0:T(32,128)(4,1)S(1)} %copy.32, pred[768,2304]{1,0:T(32,128)(4,1)S(1)} %copy.33, ...), kind=kOutput, calls=%fused_computation.53.clone.1 | convolution fusion | flops 235339008 | bytes 11410432 | tf_op jit(solution)/shard_map/while/body/eval_jaxpr/dot_general | solution.py:105
  163.4 1.1 fusion.50
  164.5 2.2 fusion.51
  166.7 0.7 dynamic_slice.34
  168.0 1.2 broadcast_in_dim.77
  169.2 1.9 copy.32
  171.6 1.9 copy.33
  173.5 3.3 %fusion.49 = (f32[768]{0:T(1024)S(1)}, f32[768,2304]{1,0:T(8,128)S(1)}) fusion(bf16[2304,384]{1,0:T(8,128)(2,1)S(1)} %get-tuple-element.177, s32[]{:T(128)S(6)} %select_n.29, bf16[768,384]{1,0:T(8,128)(2,1)} %get-tuple-element.176, pred[768,2304]{1,0:T(32,128)(4,1)S(1)} %copy.32, pred[768,2304]{1,0:T(32,128)(4,1)S(1)} %copy.33, ...), kind=kOutput, calls=%fused_computation.53.clone.1 | convolution fusion | flops 235339008 | bytes 11410432 | tf_op jit(solution)/shard_map/while/body/eval_jaxpr/dot_general | solution.py:105
  176.8 1.1 fusion.50
  177.9 2.2 fusion.51
  181.4 1.2 broadcast_in_dim.77
  182.6 1.9 copy.32
  185.0 1.9 copy.33
  186.9 3.3 %fusion.49 = (f32[768]{0:T(1024)S(1)}, f32[768,2304]{1,0:T(8,128)S(1)}) fusion(bf16[2304,384]{1,0:T(8,128)(2,1)S(1)} %get-tuple-element.177, s32[]{:T(128)S(6)} %select_n.29, bf16[768,384]{1,0:T(8,128)(2,1)} %get-tuple-element.176, pred[768,2304]{1,0:T(32,128)(4,1)S(1)} %copy.32, pred[768,2304]{1,0:T(32,128)(4,1)S(1)} %copy.33, ...), kind=kOutput, calls=%fused_computation.53.clone.1 | convolution fusion | flops 235339008 | bytes 11410432 | tf_op jit(solution)/shard_map/while/body/eval_jaxpr/dot_general | solution.py:105
  190.2 1.1 fusion.50
  191.3 2.2 fusion.51
  193.5 0.7 dynamic_slice.34
  194.8 1.2 broadcast_in_dim.77
  196.0 1.9 copy.32
  198.4 1.9 copy.33
  200.3 3.3 %fusion.49 = (f32[768]{0:T(1024)S(1)}, f32[768,2304]{1,0:T(8,128)S(1)}) fusion(bf16[2304,384]{1,0:T(8,128)(2,1)S(1)} %get-tuple-element.177, s32[]{:T(128)S(6)} %select_n.29, bf16[768,384]{1,0:T(8,128)(2,1)} %get-tuple-element.176, pred[768,2304]{1,0:T(32,128)(4,1)S(1)} %copy.32, pred[768,2304]{1,0:T(32,128)(4,1)S(1)} %copy.33, ...), kind=kOutput, calls=%fused_computation.53.clone.1 | convolution fusion | flops 235339008 | bytes 11410432 | tf_op jit(solution)/shard_map/while/body/eval_jaxpr/dot_general | solution.py:105
  203.6 1.1 fusion.50
  204.7 2.2 fusion.51
  206.9 0.7 dynamic_slice.34
  208.2 1.2 broadcast_in_dim.77
  209.4 1.9 copy.32
  211.8 1.9 copy.33
  213.7 3.3 %fusion.49 = (f32[768]{0:T(1024)S(1)}, f32[768,2304]{1,0:T(8,128)S(1)}) fusion(bf16[2304,384]{1,0:T(8,128)(2,1)S(1)} %get-tuple-element.177, s32[]{:T(128)S(6)} %select_n.29, bf16[768,384]{1,0:T(8,128)(2,1)} %get-tuple-element.176, pred[768,2304]{1,0:T(32,128)(4,1)S(1)} %copy.32, pred[768,2304]{1,0:T(32,128)(4,1)S(1)} %copy.33, ...), kind=kOutput, calls=%fused_computation.53.clone.1 | convolution fusion | flops 235339008 | bytes 11410432 | tf_op jit(solution)/shard_map/while/body/eval_jaxpr/dot_general | solution.py:105
  217.0 1.1 fusion.50
  218.1 2.2 fusion.51
  221.6 1.2 broadcast_in_dim.77
  222.8 1.9 copy.32
  225.2 1.9 copy.33
  227.1 3.3 %fusion.49 = (f32[768]{0:T(1024)S(1)}, f32[768,2304]{1,0:T(8,128)S(1)}) fusion(bf16[2304,384]{1,0:T(8,128)(2,1)S(1)} %get-tuple-element.177, s32[]{:T(128)S(6)} %select_n.29, bf16[768,384]{1,0:T(8,128)(2,1)} %get-tuple-element.176, pred[768,2304]{1,0:T(32,128)(4,1)S(1)} %copy.32, pred[768,2304]{1,0:T(32,128)(4,1)S(1)} %copy.33, ...), kind=kOutput, calls=%fused_computation.53.clone.1 | convolution fusion | flops 235339008 | bytes 11410432 | tf_op jit(solution)/shard_map/while/body/eval_jaxpr/dot_general | solution.py:105
  230.4 1.1 fusion.50
  231.5 2.2 fusion.51
  233.7 2.3 convert_element_type.42
  235.9 0.9 copy.22
  236.9 19.7 %all_to_all.16 = bf16[4,192,384]{2,1,0:T(8,128)(2,1)S(1)} all-to-all(bf16[4,192,384]{2,1,0:T(8,128)(2,1)S(1)} %copy.22), channel_id=1, replica_groups=mesh['dp'=2,'seq'=4,'head'=4] {'head'}, dimensions={0} | all-to-all | bytes 1179648 | tf_op jit(solution)/shard_map/all_to_all | solution.py:121
  256.7 4.2 %fusion.21 = bf16[1,192,1536]{2,1,0:T(8,128)(2,1)} fusion(bf16[192,1536]{1,0:T(8,128)(2,1)S(1)} %bitcast.69, bf16[1536,1536]{1,0:T(8,128)(2,1)} %all-gather.17.cloned.1.call-done), kind=kOutput, calls=%fused_computation.16 | convolution fusion | flops 906264576 | bytes 5898240 | tf_op jit(solution)/shard_map/dot_general | solution.py:123
  (66 shorter events, 7.5 us)
Async XLA Ops:
  6.5 3.4 %copy-start = (bf16[1,192,1536]{2,1,0:T(8,128)(2,1)S(1)}, bf16[1,192,1536]{2,1,0:T(8,128)(2,1)}, u32[]{:S(2)}) copy-start(bf16[1,192,1536]{2,1,0:T(8,128)(2,1)} %param.10) | copy-start | bytes 1769476
  6.5 3.4 %copy-start.4 = (f32[1536]{0:T(1024)S(1)}, f32[1536]{0:T(1024)}, u32[]{:S(2)}) copy-start(f32[1536]{0:T(1024)} %param.11) | copy-start | bytes 18436
  6.5 14.1 %all-gather.13.cloned.1.call-start = ((), (), s32[]{:S(2)}) async-start(), calls=%async_computation.4 | async-start | bytes 1769472 | tf_op jit(solution)/shard_map/all_gather | solution.py:76
  7.3 66.2 %all-gather.7.cloned.1.call-start = ((), (), s32[]{:S(2)}) async-start(), calls=%async_computation.1 | async-start | bytes 2949120 | tf_op jit(solution)/shard_map/all_gather | solution.py:58
  9.9 3.3 %copy-start.5 = (s32[1,6,12]{2,0,1:T(1,128)S(1)}, s32[1,6,12]{2,0,1:T(1,128)}, u32[]{:S(2)}) copy-start(s32[1,6,12]{2,0,1:T(1,128)} %param.16) | copy-start | bytes 868
  11.2 72.3 %all-gather.11.cloned.1.call-start = ((), (), s32[]{:S(2)}) async-start(), calls=%async_computation.3 | async-start | bytes 1769472 | tf_op jit(solution)/shard_map/all_gather | solution.py:71
  11.9 124.3 %all-gather.15.cloned.1.call-start = ((), (), s32[]{:S(2)}) async-start(), calls=%async_computation.5 | async-start | bytes 2949120 | tf_op jit(solution)/shard_map/all_gather | solution.py:122
  12.5 133.6 %all-gather.9.cloned.1.call-start = ((), (), s32[]{:S(2)}) async-start(), calls=%async_computation.2 | async-start | bytes 1769472 | tf_op jit(solution)/shard_map/all_gather | solution.py:66
  13.1 243.6 %all-gather.17.cloned.1.call-start = ((), (), s32[]{:S(2)}) async-start(), calls=%async_computation.6 | async-start | bytes 7077888 | tf_op jit(solution)/shard_map/all_gather | solution.py:125
  76.8 73.4 %collective-permute-start.2 = (bf16[768,384]{1,0:T(8,128)(2,1)S(1)}, bf16[768,384]{1,0:T(8,128)(2,1)S(1)}, u32[]{:S(2)}, u32[]{:S(2)}) collective-permute-start(bf16[768,384]{1,0:T(8,128)(2,1)S(1)} %convolution_convert_fusion.1), channel_id=1, source_target_pairs={{0,4},{4,8},{8,12},{1,5},{5,9},{9,13},{2,6},{6,10},{10,14},{3,7},{... | collective-permute-start | bytes 1769480 | tf_op jit(solution)/shard_map/ppermute | solution.py:18
  80.0 70.3 %collective-permute-start.3 = (bf16[768,384]{1,0:T(8,128)(2,1)S(1)}, bf16[768,384]{1,0:T(8,128)(2,1)}, u32[]{:S(2)}, u32[]{:S(2)}) collective-permute-start(bf16[768,384]{1,0:T(8,128)(2,1)S(1)} %convolution_convert_fusion.1), channel_id=1, source_target_pairs={{4,0},{8,4},{12,8},{5,1},{9,5},{13,9},{6,2},{10,6},{14,10},{7,3},{... | collective-permute-start | bytes 1769480 | tf_op jit(solution)/shard_map/ppermute | solution.py:18
  86.9 63.4 %copy-start.2 = (bf16[768,384]{1,0:T(8,128)(2,1)}, bf16[768,384]{1,0:T(8,128)(2,1)S(1)}, u32[]{:S(2)}) copy-start(bf16[768,384]{1,0:T(8,128)(2,1)S(1)} %convolution_convert_fusion.2) | copy-start | bytes 1769476
  86.9 64.7 %collective-permute-start = (bf16[768,384]{1,0:T(8,128)(2,1)S(1)}, bf16[768,384]{1,0:T(8,128)(2,1)}, u32[]{:S(2)}, u32[]{:S(2)}) collective-permute-start(bf16[768,384]{1,0:T(8,128)(2,1)S(1)} %convolution_convert_fusion.2), channel_id=1, source_target_pairs={{0,4},{4,8},{8,12},{1,5},{5,9},{9,13},{2,6},{6,10},{10,14},{3,7},{... | collective-permute-start | bytes 1769480 | tf_op jit(solution)/shard_map/ppermute | solution.py:18
  91.2 60.4 %collective-permute-start.1 = (bf16[768,384]{1,0:T(8,128)(2,1)S(1)}, bf16[768,384]{1,0:T(8,128)(2,1)}, u32[]{:S(2)}, u32[]{:S(2)}) collective-permute-start(bf16[768,384]{1,0:T(8,128)(2,1)S(1)} %convolution_convert_fusion.2), channel_id=1, source_target_pairs={{4,0},{8,4},{12,8},{5,1},{9,5},{13,9},{6,2},{10,6},{14,10},{7,3},{... | collective-permute-start | bytes 1769480 | tf_op jit(solution)/shard_map/ppermute | solution.py:18
  150.3 1.3 copy-start.3
  155.8 1.9 copy-start.1
  169.2 1.9 copy-start.1
  182.6 1.9 copy-start.1
  196.0 1.9 copy-start.1
  209.4 1.9 copy-start.1
  222.8 1.9 copy-start.1
Sparse Core Ops, SparseCore 0:
  8.9 11.6 all-gather.12
  22.2 51.2 all-gather.6
  75.0 8.4 all-gather.10
  84.9 51.2 all-gather.14
  137.6 8.4 all-gather.8
  147.5 15.6 all-gather.16
where the time goes:
time: 270 us; the launch traced here: 268 us
  waiting for transfers between devices  116 us (43%)
  matrix products  47.7 us (18%)
  local copies, waits for them, and re-layouts  41.7 us (15%)
  blocking collectives  19.7 us (7%)
  between operations  14.4 us (5%)
  other arithmetic  13.4 us (5%)
  starting transfers between devices  10.2 us (4%)
  loops' own time  4.66 us (2%)
    all_gather x1, waiting for transfers between devices, local(): gathered = lax.all_gather(normalized, 'head', axis=0, tiled=True)  52.8 us
    all_gather x1, waiting for transfers between devices, local(): full_rows = lax.all_gather(w_out, 'head', axis=0, tiled=True)  43.7 us
    all_to_all x1, blocking collectives, local(): lax.all_to_all(context, 'head', split_axis=0, concat_axis=1, tiled=True)  19.7 us
    dot_general x6, matrix products, head_context(): lax.dot_general(query_head, key_head, (((1,), (1,)), ((), ())), preferred...  19.7 us
    dot_general x6, matrix products, head_context(): jnp.dot(rounded, value_head, preferred_element_type=jnp.float32) / row_total  12.9 us
    reshape x6, local copies, waits for them, and re-layouts, permission(): jnp.repeat(jnp.repeat(offsets == 0, group_size, axis=0), group_size, axis=1)  11.5 us
    reshape x6, local copies, waits for them, and re-layouts, permission(): jnp.repeat(jnp.repeat(linked, group_size, axis=0), group_size, axis=1)  11.5 us
    ppermute x4, starting transfers between devices, from_behind(): lax.ppermute(value, axis, [(source, source + steps) for source in range(f...  10 us
  transfers between devices with their start and end apart: 10, of which 5 were waited for; matrix products, arithmetic and copies ran while one was open for 37% of the time, Pallas kernels for 0%

commit v1 on v0

v1 whole, which is shorter than its diff:
```python
import functools

import jax
import jax.numpy as jnp
from jax import lax
from jax.experimental import pallas as pl
from jax.experimental.pallas import tpu as pltpu
from jax.sharding import PartitionSpec as P

HD = 64
GROUP = 128
LANES = 128

epsilon = 1e-05

VMEM = pl.BlockSpec(memory_space=pltpu.VMEM)
SMEM = pl.BlockSpec(memory_space=pltpu.SMEM)
LIMIT = 56 * 1024 * 1024


def ring_successors(count):
    order = [0] + list(range(1, count, 2)) + list(range(count - 2 + count % 2, 0, -2))
    return {order[i]: order[(i + 1) % count] for i in range(count)}


def lookup(table, index):
    value = jnp.int32(table[0])
    for place in range(1, len(table)):
        value = jnp.where(index == place, jnp.int32(table[place]), value)
    return value


def project_kernel(place_ref, rows_ref, gain_ref, *refs):
    own, other, (query_ref, pair_ref) = refs[:3], refs[3:6], refs[6:]
    values = rows_ref[...].astype(jnp.float32)
    center = values - jnp.mean(values, axis=-1, keepdims=True)
    spread = jnp.mean(center * center, axis=-1, keepdims=True)
    normalized = (center * lax.rsqrt(spread + epsilon) * gain_ref[...]).astype(jnp.bfloat16)
    depth = own[0].shape[0]
    low, high = normalized[:, :depth], normalized[:, depth:]
    first = place_ref[0] == 0
    mine = jnp.where(first, low, high)
    theirs = jnp.where(first, high, low)
    width = own[0].shape[1]
    sums = [
        jnp.dot(mine, a[...], preferred_element_type=jnp.float32)
        + jnp.dot(theirs, b[...], preferred_element_type=jnp.float32)
        for a, b in zip(own, other)
    ]
    query_ref[...] = (sums[0].astype(jnp.bfloat16).astype(jnp.float32) * (HD ** -0.5)).astype(jnp.bfloat16)
    pair_ref[:, :width] = sums[1].astype(jnp.bfloat16)
    pair_ref[:, width:] = sums[2].astype(jnp.bfloat16)


def project(place, rows, gain, own, other):
    count, width = rows.shape[0], own[0].shape[1]
    return pl.pallas_call(
        project_kernel,
        out_shape=(
            jax.ShapeDtypeStruct((count, width), jnp.bfloat16),
            jax.ShapeDtypeStruct((count, 2 * width), jnp.bfloat16),
        ),
        in_specs=[SMEM] + [VMEM] * 8,
        out_specs=(VMEM, VMEM),
        compiler_params=pltpu.CompilerParams(vmem_limit_bytes=LIMIT),
        cost_estimate=pl.CostEstimate(
            flops=2 * count * rows.shape[1] * 3 * width,
            bytes_accessed=2 * (rows.shape[1] * 3 * width + count * (rows.shape[1] + 3 * width)),
            transcendentals=count,
        ),
        name="project",
    )(place, rows, gain, *own, *other)


def attend_kernel(steps, groups, reach, place_ref, band_ref, *refs):
    queries = refs[:steps]
    owns = refs[steps:2 * steps]
    sides = refs[2 * steps:4 * steps]
    outs = refs[4 * steps:5 * steps]
    q_all, k_all, v_all, vt_all, score, ctx, chosen, limits = refs[5 * steps:]
    rows, width = queries[0].shape
    pairs = width // LANES
    block = steps * rows
    core, first_group, total, length = (place_ref[i] for i in range(4))
    chip_base = jnp.where(core == 0, 2 * block, 0)
    link_base = jnp.where(core == 0, 0, 2 * block)
    for step in range(steps):
        at = place_ref[4 + step] * rows
        q_at = pl.ds(pl.multiple_of(at, 64), rows)
        for pair in range(pairs):
            cols = slice(pair * LANES, (pair + 1) * LANES)
            q_all[pair, q_at, :] = queries[step][:, cols]
        for source, base in ((owns[step], block), (sides[step], chip_base), (sides[steps + step], link_base)):
            to = pl.ds(pl.multiple_of(base + at, 64), rows)
            for pair in range(pairs):
                k_all[pair, to, :] = source[:, pair * LANES:(pair + 1) * LANES]
                v_all[pair, to, :] = source[:, width + pair * LANES:width + (pair + 1) * LANES]

    def turn(index, carry):
        for pair in range(pairs):
            vt_all[pair, index] = v_all[pair, pl.ds(pl.multiple_of(index * GROUP, GROUP), GROUP), :].T
        return carry

    lax.fori_loop(0, 3 * groups, turn, 0)

    slots = 2 * reach + 2

    def choose(group, carry):
        for slot in range(slots):
            chosen[group * slots + slot] = groups + group
            limits[group * slots + slot] = 0
        limits[group * slots] = GROUP
        count = jnp.int32(1)
        for column in range(2 * reach):
            offset = column - reach if column < reach else column - reach + 1
            there = first_group + group + offset
            left = length - there * GROUP
            good = (there >= 0) & (there < total) & (band_ref[group, column] == 1) & (left > 0)
            chosen[group * slots + count] = jnp.where(good, groups + group + offset, groups + group)
            limits[group * slots + count] = jnp.where(good, jnp.minimum(left, GROUP), 0)
            count = count + good.astype(jnp.int32)

        def run(size):
            half_mask = lax.broadcasted_iota(jnp.int32, (GROUP, LANES), 1) < HD
            row_ids = lax.broadcasted_iota(jnp.int32, (GROUP, 2 * GROUP), 0)

            def one_pair(pair, inner):
                own = q_all[pair, pl.ds(pl.multiple_of(group * GROUP, GROUP), GROUP), :]
                zero = jnp.zeros_like(own)
                both = jnp.concatenate(
                    [jnp.where(half_mask, own, zero), jnp.where(half_mask, zero, own)], axis=0
                ).T
                best = None
                for slot in range(0, size, 2):
                    tiles = []
                    for one in (slot, slot + 1):
                        index = chosen[group * slots + one]
                        tiles.append(k_all[pair, pl.ds(pl.multiple_of(index * GROUP, GROUP), GROUP), :])
                    got = jnp.dot(jnp.concatenate(tiles, axis=0), both, preferred_element_type=jnp.float32)
                    for one in (slot, slot + 1):
                        part = got[(one - slot) * GROUP:(one - slot + 1) * GROUP]
                        if one > 0:
                            part = jnp.where(row_ids < limits[group * slots + one], part, -jnp.inf)
                        score[one * GROUP:(one + 1) * GROUP, :] = part
                        top = jnp.max(part.reshape(GROUP // 8, 8, 2 * GROUP), axis=0)
                        best = top if best is None else jnp.maximum(best, top)
                row_max = jnp.max(best, axis=0, keepdims=True)
                total_sum = jnp.zeros((8, 2 * GROUP), jnp.float32)
                mixed = jnp.zeros((LANES, 2 * GROUP), jnp.float32)
                for slot in range(0, size, 2):
                    weights = jnp.exp(score[slot * GROUP:(slot + 2) * GROUP, :] - row_max)
                    total_sum += jnp.sum(weights.reshape(2 * GROUP // 8, 8, 2 * GROUP), axis=0)
                    tiles = [vt_all[pair, chosen[group * slots + one]] for one in (slot, slot + 1)]
                    mixed += jnp.dot(
                        jnp.concatenate(tiles, axis=1),
                        weights.astype(jnp.bfloat16),
                        preferred_element_type=jnp.float32,
                    )
                mixed = mixed / jnp.sum(total_sum, axis=0, keepdims=True)
                both_heads = jnp.concatenate([mixed[:HD, :GROUP], mixed[HD:, GROUP:]], axis=0)
                ctx[pair, pl.ds(pl.multiple_of(group * GROUP, GROUP), GROUP), :] = both_heads.T.astype(jnp.bfloat16)
                return inner

            lax.fori_loop(0, pairs, one_pair, 0)

        sizes = [size for size in (4, 8, 10) if size < slots] + [slots]
        for place, size in enumerate(sizes):
            low = sizes[place - 1] if place > 0 else 0

            @pl.when((count > low) & (count <= size))
            def _():
                run(size)

        return carry

    lax.fori_loop(0, groups, choose, 0)
    for step in range(steps):
        at = pl.ds(pl.multiple_of(place_ref[4 + steps + step] * rows, 64), rows)
        for pair in range(pairs):
            outs[step][:, pair * LANES:(pair + 1) * LANES] = ctx[pair, at, :]


def attend(place, band, queries, owns, chip_side, link_side):
    steps = len(queries)
    rows, width = queries[0].shape
    groups, reach = band.shape[0], band.shape[1] // 2
    pairs, block = width // LANES, steps * rows
    slots = 2 * reach + 2
    work = block * (2 * reach + 1) * GROUP * (width // HD)
    return pl.pallas_call(
        functools.partial(attend_kernel, steps, groups, reach),
        out_shape=(jax.ShapeDtypeStruct((rows, width), jnp.bfloat16),) * steps,
        in_specs=[SMEM, SMEM] + [VMEM] * (4 * steps),
        out_specs=(VMEM,) * steps,
        scratch_shapes=[
            pltpu.VMEM((pairs, block, LANES), jnp.bfloat16),
            pltpu.VMEM((pairs, 3 * block, LANES), jnp.bfloat16),
            pltpu.VMEM((pairs, 3 * block, LANES), jnp.bfloat16),
            pltpu.VMEM((pairs, 3 * groups, LANES, GROUP), jnp.bfloat16),
            pltpu.VMEM((slots * GROUP, 2 * GROUP), jnp.float32),
            pltpu.VMEM((pairs, block, LANES), jnp.bfloat16),
            pltpu.SMEM((groups * slots,), jnp.int32),
            pltpu.SMEM((groups * slots,), jnp.int32),
        ],
        compiler_params=pltpu.CompilerParams(vmem_limit_bytes=LIMIT),
        cost_estimate=pl.CostEstimate(
            flops=8 * work * HD, bytes_accessed=2 * width * block * 8, transcendentals=work
        ),
        name="attend",
    )(place, band, *queries, *owns, *chip_side, *link_side)


def output_kernel(steps, place_ref, weight_ref, *refs):
    total = None
    for step in range(steps):
        part = jnp.dot(
            refs[step][...], weight_ref[place_ref[step]], preferred_element_type=jnp.float32
        )
        total = part if total is None else total + part
    refs[steps][0] = total.astype(jnp.bfloat16)


def output(place, weight, contexts):
    steps = len(contexts)
    rows, width = contexts[0].shape
    columns = weight.shape[2]
    return pl.pallas_call(
        functools.partial(output_kernel, steps),
        out_shape=jax.ShapeDtypeStruct((1, rows, columns), jnp.bfloat16),
        in_specs=[SMEM] + [VMEM] * (1 + steps),
        out_specs=VMEM,
        compiler_params=pltpu.CompilerParams(vmem_limit_bytes=LIMIT),
        cost_estimate=pl.CostEstimate(
            flops=2 * rows * width * steps * columns,
            bytes_accessed=2 * (width * steps * columns + 2 * rows * columns),
            transcendentals=0,
        ),
        name="output",
    )(place, weight, *contexts)


def local(frames, norm_gain, w_query, w_key, w_value, w_out, group_band, lengths):
    cores, seqs, layers = lax.axis_size("dp"), lax.axis_size("seq"), lax.axis_size("head")
    core, seq, layer = lax.axis_index("dp"), lax.axis_index("seq"), lax.axis_index("head")
    groups = group_band.shape[1]
    here = [(c, s) for c in range(cores) for s in range(seqs)]

    def home(c, s):
        return s % 2, s // 2 * 2 + c

    def flat(c, s, z=None):
        return c * seqs + s if z is None else (c * seqs + s) * layers + z

    def moved(value, shift):
        pairs = [(flat(c, s, z), flat(*home(c, s), shift(z))) for c, s in here for z in range(layers)]
        return lax.ppermute(value, ("dp", "seq", "head"), pairs)

    after = ring_successors(layers)
    before = {after[z]: z for z in after}
    swap = [(c, cores - 1 - c) for c in range(cores)]
    over_link = [(flat(1, s), flat(0, s + 2)) for s in range(seqs - 2)]
    over_link += [(flat(0, s + 2), flat(1, s)) for s in range(seqs - 2)]

    ring = [(z, after[z]) for z in range(layers)]
    rows = frames[0]
    blocks = [None, moved(rows, lambda z: after[z])]
    blocks[0] = moved(rows, lambda z: z)
    for _ in range(2, layers):
        blocks.append(lax.ppermute(blocks[-1], "head", ring))
    own = (w_query, w_key, w_value)
    other = lax.ppermute(own, "dp", swap)
    facts = jnp.concatenate([group_band[0], jnp.broadcast_to(lengths[:, None], (1, group_band.shape[2]))], axis=0)
    facts = lax.ppermute(facts, ("dp", "seq"), [(flat(c, s), flat(*home(c, s))) for c, s in here])

    share = 4 if seqs % 4 == 0 else (2 if seqs % 2 == 0 else 1)
    part = w_out.shape[0] // share
    piece = lax.dynamic_slice_in_dim(w_out, seq % share * part, part, 0)
    pieces = lax.all_gather(piece, "head", axis=0)
    sets = [list(range(s, s + share)) for s in range(0, seqs, share)]
    pieces = lax.all_gather(pieces, "seq", axis=0, axis_index_groups=sets)
    pieces = lax.all_gather(pieces, "dp", axis=0)
    weight = jnp.transpose(pieces, (2, 1, 3, 0, 4)).reshape(layers, w_out.shape[0], cores * w_out.shape[1])

    gain = norm_gain[None, :]
    core_at = core[None].astype(jnp.int32)
    queries, owns, chip_side, link_side = [], [], [], []
    for rows in blocks:
        query, pair = project(core_at, rows, gain, own, other)
        queries.append(query)
        owns.append(pair)
        link_side.append(lax.ppermute(pair, ("dp", "seq"), over_link))
        chip_side.append(lax.ppermute(pair, "dp", swap))

    ids = [layer]
    for _ in range(1, layers):
        ids.append(lookup([before[z] for z in range(layers)], ids[-1]))
    targets = [lax.rem(layer + shift, layers) for shift in range(layers)]
    place = [core, (seq // 2 * 2 + core) * groups, groups * seqs, facts[groups, 0]] + ids + targets
    place = jnp.stack([jnp.asarray(value, jnp.int32) for value in place])
    contexts = attend(place, facts[:groups], queries, owns, chip_side, link_side)
    arrived = [
        moved(context, lambda z, shift=shift: (z + shift) % layers) for shift, context in enumerate(contexts)
    ]
    sources = jnp.stack([lax.rem(layer + layers - shift, layers) for shift in range(layers)]).astype(jnp.int32)
    return output(sources, weight, arrived)


def solution(mesh):
    return jax.shard_map(
        local,
        mesh=mesh,
        in_specs=(
            P("dp", ("seq", "head"), None),
            P(),
            P("dp", "head"),
            P("dp", "head"),
            P("dp", "head"),
            P("head", "dp"),
            P("dp", "seq", None),
            P("dp"),
        ),
        out_specs=P("dp", ("seq", "head"), None),
        check_vma=False,
    )
```

time: 270 us -> 203 us (0.75)
  waiting for transfers between devices: 116 us -> 67.4 us
  matrix products: 47.7 us -> 0 us
  Pallas kernels: 0 us -> 43 us
  starting transfers between devices: 10.2 us -> 33.6 us
  local copies, waits for them, and re-layouts: 41.7 us -> 28.1 us
  other arithmetic: 13.4 us -> 0.58 us
  loops' own time: 4.66 us -> 0 us
  blocking collectives: 19.7 us -> 16.2 us
    all_gather x6 -> x2, waiting for transfers between devices: 113 us -> 41 us  [the longest x1 41 us: local(): pieces = lax.all_gather(pieces, 'seq', axis=0, axis_index_groups=sets)]
    dot_general x16 -> x0, matrix products: 47.7 us -> none  [the longest x6 19.7 us: head_context(): lax.dot_general(query_head, key_head, (((1,), (1,)), ((), ())), preferred...]
    pallas_call x0 -> x6, Pallas kernels: none -> 43 us  [the longest x1 21.2 us: attend(): pl.pallas_call(functools.partial(attend_kernel, steps, groups, reach), ou...]
    ppermute x4 -> x20, waiting for transfers between devices: 0.01 us -> 26.4 us  [the longest x6 14.4 us: moved(): return lax.ppermute(value, ('dp', 'seq', 'head'), pairs)]
    ppermute x4 -> x20, starting transfers between devices: 10 us -> 33.6 us  [the longest x6 15.4 us: moved(): return lax.ppermute(value, ('dp', 'seq', 'head'), pairs)]
    all_to_all x1 -> x0, blocking collectives: 19.7 us -> none  [local(): lax.all_to_all(context, 'head', split_axis=0, concat_axis=1, tiled=True)]
    all_gather x0 -> x1, blocking collectives: none -> 16.2 us  [local(): pieces = lax.all_gather(piece, 'head', axis=0)]
    reshape x12 -> x1, local copies, waits for them, and re-layouts: 22.9 us -> 11.2 us  [local(): jnp.transpose(pieces, (2, 1, 3, 0, 4))]
  transfers between devices with their start and end apart: 10 -> 22, of which waited for: 5 -> 5; matrix products, arithmetic and copies ran while one was open for 37% -> 12% of each run, Pallas kernels for 0% -> 19%
where the time goes in v1:
time: 203 us
  waiting for transfers between devices  67.4 us (33%)
  Pallas kernels  43 us (21%)
  starting transfers between devices  33.6 us (17%)
  local copies, waits for them, and re-layouts  28.1 us (14%)
  blocking collectives  16.2 us (8%)
  between operations  14.4 us (7%)
    all_gather x1, waiting for transfers between devices, local(): pieces = lax.all_gather(pieces, 'seq', axis=0, axis_index_groups=sets)  41 us
    pallas_call x1, Pallas kernels, attend(): pl.pallas_call(functools.partial(attend_kernel, steps, groups, reach), ou...  21.2 us
    pallas_call x4, Pallas kernels, project(): pl.pallas_call(project_kernel, out_shape=(jax.ShapeDtypeStruct((count, wi...  17.1 us
    all_gather x1, blocking collectives, local(): pieces = lax.all_gather(piece, 'head', axis=0)  16.2 us
    ppermute x6, starting transfers between devices, moved(): return lax.ppermute(value, ('dp', 'seq', 'head'), pairs)  15.4 us
    ppermute x6, waiting for transfers between devices, moved(): return lax.ppermute(value, ('dp', 'seq', 'head'), pairs)  14.4 us
    reshape x1, local copies, waits for them, and re-layouts, local(): jnp.transpose(pieces, (2, 1, 3, 0, 4))  11.2 us
    ppermute x4, starting transfers between devices, local(): link_side.append(lax.ppermute(pair, ('dp', 'seq'), over_link))  10.1 us
  transfers between devices with their start and end apart: 22, of which 5 were waited for; matrix products, arithmetic and copies ran while one was open for 12% of the time, Pallas kernels for 19%

profile of v1, /device:TPU:1, one launch (start us, length us, event | category | flops | bytes accessed | tf_op | source)
XLA Modules:
  0.0 203.3 jit_solution(16852537112863907556)
XLA Ops:
  6.5 1.1 copy-done
  7.6 16.2 %all-gather = bf16[384,768]{1,0:T(8,128)(2,1)} all-gather(bf16[96,768]{1,0:T(8,128)(2,1)S(1)} %constant_dynamic-slice_fusion), channel_id=2, replica_groups=mesh['dp'=2,'seq'=4,'head'=4] {'head'}, dimensions={0}, use_global_device_ids=true | all-gather | bytes 737280 | tf_op jit(solution)/shard_map/all_gather | solution.py:278
  23.8 0.0 all-gather.6.cloned.1.call-update
  23.8 0.0 all-gather.8.cloned.1.call-start
  23.8 41.0 %all-gather.6.cloned.1.call-done = bf16[16,96,768]{2,1,0:T(8,128)(2,1)} async-done(((bf16[4,96,768]{2,1,0:T(8,128)(2,1)}), bf16[16,96,768]{2,1,0:T(8,128)(2,1)}) %all-gather.6.cloned.1.call-update) | async-done | bytes 2359312 | tf_op jit(solution)/shard_map/all_gather | solution.py:280
  64.8 0.0 all-gather.8.cloned.1.call-update
  64.9 0.0 copy-start.11
  64.9 2.7 %collective-permute-start.5 = (bf16[192,1536]{1,0:T(8,128)(2,1)}, bf16[192,1536]{1,0:T(8,128)(2,1)S(1)}, u32[]{:S(2)}, u32[]{:S(2)}) collective-permute-start(bf16[192,1536]{1,0:T(8,128)(2,1)} %bitcast.28), channel_id=1, source_target_pairs={{0,1},{1,3},{2,0},{3,2},{4,17},{5,19},{6,16},{7,18},{8,9},{9,11},{... | collective-permute-start | bytes 1769480 | tf_op jit(solution)/shard_map/ppermute | solution.py:256
  67.6 14.4 %collective-permute-done.5.rows_ref = bf16[192,1536]{1,0:T(8,128)(2,1)S(1)} collective-permute-done((bf16[192,1536]{1,0:T(8,128)(2,1)}, bf16[192,1536]{1,0:T(8,128)(2,1)S(1)}, u32[]{:S(2)}, u32[]{:S(2)}) %collective-permute-start.5) | collective-permute-done | bytes 589856 | tf_op jit(solution)/shard_map/ppermute | solution.py:256
  82.0 0.9 collective-permute-start.6
  82.9 3.6 %collective-permute-start.1 = (bf16[192,1536]{1,0:T(8,128)(2,1)}, bf16[192,1536]{1,0:T(8,128)(2,1)}, u32[]{:S(2)}, u32[]{:S(2)}) collective-permute-start(bf16[192,1536]{1,0:T(8,128)(2,1)} %bitcast.29), channel_id=1, source_target_pairs={{0,0},{1,1},{2,2},{3,3},{4,16},{5,17},{6,18},{7,19},{8,8},{9,9},{1... | collective-permute-start | bytes 1769480 | tf_op jit(solution)/shard_map/ppermute | solution.py:256
  86.5 2.7 %collective-permute-start.2 = (bf16[768,384]{1,0:T(8,128)(2,1)}, bf16[768,384]{1,0:T(8,128)(2,1)S(1)}, u32[]{:S(2)}, u32[]{:S(2)}) collective-permute-start(bf16[768,384]{1,0:T(8,128)(2,1)} %refs_0_.7), channel_id=1, source_target_pairs={{0,16},{16,0},{1,17},{17,1},{2,18},{18,2},{3,19},{19,3},{4,20},{20... | collective-permute-start | bytes 1769480 | tf_op jit(solution)/shard_map/ppermute | solution.py:271
  89.1 0.0 collective-permute-start.3
  89.1 0.5 collective-permute-start.4
  89.7 7.5 %collective-permute-done.6.rows_ref = bf16[192,1536]{1,0:T(8,128)(2,1)S(1)} collective-permute-done((bf16[192,1536]{1,0:T(8,128)(2,1)S(1)}, bf16[192,1536]{1,0:T(8,128)(2,1)S(1)}, u32[]{:S(2)}, u32[]{:S(2)}) %collective-permute-start.6) | collective-permute-done | bytes 589856 | tf_op jit(solution)/shard_map/ppermute | solution.py:269
  97.2 0.6 collective-permute-start.7
  97.8 1.3 broadcast_in_dim.5.gain_ref
  99.1 0.0 collective-permute-done.1.rows_ref
  99.1 0.0 collective-permute-done.2.refs_3_
  99.1 0.0 collective-permute-done.3.refs_4_
  99.1 0.0 collective-permute-done.4.refs_5_
  99.1 0.8 copy-done.1
  99.9 0.2 copy-done.2
  100.1 0.2 copy-done.3
  100.3 4.3 %project.4 = (bf16[192,384]{1,0:T(8,128)(2,1)}, bf16[192,768]{1,0:T(8,128)(2,1)}) custom-call(s32[1]{0:T(128)} %bitcast.8.place_ref, bf16[192,1536]{1,0:T(8,128)(2,1)} %collective-permute-done.1.rows_ref, f32[1,1536]{1,0:T(1,128)} %broadcast_in_dim.5.gain_ref, bf16[768,384]{1,0:T(8,128)(2,1)} %refs_0_.7, bf16[768,384]{1,0:T(8,128)(2,1)} %refs_1_.7, ...), custom_call_target="tpu_custom_call" | custom-call | flops 679477248 | bytes 4571136 | tf_op jit(solution)/shard_map/project/pallas_call | solution.py:57
  104.6 1.4 collective-permute-start.8
  106.0 4.3 %project.5 = (bf16[192,384]{1,0:T(8,128)(2,1)}, bf16[192,768]{1,0:T(8,128)(2,1)}) custom-call(s32[1]{0:T(128)} %bitcast.8.place_ref, bf16[192,1536]{1,0:T(8,128)(2,1)} %copy-done.6, f32[1,1536]{1,0:T(1,128)} %broadcast_in_dim.5.gain_ref, bf16[768,384]{1,0:T(8,128)(2,1)} %refs_0_.7, bf16[768,384]{1,0:T(8,128)(2,1)} %refs_1_.7, bf16[768,384]{1,0:T(8,128)(2,1)} %refs_2_.7, ...), custom_call_target="tpu_custom_call" | custom-call | flops 679477248 | bytes 4571136 | tf_op jit(solution)/shard_map/project/pallas_call | solution.py:57
  110.3 0.0 collective-permute-start.9
  110.3 2.6 %collective-permute-start.12 = (bf16[192,768]{1,0:T(8,128)(2,1)}, bf16[192,768]{1,0:T(8,128)(2,1)S(1)}, u32[]{:S(2)}, u32[]{:S(2)}) collective-permute-start(bf16[192,768]{1,0:T(8,128)(2,1)} %get-tuple-element.21.refs_4_), channel_id=1, source_target_pairs={{16,8},{20,12},{8,16},{12,20},{17,9},{21,13},{9,17},{13,21},{18,10... | collective-permute-start | bytes 884744 | tf_op jit(solution)/shard_map/ppermute | solution.py:291
  113.5 1.9 collective-permute-start
  115.5 4.3 %project.6 = (bf16[192,384]{1,0:T(8,128)(2,1)}, bf16[192,768]{1,0:T(8,128)(2,1)}) custom-call(s32[1]{0:T(128)} %bitcast.8.place_ref, bf16[192,1536]{1,0:T(8,128)(2,1)} %copy-done.4, f32[1,1536]{1,0:T(1,128)} %broadcast_in_dim.5.gain_ref, bf16[768,384]{1,0:T(8,128)(2,1)} %refs_0_.7, bf16[768,384]{1,0:T(8,128)(2,1)} %refs_1_.7, bf16[768,384]{1,0:T(8,128)(2,1)} %refs_2_.7, ...), custom_call_target="tpu_custom_call" | custom-call | flops 679477248 | bytes 4571136 | tf_op jit(solution)/shard_map/project/pallas_call | solution.py:57
  119.7 0.0 collective-permute-done.7.rows_ref
  119.7 1.9 collective-permute-start.13
  121.7 4.3 %project.7 = (bf16[192,384]{1,0:T(8,128)(2,1)}, bf16[192,768]{1,0:T(8,128)(2,1)}) custom-call(s32[1]{0:T(128)} %bitcast.8.place_ref, bf16[192,1536]{1,0:T(8,128)(2,1)} %copy-done.5, f32[1,1536]{1,0:T(1,128)} %broadcast_in_dim.5.gain_ref, bf16[768,384]{1,0:T(8,128)(2,1)} %refs_0_.7, bf16[768,384]{1,0:T(8,128)(2,1)} %refs_1_.7, bf16[768,384]{1,0:T(8,128)(2,1)} %refs_2_.7, ...), custom_call_target="tpu_custom_call" | custom-call | flops 679477248 | bytes 4571136 | tf_op jit(solution)/shard_map/project/pallas_call | solution.py:57
  125.9 0.0 collective-permute-done
  125.9 0.1 collective-permute-start.10
  126.0 0.0 collective-permute-done.8.refs_8_
  126.0 0.0 copy-start.12
  126.0 3.6 %collective-permute-start.14 = (bf16[192,768]{1,0:T(8,128)(2,1)}, bf16[192,768]{1,0:T(8,128)(2,1)S(1)}, u32[]{:S(2)}, u32[]{:S(2)}) collective-permute-start(bf16[192,768]{1,0:T(8,128)(2,1)} %get-tuple-element.23.refs_6_), channel_id=1, source_target_pairs={{16,8},{20,12},{8,16},{12,20},{17,9},{21,13},{9,17},{13,21},{18,10... | collective-permute-start | bytes 884744 | tf_op jit(solution)/shard_map/ppermute | solution.py:291
  129.7 0.0 collective-permute-done.9.refs_9_
  129.7 0.1 collective-permute-start.11
  129.8 0.0 collective-permute-done.12.refs_12_
  129.8 1.9 collective-permute-start.15
  131.8 0.5 slice.6
  132.3 1.2 stack.54.place_ref
  133.6 0.0 collective-permute-done.13.refs_13_
  133.6 0.0 collective-permute-done.10.refs_10_
  133.6 0.7 collective-permute-done.14.refs_14_
  134.3 0.0 collective-permute-done.11.refs_11_
  134.3 3.8 %collective-permute-done.15.refs_15_ = bf16[192,768]{1,0:T(8,128)(2,1)S(1)} collective-permute-done((bf16[192,768]{1,0:T(8,128)(2,1)}, bf16[192,768]{1,0:T(8,128)(2,1)S(1)}, u32[]{:S(2)}, u32[]{:S(2)}) %collective-permute-start.15) | collective-permute-done | bytes 294944 | tf_op jit(solution)/shard_map/ppermute | solution.py:291
  138.1 0.7 copy-done.19
  138.8 21.2 %attend.1 = (bf16[192,384]{1,0:T(8,128)(2,1)}, bf16[192,384]{1,0:T(8,128)(2,1)}, bf16[192,384]{1,0:T(8,128)(2,1)}, bf16[192,384]{1,0:T(8,128)(2,1)}) custom-call(s32[12]{0:T(128)} %stack.54.place_ref, s32[6,12]{1,0:T(8,128)} %bitcast.30, bf16[192,384]{1,0:T(8,128)(2,1)} %get-tuple-element.17.refs_0_, bf16[192,384]{1,0:T(8,128)(2,1)} %get-tuple-element.18.refs_1_, ...), custom_call_target="tpu_custom_call" | custom-call | flops 3925868544 | bytes 4718592 | tf_op jit(solution)/shard_map/attend/pallas_call | solution.py:190
  160.0 1.9 collective-permute-start.16
  161.9 4.6 %collective-permute-start.17 = (bf16[192,384]{1,0:T(8,128)(2,1)}, bf16[192,384]{1,0:T(8,128)(2,1)S(1)}, u32[]{:S(2)}, u32[]{:S(2)}) collective-permute-start(bf16[192,384]{1,0:T(8,128)(2,1)} %get-tuple-element.26), channel_id=1, source_target_pairs={{0,1},{1,2},{2,3},{3,0},{4,17},{5,18},{6,19},{7,16},{8,9},{9,10},{... | collective-permute-start | bytes 442376 | tf_op jit(solution)/shard_map/ppermute | solution.py:256
  166.5 2.6 %collective-permute-start.19 = (bf16[192,384]{1,0:T(8,128)(2,1)}, bf16[192,384]{1,0:T(8,128)(2,1)S(1)}, u32[]{:S(2)}, u32[]{:S(2)}) collective-permute-start(bf16[192,384]{1,0:T(8,128)(2,1)} %get-tuple-element.28), channel_id=1, source_target_pairs={{0,3},{1,0},{2,1},{3,2},{4,19},{5,16},{6,17},{7,18},{8,11},{9,8},{... | collective-permute-start | bytes 442376 | tf_op jit(solution)/shard_map/ppermute | solution.py:256
  169.1 0.6 pad_add_fusion.place_ref
  169.7 9.4 %copy.10 = bf16[4,4,96,2,768]{4,3,2,1,0:T(2,128)(2,1)} copy(bf16[4,4,96,2,768]{4,2,0,1,3:T(8,128)(2,1)} %bitcast.24) | data formatting | bytes 9437184 | tf_op jit(solution)/shard_map/transpose | solution.py:282
  179.0 11.2 %reshape.6.weight_ref = bf16[4,384,1536]{2,1,0:T(8,128)(2,1)} reshape(bf16[4,4,96,2,768]{4,3,2,1,0:T(2,128)(2,1)} %copy.10) | data formatting | bytes 9437184 | tf_op jit(solution)/shard_map/reshape | solution.py:282
  190.3 0.0 collective-permute-done.17.refs_1_
  190.3 0.6 copy-done.7
  191.0 0.1 copy-done.8
  191.0 0.1 copy-done.9
  191.1 0.7 copy-done.10
  191.8 4.7 %output.1 = bf16[1,192,1536]{2,1,0:T(8,128)(2,1)} custom-call(s32[4]{0:T(128)} %pad_add_fusion.place_ref, bf16[4,384,1536]{2,1,0:T(8,128)(2,1)} %reshape.6.weight_ref, bf16[192,384]{1,0:T(8,128)(2,1)} %copy-done.7, bf16[192,384]{1,0:T(8,128)(2,1)} %copy-done.8, bf16[192,384]{1,0:T(8,128)(2,1)} %copy-done.9, bf16[192,384]{1,0:T(8,128)(2,1)} %copy-done.10), custom_call_target="tpu_custom_call" | custom-call | flops 905969664 | bytes 5898240 | tf_op jit(solution)/shard_map/output/pallas_call | solution.py:227
  (40 shorter events, 0.1 us)
Async XLA Ops:
  6.5 1.1 copy-start
  6.5 58.3 %all-gather.6.cloned.1.call-start = ((), (), s32[]{:S(2)}) async-start(), calls=%async_computation | async-start | bytes 2949120 | tf_op jit(solution)/shard_map/all_gather | solution.py:280
  23.8 145.9 %all-gather.8.cloned.1.call-start = ((), (), s32[]{:S(2)}) async-start(), calls=%async_computation.1 | async-start | bytes 7077888 | tf_op jit(solution)/shard_map/all_gather | solution.py:281
  64.9 48.0 %copy-start.11 = (s32[1,6,12]{2,0,1:T(1,128)S(1)}, s32[1,6,12]{2,0,1:T(1,128)}, u32[]{:S(2)}) copy-start(s32[1,6,12]{2,0,1:T(1,128)} %param.14) | copy-start | bytes 868
  64.9 17.1 %collective-permute-start.5 = (bf16[192,1536]{1,0:T(8,128)(2,1)}, bf16[192,1536]{1,0:T(8,128)(2,1)S(1)}, u32[]{:S(2)}, u32[]{:S(2)}) collective-permute-start(bf16[192,1536]{1,0:T(8,128)(2,1)} %bitcast.28), channel_id=1, source_target_pairs={{0,1},{1,3},{2,0},{3,2},{4,17},{5,19},{6,16},{7,18},{8,9},{9,11},{... | collective-permute-start | bytes 1769480 | tf_op jit(solution)/shard_map/ppermute | solution.py:256
  82.0 15.2 %copy-start.6 = (bf16[192,1536]{1,0:T(8,128)(2,1)}, bf16[192,1536]{1,0:T(8,128)(2,1)S(1)}, u32[]{:S(2)}) copy-start(bf16[192,1536]{1,0:T(8,128)(2,1)S(1)} %collective-permute-done.5.rows_ref) | copy-start | bytes 1769476
  82.0 15.2 %collective-permute-start.6 = (bf16[192,1536]{1,0:T(8,128)(2,1)S(1)}, bf16[192,1536]{1,0:T(8,128)(2,1)S(1)}, u32[]{:S(2)}, u32[]{:S(2)}) collective-permute-start(bf16[192,1536]{1,0:T(8,128)(2,1)S(1)} %collective-permute-done.5.rows_ref), channel_id=1, source_target_pairs={{0,1},{1,3},{2,0},{3,2},{4,5},{5,7},{6,4},{7,6},{8,9},{9,11},{10,8... | collective-permute-start | bytes 1769480 | tf_op jit(solution)/shard_map/ppermute | solution.py:269
  82.9 16.2 %collective-permute-start.1 = (bf16[192,1536]{1,0:T(8,128)(2,1)}, bf16[192,1536]{1,0:T(8,128)(2,1)}, u32[]{:S(2)}, u32[]{:S(2)}) collective-permute-start(bf16[192,1536]{1,0:T(8,128)(2,1)} %bitcast.29), channel_id=1, source_target_pairs={{0,0},{1,1},{2,2},{3,3},{4,16},{5,17},{6,18},{7,19},{8,8},{9,9},{1... | collective-permute-start | bytes 1769480 | tf_op jit(solution)/shard_map/ppermute | solution.py:256
  86.5 12.6 %collective-permute-start.2 = (bf16[768,384]{1,0:T(8,128)(2,1)}, bf16[768,384]{1,0:T(8,128)(2,1)S(1)}, u32[]{:S(2)}, u32[]{:S(2)}) collective-permute-start(bf16[768,384]{1,0:T(8,128)(2,1)} %refs_0_.7), channel_id=1, source_target_pairs={{0,16},{16,0},{1,17},{17,1},{2,18},{18,2},{3,19},{19,3},{4,20},{20... | collective-permute-start | bytes 1769480 | tf_op jit(solution)/shard_map/ppermute | solution.py:271
  89.1 9.9 %collective-permute-start.3 = (bf16[768,384]{1,0:T(8,128)(2,1)}, bf16[768,384]{1,0:T(8,128)(2,1)S(1)}, u32[]{:S(2)}, u32[]{:S(2)}) collective-permute-start(bf16[768,384]{1,0:T(8,128)(2,1)} %refs_1_.7), channel_id=1, source_target_pairs={{0,16},{16,0},{1,17},{17,1},{2,18},{18,2},{3,19},{19,3},{4,20},{20... | collective-permute-start | bytes 1769480 | tf_op jit(solution)/shard_map/ppermute | solution.py:271
  89.1 9.9 %collective-permute-start.4 = (bf16[768,384]{1,0:T(8,128)(2,1)}, bf16[768,384]{1,0:T(8,128)(2,1)S(1)}, u32[]{:S(2)}, u32[]{:S(2)}) collective-permute-start(bf16[768,384]{1,0:T(8,128)(2,1)} %refs_2_.7), channel_id=1, source_target_pairs={{0,16},{16,0},{1,17},{17,1},{2,18},{18,2},{3,19},{19,3},{4,20},{20... | collective-permute-start | bytes 1769480 | tf_op jit(solution)/shard_map/ppermute | solution.py:271
  97.2 18.3 %copy-start.4 = (bf16[192,1536]{1,0:T(8,128)(2,1)}, bf16[192,1536]{1,0:T(8,128)(2,1)S(1)}, u32[]{:S(2)}) copy-start(bf16[192,1536]{1,0:T(8,128)(2,1)S(1)} %collective-permute-done.6.rows_ref) | copy-start | bytes 1769476
  97.2 22.5 %collective-permute-start.7 = (bf16[192,1536]{1,0:T(8,128)(2,1)S(1)}, bf16[192,1536]{1,0:T(8,128)(2,1)S(1)}, u32[]{:S(2)}, u32[]{:S(2)}) collective-permute-start(bf16[192,1536]{1,0:T(8,128)(2,1)S(1)} %collective-permute-done.6.rows_ref), channel_id=1, source_target_pairs={{0,1},{1,3},{2,0},{3,2},{4,5},{5,7},{6,4},{7,6},{8,9},{9,11},{10,8... | collective-permute-start | bytes 1769480 | tf_op jit(solution)/shard_map/ppermute | solution.py:269
  99.1 0.8 copy-start.1
  99.1 1.0 copy-start.2
  99.1 1.2 copy-start.3
  104.6 21.4 %collective-permute-start.8 = (bf16[192,768]{1,0:T(8,128)(2,1)}, bf16[192,768]{1,0:T(8,128)(2,1)S(1)}, u32[]{:S(2)}, u32[]{:S(2)}) collective-permute-start(bf16[192,768]{1,0:T(8,128)(2,1)} %get-tuple-element.21.refs_4_), channel_id=1, source_target_pairs={{0,16},{16,0},{1,17},{17,1},{2,18},{18,2},{3,19},{19,3},{4,20},{20... | collective-permute-start | bytes 884744 | tf_op jit(solution)/shard_map/ppermute | solution.py:292
  110.3 19.4 %collective-permute-start.9 = (bf16[192,768]{1,0:T(8,128)(2,1)}, bf16[192,768]{1,0:T(8,128)(2,1)S(1)}, u32[]{:S(2)}, u32[]{:S(2)}) collective-permute-start(bf16[192,768]{1,0:T(8,128)(2,1)} %get-tuple-element.22.refs_5_), channel_id=1, source_target_pairs={{0,16},{16,0},{1,17},{17,1},{2,18},{18,2},{3,19},{19,3},{4,20},{20... | collective-permute-start | bytes 884744 | tf_op jit(solution)/shard_map/ppermute | solution.py:292
  110.3 19.5 %collective-permute-start.12 = (bf16[192,768]{1,0:T(8,128)(2,1)}, bf16[192,768]{1,0:T(8,128)(2,1)S(1)}, u32[]{:S(2)}, u32[]{:S(2)}) collective-permute-start(bf16[192,768]{1,0:T(8,128)(2,1)} %get-tuple-element.21.refs_4_), channel_id=1, source_target_pairs={{16,8},{20,12},{8,16},{12,20},{17,9},{21,13},{9,17},{13,21},{18,10... | collective-permute-start | bytes 884744 | tf_op jit(solution)/shard_map/ppermute | solution.py:291
  113.5 12.4 %collective-permute-start = (s32[7,12]{1,0:T(8,128)S(1)}, s32[7,12]{1,0:T(8,128)S(1)}, u32[]{:S(2)}, u32[]{:S(2)}) collective-permute-start(s32[7,12]{1,0:T(8,128)S(1)} %concatenate.3), channel_id=1, source_target_pairs={{0,0},{4,16},{8,8},{12,24},{16,4},{20,20},{24,12},{28,28},{1,1},{5... | collective-permute-start | bytes 1016 | tf_op jit(solution)/shard_map/ppermute | solution.py:273
  119.7 1.9 copy-start.5
  119.7 13.9 %collective-permute-start.13 = (bf16[192,768]{1,0:T(8,128)(2,1)}, bf16[192,768]{1,0:T(8,128)(2,1)S(1)}, u32[]{:S(2)}, u32[]{:S(2)}) collective-permute-start(bf16[192,768]{1,0:T(8,128)(2,1)} %get-tuple-element.22.refs_5_), channel_id=1, source_target_pairs={{16,8},{20,12},{8,16},{12,20},{17,9},{21,13},{9,17},{13,21},{18,10... | collective-permute-start | bytes 884744 | tf_op jit(solution)/shard_map/ppermute | solution.py:291
  125.9 12.1 %copy-start.20 = (s32[7,12]{1,0:T(8,128)}, s32[7,12]{1,0:T(8,128)S(1)}, u32[]{:S(2)}) copy-start(s32[7,12]{1,0:T(8,128)S(1)} %collective-permute-done) | copy-start | bytes 1012
  125.9 7.6 %collective-permute-start.10 = (bf16[192,768]{1,0:T(8,128)(2,1)}, bf16[192,768]{1,0:T(8,128)(2,1)S(1)}, u32[]{:S(2)}, u32[]{:S(2)}) collective-permute-start(bf16[192,768]{1,0:T(8,128)(2,1)} %get-tuple-element.23.refs_6_), channel_id=1, source_target_pairs={{0,16},{16,0},{1,17},{17,1},{2,18},{18,2},{3,19},{19,3},{4,20},{20... | collective-permute-start | bytes 884744 | tf_op jit(solution)/shard_map/ppermute | solution.py:292
  126.0 12.0 %copy-start.12 = (bf16[192,768]{1,0:T(8,128)(2,1)}, bf16[192,768]{1,0:T(8,128)(2,1)S(1)}, u32[]{:S(2)}) copy-start(bf16[192,768]{1,0:T(8,128)(2,1)S(1)} %collective-permute-done.8.refs_8_) | copy-start | bytes 884740
  126.0 8.3 %collective-permute-start.14 = (bf16[192,768]{1,0:T(8,128)(2,1)}, bf16[192,768]{1,0:T(8,128)(2,1)S(1)}, u32[]{:S(2)}, u32[]{:S(2)}) collective-permute-start(bf16[192,768]{1,0:T(8,128)(2,1)} %get-tuple-element.23.refs_6_), channel_id=1, source_target_pairs={{16,8},{20,12},{8,16},{12,20},{17,9},{21,13},{9,17},{13,21},{18,10... | collective-permute-start | bytes 884744 | tf_op jit(solution)/shard_map/ppermute | solution.py:291
  129.7 8.4 %copy-start.13 = (bf16[192,768]{1,0:T(8,128)(2,1)}, bf16[192,768]{1,0:T(8,128)(2,1)S(1)}, u32[]{:S(2)}) copy-start(bf16[192,768]{1,0:T(8,128)(2,1)S(1)} %collective-permute-done.9.refs_9_) | copy-start | bytes 884740
  129.7 4.6 %collective-permute-start.11 = (bf16[192,768]{1,0:T(8,128)(2,1)}, bf16[192,768]{1,0:T(8,128)(2,1)S(1)}, u32[]{:S(2)}, u32[]{:S(2)}) collective-permute-start(bf16[192,768]{1,0:T(8,128)(2,1)} %get-tuple-element.24.refs_7_), channel_id=1, source_target_pairs={{0,16},{16,0},{1,17},{17,1},{2,18},{18,2},{3,19},{19,3},{4,20},{20... | collective-permute-start | bytes 884744 | tf_op jit(solution)/shard_map/ppermute | solution.py:292
  129.8 8.3 %copy-start.14 = (bf16[192,768]{1,0:T(8,128)(2,1)}, bf16[192,768]{1,0:T(8,128)(2,1)S(1)}, u32[]{:S(2)}) copy-start(bf16[192,768]{1,0:T(8,128)(2,1)S(1)} %collective-permute-done.12.refs_12_) | copy-start | bytes 884740
  129.8 8.3 %collective-permute-start.15 = (bf16[192,768]{1,0:T(8,128)(2,1)}, bf16[192,768]{1,0:T(8,128)(2,1)S(1)}, u32[]{:S(2)}, u32[]{:S(2)}) collective-permute-start(bf16[192,768]{1,0:T(8,128)(2,1)} %get-tuple-element.24.refs_7_), channel_id=1, source_target_pairs={{16,8},{20,12},{8,16},{12,20},{17,9},{21,13},{9,17},{13,21},{18,10... | collective-permute-start | bytes 884744 | tf_op jit(solution)/shard_map/ppermute | solution.py:291
  133.6 4.5 %copy-start.15 = (bf16[192,768]{1,0:T(8,128)(2,1)}, bf16[192,768]{1,0:T(8,128)(2,1)S(1)}, u32[]{:S(2)}) copy-start(bf16[192,768]{1,0:T(8,128)(2,1)S(1)} %collective-permute-done.13.refs_13_) | copy-start | bytes 884740
  133.6 4.5 %copy-start.16 = (bf16[192,768]{1,0:T(8,128)(2,1)}, bf16[192,768]{1,0:T(8,128)(2,1)S(1)}, u32[]{:S(2)}) copy-start(bf16[192,768]{1,0:T(8,128)(2,1)S(1)} %collective-permute-done.10.refs_10_) | copy-start | bytes 884740
  134.3 3.8 %copy-start.17 = (bf16[192,768]{1,0:T(8,128)(2,1)}, bf16[192,768]{1,0:T(8,128)(2,1)S(1)}, u32[]{:S(2)}) copy-start(bf16[192,768]{1,0:T(8,128)(2,1)S(1)} %collective-permute-done.14.refs_14_) | copy-start | bytes 884740
  134.3 3.8 %copy-start.18 = (bf16[192,768]{1,0:T(8,128)(2,1)}, bf16[192,768]{1,0:T(8,128)(2,1)S(1)}, u32[]{:S(2)}) copy-start(bf16[192,768]{1,0:T(8,128)(2,1)S(1)} %collective-permute-done.11.refs_11_) | copy-start | bytes 884740
  138.1 0.7 copy-start.19
  160.0 30.3 %collective-permute-start.16 = (bf16[192,384]{1,0:T(8,128)(2,1)}, bf16[192,384]{1,0:T(8,128)(2,1)S(1)}, u32[]{:S(2)}, u32[]{:S(2)}) collective-permute-start(bf16[192,384]{1,0:T(8,128)(2,1)} %get-tuple-element.25), channel_id=1, source_target_pairs={{0,0},{1,1},{2,2},{3,3},{4,16},{5,17},{6,18},{7,19},{8,8},{9,9},{1... | collective-permute-start | bytes 442376 | tf_op jit(solution)/shard_map/ppermute | solution.py:256
  161.9 28.4 %collective-permute-start.17 = (bf16[192,384]{1,0:T(8,128)(2,1)}, bf16[192,384]{1,0:T(8,128)(2,1)S(1)}, u32[]{:S(2)}, u32[]{:S(2)}) collective-permute-start(bf16[192,384]{1,0:T(8,128)(2,1)} %get-tuple-element.26), channel_id=1, source_target_pairs={{0,1},{1,2},{2,3},{3,0},{4,17},{5,18},{6,19},{7,16},{8,9},{9,10},{... | collective-permute-start | bytes 442376 | tf_op jit(solution)/shard_map/ppermute | solution.py:256
  166.5 23.8 %collective-permute-start.18 = (bf16[192,384]{1,0:T(8,128)(2,1)}, bf16[192,384]{1,0:T(8,128)(2,1)S(1)}, u32[]{:S(2)}, u32[]{:S(2)}) collective-permute-start(bf16[192,384]{1,0:T(8,128)(2,1)} %get-tuple-element.27), channel_id=1, source_target_pairs={{0,2},{1,3},{2,0},{3,1},{4,18},{5,19},{6,16},{7,17},{8,10},{9,11},... | collective-permute-start | bytes 442376 | tf_op jit(solution)/shard_map/ppermute | solution.py:256
  166.5 23.8 %collective-permute-start.19 = (bf16[192,384]{1,0:T(8,128)(2,1)}, bf16[192,384]{1,0:T(8,128)(2,1)S(1)}, u32[]{:S(2)}, u32[]{:S(2)}) collective-permute-start(bf16[192,384]{1,0:T(8,128)(2,1)} %get-tuple-element.28), channel_id=1, source_target_pairs={{0,3},{1,0},{2,1},{3,2},{4,19},{5,16},{6,17},{7,18},{8,11},{9,8},{... | collective-permute-start | bytes 442376 | tf_op jit(solution)/shard_map/ppermute | solution.py:256
  190.3 0.7 copy-start.7
  190.3 0.7 copy-start.8
  190.3 0.8 copy-start.9
  191.1 0.7 copy-start.10
Sparse Core Ops, SparseCore 0:
  23.9 40.8 all-gather.5
  66.4 14.8 all-gather.7

commit v2 on v1

v2 whole, which is shorter than its diff:
```python
import functools

import jax
import jax.numpy as jnp
from jax import lax
from jax.experimental import pallas as pl
from jax.experimental.pallas import tpu as pltpu
from jax.sharding import PartitionSpec as P

HD = 64
GROUP = 128
LANES = 128

epsilon = 1e-05

VMEM = pl.BlockSpec(memory_space=pltpu.VMEM)
SMEM = pl.BlockSpec(memory_space=pltpu.SMEM)
MIB = 1024 * 1024


def ring_successors(count):
    order = [0] + list(range(1, count, 2)) + list(range(count - 2 + count % 2, 0, -2))
    return {order[i]: order[(i + 1) % count] for i in range(count)}


def lookup(table, index):
    value = jnp.int32(table[0])
    for place in range(1, len(table)):
        value = jnp.where(index == place, jnp.int32(table[place]), value)
    return value


def project_kernel(parts, place_ref, gain_ref, *refs):
    rows, own, other, (query_ref, pair_ref) = refs[:parts], refs[parts:parts + 3], refs[parts + 3:parts + 6], refs[parts + 6:]
    gain = gain_ref[...]
    pieces = []
    for part in rows:
        values = part[...].astype(jnp.float32)
        center = values - jnp.mean(values, axis=-1, keepdims=True)
        spread = jnp.mean(center * center, axis=-1, keepdims=True)
        pieces.append((center * lax.rsqrt(spread + epsilon) * gain).astype(jnp.bfloat16))
    normalized = pieces[0] if parts == 1 else jnp.concatenate(pieces, axis=0)
    depth, width = own[0].shape
    low, high = normalized[:, :depth], normalized[:, depth:]
    first = place_ref[0] == 0
    mine = jnp.where(first, low, high)
    theirs = jnp.where(first, high, low)
    sums = [
        jnp.dot(mine, a[...], preferred_element_type=jnp.float32)
        + jnp.dot(theirs, b[...], preferred_element_type=jnp.float32)
        for a, b in zip(own, other)
    ]
    query_ref[...] = (sums[0].astype(jnp.bfloat16).astype(jnp.float32) * (HD ** -0.5)).astype(jnp.bfloat16)
    pair_ref[:, :width] = sums[1].astype(jnp.bfloat16)
    pair_ref[:, width:] = sums[2].astype(jnp.bfloat16)


def project(place, rows, gain, own, other):
    count, depth, width = sum(part.shape[0] for part in rows), rows[0].shape[1], own[0].shape[1]
    return pl.pallas_call(
        functools.partial(project_kernel, len(rows)),
        out_shape=(
            jax.ShapeDtypeStruct((count, width), jnp.bfloat16),
            jax.ShapeDtypeStruct((count, 2 * width), jnp.bfloat16),
        ),
        in_specs=[SMEM] + [VMEM] * (7 + len(rows)),
        out_specs=(VMEM, VMEM),
        compiler_params=pltpu.CompilerParams(vmem_limit_bytes=16 * MIB),
        cost_estimate=pl.CostEstimate(
            flops=2 * count * depth * 3 * width,
            bytes_accessed=2 * (depth * 3 * width + count * (depth + 3 * width)),
            transcendentals=count,
        ),
        name="project",
    )(place, gain, *rows, *own, *other)


def window_kernel(steps, groups, place_ref, *refs):
    queries, owns, sides = refs[:steps], refs[steps:2 * steps], refs[2 * steps:4 * steps]
    q_all, k_all, vt_all, v_all = refs[4 * steps:]
    rows, width = queries[0].shape
    pairs, block = width // LANES, steps * rows
    core = place_ref[0]
    chip_base = jnp.where(core == 0, 2 * block, 0)
    link_base = jnp.where(core == 0, 0, 2 * block)
    for step in range(steps):
        at = place_ref[4 + step] * rows
        q_at = pl.ds(pl.multiple_of(at, 64), rows)
        for pair in range(pairs):
            q_all[pair, q_at, :] = queries[step][:, pair * LANES:(pair + 1) * LANES]
        for source, base in ((owns[step], block), (sides[step], chip_base), (sides[steps + step], link_base)):
            to = pl.ds(pl.multiple_of(base + at, 64), rows)
            for pair in range(pairs):
                k_all[pair, to, :] = source[:, pair * LANES:(pair + 1) * LANES]
                v_all[pair, to, :] = source[:, width + pair * LANES:width + (pair + 1) * LANES]
    for index in range(3 * groups):
        for pair in range(pairs):
            vt_all[pair, index] = v_all[pair, index * GROUP:(index + 1) * GROUP, :].T


def window(place, groups, queries, owns, chip_side, link_side):
    steps = len(queries)
    rows, width = queries[0].shape
    pairs, block = width // LANES, steps * rows
    return pl.pallas_call(
        functools.partial(window_kernel, steps, groups),
        out_shape=(
            jax.ShapeDtypeStruct((pairs, block, LANES), jnp.bfloat16),
            jax.ShapeDtypeStruct((pairs, 3 * block, LANES), jnp.bfloat16),
            jax.ShapeDtypeStruct((pairs, 3 * groups, LANES, GROUP), jnp.bfloat16),
        ),
        in_specs=[SMEM] + [VMEM] * (4 * steps),
        out_specs=(VMEM,) * 3,
        scratch_shapes=[pltpu.VMEM((pairs, 3 * block, LANES), jnp.bfloat16)],
        compiler_params=pltpu.CompilerParams(vmem_limit_bytes=16 * MIB),
        cost_estimate=pl.CostEstimate(flops=0, bytes_accessed=2 * 14 * block * width, transcendentals=0),
        name="window",
    )(place, *queries, *owns, *chip_side, *link_side)


def attend_kernel(groups, reach, count_rows, place_ref, band_ref, turn_ref, q_all, k_all, vt_all, *refs):
    outs, (score, ctx, chosen, limits) = refs[:-4], refs[-4:]
    pairs, rows = q_all.shape[0], outs[0].shape[0]
    first_group, total, length = (place_ref[i] for i in range(1, 4))
    first_row = turn_ref[0]
    slots = 2 * reach + 2
    half_mask = lax.broadcasted_iota(jnp.int32, (GROUP, LANES), 1) < HD
    row_ids = lax.broadcasted_iota(jnp.int32, (GROUP, 2 * GROUP), 0)
    part_group = lax.div(length, jnp.int32(GROUP))
    part_left = lax.rem(length, jnp.int32(GROUP))

    def one_group(place, carry):
        group = first_row // GROUP + place
        for slot in range(slots):
            chosen[slot] = groups + group
        offset = part_group - first_group - group
        column = jnp.clip(jnp.where(offset < 0, offset + reach, offset + reach - 1), 0, 2 * reach - 1)
        cut = (part_left > 0) & (offset != 0) & (jnp.abs(offset) <= reach) & (part_group < total)
        cut = cut & (band_ref[group, column] == 1)
        chosen[1] = jnp.where(cut, groups + group + offset, groups + group)
        limits[0] = jnp.where(cut, part_left, 0)
        count = 1 + cut.astype(jnp.int32)
        for column in range(2 * reach):
            offset = column - reach if column < reach else column - reach + 1
            there = first_group + group + offset
            good = (there >= 0) & (there < part_group) & (there < total) & (band_ref[group, column] == 1)
            chosen[count] = jnp.where(good, groups + group + offset, groups + group)
            limits[0] = jnp.where(good & (count == 1), GROUP, limits[0])
            count = count + good.astype(jnp.int32)
        query_at = pl.ds(pl.multiple_of(group * GROUP, GROUP), GROUP)
        out_at = pl.ds(pl.multiple_of(place * GROUP, GROUP), GROUP)

        def run(size):
            first_limit = limits[0]
            last_limit = jnp.where(count == size, GROUP, 0)
            indices = [chosen[slot] for slot in range(size)]
            best = []
            for pair in range(pairs):
                own = q_all[pair, query_at, :]
                zero = jnp.zeros_like(own)
                both = jnp.concatenate(
                    [jnp.where(half_mask, own, zero), jnp.where(half_mask, zero, own)], axis=0
                ).T
                top = None
                for slot in range(0, size, 2):
                    tiles = [
                        k_all[pair, pl.ds(pl.multiple_of(index * GROUP, GROUP), GROUP), :]
                        for index in indices[slot:slot + 2]
                    ]
                    got = jnp.dot(jnp.concatenate(tiles, axis=0), both, preferred_element_type=jnp.float32)
                    for one in (slot, slot + 1):
                        part = got[(one - slot) * GROUP:(one - slot + 1) * GROUP]
                        if one == 1:
                            part = jnp.where(row_ids < first_limit, part, -jnp.inf)
                        elif one == size - 1:
                            part = jnp.where(row_ids < last_limit, part, -jnp.inf)
                        score[pair, one * GROUP:(one + 1) * GROUP, :] = part
                        high = jnp.max(part.reshape(GROUP // 8, 8, 2 * GROUP), axis=0)
                        top = high if top is None else jnp.maximum(top, high)
                best.append(jnp.max(top, axis=0, keepdims=True))
            for pair in range(pairs):
                total_sum = jnp.zeros((8, 2 * GROUP), jnp.float32)
                mixed = jnp.zeros((LANES, 2 * GROUP), jnp.float32)
                for slot in range(0, size, 2):
                    weights = jnp.exp(score[pair, slot * GROUP:(slot + 2) * GROUP, :] - best[pair])
                    total_sum += jnp.sum(weights.reshape(2 * GROUP // 8, 8, 2 * GROUP), axis=0)
                    tiles = [vt_all[pair, index] for index in indices[slot:slot + 2]]
                    mixed += jnp.dot(
                        jnp.concatenate(tiles, axis=1),
                        weights.astype(jnp.bfloat16),
                        preferred_element_type=jnp.float32,
                    )
                mixed = mixed / jnp.sum(total_sum, axis=0, keepdims=True)
                both_heads = jnp.concatenate([mixed[:HD, :GROUP], mixed[HD:, GROUP:]], axis=0)
                ctx[pair, out_at, :] = both_heads.T.astype(jnp.bfloat16)

        for size in range(2, slots + 1, 2):
            @pl.when((count == size) | (count == size - 1))
            def _():
                run(size)

        return carry

    lax.fori_loop(0, count_rows // GROUP, one_group, 0)
    for place, out in enumerate(outs):
        at = pl.ds(pl.multiple_of(turn_ref[1 + place], 64), rows)
        for pair in range(pairs):
            out[:, pair * LANES:(pair + 1) * LANES] = ctx[pair, at, :]


def attend(place, band, turn, outs, q_all, k_all, vt_all):
    groups, reach = band.shape[0], band.shape[1] // 2
    pairs, block = q_all.shape[:2]
    rows = block // (2 * outs)
    slots = 2 * reach + 2
    work = block // 2 * (reach + 1) * GROUP * 2 * pairs
    return pl.pallas_call(
        functools.partial(attend_kernel, groups, reach, block // 2),
        out_shape=(jax.ShapeDtypeStruct((rows, pairs * LANES), jnp.bfloat16),) * outs,
        in_specs=[SMEM, SMEM, SMEM] + [VMEM] * 3,
        out_specs=(VMEM,) * outs,
        scratch_shapes=[
            pltpu.VMEM((pairs, slots * GROUP, 2 * GROUP), jnp.float32),
            pltpu.VMEM((pairs, block // 2, LANES), jnp.bfloat16),
            pltpu.SMEM((slots + 2,), jnp.int32),
            pltpu.SMEM((1,), jnp.int32),
        ],
        compiler_params=pltpu.CompilerParams(vmem_limit_bytes=20 * MIB),
        cost_estimate=pl.CostEstimate(
            flops=16 * work * HD, bytes_accessed=2 * 7 * block * pairs * LANES, transcendentals=work
        ),
        name="attend",
    )(place, band, turn, q_all, k_all, vt_all)


def output_kernel(share, layers, place_ref, own_ref, far_ref, *refs):
    mine, theirs, contexts, (out_ref, weight) = (
        refs[:share], refs[share:2 * share], refs[2 * share:2 * share + layers], refs[2 * share + layers:]
    )
    core, layer, sharer = (place_ref[i] for i in range(3))
    depth, columns = own_ref.shape
    part = depth // share
    weight[layer, core] = own_ref[...]
    weight[layer, 1 - core] = far_ref[...]
    for other in range(share):
        to = pl.ds(pl.multiple_of((sharer ^ other) * part, part), part)
        for step in range(1, layers):
            there = lax.rem(layer + layers - step, layers)
            weight[there, core, to, :] = mine[other][(step - 1) * part:step * part, :]
            weight[there, 1 - core, to, :] = theirs[other][(step - 1) * part:step * part, :]
    for side in range(2):
        total = None
        for step in range(layers):
            got = jnp.dot(
                contexts[step][...], weight[place_ref[3 + step], side], preferred_element_type=jnp.float32
            )
            total = got if total is None else total + got
        out_ref[0, :, side * columns:(side + 1) * columns] = total.astype(jnp.bfloat16)


def output(place, own, far, mine, theirs, contexts):
    layers = len(contexts)
    rows, width = contexts[0].shape
    depth, columns = own.shape
    return pl.pallas_call(
        functools.partial(output_kernel, len(mine), layers),
        out_shape=jax.ShapeDtypeStruct((1, rows, 2 * columns), jnp.bfloat16),
        in_specs=[SMEM] + [VMEM] * (2 + 2 * len(mine) + layers),
        out_specs=VMEM,
        scratch_shapes=[pltpu.VMEM((layers, 2, depth, columns), jnp.bfloat16)],
        compiler_params=pltpu.CompilerParams(vmem_limit_bytes=20 * MIB),
        cost_estimate=pl.CostEstimate(
            flops=2 * rows * width * layers * 2 * columns,
            bytes_accessed=2 * (width * layers * 2 * columns + 4 * rows * columns),
            transcendentals=0,
        ),
        name="output",
    )(place, own, far, *mine, *theirs, *contexts)


def local(frames, norm_gain, w_query, w_key, w_value, w_out, group_band, lengths):
    cores, seqs, layers = lax.axis_size("dp"), lax.axis_size("seq"), lax.axis_size("head")
    core, seq, layer = lax.axis_index("dp"), lax.axis_index("seq"), lax.axis_index("head")
    groups = group_band.shape[1]
    here = [(c, s) for c in range(cores) for s in range(seqs)]

    def home(c, s):
        return s % 2, s // 2 * 2 + c

    def flat(c, s, z=None):
        return c * seqs + s if z is None else (c * seqs + s) * layers + z

    def moved(value, shift):
        pairs = [(flat(c, s, z), flat(*home(c, s), shift(z))) for c, s in here for z in range(layers)]
        return lax.ppermute(value, ("dp", "seq", "head"), pairs)

    after = ring_successors(layers)
    before = {after[z]: z for z in after}
    swap = [(c, cores - 1 - c) for c in range(cores)]
    over_link = [(flat(1, s), flat(0, s + 2)) for s in range(seqs - 2)]
    over_link += [(flat(0, s + 2), flat(1, s)) for s in range(seqs - 2)]

    ring = [(z, after[z]) for z in range(layers)]
    rows = frames[0]
    middle = rows.shape[0] // 2
    hops = [[moved(part, lambda z: after[z]) for part in (rows[:middle], rows[middle:])]]
    whole = moved(rows, lambda z: z)
    own = (w_query, w_key, w_value)
    other = lax.ppermute(own, "dp", swap)
    facts = jnp.concatenate([group_band[0], jnp.broadcast_to(lengths[:, None], (1, group_band.shape[2]))], axis=0)
    facts = lax.ppermute(facts, ("dp", "seq"), [(flat(c, s), flat(*home(c, s))) for c, s in here])
    w_far = lax.ppermute(w_out, "dp", swap)
    for _ in range(2, layers):
        hops.append([lax.ppermute(part, "head", ring) for part in hops[-1]])

    share = 4 if seqs % 4 == 0 else 2
    part = w_out.shape[0] // share
    piece = lax.dynamic_slice_in_dim(w_out, seq % share * part, part, 0)
    piece, hops[-1][1] = lax.optimization_barrier((piece, hops[-1][1]))
    pieces = [
        lax.ppermute(piece, "head", [(z, (z + step) % layers) for z in range(layers)]) for step in range(1, layers)
    ]
    mine = [jnp.concatenate(pieces, axis=0)]
    for other_sharer in range(1, share):
        mine.append(lax.ppermute(mine[0], "seq", [(s, s ^ other_sharer) for s in range(seqs)]))
    theirs = [lax.ppermute(value, "dp", swap) for value in mine]

    gain = norm_gain[None, :]
    core_at = core[None].astype(jnp.int32)
    queries, owns, chip_side, link_side = [], [], [], []
    for parts in [[whole]] + hops:
        query, pair = project(core_at, parts, gain, own, other)
        queries.append(query)
        owns.append(pair)
        link_side.append(lax.ppermute(pair, ("dp", "seq"), over_link))
        chip_side.append(lax.ppermute(pair, "dp", swap))

    ids = [layer]
    for _ in range(1, layers):
        ids.append(lookup([before[z] for z in range(layers)], ids[-1]))
    place = [core, (seq // 2 * 2 + core) * groups, groups * seqs, facts[groups, 0]] + ids
    place = jnp.stack([jnp.asarray(value, jnp.int32) for value in place])
    band = facts[:groups]
    q_all, k_all, vt_all = window(place, groups, queries, owns, chip_side, link_side)

    half = layers // 2
    arrived, sources = [], []
    for near in (0, 1):
        side = layer // half if near else 1 - layer // half
        first_row = side * half * rows.shape[0]
        turn = [first_row] + [lax.rem(layer + e, half) * rows.shape[0] for e in range(half)]
        turn = jnp.stack([jnp.asarray(value, jnp.int32) for value in turn])
        for e, context in enumerate(attend(place, band, turn, half, q_all, k_all, vt_all)):
            def target(z, e=e):
                return (z // half if near else 1 - z // half) * half + (z + e) % half

            arrived.append(moved(context, target))
            sources.append(side * half + lax.rem(layer + half - e, half))
    last = jnp.stack([jnp.asarray(value, jnp.int32) for value in [core, layer, seq % share] + sources])
    return output(last, w_out, w_far, mine, theirs, arrived)


def solution(mesh):
    return jax.shard_map(
        local,
        mesh=mesh,
        in_specs=(
            P("dp", ("seq", "head"), None),
            P(),
            P("dp", "head"),
            P("dp", "head"),
            P("dp", "head"),
            P("head", "dp"),
            P("dp", "seq", None),
            P("dp"),
        ),
        out_specs=P("dp", ("seq", "head"), None),
        check_vma=False,
    )
```

time: 203 us -> 144 us (0.71); the launches traced: 203 us -> 141 us
  waiting for transfers between devices: 67.4 us -> 47.4 us
  Pallas kernels: 43 us -> 26.4 us
  blocking collectives: 16.2 us -> 0 us
  starting transfers between devices: 33.6 us -> 48 us
  between operations: 14.4 us -> 1.01 us
  local copies, waits for them, and re-layouts: 28.1 us -> 18.5 us
    all_gather x2 -> x0, waiting for transfers between devices: 41 us -> none  [the longest x1 41 us: local(): pieces = lax.all_gather(pieces, 'seq', axis=0, axis_index_groups=sets)]
    ppermute x6 -> x7, waiting for transfers between devices: 14.4 us -> 31.2 us  [moved(): return lax.ppermute(value, ('dp', 'seq', 'head'), pairs)]
    pallas_call x6 -> x8, Pallas kernels: 43 us -> 26.4 us  [the longest x4 11 us: project(): pl.pallas_call(functools.partial(project_kernel, len(rows)), out_shape=(j...]
    all_gather x1 -> x0, blocking collectives: 16.2 us -> none  [local(): pieces = lax.all_gather(piece, 'head', axis=0)]
    reshape x1 -> x0, local copies, waits for them, and re-layouts: 11.2 us -> none  [local(): jnp.transpose(pieces, (2, 1, 3, 0, 4))]
    ppermute x2 -> x15, starting transfers between devices: 1.45 us -> 12.1 us  [the longest x4 5.1 us: local(): hops.append([lax.ppermute(part, 'head', ring) for part in hops[-1]])]
    transpose x1 -> x0, local copies, waits for them, and re-layouts: 9.38 us -> none  [local(): jnp.transpose(pieces, (2, 1, 3, 0, 4))]
    unnamed x43 -> x47, local copies, waits for them, and re-layouts: 4.39 us -> 13.8 us
  transfers between devices with their start and end apart: 22 -> 34, of which waited for: 5 -> 10; matrix products, arithmetic and copies ran while one was open for 12% -> 4% of each run, Pallas kernels for 19% -> 16%
where the time goes in v2:
time: 144 us; the launch traced here: 141 us
  starting transfers between devices  48 us (33%)
  waiting for transfers between devices  47.4 us (33%)
  Pallas kernels  26.4 us (18%)
  local copies, waits for them, and re-layouts  18.5 us (13%)
    ppermute x7, waiting for transfers between devices, moved(): return lax.ppermute(value, ('dp', 'seq', 'head'), pairs)  31.2 us
    ppermute x7, starting transfers between devices, moved(): return lax.ppermute(value, ('dp', 'seq', 'head'), pairs)  19.5 us
    unnamed x47, local copies, waits for them, and re-layouts  13.8 us
    ppermute x4, starting transfers between devices, local(): link_side.append(lax.ppermute(pair, ('dp', 'seq'), over_link))  11.9 us
    pallas_call x4, Pallas kernels, project(): pl.pallas_call(functools.partial(project_kernel, len(rows)), out_shape=(j...  11 us
    ppermute x4, waiting for transfers between devices, local(): hops.append([lax.ppermute(part, 'head', ring) for part in hops[-1]])  9.98 us
    pallas_call x2, Pallas kernels, attend(): pl.pallas_call(functools.partial(attend_kernel, groups, reach, block // 2...  8.8 us
    ppermute x4, waiting for transfers between devices, local(): link_side.append(lax.ppermute(pair, ('dp', 'seq'), over_link))  6.19 us
  transfers between devices with their start and end apart: 34, of which 10 were waited for; matrix products, arithmetic and copies ran while one was open for 4% of the time, Pallas kernels for 16%

profile of v2, /device:TPU:1, one launch (start us, length us, event | category | flops | bytes accessed | tf_op | source)
XLA Modules:
  0.0 141.4 jit_solution(4090272678684395632)
XLA Ops:
  0.0 1.1 slice_bitcast_fusion
  1.1 3.7 %collective-permute-start.1 = (bf16[96,1536]{1,0:T(8,128)(2,1)S(1)}, bf16[96,1536]{1,0:T(8,128)(2,1)S(1)}, u32[]{:S(2)}, u32[]{:S(2)}) collective-permute-start(bf16[96,1536]{1,0:T(8,128)(2,1)S(1)} %get-tuple-element.40), channel_id=1, source_target_pairs={{0,1},{1,3},{2,0},{3,2},{4,17},{5,19},{6,16},{7,18},{8,9},{9,11},{... | collective-permute-start | bytes 884744 | tf_op jit(solution)/shard_map/ppermute | solution.py:295
  4.8 2.0 %collective-permute-start.19 = (bf16[96,1536]{1,0:T(8,128)(2,1)S(1)}, bf16[96,1536]{1,0:T(8,128)(2,1)S(1)}, u32[]{:S(2)}, u32[]{:S(2)}) collective-permute-start(bf16[96,1536]{1,0:T(8,128)(2,1)S(1)} %get-tuple-element.39), channel_id=1, source_target_pairs={{0,1},{1,3},{2,0},{3,2},{4,17},{5,19},{6,16},{7,18},{8,9},{9,11},{... | collective-permute-start | bytes 884744 | tf_op jit(solution)/shard_map/ppermute | solution.py:295
  6.8 6.5 %collective-permute-done.1.refs_1_ = bf16[96,1536]{1,0:T(8,128)(2,1)S(1)} collective-permute-done((bf16[96,1536]{1,0:T(8,128)(2,1)S(1)}, bf16[96,1536]{1,0:T(8,128)(2,1)S(1)}, u32[]{:S(2)}, u32[]{:S(2)}) %collective-permute-start.1) | collective-permute-done | bytes 294944 | tf_op jit(solution)/shard_map/ppermute | solution.py:295
  13.3 0.5 collective-permute-start.2
  13.8 0.7 copy-done.8
  14.5 0.2 collective-permute-start.16
  14.7 0.4 collective-permute-start.17
  15.0 0.2 collective-permute-start.18
  15.2 4.4 %collective-permute-done.19.refs_0_ = bf16[96,1536]{1,0:T(8,128)(2,1)S(1)} collective-permute-done((bf16[96,1536]{1,0:T(8,128)(2,1)S(1)}, bf16[96,1536]{1,0:T(8,128)(2,1)S(1)}, u32[]{:S(2)}, u32[]{:S(2)}) %collective-permute-start.19) | collective-permute-done | bytes 294944 | tf_op jit(solution)/shard_map/ppermute | solution.py:295
  19.6 3.4 %collective-permute-start.15 = (bf16[192,1536]{1,0:T(8,128)(2,1)}, bf16[192,1536]{1,0:T(8,128)(2,1)}, u32[]{:S(2)}, u32[]{:S(2)}) collective-permute-start(bf16[192,1536]{1,0:T(8,128)(2,1)} %bitcast.29), channel_id=1, source_target_pairs={{0,0},{1,1},{2,2},{3,3},{4,16},{5,17},{6,18},{7,19},{8,8},{9,9},{1... | collective-permute-start | bytes 1769480 | tf_op jit(solution)/shard_map/ppermute | solution.py:295
  23.0 2.1 %collective-permute-done.2.refs_1_ = bf16[96,1536]{1,0:T(8,128)(2,1)} collective-permute-done((bf16[96,1536]{1,0:T(8,128)(2,1)S(1)}, bf16[96,1536]{1,0:T(8,128)(2,1)}, u32[]{:S(2)}, u32[]{:S(2)}) %collective-permute-start.2) | collective-permute-done | bytes 294944 | tf_op jit(solution)/shard_map/ppermute | solution.py:314
  25.2 1.0 collective-permute-start.20
  26.2 0.7 copy-done.10
  26.9 7.8 %collective-permute-done.20.refs_0_ = bf16[96,1536]{1,0:T(8,128)(2,1)} collective-permute-done((bf16[96,1536]{1,0:T(8,128)(2,1)S(1)}, bf16[96,1536]{1,0:T(8,128)(2,1)}, u32[]{:S(2)}, u32[]{:S(2)}) %collective-permute-start.20) | collective-permute-done | bytes 294944 | tf_op jit(solution)/shard_map/ppermute | solution.py:314
  34.7 0.4 collective-permute-start.3
  35.1 3.2 %collective-permute-start.21 = (bf16[96,1536]{1,0:T(8,128)(2,1)}, bf16[96,1536]{1,0:T(8,128)(2,1)}, u32[]{:S(2)}, u32[]{:S(2)}) collective-permute-start(bf16[96,1536]{1,0:T(8,128)(2,1)} %collective-permute-done.20.refs_0_), channel_id=1, source_target_pairs={{0,1},{1,3},{2,0},{3,2},{4,5},{5,7},{6,4},{7,6},{8,9},{9,11},{10,8... | collective-permute-start | bytes 884744 | tf_op jit(solution)/shard_map/ppermute | solution.py:314
  38.3 0.7 broadcast_in_dim.5.gain_ref
  39.0 0.7 copy.11
  40.4 3.4 %collective-permute-start.14 = (s32[7,12]{1,0:T(8,128)S(1)}, s32[7,12]{1,0:T(8,128)S(1)}, u32[]{:S(2)}, u32[]{:S(2)}) collective-permute-start(s32[7,12]{1,0:T(8,128)S(1)} %concatenate.7), channel_id=1, source_target_pairs={{0,0},{4,16},{8,8},{12,24},{16,4},{20,20},{24,12},{28,28},{1,1},{5... | collective-permute-start | bytes 1016 | tf_op jit(solution)/shard_map/ppermute | solution.py:311
  43.9 1.1 copy-done
  44.9 1.1 copy-done.2
  46.0 1.1 copy-done.4
  47.0 3.2 %project.6 = (bf16[192,384]{1,0:T(8,128)(2,1)S(1)}, bf16[192,768]{1,0:T(8,128)(2,1)}) custom-call(s32[1]{0:T(128)} %bitcast.place_ref, f32[1,1536]{1,0:T(1,128)S(1)} %broadcast_in_dim.5.gain_ref, bf16[96,1536]{1,0:T(8,128)(2,1)} %collective-permute-done.20.refs_0_, bf16[96,1536]{1,0:T(8,128)(2,1)} %collective-permute-done.2.refs_1_, ...), custom_call_target="tpu_custom_call" | custom-call | flops 679477248 | bytes 4571136 | tf_op jit(solution)/shard_map/project/pallas_call | solution.py:60
  50.3 0.7 copy-done.12
  51.0 3.5 %collective-permute-start.28 = (bf16[192,768]{1,0:T(8,128)(2,1)}, bf16[192,768]{1,0:T(8,128)(2,1)}, u32[]{:S(2)}, u32[]{:S(2)}) collective-permute-start(bf16[192,768]{1,0:T(8,128)(2,1)} %get-tuple-element.30.refs_6_), channel_id=1, source_target_pairs={{16,8},{20,12},{8,16},{12,20},{17,9},{21,13},{9,17},{13,21},{18,10... | collective-permute-start | bytes 884744 | tf_op jit(solution)/shard_map/ppermute | solution.py:335
  54.5 2.1 %project.5 = (bf16[192,384]{1,0:T(8,128)(2,1)S(1)}, bf16[192,768]{1,0:T(8,128)(2,1)}) custom-call(s32[1]{0:T(128)} %bitcast.place_ref, f32[1,1536]{1,0:T(1,128)S(1)} %broadcast_in_dim.5.gain_ref, bf16[96,1536]{1,0:T(8,128)(2,1)S(1)} %copy-done.11, bf16[96,1536]{1,0:T(8,128)(2,1)S(1)} %copy-done.9, bf16[768,384]{1,0:T(8,128)(2,1)S(1)} %copy-done, ...), custom_call_target="tpu_custom_call" | custom-call | flops 679477248 | bytes 4571136 | tf_op jit(solution)/shard_map/project/pallas_call | solution.py:60
  56.6 0.7 copy-done.14
  57.3 2.2 %collective-permute-start.27 = (bf16[192,768]{1,0:T(8,128)(2,1)}, bf16[192,768]{1,0:T(8,128)(2,1)}, u32[]{:S(2)}, u32[]{:S(2)}) collective-permute-start(bf16[192,768]{1,0:T(8,128)(2,1)} %get-tuple-element.29.refs_5_), channel_id=1, source_target_pairs={{16,8},{20,12},{8,16},{12,20},{17,9},{21,13},{9,17},{13,21},{18,10... | collective-permute-start | bytes 884744 | tf_op jit(solution)/shard_map/ppermute | solution.py:335
  59.5 1.6 %constant_dynamic-slice_fusion = bf16[96,768]{1,0:T(8,128)(2,1)} fusion(bf16[384,768]{1,0:T(8,128)(2,1)} %own_ref.1, s32[]{:T(128)S(6)} %select_n.49), kind=kLoop, calls=%fused_computation.8 | loop fusion | bytes 294916 | tf_op jit(solution)/shard_map/dynamic_slice | solution.py:318
  61.1 2.4 %project.4 = (bf16[192,384]{1,0:T(8,128)(2,1)S(1)}, bf16[192,768]{1,0:T(8,128)(2,1)S(1)}) custom-call(s32[1]{0:T(128)} %bitcast.place_ref, f32[1,1536]{1,0:T(1,128)S(1)} %broadcast_in_dim.5.gain_ref, bf16[192,1536]{1,0:T(8,128)(2,1)} %collective-permute-done.15.refs_0_, bf16[768,384]{1,0:T(8,128)(2,1)S(1)} %copy-done.1, bf16[768,384]{1,0:T(8,128)(2,1)S(1)} %copy-done.3, ...), custom_call_target="tpu_custom_call" | custom-call | flops 679477248 | bytes 4571136 | tf_op jit(solution)/shard_map/project/pallas_call | solution.py:60
  63.7 3.3 %collective-permute-start.6 = (bf16[96,768]{1,0:T(8,128)(2,1)}, bf16[96,768]{1,0:T(8,128)(2,1)S(1)}, u32[]{:S(2)}, u32[]{:S(2)}) collective-permute-start(bf16[96,768]{1,0:T(8,128)(2,1)} %constant_dynamic-slice_fusion), channel_id=1, source_target_pairs={{0,3},{1,0},{2,1},{3,2},{4,7},{5,4},{6,5},{7,6},{8,11},{9,8},{10,9... | collective-permute-start | bytes 442376 | tf_op jit(solution)/shard_map/ppermute | solution.py:321
  67.0 3.2 %project.7 = (bf16[192,384]{1,0:T(8,128)(2,1)S(1)}, bf16[192,768]{1,0:T(8,128)(2,1)}) custom-call(s32[1]{0:T(128)} %bitcast.place_ref, f32[1,1536]{1,0:T(1,128)S(1)} %broadcast_in_dim.5.gain_ref, bf16[96,1536]{1,0:T(8,128)(2,1)} %collective-permute-done.21.refs_0_, bf16[96,1536]{1,0:T(8,128)(2,1)} %collective-permute-done.3.refs_1_, ...), custom_call_target="tpu_custom_call" | custom-call | flops 679477248 | bytes 4571136 | tf_op jit(solution)/shard_map/project/pallas_call | solution.py:60
  70.2 0.3 collective-permute-start.22
  70.5 3.7 %collective-permute-start.26 = (bf16[192,768]{1,0:T(8,128)(2,1)S(1)}, bf16[192,768]{1,0:T(8,128)(2,1)S(1)}, u32[]{:S(2)}, u32[]{:S(2)}) collective-permute-start(bf16[192,768]{1,0:T(8,128)(2,1)S(1)} %get-tuple-element.28.refs_4_), channel_id=1, source_target_pairs={{16,8},{20,12},{8,16},{12,20},{17,9},{21,13},{9,17},{13,21},{18,10... | collective-permute-start | bytes 884744 | tf_op jit(solution)/shard_map/ppermute | solution.py:335
  74.3 0.9 constant_dynamic-update-slice_fusion.2
  75.3 0.5 collective-permute-start
  75.8 2.5 %collective-permute-start.29 = (bf16[192,768]{1,0:T(8,128)(2,1)}, bf16[192,768]{1,0:T(8,128)(2,1)S(1)}, u32[]{:S(2)}, u32[]{:S(2)}) collective-permute-start(bf16[192,768]{1,0:T(8,128)(2,1)} %get-tuple-element.31.refs_7_), channel_id=1, source_target_pairs={{16,8},{20,12},{8,16},{12,20},{17,9},{21,13},{9,17},{13,21},{18,10... | collective-permute-start | bytes 884744 | tf_op jit(solution)/shard_map/ppermute | solution.py:335
  78.3 0.1 collective-permute-start.7
  78.4 0.2 collective-permute-done.26.refs_12_
  78.6 2.4 %collective-permute-start.9 = (bf16[288,768]{1,0:T(8,128)(2,1)S(1)}, bf16[288,768]{1,0:T(8,128)(2,1)S(1)}, u32[]{:S(2)}, u32[]{:S(2)}) collective-permute-start(bf16[288,768]{1,0:T(8,128)(2,1)S(1)} %constant_dynamic-update-slice_fusion.refs_0_), channel_id=1, source_target_pairs={{0,12},{4,8},{8,4},{12,0},{1,13},{5,9},{9,5},{13,1},{2,14},{6,10},... | collective-permute-start | bytes 1327112 | tf_op jit(solution)/shard_map/ppermute | solution.py:325
  81.1 0.1 add_add_fusion
  81.1 0.5 slice.20
  81.7 0.7 stack.73.place_ref
  82.4 6.0 %collective-permute-done.29.refs_15_ = bf16[192,768]{1,0:T(8,128)(2,1)S(1)} collective-permute-done((bf16[192,768]{1,0:T(8,128)(2,1)}, bf16[192,768]{1,0:T(8,128)(2,1)S(1)}, u32[]{:S(2)}, u32[]{:S(2)}) %collective-permute-start.29) | collective-permute-done | bytes 294944 | tf_op jit(solution)/shard_map/ppermute | solution.py:335
  88.4 1.0 copy-done.7
  89.3 0.9 copy-done.13
  90.3 0.9 copy-done.15
  91.2 0.9 copy-done.17
  92.1 0.9 copy-done.19
  93.0 2.8 %window.1 = (bf16[3,768,128]{2,1,0:T(8,128)(2,1)S(1)}, bf16[3,2304,128]{2,1,0:T(8,128)(2,1)S(1)}, bf16[3,18,128,128]{3,2,1,0:T(8,128)(2,1)S(1)}) custom-call(s32[8]{0:T(128)S(1)} %stack.73.place_ref, bf16[192,384]{1,0:T(8,128)(2,1)S(1)} %copy-done.17, bf16[192,384]{1,0:T(8,128)(2,1)S(1)} %copy-done.15, bf16[192,384]{1,0:T(8,128)(2,1)S(1)} %copy-done.13, ...), custom_call_target="tpu_custom_call" | custom-call | bytes 8257536 | tf_op jit(solution)/shard_map/window/pallas_call | solution.py:105
  95.8 3.9 %attend.3 = (bf16[192,384]{1,0:T(8,128)(2,1)S(1)}, bf16[192,384]{1,0:T(8,128)(2,1)S(1)}) custom-call(s32[8]{0:T(128)S(1)} %stack.73.place_ref, s32[6,12]{1,0:T(8,128)S(1)} %bitcast.27, s32[3]{0:T(128)S(1)} %get-tuple-element.42.turn_ref, bf16[3,768,128]{2,1,0:T(8,128)(2,1)S(1)} %get-tuple-element.32.q_all, ...), custom_call_target="tpu_custom_call" | custom-call | flops 2113929216 | bytes 4128768 | tf_op jit(solution)/shard_map/attend/pallas_call | solution.py:217
  99.7 2.1 %collective-permute-start.32 = (bf16[192,384]{1,0:T(8,128)(2,1)S(1)}, bf16[192,384]{1,0:T(8,128)(2,1)S(1)}, u32[]{:S(2)}, u32[]{:S(2)}) collective-permute-start(bf16[192,384]{1,0:T(8,128)(2,1)S(1)} %get-tuple-element.37), channel_id=1, source_target_pairs={{0,0},{1,1},{2,2},{3,3},{4,16},{5,17},{6,18},{7,19},{8,8},{9,9},{1... | collective-permute-start | bytes 442376 | tf_op jit(solution)/shard_map/ppermute | solution.py:295
  102.0 4.2 %collective-permute-done.32.refs_10_ = bf16[192,384]{1,0:T(8,128)(2,1)S(1)} collective-permute-done((bf16[192,384]{1,0:T(8,128)(2,1)S(1)}, bf16[192,384]{1,0:T(8,128)(2,1)S(1)}, u32[]{:S(2)}, u32[]{:S(2)}) %collective-permute-start.32) | collective-permute-done | bytes 147488 | tf_op jit(solution)/shard_map/ppermute | solution.py:295
  106.2 6.7 %collective-permute-start.33 = (bf16[192,384]{1,0:T(8,128)(2,1)S(1)}, bf16[192,384]{1,0:T(8,128)(2,1)S(1)}, u32[]{:S(2)}, u32[]{:S(2)}) collective-permute-start(bf16[192,384]{1,0:T(8,128)(2,1)S(1)} %get-tuple-element.38), channel_id=1, source_target_pairs={{0,1},{1,0},{2,3},{3,2},{4,17},{5,16},{6,19},{7,18},{8,9},{9,8},{1... | collective-permute-start | bytes 442376 | tf_op jit(solution)/shard_map/ppermute | solution.py:295
  112.9 0.5 collective-permute-start.12
  113.4 4.9 %attend.2 = (bf16[192,384]{1,0:T(8,128)(2,1)S(1)}, bf16[192,384]{1,0:T(8,128)(2,1)}) custom-call(s32[8]{0:T(128)S(1)} %stack.73.place_ref, s32[6,12]{1,0:T(8,128)S(1)} %bitcast.28, s32[3]{0:T(128)S(1)} %get-tuple-element.41.turn_ref, bf16[3,768,128]{2,1,0:T(8,128)(2,1)S(1)} %get-tuple-element.32.q_all, bf16[3,2304,128]{2,1,0:T(8,128)(2,1)S(1)} %get-tuple-element.33.k_all, ...), custom_call_target="tpu_custom_call" | custom-call | flops 2113929216 | bytes 4128768 | tf_op jit(solution)/shard_map/attend/pallas_call | solution.py:217
  118.3 9.4 %collective-permute-done.30.refs_8_ = bf16[192,384]{1,0:T(8,128)(2,1)S(1)} collective-permute-done((bf16[192,384]{1,0:T(8,128)(2,1)S(1)}, bf16[192,384]{1,0:T(8,128)(2,1)S(1)}, u32[]{:S(2)}, u32[]{:S(2)}) %collective-permute-start.30) | collective-permute-done | bytes 147488 | tf_op jit(solution)/shard_map/ppermute | solution.py:295
  127.8 0.7 copy-done.20
  128.4 1.6 %collective-permute-start.31 = (bf16[192,384]{1,0:T(8,128)(2,1)}, bf16[192,384]{1,0:T(8,128)(2,1)}, u32[]{:S(2)}, u32[]{:S(2)}) collective-permute-start(bf16[192,384]{1,0:T(8,128)(2,1)} %get-tuple-element.36), channel_id=1, source_target_pairs={{0,3},{1,2},{2,1},{3,0},{4,19},{5,18},{6,17},{7,16},{8,11},{9,10},... | collective-permute-start | bytes 442376 | tf_op jit(solution)/shard_map/ppermute | solution.py:295
  130.0 0.1 stack.68.place_ref
  130.1 6.5 %collective-permute-done.31.refs_9_ = bf16[192,384]{1,0:T(8,128)(2,1)} collective-permute-done((bf16[192,384]{1,0:T(8,128)(2,1)}, bf16[192,384]{1,0:T(8,128)(2,1)}, u32[]{:S(2)}, u32[]{:S(2)}) %collective-permute-start.31) | collective-permute-done | bytes 147488 | tf_op jit(solution)/shard_map/ppermute | solution.py:295
  136.7 0.9 copy-done.21
  137.6 3.9 %output.1 = bf16[1,192,1536]{2,1,0:T(8,128)(2,1)} custom-call(s32[7]{0:T(128)S(1)} %stack.68.place_ref, bf16[384,768]{1,0:T(8,128)(2,1)} %own_ref.1, bf16[384,768]{1,0:T(8,128)(2,1)S(1)} %collective-permute-done.far_ref, bf16[288,768]{1,0:T(8,128)(2,1)S(1)} %constant_dynamic-update-slice_fusion.refs_0_, bf16[288,768]{1,0:T(8,128)(2,1)S(1)} %collective-permute-done.7.refs_1_, ...), custom_call_target="tpu_custom_call" | custom-call | flops 905969664 | bytes 5898240 | tf_op jit(solution)/shard_map/output/pallas_call | solution.py:265
  (68 shorter events, 0.5 us)
Async XLA Ops:
  1.1 12.2 %collective-permute-start.1 = (bf16[96,1536]{1,0:T(8,128)(2,1)S(1)}, bf16[96,1536]{1,0:T(8,128)(2,1)S(1)}, u32[]{:S(2)}, u32[]{:S(2)}) collective-permute-start(bf16[96,1536]{1,0:T(8,128)(2,1)S(1)} %get-tuple-element.40), channel_id=1, source_target_pairs={{0,1},{1,3},{2,0},{3,2},{4,17},{5,19},{6,16},{7,18},{8,9},{9,11},{... | collective-permute-start | bytes 884744 | tf_op jit(solution)/shard_map/ppermute | solution.py:295
  4.8 14.9 %collective-permute-start.19 = (bf16[96,1536]{1,0:T(8,128)(2,1)S(1)}, bf16[96,1536]{1,0:T(8,128)(2,1)S(1)}, u32[]{:S(2)}, u32[]{:S(2)}) collective-permute-start(bf16[96,1536]{1,0:T(8,128)(2,1)S(1)} %get-tuple-element.39), channel_id=1, source_target_pairs={{0,1},{1,3},{2,0},{3,2},{4,17},{5,19},{6,16},{7,18},{8,9},{9,11},{... | collective-permute-start | bytes 884744 | tf_op jit(solution)/shard_map/ppermute | solution.py:295
  13.3 11.8 %collective-permute-start.2 = (bf16[96,1536]{1,0:T(8,128)(2,1)S(1)}, bf16[96,1536]{1,0:T(8,128)(2,1)}, u32[]{:S(2)}, u32[]{:S(2)}) collective-permute-start(bf16[96,1536]{1,0:T(8,128)(2,1)S(1)} %collective-permute-done.1.refs_1_), channel_id=1, source_target_pairs={{0,1},{1,3},{2,0},{3,2},{4,5},{5,7},{6,4},{7,6},{8,9},{9,11},{10,8... | collective-permute-start | bytes 884744 | tf_op jit(solution)/shard_map/ppermute | solution.py:314
  13.8 0.7 copy-start.8
  14.5 20.6 %collective-permute-start.16 = (bf16[768,384]{1,0:T(8,128)(2,1)}, bf16[768,384]{1,0:T(8,128)(2,1)S(1)}, u32[]{:S(2)}, u32[]{:S(2)}) collective-permute-start(bf16[768,384]{1,0:T(8,128)(2,1)} %refs_2_.7), channel_id=1, source_target_pairs={{0,16},{16,0},{1,17},{17,1},{2,18},{18,2},{3,19},{19,3},{4,20},{20... | collective-permute-start | bytes 1769480 | tf_op jit(solution)/shard_map/ppermute | solution.py:309
  14.7 25.7 %collective-permute-start.17 = (bf16[768,384]{1,0:T(8,128)(2,1)}, bf16[768,384]{1,0:T(8,128)(2,1)S(1)}, u32[]{:S(2)}, u32[]{:S(2)}) collective-permute-start(bf16[768,384]{1,0:T(8,128)(2,1)} %refs_3_.7), channel_id=1, source_target_pairs={{0,16},{16,0},{1,17},{17,1},{2,18},{18,2},{3,19},{19,3},{4,20},{20... | collective-permute-start | bytes 1769480 | tf_op jit(solution)/shard_map/ppermute | solution.py:309
  15.0 28.8 %collective-permute-start.18 = (bf16[768,384]{1,0:T(8,128)(2,1)}, bf16[768,384]{1,0:T(8,128)(2,1)S(1)}, u32[]{:S(2)}, u32[]{:S(2)}) collective-permute-start(bf16[768,384]{1,0:T(8,128)(2,1)} %refs_4_.5), channel_id=1, source_target_pairs={{0,16},{16,0},{1,17},{17,1},{2,18},{18,2},{3,19},{19,3},{4,20},{20... | collective-permute-start | bytes 1769480 | tf_op jit(solution)/shard_map/ppermute | solution.py:309
  19.6 37.7 %collective-permute-start.15 = (bf16[192,1536]{1,0:T(8,128)(2,1)}, bf16[192,1536]{1,0:T(8,128)(2,1)}, u32[]{:S(2)}, u32[]{:S(2)}) collective-permute-start(bf16[192,1536]{1,0:T(8,128)(2,1)} %bitcast.29), channel_id=1, source_target_pairs={{0,0},{1,1},{2,2},{3,3},{4,16},{5,17},{6,18},{7,19},{8,8},{9,9},{1... | collective-permute-start | bytes 1769480 | tf_op jit(solution)/shard_map/ppermute | solution.py:295
  25.2 9.6 %collective-permute-start.20 = (bf16[96,1536]{1,0:T(8,128)(2,1)S(1)}, bf16[96,1536]{1,0:T(8,128)(2,1)}, u32[]{:S(2)}, u32[]{:S(2)}) collective-permute-start(bf16[96,1536]{1,0:T(8,128)(2,1)S(1)} %collective-permute-done.19.refs_0_), channel_id=1, source_target_pairs={{0,1},{1,3},{2,0},{3,2},{4,5},{5,7},{6,4},{7,6},{8,9},{9,11},{10,8... | collective-permute-start | bytes 884744 | tf_op jit(solution)/shard_map/ppermute | solution.py:314
  26.2 0.7 copy-start.10
  34.7 22.5 %collective-permute-start.3 = (bf16[96,1536]{1,0:T(8,128)(2,1)}, bf16[96,1536]{1,0:T(8,128)(2,1)}, u32[]{:S(2)}, u32[]{:S(2)}) collective-permute-start(bf16[96,1536]{1,0:T(8,128)(2,1)} %collective-permute-done.2.refs_1_), channel_id=1, source_target_pairs={{0,1},{1,3},{2,0},{3,2},{4,5},{5,7},{6,4},{7,6},{8,9},{9,11},{10,8... | collective-permute-start | bytes 884744 | tf_op jit(solution)/shard_map/ppermute | solution.py:314
  35.1 26.0 %collective-permute-start.21 = (bf16[96,1536]{1,0:T(8,128)(2,1)}, bf16[96,1536]{1,0:T(8,128)(2,1)}, u32[]{:S(2)}, u32[]{:S(2)}) collective-permute-start(bf16[96,1536]{1,0:T(8,128)(2,1)} %collective-permute-done.20.refs_0_), channel_id=1, source_target_pairs={{0,1},{1,3},{2,0},{3,2},{4,5},{5,7},{6,4},{7,6},{8,9},{9,11},{10,8... | collective-permute-start | bytes 884744 | tf_op jit(solution)/shard_map/ppermute | solution.py:314
  40.4 10.6 %collective-permute-start.14 = (s32[7,12]{1,0:T(8,128)S(1)}, s32[7,12]{1,0:T(8,128)S(1)}, u32[]{:S(2)}, u32[]{:S(2)}) collective-permute-start(s32[7,12]{1,0:T(8,128)S(1)} %concatenate.7), channel_id=1, source_target_pairs={{0,0},{4,16},{8,8},{12,24},{16,4},{20,20},{24,12},{28,28},{1,1},{5... | collective-permute-start | bytes 1016 | tf_op jit(solution)/shard_map/ppermute | solution.py:311
  43.8 1.1 copy-start
  44.9 1.1 copy-start.2
  46.0 1.1 copy-start.4
  47.0 7.4 %copy-start.9 = (bf16[96,1536]{1,0:T(8,128)(2,1)S(1)}, bf16[96,1536]{1,0:T(8,128)(2,1)}, u32[]{:S(2)}) copy-start(bf16[96,1536]{1,0:T(8,128)(2,1)} %copy-done.8) | copy-start | bytes 884740
  47.0 7.5 %copy-start.11 = (bf16[96,1536]{1,0:T(8,128)(2,1)S(1)}, bf16[96,1536]{1,0:T(8,128)(2,1)}, u32[]{:S(2)}) copy-start(bf16[96,1536]{1,0:T(8,128)(2,1)} %copy-done.10) | copy-start | bytes 884740
  50.3 0.7 copy-start.12
  51.0 10.1 %copy-start.1 = (bf16[768,384]{1,0:T(8,128)(2,1)S(1)}, bf16[768,384]{1,0:T(8,128)(2,1)}, u32[]{:S(2)}) copy-start(bf16[768,384]{1,0:T(8,128)(2,1)} %refs_2_.7) | copy-start | bytes 1769476
  51.0 10.1 %copy-start.3 = (bf16[768,384]{1,0:T(8,128)(2,1)S(1)}, bf16[768,384]{1,0:T(8,128)(2,1)}, u32[]{:S(2)}) copy-start(bf16[768,384]{1,0:T(8,128)(2,1)} %refs_3_.7) | copy-start | bytes 1769476
  51.0 10.2 %copy-start.5 = (bf16[768,384]{1,0:T(8,128)(2,1)S(1)}, bf16[768,384]{1,0:T(8,128)(2,1)}, u32[]{:S(2)}) copy-start(bf16[768,384]{1,0:T(8,128)(2,1)} %refs_4_.5) | copy-start | bytes 1769476
  51.0 12.6 %collective-permute-start.24 = (bf16[192,768]{1,0:T(8,128)(2,1)}, bf16[192,768]{1,0:T(8,128)(2,1)}, u32[]{:S(2)}, u32[]{:S(2)}) collective-permute-start(bf16[192,768]{1,0:T(8,128)(2,1)} %get-tuple-element.30.refs_6_), channel_id=1, source_target_pairs={{0,16},{16,0},{1,17},{17,1},{2,18},{18,2},{3,19},{19,3},{4,20},{20... | collective-permute-start | bytes 884744 | tf_op jit(solution)/shard_map/ppermute | solution.py:336
  51.0 12.7 %collective-permute-start.28 = (bf16[192,768]{1,0:T(8,128)(2,1)}, bf16[192,768]{1,0:T(8,128)(2,1)}, u32[]{:S(2)}, u32[]{:S(2)}) collective-permute-start(bf16[192,768]{1,0:T(8,128)(2,1)} %get-tuple-element.30.refs_6_), channel_id=1, source_target_pairs={{16,8},{20,12},{8,16},{12,20},{17,9},{21,13},{9,17},{13,21},{18,10... | collective-permute-start | bytes 884744 | tf_op jit(solution)/shard_map/ppermute | solution.py:335
  56.6 0.7 copy-start.14
  57.3 12.9 %collective-permute-start.23 = (bf16[192,768]{1,0:T(8,128)(2,1)}, bf16[192,768]{1,0:T(8,128)(2,1)}, u32[]{:S(2)}, u32[]{:S(2)}) collective-permute-start(bf16[192,768]{1,0:T(8,128)(2,1)} %get-tuple-element.29.refs_5_), channel_id=1, source_target_pairs={{0,16},{16,0},{1,17},{17,1},{2,18},{18,2},{3,19},{19,3},{4,20},{20... | collective-permute-start | bytes 884744 | tf_op jit(solution)/shard_map/ppermute | solution.py:336
  57.3 13.2 %collective-permute-start.27 = (bf16[192,768]{1,0:T(8,128)(2,1)}, bf16[192,768]{1,0:T(8,128)(2,1)}, u32[]{:S(2)}, u32[]{:S(2)}) collective-permute-start(bf16[192,768]{1,0:T(8,128)(2,1)} %get-tuple-element.29.refs_5_), channel_id=1, source_target_pairs={{16,8},{20,12},{8,16},{12,20},{17,9},{21,13},{9,17},{13,21},{18,10... | collective-permute-start | bytes 884744 | tf_op jit(solution)/shard_map/ppermute | solution.py:335
  61.1 13.1 %collective-permute-start.4 = (bf16[96,768]{1,0:T(8,128)(2,1)}, bf16[96,768]{1,0:T(8,128)(2,1)}, u32[]{:S(2)}, u32[]{:S(2)}) collective-permute-start(bf16[96,768]{1,0:T(8,128)(2,1)} %constant_dynamic-slice_fusion), channel_id=1, source_target_pairs={{0,1},{1,2},{2,3},{3,0},{4,5},{5,6},{6,7},{7,4},{8,9},{9,10},{10,1... | collective-permute-start | bytes 442376 | tf_op jit(solution)/shard_map/ppermute | solution.py:321
  63.6 6.6 %copy-start.16 = (bf16[192,384]{1,0:T(8,128)(2,1)}, bf16[192,384]{1,0:T(8,128)(2,1)S(1)}, u32[]{:S(2)}) copy-start(bf16[192,384]{1,0:T(8,128)(2,1)S(1)} %get-tuple-element.23.refs_0_) | copy-start | bytes 442372
  63.6 6.9 %copy-start.6 = (bf16[192,768]{1,0:T(8,128)(2,1)}, bf16[192,768]{1,0:T(8,128)(2,1)S(1)}, u32[]{:S(2)}) copy-start(bf16[192,768]{1,0:T(8,128)(2,1)S(1)} %get-tuple-element.28.refs_4_) | copy-start | bytes 884740
  63.6 11.7 %collective-permute-start.5 = (bf16[96,768]{1,0:T(8,128)(2,1)}, bf16[96,768]{1,0:T(8,128)(2,1)S(1)}, u32[]{:S(2)}, u32[]{:S(2)}) collective-permute-start(bf16[96,768]{1,0:T(8,128)(2,1)} %constant_dynamic-slice_fusion), channel_id=1, source_target_pairs={{0,2},{1,3},{2,0},{3,1},{4,6},{5,7},{6,4},{7,5},{8,10},{9,11},{10,... | collective-permute-start | bytes 442376 | tf_op jit(solution)/shard_map/ppermute | solution.py:321
  63.7 12.1 %collective-permute-start.6 = (bf16[96,768]{1,0:T(8,128)(2,1)}, bf16[96,768]{1,0:T(8,128)(2,1)S(1)}, u32[]{:S(2)}, u32[]{:S(2)}) collective-permute-start(bf16[96,768]{1,0:T(8,128)(2,1)} %constant_dynamic-slice_fusion), channel_id=1, source_target_pairs={{0,3},{1,0},{2,1},{3,2},{4,7},{5,4},{6,5},{7,6},{8,11},{9,8},{10,9... | collective-permute-start | bytes 442376 | tf_op jit(solution)/shard_map/ppermute | solution.py:321
  70.2 8.5 %copy-start.18 = (bf16[192,384]{1,0:T(8,128)(2,1)}, bf16[192,384]{1,0:T(8,128)(2,1)S(1)}, u32[]{:S(2)}) copy-start(bf16[192,384]{1,0:T(8,128)(2,1)S(1)} %get-tuple-element.27.refs_3_) | copy-start | bytes 442372
  70.2 8.2 %collective-permute-start.22 = (bf16[192,768]{1,0:T(8,128)(2,1)S(1)}, bf16[192,768]{1,0:T(8,128)(2,1)S(1)}, u32[]{:S(2)}, u32[]{:S(2)}) collective-permute-start(bf16[192,768]{1,0:T(8,128)(2,1)S(1)} %get-tuple-element.28.refs_4_), channel_id=1, source_target_pairs={{0,16},{16,0},{1,17},{17,1},{2,18},{18,2},{3,19},{19,3},{4,20},{20... | collective-permute-start | bytes 884744 | tf_op jit(solution)/shard_map/ppermute | solution.py:336
  70.5 8.1 %collective-permute-start.26 = (bf16[192,768]{1,0:T(8,128)(2,1)S(1)}, bf16[192,768]{1,0:T(8,128)(2,1)S(1)}, u32[]{:S(2)}, u32[]{:S(2)}) collective-permute-start(bf16[192,768]{1,0:T(8,128)(2,1)S(1)} %get-tuple-element.28.refs_4_), channel_id=1, source_target_pairs={{16,8},{20,12},{8,16},{12,20},{17,9},{21,13},{9,17},{13,21},{18,10... | collective-permute-start | bytes 884744 | tf_op jit(solution)/shard_map/ppermute | solution.py:335
  74.2 4.4 %collective-permute-start.25 = (bf16[192,768]{1,0:T(8,128)(2,1)}, bf16[192,768]{1,0:T(8,128)(2,1)S(1)}, u32[]{:S(2)}, u32[]{:S(2)}) collective-permute-start(bf16[192,768]{1,0:T(8,128)(2,1)} %get-tuple-element.31.refs_7_), channel_id=1, source_target_pairs={{0,16},{16,0},{1,17},{17,1},{2,18},{18,2},{3,19},{19,3},{4,20},{20... | collective-permute-start | bytes 884744 | tf_op jit(solution)/shard_map/ppermute | solution.py:336
  75.3 26.6 %collective-permute-start = (bf16[384,768]{1,0:T(8,128)(2,1)}, bf16[384,768]{1,0:T(8,128)(2,1)S(1)}, u32[]{:S(2)}, u32[]{:S(2)}) collective-permute-start(bf16[384,768]{1,0:T(8,128)(2,1)} %own_ref.1), channel_id=1, source_target_pairs={{0,16},{16,0},{1,17},{17,1},{2,18},{18,2},{3,19},{19,3},{4,20},{20... | collective-permute-start | bytes 1769480 | tf_op jit(solution)/shard_map/ppermute | solution.py:312
  75.8 12.6 %collective-permute-start.29 = (bf16[192,768]{1,0:T(8,128)(2,1)}, bf16[192,768]{1,0:T(8,128)(2,1)S(1)}, u32[]{:S(2)}, u32[]{:S(2)}) collective-permute-start(bf16[192,768]{1,0:T(8,128)(2,1)} %get-tuple-element.31.refs_7_), channel_id=1, source_target_pairs={{16,8},{20,12},{8,16},{12,20},{17,9},{21,13},{9,17},{13,21},{18,10... | collective-permute-start | bytes 884744 | tf_op jit(solution)/shard_map/ppermute | solution.py:335
  78.3 34.5 %collective-permute-start.7 = (bf16[288,768]{1,0:T(8,128)(2,1)S(1)}, bf16[288,768]{1,0:T(8,128)(2,1)S(1)}, u32[]{:S(2)}, u32[]{:S(2)}) collective-permute-start(bf16[288,768]{1,0:T(8,128)(2,1)S(1)} %constant_dynamic-update-slice_fusion.refs_0_), channel_id=1, source_target_pairs={{0,4},{4,0},{8,12},{12,8},{1,5},{5,1},{9,13},{13,9},{2,6},{6,2},{1... | collective-permute-start | bytes 1327112 | tf_op jit(solution)/shard_map/ppermute | solution.py:325
  78.6 34.3 %collective-permute-start.8 = (bf16[288,768]{1,0:T(8,128)(2,1)S(1)}, bf16[288,768]{1,0:T(8,128)(2,1)S(1)}, u32[]{:S(2)}, u32[]{:S(2)}) collective-permute-start(bf16[288,768]{1,0:T(8,128)(2,1)S(1)} %constant_dynamic-update-slice_fusion.refs_0_), channel_id=1, source_target_pairs={{0,8},{4,12},{8,0},{12,4},{1,9},{5,13},{9,1},{13,5},{2,10},{6,14},... | collective-permute-start | bytes 1327112 | tf_op jit(solution)/shard_map/ppermute | solution.py:325
  78.6 34.8 %collective-permute-start.9 = (bf16[288,768]{1,0:T(8,128)(2,1)S(1)}, bf16[288,768]{1,0:T(8,128)(2,1)S(1)}, u32[]{:S(2)}, u32[]{:S(2)}) collective-permute-start(bf16[288,768]{1,0:T(8,128)(2,1)S(1)} %constant_dynamic-update-slice_fusion.refs_0_), channel_id=1, source_target_pairs={{0,12},{4,8},{8,4},{12,0},{1,13},{5,9},{9,5},{13,1},{2,14},{6,10},... | collective-permute-start | bytes 1327112 | tf_op jit(solution)/shard_map/ppermute | solution.py:325
  88.4 1.0 copy-start.7
  89.3 0.9 copy-start.13
  90.3 0.9 copy-start.15
  91.2 0.9 copy-start.17
  92.1 0.9 copy-start.19
  99.7 6.5 %collective-permute-start.32 = (bf16[192,384]{1,0:T(8,128)(2,1)S(1)}, bf16[192,384]{1,0:T(8,128)(2,1)S(1)}, u32[]{:S(2)}, u32[]{:S(2)}) collective-permute-start(bf16[192,384]{1,0:T(8,128)(2,1)S(1)} %get-tuple-element.37), channel_id=1, source_target_pairs={{0,0},{1,1},{2,2},{3,3},{4,16},{5,17},{6,18},{7,19},{8,8},{9,9},{1... | collective-permute-start | bytes 442376 | tf_op jit(solution)/shard_map/ppermute | solution.py:295
  101.9 34.7 %collective-permute-start.10 = (bf16[288,768]{1,0:T(8,128)(2,1)S(1)}, bf16[288,768]{1,0:T(8,128)(2,1)S(1)}, u32[]{:S(2)}, u32[]{:S(2)}) collective-permute-start(bf16[288,768]{1,0:T(8,128)(2,1)S(1)} %constant_dynamic-update-slice_fusion.refs_0_), channel_id=1, source_target_pairs={{0,16},{16,0},{1,17},{17,1},{2,18},{18,2},{3,19},{19,3},{4,20},{20... | collective-permute-start | bytes 1327112 | tf_op jit(solution)/shard_map/ppermute | solution.py:326
  106.2 12.1 %collective-permute-start.33 = (bf16[192,384]{1,0:T(8,128)(2,1)S(1)}, bf16[192,384]{1,0:T(8,128)(2,1)S(1)}, u32[]{:S(2)}, u32[]{:S(2)}) collective-permute-start(bf16[192,384]{1,0:T(8,128)(2,1)S(1)} %get-tuple-element.38), channel_id=1, source_target_pairs={{0,1},{1,0},{2,3},{3,2},{4,17},{5,16},{6,19},{7,18},{8,9},{9,8},{1... | collective-permute-start | bytes 442376 | tf_op jit(solution)/shard_map/ppermute | solution.py:295
  112.9 23.8 %collective-permute-start.11 = (bf16[288,768]{1,0:T(8,128)(2,1)S(1)}, bf16[288,768]{1,0:T(8,128)(2,1)S(1)}, u32[]{:S(2)}, u32[]{:S(2)}) collective-permute-start(bf16[288,768]{1,0:T(8,128)(2,1)S(1)} %collective-permute-done.7.refs_1_), channel_id=1, source_target_pairs={{0,16},{16,0},{1,17},{17,1},{2,18},{18,2},{3,19},{19,3},{4,20},{20... | collective-permute-start | bytes 1327112 | tf_op jit(solution)/shard_map/ppermute | solution.py:326
  112.9 23.8 %collective-permute-start.12 = (bf16[288,768]{1,0:T(8,128)(2,1)S(1)}, bf16[288,768]{1,0:T(8,128)(2,1)}, u32[]{:S(2)}, u32[]{:S(2)}) collective-permute-start(bf16[288,768]{1,0:T(8,128)(2,1)S(1)} %collective-permute-done.8.refs_2_), channel_id=1, source_target_pairs={{0,16},{16,0},{1,17},{17,1},{2,18},{18,2},{3,19},{19,3},{4,20},{20... | collective-permute-start | bytes 1327112 | tf_op jit(solution)/shard_map/ppermute | solution.py:326
  113.4 23.3 %collective-permute-start.13 = (bf16[288,768]{1,0:T(8,128)(2,1)S(1)}, bf16[288,768]{1,0:T(8,128)(2,1)}, u32[]{:S(2)}, u32[]{:S(2)}) collective-permute-start(bf16[288,768]{1,0:T(8,128)(2,1)S(1)} %collective-permute-done.9.refs_3_), channel_id=1, source_target_pairs={{0,16},{16,0},{1,17},{17,1},{2,18},{18,2},{3,19},{19,3},{4,20},{20... | collective-permute-start | bytes 1327112 | tf_op jit(solution)/shard_map/ppermute | solution.py:326
  118.3 9.4 %collective-permute-start.30 = (bf16[192,384]{1,0:T(8,128)(2,1)S(1)}, bf16[192,384]{1,0:T(8,128)(2,1)S(1)}, u32[]{:S(2)}, u32[]{:S(2)}) collective-permute-start(bf16[192,384]{1,0:T(8,128)(2,1)S(1)} %get-tuple-element.35), channel_id=1, source_target_pairs={{0,2},{1,3},{2,0},{3,1},{4,18},{5,19},{6,16},{7,17},{8,10},{9,11},... | collective-permute-start | bytes 442376 | tf_op jit(solution)/shard_map/ppermute | solution.py:295
  127.8 0.7 copy-start.20
  128.4 8.2 %collective-permute-start.31 = (bf16[192,384]{1,0:T(8,128)(2,1)}, bf16[192,384]{1,0:T(8,128)(2,1)}, u32[]{:S(2)}, u32[]{:S(2)}) collective-permute-start(bf16[192,384]{1,0:T(8,128)(2,1)} %get-tuple-element.36), channel_id=1, source_target_pairs={{0,3},{1,2},{2,1},{3,0},{4,19},{5,18},{6,17},{7,16},{8,11},{9,10},... | collective-permute-start | bytes 442376 | tf_op jit(solution)/shard_map/ppermute | solution.py:295
  136.6 0.9 copy-start.21

commit v3 on v2

v3 whole, which is shorter than its diff:
```python
import functools

import jax
import jax.numpy as jnp
from jax import lax
from jax.experimental import pallas as pl
from jax.experimental.pallas import tpu as pltpu
from jax.sharding import PartitionSpec as P

HD = 64
GROUP = 128
LANES = 128

epsilon = 1e-05

VMEM = pl.BlockSpec(memory_space=pltpu.VMEM)
SMEM = pl.BlockSpec(memory_space=pltpu.SMEM)
ANY = pl.BlockSpec(memory_space=pl.ANY)
MIB = 1024 * 1024
LIGHT = pl.CostEstimate(flops=1, bytes_accessed=1, transcendentals=0)


def ring_successors(count):
    order = [0] + list(range(1, count, 2)) + list(range(count - 2 + count % 2, 0, -2))
    return {order[i]: order[(i + 1) % count] for i in range(count)}


def lookup(table, index):
    value = jnp.int32(table[0])
    for place in range(1, len(table)):
        value = jnp.where(index == place, jnp.int32(table[place]), value)
    return value


def copy_all(pairs, sems):
    copies = [pltpu.make_async_copy(source, target, sems.at[i]) for i, (source, target) in enumerate(pairs)]
    for copy in copies:
        copy.start()
    return copies


def pack_kernel(place_ref, rows_ref, w_out_ref, out_ref, sems):
    count = rows_ref.shape[0]
    part, columns = (out_ref.shape[0] - count), w_out_ref.shape[1]
    first = pl.multiple_of(place_ref[0] * 2 * part, 2 * part)
    pairs = [(rows_ref, out_ref.at[pl.ds(0, count), :])]
    for side in range(2):
        pairs.append((
            w_out_ref.at[pl.ds(first + side * part, part), :],
            out_ref.at[pl.ds(count, part), pl.ds(side * columns, columns)],
        ))
    for copy in copy_all(pairs, sems):
        copy.wait()


def pack(place, rows, w_out, share):
    part = w_out.shape[0] // share // 2
    return pl.pallas_call(
        pack_kernel,
        out_shape=jax.ShapeDtypeStruct((rows.shape[0] + part, rows.shape[1]), jnp.bfloat16),
        in_specs=[SMEM, ANY, ANY],
        out_specs=ANY,
        scratch_shapes=[pltpu.SemaphoreType.DMA((3,))],
        compiler_params=pltpu.CompilerParams(vmem_limit_bytes=MIB),
        cost_estimate=LIGHT,
        name="pack",
    )(place, rows, w_out)


def project_kernel(blocks, count, stacked, place_ref, gain_ref, *refs):
    rows, own, other = refs[:blocks], refs[blocks], refs[blocks + 1]
    extra = refs[blocks + 2:blocks + 2 + stacked]
    outs = refs[blocks + 2 + stacked:]
    query_ref, pair_ref = outs[:2]
    held, mine_ref, theirs_ref, sems = outs[-4:]
    depth, width = own.shape[0], query_ref.shape[1]
    loads = copy_all(
        [(rows[i].at[pl.ds(0, count), :], held.at[pl.ds(i * count, count), :]) for i in range(blocks)], sems
    )
    loads += copy_all(
        [(own.at[:, pl.ds(0, 3 * width)], mine_ref), (other.at[:, pl.ds(0, 3 * width)], theirs_ref)],
        sems.at[pl.ds(blocks, 2)],
    )
    sides = []
    for i, source in enumerate(extra):
        part = source.shape[0] - count
        sides.append((source.at[pl.ds(count, part), :], outs[2].at[pl.ds(i * part, part), :]))
    sides = copy_all(sides, sems.at[pl.ds(blocks + 2, max(1, stacked))])
    gain = gain_ref[...]
    first = place_ref[0] == 0
    mine, theirs = [], []
    for i in range(blocks):
        loads[i].wait()
        values = held[i * count:(i + 1) * count, :].astype(jnp.float32)
        center = values - jnp.mean(values, axis=-1, keepdims=True)
        spread = jnp.mean(center * center, axis=-1, keepdims=True)
        normalized = (center * lax.rsqrt(spread + epsilon) * gain).astype(jnp.bfloat16)
        low, high = normalized[:, :depth], normalized[:, depth:]
        mine.append(jnp.where(first, low, high))
        theirs.append(jnp.where(first, high, low))
    for load in loads[blocks:]:
        load.wait()
    mine = mine[0] if blocks == 1 else jnp.concatenate(mine, axis=0)
    theirs = theirs[0] if blocks == 1 else jnp.concatenate(theirs, axis=0)
    for place in range(3):
        columns = slice(place * width, (place + 1) * width)
        got = jnp.dot(mine, mine_ref[:, columns], preferred_element_type=jnp.float32)
        got = (got + jnp.dot(theirs, theirs_ref[:, columns], preferred_element_type=jnp.float32)).astype(jnp.bfloat16)
        if place == 0:
            query_ref[...] = (got.astype(jnp.float32) * (HD ** -0.5)).astype(jnp.bfloat16)
        else:
            pair_ref[:, (place - 1) * width:place * width] = got
    for copy in sides:
        copy.wait()


def project(place, rows, count, width, gain, own, other, extra=()):
    blocks, depth = len(rows), rows[0].shape[1]
    total = blocks * count
    part = extra[0].shape[0] - count if extra else 0
    out_shape = [
        jax.ShapeDtypeStruct((total, width), jnp.bfloat16),
        jax.ShapeDtypeStruct((total, 2 * width), jnp.bfloat16),
    ]
    if extra:
        out_shape.append(jax.ShapeDtypeStruct((len(extra) * part, depth), jnp.bfloat16))
    return pl.pallas_call(
        functools.partial(project_kernel, blocks, count, len(extra)),
        out_shape=out_shape,
        in_specs=[SMEM, VMEM] + [ANY] * (blocks + 2 + len(extra)),
        out_specs=[VMEM, VMEM] + [ANY] * (1 if extra else 0),
        scratch_shapes=[
            pltpu.VMEM((total, depth), jnp.bfloat16),
            pltpu.VMEM((own.shape[0], 3 * width), jnp.bfloat16),
            pltpu.VMEM((own.shape[0], 3 * width), jnp.bfloat16),
            pltpu.SemaphoreType.DMA((blocks + 2 + max(1, len(extra)),)),
        ],
        compiler_params=pltpu.CompilerParams(vmem_limit_bytes=20 * MIB),
        cost_estimate=pl.CostEstimate(
            flops=2 * total * depth * 3 * width,
            bytes_accessed=2 * (depth * 3 * width + total * (depth + 3 * width)),
            transcendentals=total,
        ),
        name="project",
    )(place, gain, *rows, own, other, *extra)


def window_kernel(shape, groups, place_ref, *refs):
    kinds = len(shape)
    queries, owns, sides = refs[:kinds], refs[kinds:2 * kinds], refs[2 * kinds:4 * kinds]
    q_all, kv_all, vt_all, sems = refs[4 * kinds:]
    block, width = q_all.shape
    rows = block // sum(shape)
    core = place_ref[0]
    chip_base = jnp.where(core == 0, 2 * block, 0)
    link_base = jnp.where(core == 0, 0, 2 * block)
    pairs, step = [], 0
    for kind in range(kinds):
        for inside in range(shape[kind]):
            at = place_ref[4 + step] * rows
            part = pl.ds(inside * rows, rows)
            pairs.append((queries[kind].at[part, :], q_all.at[pl.ds(pl.multiple_of(at, 64), rows), :]))
            for source, base in (
                (owns[kind], block), (sides[kind], chip_base), (sides[kinds + kind], link_base)
            ):
                to = pl.ds(pl.multiple_of(base + at, 64), rows)
                pairs.append((source.at[part, :], kv_all.at[to, :]))
            step += 1
    for copy in copy_all(pairs, sems):
        copy.wait()
    for index in range(3 * groups):
        for pair in range(width // LANES):
            columns = slice(width + pair * LANES, width + (pair + 1) * LANES)
            vt_all[pair, index] = kv_all[index * GROUP:(index + 1) * GROUP, columns].T


def window(place, groups, rows, queries, owns, chip_side, link_side):
    shape = [query.shape[0] // rows for query in queries]
    width, block = queries[0].shape[1], sum(shape) * rows
    pairs = width // LANES
    return pl.pallas_call(
        functools.partial(window_kernel, shape, groups),
        out_shape=(
            jax.ShapeDtypeStruct((block, width), jnp.bfloat16),
            jax.ShapeDtypeStruct((3 * block, 2 * width), jnp.bfloat16),
            jax.ShapeDtypeStruct((pairs, 3 * groups, LANES, GROUP), jnp.bfloat16),
        ),
        in_specs=[SMEM] + [ANY] * (4 * len(shape)),
        out_specs=(VMEM,) * 3,
        scratch_shapes=[pltpu.SemaphoreType.DMA((4 * sum(shape),))],
        compiler_params=pltpu.CompilerParams(vmem_limit_bytes=16 * MIB),
        cost_estimate=pl.CostEstimate(flops=0, bytes_accessed=2 * 14 * block * width, transcendentals=0),
        name="window",
    )(place, *queries, *owns, *chip_side, *link_side)


def attend_kernel(groups, reach, count_rows, place_ref, band_ref, turn_ref, q_all, kv_all, vt_all, *refs):
    outs, (score, ctx, chosen, limits) = refs[:-4], refs[-4:]
    pairs, rows = vt_all.shape[0], outs[0].shape[0]
    first_group, total, length = (place_ref[i] for i in range(1, 4))
    first_row = turn_ref[0]
    slots = 2 * reach + 2
    half_mask = lax.broadcasted_iota(jnp.int32, (GROUP, LANES), 1) < HD
    row_ids = lax.broadcasted_iota(jnp.int32, (GROUP, 2 * GROUP), 0)
    part_group = lax.div(length, jnp.int32(GROUP))
    part_left = lax.rem(length, jnp.int32(GROUP))

    def one_group(place, carry):
        group = first_row // GROUP + place
        for slot in range(slots):
            chosen[slot] = groups + group
        offset = part_group - first_group - group
        column = jnp.clip(jnp.where(offset < 0, offset + reach, offset + reach - 1), 0, 2 * reach - 1)
        cut = (part_left > 0) & (offset != 0) & (jnp.abs(offset) <= reach) & (part_group < total)
        cut = cut & (band_ref[group, column] == 1)
        chosen[1] = jnp.where(cut, groups + group + offset, groups + group)
        limits[0] = jnp.where(cut, part_left, 0)
        count = 1 + cut.astype(jnp.int32)
        for column in range(2 * reach):
            offset = column - reach if column < reach else column - reach + 1
            there = first_group + group + offset
            good = (there >= 0) & (there < part_group) & (there < total) & (band_ref[group, column] == 1)
            chosen[count] = jnp.where(good, groups + group + offset, groups + group)
            limits[0] = jnp.where(good & (count == 1), GROUP, limits[0])
            count = count + good.astype(jnp.int32)
        query_at = pl.ds(pl.multiple_of(group * GROUP, GROUP), GROUP)
        out_at = pl.ds(pl.multiple_of(place * GROUP, GROUP), GROUP)

        def run(size):
            first_limit = limits[0]
            last_limit = jnp.where(count == size, GROUP, 0)
            indices = [chosen[slot] for slot in range(size)]
            best = []
            for pair in range(pairs):
                own = q_all[query_at, pair * LANES:(pair + 1) * LANES]
                zero = jnp.zeros_like(own)
                both = jnp.concatenate(
                    [jnp.where(half_mask, own, zero), jnp.where(half_mask, zero, own)], axis=0
                ).T
                top = None
                for slot in range(0, size, 2):
                    tiles = [
                        kv_all[pl.ds(pl.multiple_of(index * GROUP, GROUP), GROUP), pair * LANES:(pair + 1) * LANES]
                        for index in indices[slot:slot + 2]
                    ]
                    got = jnp.dot(jnp.concatenate(tiles, axis=0), both, preferred_element_type=jnp.float32)
                    for one in (slot, slot + 1):
                        part = got[(one - slot) * GROUP:(one - slot + 1) * GROUP]
                        if one == 1:
                            part = jnp.where(row_ids < first_limit, part, -jnp.inf)
                        elif one == size - 1:
                            part = jnp.where(row_ids < last_limit, part, -jnp.inf)
                        score[pair, one * GROUP:(one + 1) * GROUP, :] = part
                        high = jnp.max(part.reshape(GROUP // 8, 8, 2 * GROUP), axis=0)
                        top = high if top is None else jnp.maximum(top, high)
                best.append(jnp.max(top, axis=0, keepdims=True))
            for pair in range(pairs):
                total_sum = jnp.zeros((8, 2 * GROUP), jnp.float32)
                mixed = jnp.zeros((LANES, 2 * GROUP), jnp.float32)
                for slot in range(0, size, 2):
                    weights = jnp.exp(score[pair, slot * GROUP:(slot + 2) * GROUP, :] - best[pair])
                    total_sum += jnp.sum(weights.reshape(2 * GROUP // 8, 8, 2 * GROUP), axis=0)
                    tiles = [vt_all[pair, index] for index in indices[slot:slot + 2]]
                    mixed += jnp.dot(
                        jnp.concatenate(tiles, axis=1),
                        weights.astype(jnp.bfloat16),
                        preferred_element_type=jnp.float32,
                    )
                mixed = mixed / jnp.sum(total_sum, axis=0, keepdims=True)
                both_heads = jnp.concatenate([mixed[:HD, :GROUP], mixed[HD:, GROUP:]], axis=0)
                ctx[pair, out_at, :] = both_heads.T.astype(jnp.bfloat16)

        for size in range(2, slots + 1, 2):
            @pl.when((count == size) | (count == size - 1))
            def _():
                run(size)

        return carry

    lax.fori_loop(0, count_rows // GROUP, one_group, 0)
    for place, out in enumerate(outs):
        at = pl.ds(pl.multiple_of(turn_ref[1 + place], 64), rows)
        for pair in range(pairs):
            out[:, pair * LANES:(pair + 1) * LANES] = ctx[pair, at, :]


def attend(place, band, turn, outs, q_all, kv_all, vt_all):
    groups, reach = band.shape[0], band.shape[1] // 2
    pairs, block = vt_all.shape[0], q_all.shape[0]
    rows = block // (2 * outs)
    slots = 2 * reach + 2
    return pl.pallas_call(
        functools.partial(attend_kernel, groups, reach, block // 2),
        out_shape=[jax.ShapeDtypeStruct((rows, pairs * LANES), jnp.bfloat16)] * outs,
        in_specs=[SMEM, SMEM, SMEM] + [VMEM] * 3,
        out_specs=[VMEM] * outs,
        scratch_shapes=[
            pltpu.VMEM((pairs, slots * GROUP, 2 * GROUP), jnp.float32),
            pltpu.VMEM((pairs, block // 2, LANES), jnp.bfloat16),
            pltpu.SMEM((slots + 2,), jnp.int32),
            pltpu.SMEM((1,), jnp.int32),
        ],
        compiler_params=pltpu.CompilerParams(vmem_limit_bytes=16 * MIB),
        cost_estimate=pl.CostEstimate(flops=1 << 32, bytes_accessed=1 << 20, transcendentals=0),
        name="attend",
    )(place, band, turn, q_all, kv_all, vt_all)


def join_kernel(*refs):
    sources, out, sems = refs[:-2], refs[-2], refs[-1]
    pairs, at = [], 0
    for source in sources:
        pairs.append((source, out.at[pl.ds(at, source.shape[0]), :]))
        at += source.shape[0]
    for copy in copy_all(pairs, sems):
        copy.wait()


def join(values):
    rows = sum(value.shape[0] for value in values)
    return pl.pallas_call(
        join_kernel,
        out_shape=jax.ShapeDtypeStruct((rows, values[0].shape[1]), jnp.bfloat16),
        in_specs=[ANY] * len(values),
        out_specs=ANY,
        scratch_shapes=[pltpu.SemaphoreType.DMA((len(values),))],
        compiler_params=pltpu.CompilerParams(vmem_limit_bytes=MIB),
        cost_estimate=LIGHT,
        name="join",
    )(*values)


def place_kernel(share, place_ref, own_ref, far_ref, mine_ref, theirs_ref, *refs):
    out_ref, sems = refs[-2:]
    core, layer, seq = (place_ref[i] for i in range(3))
    layers, _, depth, columns = out_ref.shape
    part = depth // share // 2
    half = columns // 2
    pairs = [(own_ref, out_ref.at[layer, core])]
    for side in range(2):
        pairs.append((
            far_ref.at[pl.ds(side * depth, depth), pl.ds(far_ref.shape[1] - half, half)],
            out_ref.at[layer, 1 - core, :, pl.ds(side * half, half)],
        ))
    for other in range(share):
        there = seq ^ other
        for source, source_core in ((mine_ref, core), (theirs_ref, 1 - core)):
            at = lax.rem(there // 2 * 2 + source_core, share) * 2 * part
            for step in range(layers - 1):
                row = (other * (layers - 1) + step) * part
                for side in range(2):
                    pairs.append((
                        source.at[pl.ds(row, part), pl.ds(side * columns, columns)],
                        out_ref.at[
                            place_ref[3 + step], lax.rem(there, 2),
                            pl.ds(pl.multiple_of(at + side * part, 16), part), :
                        ],
                    ))
    for copy in copy_all(pairs, sems):
        copy.wait()


def place_weights(place, share, layers, own, far, mine, theirs, held):
    depth, columns = own.shape
    return pl.pallas_call(
        functools.partial(place_kernel, share),
        out_shape=jax.ShapeDtypeStruct((layers, 2, depth, columns), jnp.bfloat16),
        in_specs=[SMEM] + [ANY] * (4 + len(held)),
        out_specs=VMEM,
        scratch_shapes=[pltpu.SemaphoreType.DMA((3 + 4 * share * (layers - 1),))],
        compiler_params=pltpu.CompilerParams(vmem_limit_bytes=8 * MIB),
        cost_estimate=LIGHT,
        name="place",
    )(place, own, far, mine, theirs, *held)


def output_kernel(layers, place_ref, weight, *refs):
    contexts, out_ref = refs[:layers], refs[layers]
    columns = weight.shape[3]
    for side in range(2):
        total = None
        for step in range(layers):
            got = jnp.dot(contexts[step][...], weight[place_ref[step], side], preferred_element_type=jnp.float32)
            total = got if total is None else total + got
        out_ref[0, :, side * columns:(side + 1) * columns] = total.astype(jnp.bfloat16)


def output(place, weight, contexts):
    layers, _, depth, columns = weight.shape
    rows, width = contexts[0].shape
    return pl.pallas_call(
        functools.partial(output_kernel, layers),
        out_shape=jax.ShapeDtypeStruct((1, rows, 2 * columns), jnp.bfloat16),
        in_specs=[SMEM] + [VMEM] * (1 + layers),
        out_specs=VMEM,
        compiler_params=pltpu.CompilerParams(vmem_limit_bytes=12 * MIB),
        cost_estimate=LIGHT,
        name="output",
    )(place, weight, *contexts)


def hold_kernel(*refs):
    del refs


def hold(values):
    return pl.pallas_call(
        hold_kernel,
        out_shape=[jax.ShapeDtypeStruct(value.shape, value.dtype) for value in values],
        in_specs=[ANY] * len(values),
        out_specs=[ANY] * len(values),
        input_output_aliases={i: i for i in range(len(values))},
        compiler_params=pltpu.CompilerParams(vmem_limit_bytes=MIB),
        cost_estimate=pl.CostEstimate(flops=1 << 30, bytes_accessed=1, transcendentals=0),
        name="hold",
    )(*values)


def together(*values):
    return lax.optimization_barrier(values)


def numbers(*values):
    return jnp.stack([jnp.asarray(value, jnp.int32) for value in values])


def local(frames, norm_gain, w_query, w_key, w_value, w_out, group_band, lengths):
    cores, seqs, layers = lax.axis_size("dp"), lax.axis_size("seq"), lax.axis_size("head")
    core, seq, layer = lax.axis_index("dp"), lax.axis_index("seq"), lax.axis_index("head")
    groups = group_band.shape[1]
    width = w_query.shape[1]
    here = [(c, s) for c in range(cores) for s in range(seqs)]

    def home(c, s):
        return s % 2, s // 2 * 2 + c

    def flat(c, s, z=None):
        return c * seqs + s if z is None else (c * seqs + s) * layers + z

    def moved(value, shift):
        pairs = [(flat(c, s, z), flat(*home(c, s), shift(z))) for c, s in here for z in range(layers)]
        return lax.ppermute(value, ("dp", "seq", "head"), pairs)

    after = ring_successors(layers)
    before = {after[z]: z for z in after}
    swap = [(c, cores - 1 - c) for c in range(cores)]
    over_link = [(flat(1, s), flat(0, s + 2)) for s in range(seqs - 2)]
    over_link += [(flat(0, s + 2), flat(1, s)) for s in range(seqs - 2)]
    share = 4 if seqs % 4 == 0 else 2

    def halos(pair):
        return lax.ppermute(pair, ("dp", "seq"), over_link), lax.ppermute(pair, "dp", swap)

    def shared(value):
        return [value] + [
            lax.ppermute(value, "seq", [(s, s ^ other) for s in range(seqs)]) for other in range(1, share)
        ]

    rows = frames[0]
    count = rows.shape[0]
    sent = pack(numbers(lax.rem(seq, share)), rows, w_out, share)
    first = moved(sent, lambda z: after[z])
    whole = moved(rows, lambda z: z)
    sent, w_query, w_key, w_value, weights_out = together(sent, w_query, w_key, w_value, w_out)
    half = w_out.shape[1] // 2
    own = jnp.concatenate(
        [w_query, w_key, w_value, jnp.concatenate([weights_out[:, :half], weights_out[:, half:]], axis=0)], axis=1
    )
    third = moved(sent, lambda z: before[z])
    facts = jnp.concatenate([group_band[0], jnp.broadcast_to(lengths[:, None], (1, group_band.shape[2]))], axis=0)
    facts = lax.ppermute(facts, ("dp", "seq"), [(flat(c, s), flat(*home(c, s))) for c, s in here])
    far = lax.ppermute(own, "dp", swap)
    second = lax.ppermute(first, "head", [(z, after[z]) for z in range(layers)])

    gain = norm_gain[None, :]
    far, facts = together(far, facts)
    core_at = numbers(core)
    query_a, pair_a = project(core_at, [whole, first], count, width, gain, own, far)
    link_a, chip_a = halos(pair_a)
    third, pair_a = together(third, pair_a)
    query_b, pair_b = project(core_at, [third], count, width, gain, own, far)
    link_b, chip_b = halos(pair_b)
    second, pair_b = together(second, pair_b)
    query_c, pair_c, stack = project(core_at, [second], count, width, gain, own, far, extra=(first, third, second))
    pair_c, link_a, chip_a, link_b, chip_b = together(pair_c, link_a, chip_a, link_b, chip_b)
    link_c, chip_c = halos(pair_c)
    shares = shared(stack)

    back = {z: before[z] for z in range(layers)}
    ids = [layer, lookup([back[z] for z in range(layers)], layer)]
    ids.append(lookup([after[z] for z in range(layers)], layer))
    ids.append(lookup([back[back[z]] for z in range(layers)], layer))
    place = numbers(core, (seq // 2 * 2 + core) * groups, groups * seqs, facts[groups, 0], *ids)
    band = facts[:groups]
    q_all, kv_all, vt_all = window(
        place, groups, count, [query_a, query_b, query_c], [pair_a, pair_b, pair_c],
        [chip_a, chip_b, chip_c], [link_a, link_b, link_c],
    )
    half = layers // 2
    arrived, sources = [], []
    for near in (0, 1):
        side = layer // half if near else 1 - layer // half
        turn = numbers(side * half * count, *[lax.rem(layer + e, half) * count for e in range(half)])
        contexts = list(attend(place, band, turn, half, q_all, kv_all, vt_all))
        if near:
            contexts[0], contexts[1], *shares = together(contexts[0], contexts[1], *shares)
            mine = join(shares)
            theirs = lax.ppermute(mine, "dp", swap)
        else:
            contexts[0], q_all = together(contexts[0], q_all)
        for e, context in enumerate(contexts):
            def target(z, e=e):
                return (z // half if near else 1 - z // half) * half + (z + e) % half

            arrived.append(moved(context, target))
            sources.append(side * half + lax.rem(layer + half - e, half))
    held = hold(arrived[:half])
    weight = place_weights(numbers(core, layer, seq, *ids[1:]), share, layers, w_out, far, mine, theirs, held)
    arrived = list(held) + arrived[half:]
    return output(numbers(*sources), weight, arrived)


def solution(mesh):
    return jax.shard_map(
        local,
        mesh=mesh,
        in_specs=(
            P("dp", ("seq", "head"), None),
            P(),
            P("dp", "head"),
            P("dp", "head"),
            P("dp", "head"),
            P("head", "dp"),
            P("dp", "seq", None),
            P("dp"),
        ),
        out_specs=P("dp", ("seq", "head"), None),
        check_vma=False,
    )
```

time: 144 us -> 183 us (1.27)
  Pallas kernels: 26.4 us -> 77.4 us
  waiting for transfers between devices: 47.4 us -> 21.9 us
  other arithmetic: 0.08 us -> 9.61 us
  starting transfers between devices: 48 us -> 51.4 us
    pallas_call x6 -> x9, Pallas kernels: 17.6 us -> 66.8 us  [the longest x1 27.9 us: join(): pl.pallas_call(join_kernel, out_shape=jax.ShapeDtypeStruct((rows, values[...]
    ppermute x7, waiting for transfers between devices: 31.2 us -> 16 us  [moved(): return lax.ppermute(value, ('dp', 'seq', 'head'), pairs)]
    ppermute x26 -> x12, waiting for transfers between devices: 16.3 us -> 3.85 us  [the longest x3 3.83 us: halos(): lax.ppermute(pair, ('dp', 'seq'), over_link)]
    concatenate x0 -> x1, other arithmetic: none -> 9.46 us  [local(): jnp.concatenate([w_query, w_key, w_value, jnp.concatenate([weights_out[:,...]
    unnamed x47 -> x51, local copies, waits for them, and re-layouts: 13.8 us -> 17.5 us
    ppermute x26 -> x12, starting transfers between devices: 25.1 us -> 27.6 us  [the longest x1 16.2 us: local(): second = lax.ppermute(first, 'head', [(z, after[z]) for z in range(layers)])]
    ppermute x1, waiting for transfers between devices: 0.01 us -> 2.07 us  [local(): lax.ppermute(facts, ('dp', 'seq'), [(flat(c, s), flat(*home(c, s))) for c...]
  transfers between devices with their start and end apart: 34 -> 20, of which waited for: 10 -> 5; matrix products, arithmetic and copies ran while one was open for 4% -> 1% of each run, Pallas kernels for 16% -> 15%
where the time goes in v3:
time: 183 us; the launch traced here: 180 us
  Pallas kernels  77.4 us (42%)
  starting transfers between devices  51.4 us (28%)
  waiting for transfers between devices  21.9 us (12%)
  local copies, waits for them, and re-layouts  18.9 us (10%)
  other arithmetic  9.61 us (5%)
    pallas_call x1, Pallas kernels, join(): pl.pallas_call(join_kernel, out_shape=jax.ShapeDtypeStruct((rows, values[...  27.9 us
    ppermute x7, starting transfers between devices, moved(): return lax.ppermute(value, ('dp', 'seq', 'head'), pairs)  20.6 us
    pallas_call x1, Pallas kernels, pack(): pl.pallas_call(pack_kernel, out_shape=jax.ShapeDtypeStruct((rows.shape[0]...  19 us
    unnamed x51, local copies, waits for them, and re-layouts  17.5 us
    ppermute x1, starting transfers between devices, local(): second = lax.ppermute(first, 'head', [(z, after[z]) for z in range(layers)])  16.2 us
    ppermute x7, waiting for transfers between devices, moved(): return lax.ppermute(value, ('dp', 'seq', 'head'), pairs)  16 us
    pallas_call x2, Pallas kernels, attend(): pl.pallas_call(functools.partial(attend_kernel, groups, reach, block // 2...  10.6 us
    pallas_call x3, Pallas kernels, project(): pl.pallas_call(functools.partial(project_kernel, blocks, count, len(extra...  10.2 us
  transfers between devices with their start and end apart: 20, of which 5 were waited for; matrix products, arithmetic and copies ran while one was open for 1% of the time, Pallas kernels for 15%

profile of v3, /device:TPU:1, one launch (start us, length us, event | category | flops | bytes accessed | tf_op | source)
XLA Modules:
  0.0 180.3 jit_solution(13171165186652382018)
XLA Ops:
  0.0 1.1 copy-done
  1.1 19.0 %pack.1 = bf16[240,1536]{1,0:T(8,128)(2,1)} custom-call(s32[1]{0:T(128)} %bitcast.10.place_ref, bf16[192,1536]{1,0:T(8,128)(2,1)} %bitcast.11.rows_ref, bf16[384,768]{1,0:T(8,128)(2,1)S(1)} %copy-done), custom_call_target="tpu_custom_call" | custom-call | flops 1 | bytes 1 | tf_op jit(solution)/shard_map/pack/pallas_call | solution.py:58
  20.1 0.1 fusion
  20.1 9.5 %maximum_maximum_fusion.refs_2_.refs_1_ = bf16[768,1536]{1,0:T(8,128)(2,1)} fusion(bf16[384,384]{1,0:T(8,128)(2,1)S(1)} %get-tuple-element.86, bf16[384,384]{1,0:T(8,128)(2,1)S(1)} %get-tuple-element.85, bf16[768,384]{1,0:T(8,128)(2,1)} %param.12, bf16[768,384]{1,0:T(8,128)(2,1)} %param.11, bf16[768,384]{1,0:T(8,128)(2,1)} %param.10), kind=kLoop, calls=%fused_computation | loop fusion | flops 11796480 | bytes 4718592 | tf_op jit(solution)/shard_map/concatenate | solution.py:466
  29.6 0.1 collective-permute-start
  29.7 3.6 %collective-permute-start.3 = (bf16[240,1536]{1,0:T(8,128)(2,1)}, bf16[240,1536]{1,0:T(8,128)(2,1)S(1)}, u32[]{:S(2)}, u32[]{:S(2)}) collective-permute-start(bf16[240,1536]{1,0:T(8,128)(2,1)} %pack.1), channel_id=1, source_target_pairs={{0,1},{1,3},{2,0},{3,2},{4,17},{5,19},{6,16},{7,18},{8,9},{9,11},{... | collective-permute-start | bytes 2211848 | tf_op jit(solution)/shard_map/ppermute | solution.py:442
  33.2 2.5 %collective-permute-start.2 = (bf16[192,1536]{1,0:T(8,128)(2,1)}, bf16[192,1536]{1,0:T(8,128)(2,1)}, u32[]{:S(2)}, u32[]{:S(2)}) collective-permute-start(bf16[192,1536]{1,0:T(8,128)(2,1)} %bitcast.11.rows_ref), channel_id=1, source_target_pairs={{0,0},{1,1},{2,2},{3,3},{4,16},{5,17},{6,18},{7,19},{8,8},{9,9},{1... | collective-permute-start | bytes 1769480 | tf_op jit(solution)/shard_map/ppermute | solution.py:442
  35.8 1.9 %collective-permute-start.4 = (bf16[240,1536]{1,0:T(8,128)(2,1)}, bf16[240,1536]{1,0:T(8,128)(2,1)}, u32[]{:S(2)}, u32[]{:S(2)}) collective-permute-start(bf16[240,1536]{1,0:T(8,128)(2,1)} %pack.1), channel_id=1, source_target_pairs={{0,2},{1,0},{2,3},{3,1},{4,18},{5,16},{6,19},{7,17},{8,10},{9,8},{... | collective-permute-start | bytes 2211848 | tf_op jit(solution)/shard_map/ppermute | solution.py:442
  37.7 13.7 %collective-permute-done.3.refs_1_.refs_3_ = bf16[240,1536]{1,0:T(8,128)(2,1)S(1)} collective-permute-done((bf16[240,1536]{1,0:T(8,128)(2,1)}, bf16[240,1536]{1,0:T(8,128)(2,1)S(1)}, u32[]{:S(2)}, u32[]{:S(2)}) %collective-permute-start.3) | collective-permute-done | bytes 737312 | tf_op jit(solution)/shard_map/ppermute | solution.py:442
  51.5 16.2 %collective-permute-start.5 = (bf16[240,1536]{1,0:T(8,128)(2,1)S(1)}, bf16[240,1536]{1,0:T(8,128)(2,1)}, u32[]{:S(2)}, u32[]{:S(2)}) collective-permute-start(bf16[240,1536]{1,0:T(8,128)(2,1)S(1)} %collective-permute-done.3.refs_1_.refs_3_), channel_id=1, source_target_pairs={{0,1},{1,3},{2,0},{3,2},{4,5},{5,7},{6,4},{7,6},{8,9},{9,11},{10,8... | collective-permute-start | bytes 2211848 | tf_op jit(solution)/shard_map/ppermute | solution.py:473
  68.3 3.2 %collective-permute-start.1 = (s32[7,12]{1,0:T(8,128)S(1)}, s32[7,12]{1,0:T(8,128)S(1)}, u32[]{:S(2)}, u32[]{:S(2)}) collective-permute-start(s32[7,12]{1,0:T(8,128)S(1)} %concatenate.11), channel_id=1, source_target_pairs={{0,0},{4,16},{8,8},{12,24},{16,4},{20,20},{24,12},{28,28},{1,1},{5... | collective-permute-start | bytes 1016 | tf_op jit(solution)/shard_map/ppermute | solution.py:471
  71.6 2.1 %collective-permute-done.1 = s32[7,12]{1,0:T(8,128)S(1)} collective-permute-done((s32[7,12]{1,0:T(8,128)S(1)}, s32[7,12]{1,0:T(8,128)S(1)}, u32[]{:S(2)}, u32[]{:S(2)}) %collective-permute-start.1) | collective-permute-done | bytes 368 | tf_op jit(solution)/shard_map/ppermute | solution.py:471
  73.6 3.8 %project.3 = (bf16[384,384]{1,0:T(8,128)(2,1)S(1)}, bf16[384,768]{1,0:T(8,128)(2,1)S(1)}) custom-call(s32[1]{0:T(128)} %bitcast.4.place_ref, f32[1,1536]{1,0:T(1,128)S(1)} %broadcast_in_dim.10.gain_ref, bf16[192,1536]{1,0:T(8,128)(2,1)} %collective-permute-done.2.refs_0_, bf16[240,1536]{1,0:T(8,128)(2,1)S(1)} %collective-permute-done.3.refs_1_.refs_3_, ...), custom_call_target="tpu_custom_call" | custom-call | flops 1358954496 | bytes 5603328 | tf_op jit(solution)/shard_map/project/pallas_call | solution.py:127
  77.5 0.7 copy-done.10
  78.2 1.9 %collective-permute-start.6 = (bf16[384,768]{1,0:T(8,128)(2,1)S(1)}, bf16[384,768]{1,0:T(8,128)(2,1)S(1)}, u32[]{:S(2)}, u32[]{:S(2)}) collective-permute-start(bf16[384,768]{1,0:T(8,128)(2,1)S(1)} %get-tuple-element.59.refs_3_), channel_id=1, source_target_pairs={{16,8},{20,12},{8,16},{12,20},{17,9},{21,13},{9,17},{13,21},{18,10... | collective-permute-start | bytes 1769480 | tf_op jit(solution)/shard_map/ppermute | solution.py:452
  80.1 0.1 collective-permute-start.7
  80.2 2.8 %project.4 = (bf16[192,384]{1,0:T(8,128)(2,1)S(1)}, bf16[192,768]{1,0:T(8,128)(2,1)S(1)}) custom-call(s32[1]{0:T(128)} %bitcast.4.place_ref, f32[1,1536]{1,0:T(1,128)S(1)} %broadcast_in_dim.10.gain_ref, bf16[240,1536]{1,0:T(8,128)(2,1)} %collective-permute-done.4.refs_0_.refs_4_, bf16[768,1536]{1,0:T(8,128)(2,1)} %maximum_maximum_fusion.refs_2_.refs_1_, ...), custom_call_target="tpu_custom_call" | custom-call | flops 679477248 | bytes 4571136 | tf_op jit(solution)/shard_map/project/pallas_call | solution.py:127
  83.0 0.6 copy-done.18
  83.7 3.6 %collective-permute-start.8 = (bf16[192,768]{1,0:T(8,128)(2,1)S(1)}, bf16[192,768]{1,0:T(8,128)(2,1)S(1)}, u32[]{:S(2)}, u32[]{:S(2)}) collective-permute-start(bf16[192,768]{1,0:T(8,128)(2,1)S(1)} %get-tuple-element.60.refs_4_), channel_id=1, source_target_pairs={{16,8},{20,12},{8,16},{12,20},{17,9},{21,13},{9,17},{13,21},{18,10... | collective-permute-start | bytes 884744 | tf_op jit(solution)/shard_map/ppermute | solution.py:452
  87.3 0.1 collective-permute-start.9
  87.4 0.0 collective-permute-done.5.refs_0_.refs_5_
  87.4 3.5 %project.5 = (bf16[192,384]{1,0:T(8,128)(2,1)S(1)}, bf16[192,768]{1,0:T(8,128)(2,1)}, bf16[144,1536]{1,0:T(8,128)(2,1)S(1)}) custom-call(s32[1]{0:T(128)} %bitcast.4.place_ref, f32[1,1536]{1,0:T(1,128)S(1)} %broadcast_in_dim.10.gain_ref, bf16[240,1536]{1,0:T(8,128)(2,1)} %collective-permute-done.5.refs_0_.refs_5_, ...), custom_call_target="tpu_custom_call" | custom-call | flops 679477248 | bytes 4571136 | tf_op jit(solution)/shard_map/project/pallas_call | solution.py:127
  91.0 0.6 copy-done.20
  91.6 1.0 collective-permute-done.8.refs_10_
  92.6 0.7 copy-done.14
  93.3 0.7 copy-done.16
  94.0 0.0 collective-permute-done.6.refs_9_
  94.0 0.8 copy-done.4
  94.9 0.8 copy-done.6
  95.7 2.9 %collective-permute-start.11 = (bf16[192,768]{1,0:T(8,128)(2,1)}, bf16[192,768]{1,0:T(8,128)(2,1)}, u32[]{:S(2)}, u32[]{:S(2)}) collective-permute-start(bf16[192,768]{1,0:T(8,128)(2,1)} %get-tuple-element.62.refs_5_), channel_id=1, source_target_pairs={{16,8},{20,12},{8,16},{12,20},{17,9},{21,13},{9,17},{13,21},{18,10... | collective-permute-start | bytes 884744 | tf_op jit(solution)/shard_map/ppermute | solution.py:452
  98.7 0.1 add_add_fusion
  98.8 1.3 collective-permute-start.12
  100.1 0.0 collective-permute-start.13
  100.1 1.4 collective-permute-start.14
  101.4 0.6 slice.14
  102.0 0.7 stack.85.place_ref
  102.7 2.9 %collective-permute-done.11.refs_11_ = bf16[192,768]{1,0:T(8,128)(2,1)} collective-permute-done((bf16[192,768]{1,0:T(8,128)(2,1)}, bf16[192,768]{1,0:T(8,128)(2,1)}, u32[]{:S(2)}, u32[]{:S(2)}) %collective-permute-start.11) | collective-permute-done | bytes 294944 | tf_op jit(solution)/shard_map/ppermute | solution.py:452
  105.6 1.1 copy-done.3
  106.7 1.1 copy-done.5
  107.7 1.1 copy-done.7
  108.8 1.0 copy-done.11
  109.8 1.0 copy-done.13
  110.7 1.0 copy-done.15
  111.7 1.0 copy-done.17
  112.6 0.9 copy-done.19
  113.6 0.9 copy-done.21
  114.5 3.6 %window.1 = (bf16[768,384]{1,0:T(8,128)(2,1)S(1)}, bf16[2304,768]{1,0:T(8,128)(2,1)S(1)}, bf16[3,18,128,128]{3,2,1,0:T(8,128)(2,1)S(1)}) custom-call(s32[8]{0:T(128)S(1)} %stack.85.place_ref, bf16[384,384]{1,0:T(8,128)(2,1)S(1)} %copy-done.11, bf16[192,384]{1,0:T(8,128)(2,1)S(1)} %copy-done.19, bf16[192,384]{1,0:T(8,128)(2,1)S(1)} %copy-done.21, ...), custom_call_target="tpu_custom_call" | custom-call | bytes 8257536 | tf_op jit(solution)/shard_map/window/pallas_call | solution.py:181
  118.1 4.9 %attend.2 = (bf16[192,384]{1,0:T(8,128)(2,1)}, bf16[192,384]{1,0:T(8,128)(2,1)}) custom-call(s32[8]{0:T(128)S(1)} %stack.85.place_ref, s32[6,12]{1,0:T(8,128)S(1)} %bitcast.24, s32[3]{0:T(128)S(1)} %get-tuple-element.88.turn_ref, bf16[768,384]{1,0:T(8,128)(2,1)S(1)} %get-tuple-element.71.q_all, bf16[2304,768]{1,0:T(8,128)(2,1)S(1)} %get-tuple-element.68.kv_all, ...), custom_call_target="tpu_custom_call" | custom-call | flops 4294967296 | bytes 1048576 | tf_op jit(solution)/shard_map/attend/pallas_call | solution.py:292
  123.1 5.7 %attend.3 = (bf16[192,384]{1,0:T(8,128)(2,1)}, bf16[192,384]{1,0:T(8,128)(2,1)S(1)}) custom-call(s32[8]{0:T(128)S(1)} %stack.85.place_ref, s32[6,12]{1,0:T(8,128)S(1)} %bitcast.25, s32[3]{0:T(128)S(1)} %get-tuple-element.87.turn_ref, bf16[768,384]{1,0:T(8,128)(2,1)S(1)} %get-tuple-element.71.q_all, bf16[2304,768]{1,0:T(8,128)(2,1)S(1)} %get-tuple-element.68.kv_all, ...), custom_call_target="tpu_custom_call" | custom-call | flops 4294967296 | bytes 1048576 | tf_op jit(solution)/shard_map/attend/pallas_call | solution.py:292
  128.7 0.7 copy-done.22
  129.4 0.8 copy-done.8
  130.2 0.0 collective-permute-done.13.refs_2_
  130.2 1.0 copy-done.9
  131.2 27.9 %join.1.mine_ref = bf16[576,1536]{1,0:T(8,128)(2,1)} custom-call(bf16[144,1536]{1,0:T(8,128)(2,1)S(1)} %get-tuple-element.75.refs_0_, bf16[144,1536]{1,0:T(8,128)(2,1)S(1)} %copy-done.9, bf16[144,1536]{1,0:T(8,128)(2,1)} %collective-permute-done.13.refs_2_, bf16[144,1536]{1,0:T(8,128)(2,1)} %collective-permute-done.14.refs_3_), custom_call_target="tpu_custom_call" | custom-call | flops 1 | bytes 1 | tf_op jit(solution)/shard_map/join/pallas_call | solution.py:321
  159.1 0.1 collective-permute-start.15
  159.2 0.7 collective-permute-start.16
  159.9 5.6 %collective-permute-start.17 = (bf16[192,384]{1,0:T(8,128)(2,1)}, bf16[192,384]{1,0:T(8,128)(2,1)S(1)}, u32[]{:S(2)}, u32[]{:S(2)}) collective-permute-start(bf16[192,384]{1,0:T(8,128)(2,1)} %get-tuple-element.80), channel_id=1, source_target_pairs={{0,3},{1,2},{2,1},{3,0},{4,19},{5,18},{6,17},{7,16},{8,11},{9,10},... | collective-permute-start | bytes 442376 | tf_op jit(solution)/shard_map/ppermute | solution.py:442
  165.5 6.1 %collective-permute-start.18 = (bf16[192,384]{1,0:T(8,128)(2,1)}, bf16[192,384]{1,0:T(8,128)(2,1)S(1)}, u32[]{:S(2)}, u32[]{:S(2)}) collective-permute-start(bf16[192,384]{1,0:T(8,128)(2,1)} %get-tuple-element.83), channel_id=1, source_target_pairs={{0,0},{1,1},{2,2},{3,3},{4,16},{5,17},{6,18},{7,19},{8,8},{9,9},{1... | collective-permute-start | bytes 442376 | tf_op jit(solution)/shard_map/ppermute | solution.py:442
  171.7 0.1 collective-permute-start.19
  171.8 0.1 pad_add_fusion.place_ref
  171.8 0.1 stack.82.place_ref
  172.0 3.3 %place.1.weight = bf16[4,2,384,768]{3,2,1,0:T(8,128)(2,1)S(1)} custom-call(s32[6]{0:T(128)S(1)} %stack.82.place_ref, bf16[384,768]{1,0:T(8,128)(2,1)S(1)} %copy-done.1, bf16[768,1536]{1,0:T(8,128)(2,1)S(1)} %collective-permute-done.refs_3_.refs_2_.far_ref, bf16[576,1536]{1,0:T(8,128)(2,1)} %join.1.mine_ref, ...), custom_call_target="tpu_custom_call" | custom-call | flops 1 | bytes 1 | tf_op jit(solution)/shard_map/place/pallas_call | solution.py:365
  175.3 2.2 %collective-permute-done.18.refs_2_ = bf16[192,384]{1,0:T(8,128)(2,1)S(1)} collective-permute-done((bf16[192,384]{1,0:T(8,128)(2,1)}, bf16[192,384]{1,0:T(8,128)(2,1)S(1)}, u32[]{:S(2)}, u32[]{:S(2)}) %collective-permute-start.18) | collective-permute-done | bytes 147488 | tf_op jit(solution)/shard_map/ppermute | solution.py:442
  177.5 2.7 %output.1 = bf16[1,192,1536]{2,1,0:T(8,128)(2,1)} custom-call(s32[4]{0:T(128)S(1)} %pad_add_fusion.place_ref, bf16[4,2,384,768]{3,2,1,0:T(8,128)(2,1)S(1)} %place.1.weight, bf16[192,384]{1,0:T(8,128)(2,1)S(1)} %get-tuple-element.81.refs_0_, bf16[192,384]{1,0:T(8,128)(2,1)S(1)} %get-tuple-element.82.refs_1_, ...), custom_call_target="tpu_custom_call" | custom-call | flops 1 | bytes 1 | tf_op jit(solution)/shard_map/output/pallas_call | solution.py:391
  (47 shorter events, 0.1 us)
Async XLA Ops:
  0.0 1.1 copy-start
  1.1 66.6 %copy-start.24 = (s32[1,6,12]{2,0,1:T(1,128)S(1)}, s32[1,6,12]{2,0,1:T(1,128)}, u32[]{:S(2)}) copy-start(s32[1,6,12]{2,0,1:T(1,128)} %param.14) | copy-start | bytes 868
  1.1 70.5 %copy-start.23 = (f32[1536]{0:T(1024)S(1)}, f32[1536]{0:T(1024)}, u32[]{:S(2)}) copy-start(f32[1536]{0:T(1024)} %param.9) | copy-start | bytes 18436
  29.6 44.0 %collective-permute-start = (bf16[768,1536]{1,0:T(8,128)(2,1)}, bf16[768,1536]{1,0:T(8,128)(2,1)S(1)}, u32[]{:S(2)}, u32[]{:S(2)}) collective-permute-start(bf16[768,1536]{1,0:T(8,128)(2,1)} %maximum_maximum_fusion.refs_2_.refs_1_), channel_id=1, source_target_pairs={{0,16},{16,0},{1,17},{17,1},{2,18},{18,2},{3,19},{19,3},{4,20},{20... | collective-permute-start | bytes 7077896 | tf_op jit(solution)/shard_map/ppermute | solution.py:472
  29.7 21.8 %collective-permute-start.3 = (bf16[240,1536]{1,0:T(8,128)(2,1)}, bf16[240,1536]{1,0:T(8,128)(2,1)S(1)}, u32[]{:S(2)}, u32[]{:S(2)}) collective-permute-start(bf16[240,1536]{1,0:T(8,128)(2,1)} %pack.1), channel_id=1, source_target_pairs={{0,1},{1,3},{2,0},{3,2},{4,17},{5,19},{6,16},{7,18},{8,9},{9,11},{... | collective-permute-start | bytes 2211848 | tf_op jit(solution)/shard_map/ppermute | solution.py:442
  33.2 40.4 %collective-permute-start.2 = (bf16[192,1536]{1,0:T(8,128)(2,1)}, bf16[192,1536]{1,0:T(8,128)(2,1)}, u32[]{:S(2)}, u32[]{:S(2)}) collective-permute-start(bf16[192,1536]{1,0:T(8,128)(2,1)} %bitcast.11.rows_ref), channel_id=1, source_target_pairs={{0,0},{1,1},{2,2},{3,3},{4,16},{5,17},{6,18},{7,19},{8,8},{9,9},{1... | collective-permute-start | bytes 1769480 | tf_op jit(solution)/shard_map/ppermute | solution.py:442
  35.8 44.5 %collective-permute-start.4 = (bf16[240,1536]{1,0:T(8,128)(2,1)}, bf16[240,1536]{1,0:T(8,128)(2,1)}, u32[]{:S(2)}, u32[]{:S(2)}) collective-permute-start(bf16[240,1536]{1,0:T(8,128)(2,1)} %pack.1), channel_id=1, source_target_pairs={{0,2},{1,0},{2,3},{3,1},{4,18},{5,16},{6,19},{7,17},{8,10},{9,8},{... | collective-permute-start | bytes 2211848 | tf_op jit(solution)/shard_map/ppermute | solution.py:442
  51.5 36.0 %collective-permute-start.5 = (bf16[240,1536]{1,0:T(8,128)(2,1)S(1)}, bf16[240,1536]{1,0:T(8,128)(2,1)}, u32[]{:S(2)}, u32[]{:S(2)}) collective-permute-start(bf16[240,1536]{1,0:T(8,128)(2,1)S(1)} %collective-permute-done.3.refs_1_.refs_3_), channel_id=1, source_target_pairs={{0,1},{1,3},{2,0},{3,2},{4,5},{5,7},{6,4},{7,6},{8,9},{9,11},{10,8... | collective-permute-start | bytes 2211848 | tf_op jit(solution)/shard_map/ppermute | solution.py:473
  68.3 5.3 %collective-permute-start.1 = (s32[7,12]{1,0:T(8,128)S(1)}, s32[7,12]{1,0:T(8,128)S(1)}, u32[]{:S(2)}, u32[]{:S(2)}) collective-permute-start(s32[7,12]{1,0:T(8,128)S(1)} %concatenate.11), channel_id=1, source_target_pairs={{0,0},{4,16},{8,8},{12,24},{16,4},{20,20},{24,12},{28,28},{1,1},{5... | collective-permute-start | bytes 1016 | tf_op jit(solution)/shard_map/ppermute | solution.py:471
  77.5 0.7 copy-start.10
  78.2 12.7 %copy-start.2 = (bf16[384,768]{1,0:T(8,128)(2,1)}, bf16[384,768]{1,0:T(8,128)(2,1)S(1)}, u32[]{:S(2)}) copy-start(bf16[384,768]{1,0:T(8,128)(2,1)S(1)} %get-tuple-element.59.refs_3_) | copy-start | bytes 1769476
  78.2 15.8 %collective-permute-start.6 = (bf16[384,768]{1,0:T(8,128)(2,1)S(1)}, bf16[384,768]{1,0:T(8,128)(2,1)S(1)}, u32[]{:S(2)}, u32[]{:S(2)}) collective-permute-start(bf16[384,768]{1,0:T(8,128)(2,1)S(1)} %get-tuple-element.59.refs_3_), channel_id=1, source_target_pairs={{16,8},{20,12},{8,16},{12,20},{17,9},{21,13},{9,17},{13,21},{18,10... | collective-permute-start | bytes 1769480 | tf_op jit(solution)/shard_map/ppermute | solution.py:452
  80.1 14.7 %collective-permute-start.7 = (bf16[384,768]{1,0:T(8,128)(2,1)S(1)}, bf16[384,768]{1,0:T(8,128)(2,1)S(1)}, u32[]{:S(2)}, u32[]{:S(2)}) collective-permute-start(bf16[384,768]{1,0:T(8,128)(2,1)S(1)} %get-tuple-element.59.refs_3_), channel_id=1, source_target_pairs={{0,16},{16,0},{1,17},{17,1},{2,18},{18,2},{3,19},{19,3},{4,20},{20... | collective-permute-start | bytes 1769480 | tf_op jit(solution)/shard_map/ppermute | solution.py:452
  83.0 0.7 copy-start.18
  83.7 7.3 %copy-start.12 = (bf16[192,768]{1,0:T(8,128)(2,1)}, bf16[192,768]{1,0:T(8,128)(2,1)S(1)}, u32[]{:S(2)}) copy-start(bf16[192,768]{1,0:T(8,128)(2,1)S(1)} %get-tuple-element.60.refs_4_) | copy-start | bytes 884740
  83.7 8.9 %collective-permute-start.8 = (bf16[192,768]{1,0:T(8,128)(2,1)S(1)}, bf16[192,768]{1,0:T(8,128)(2,1)S(1)}, u32[]{:S(2)}, u32[]{:S(2)}) collective-permute-start(bf16[192,768]{1,0:T(8,128)(2,1)S(1)} %get-tuple-element.60.refs_4_), channel_id=1, source_target_pairs={{16,8},{20,12},{8,16},{12,20},{17,9},{21,13},{9,17},{13,21},{18,10... | collective-permute-start | bytes 884744 | tf_op jit(solution)/shard_map/ppermute | solution.py:452
  87.3 6.0 %collective-permute-start.9 = (bf16[192,768]{1,0:T(8,128)(2,1)S(1)}, bf16[192,768]{1,0:T(8,128)(2,1)S(1)}, u32[]{:S(2)}, u32[]{:S(2)}) collective-permute-start(bf16[192,768]{1,0:T(8,128)(2,1)S(1)} %get-tuple-element.60.refs_4_), channel_id=1, source_target_pairs={{0,16},{16,0},{1,17},{17,1},{2,18},{18,2},{3,19},{19,3},{4,20},{20... | collective-permute-start | bytes 884744 | tf_op jit(solution)/shard_map/ppermute | solution.py:452
  91.0 0.7 copy-start.20
  92.6 0.7 copy-start.14
  93.3 0.7 copy-start.16
  94.0 0.8 copy-start.4
  94.9 0.8 copy-start.6
  95.7 7.1 %collective-permute-start.10 = (bf16[192,768]{1,0:T(8,128)(2,1)}, bf16[192,768]{1,0:T(8,128)(2,1)S(1)}, u32[]{:S(2)}, u32[]{:S(2)}) collective-permute-start(bf16[192,768]{1,0:T(8,128)(2,1)} %get-tuple-element.62.refs_5_), channel_id=1, source_target_pairs={{0,16},{16,0},{1,17},{17,1},{2,18},{18,2},{3,19},{19,3},{4,20},{20... | collective-permute-start | bytes 884744 | tf_op jit(solution)/shard_map/ppermute | solution.py:452
  95.7 9.9 %collective-permute-start.11 = (bf16[192,768]{1,0:T(8,128)(2,1)}, bf16[192,768]{1,0:T(8,128)(2,1)}, u32[]{:S(2)}, u32[]{:S(2)}) collective-permute-start(bf16[192,768]{1,0:T(8,128)(2,1)} %get-tuple-element.62.refs_5_), channel_id=1, source_target_pairs={{16,8},{20,12},{8,16},{12,20},{17,9},{21,13},{9,17},{13,21},{18,10... | collective-permute-start | bytes 884744 | tf_op jit(solution)/shard_map/ppermute | solution.py:452
  98.8 30.6 %collective-permute-start.12 = (bf16[144,1536]{1,0:T(8,128)(2,1)S(1)}, bf16[144,1536]{1,0:T(8,128)(2,1)S(1)}, u32[]{:S(2)}, u32[]{:S(2)}) collective-permute-start(bf16[144,1536]{1,0:T(8,128)(2,1)S(1)} %get-tuple-element.75.refs_0_), channel_id=1, source_target_pairs={{0,4},{4,0},{8,12},{12,8},{1,5},{5,1},{9,13},{13,9},{2,6},{6,2},{1... | collective-permute-start | bytes 1327112 | tf_op jit(solution)/shard_map/ppermute | solution.py:456
  100.1 30.1 %collective-permute-start.13 = (bf16[144,1536]{1,0:T(8,128)(2,1)S(1)}, bf16[144,1536]{1,0:T(8,128)(2,1)}, u32[]{:S(2)}, u32[]{:S(2)}) collective-permute-start(bf16[144,1536]{1,0:T(8,128)(2,1)S(1)} %get-tuple-element.75.refs_0_), channel_id=1, source_target_pairs={{0,8},{4,12},{8,0},{12,4},{1,9},{5,13},{9,1},{13,5},{2,10},{6,14},... | collective-permute-start | bytes 1327112 | tf_op jit(solution)/shard_map/ppermute | solution.py:456
  100.1 30.1 %collective-permute-start.14 = (bf16[144,1536]{1,0:T(8,128)(2,1)S(1)}, bf16[144,1536]{1,0:T(8,128)(2,1)}, u32[]{:S(2)}, u32[]{:S(2)}) collective-permute-start(bf16[144,1536]{1,0:T(8,128)(2,1)S(1)} %get-tuple-element.75.refs_0_), channel_id=1, source_target_pairs={{0,12},{4,8},{8,4},{12,0},{1,13},{5,9},{9,5},{13,1},{2,14},{6,10},... | collective-permute-start | bytes 1327112 | tf_op jit(solution)/shard_map/ppermute | solution.py:456
  105.6 1.1 copy-start.3
  106.7 1.1 copy-start.5
  107.7 1.1 copy-start.7
  108.8 1.0 copy-start.11
  109.8 1.0 copy-start.13
  110.7 1.0 copy-start.15
  111.7 1.0 copy-start.17
  112.6 0.9 copy-start.19
  113.6 0.9 copy-start.21
  128.7 0.7 copy-start.22
  129.4 0.8 copy-start.8
  130.2 1.0 copy-start.9
  131.2 40.8 %copy-start.1 = (bf16[384,768]{1,0:T(8,128)(2,1)S(1)}, bf16[384,768]{1,0:T(8,128)(2,1)}, u32[]{:S(2)}) copy-start(bf16[384,768]{1,0:T(8,128)(2,1)} %own_ref.1) | copy-start | bytes 1769476
  159.1 12.8 %collective-permute-start.15 = (bf16[576,1536]{1,0:T(8,128)(2,1)}, bf16[576,1536]{1,0:T(8,128)(2,1)}, u32[]{:S(2)}, u32[]{:S(2)}) collective-permute-start(bf16[576,1536]{1,0:T(8,128)(2,1)} %join.1.mine_ref), channel_id=1, source_target_pairs={{0,16},{16,0},{1,17},{17,1},{2,18},{18,2},{3,19},{19,3},{4,20},{20... | collective-permute-start | bytes 5308424 | tf_op jit(solution)/shard_map/ppermute | solution.py:508
  159.2 12.7 %collective-permute-start.16 = (bf16[192,384]{1,0:T(8,128)(2,1)}, bf16[192,384]{1,0:T(8,128)(2,1)S(1)}, u32[]{:S(2)}, u32[]{:S(2)}) collective-permute-start(bf16[192,384]{1,0:T(8,128)(2,1)} %get-tuple-element.79), channel_id=1, source_target_pairs={{0,2},{1,3},{2,0},{3,1},{4,18},{5,19},{6,16},{7,17},{8,10},{9,11},... | collective-permute-start | bytes 442376 | tf_op jit(solution)/shard_map/ppermute | solution.py:442
  159.9 12.0 %collective-permute-start.17 = (bf16[192,384]{1,0:T(8,128)(2,1)}, bf16[192,384]{1,0:T(8,128)(2,1)S(1)}, u32[]{:S(2)}, u32[]{:S(2)}) collective-permute-start(bf16[192,384]{1,0:T(8,128)(2,1)} %get-tuple-element.80), channel_id=1, source_target_pairs={{0,3},{1,2},{2,1},{3,0},{4,19},{5,18},{6,17},{7,16},{8,11},{9,10},... | collective-permute-start | bytes 442376 | tf_op jit(solution)/shard_map/ppermute | solution.py:442
  165.5 12.0 %collective-permute-start.18 = (bf16[192,384]{1,0:T(8,128)(2,1)}, bf16[192,384]{1,0:T(8,128)(2,1)S(1)}, u32[]{:S(2)}, u32[]{:S(2)}) collective-permute-start(bf16[192,384]{1,0:T(8,128)(2,1)} %get-tuple-element.83), channel_id=1, source_target_pairs={{0,0},{1,1},{2,2},{3,3},{4,16},{5,17},{6,18},{7,19},{8,8},{9,9},{1... | collective-permute-start | bytes 442376 | tf_op jit(solution)/shard_map/ppermute | solution.py:442
  171.7 5.8 %collective-permute-start.19 = (bf16[192,384]{1,0:T(8,128)(2,1)}, bf16[192,384]{1,0:T(8,128)(2,1)S(1)}, u32[]{:S(2)}, u32[]{:S(2)}) collective-permute-start(bf16[192,384]{1,0:T(8,128)(2,1)} %copy-done.22), channel_id=1, source_target_pairs={{0,1},{1,0},{2,3},{3,2},{4,17},{5,16},{6,19},{7,18},{8,9},{9,8},{1... | collective-permute-start | bytes 442376 | tf_op jit(solution)/shard_map/ppermute | solution.py:442

commit v4 on v3

v4 whole, which is shorter than its diff:
```python
import functools

import jax
import jax.numpy as jnp
from jax import lax
from jax.experimental import pallas as pl
from jax.experimental.pallas import tpu as pltpu
from jax.sharding import PartitionSpec as P

HD = 64
GROUP = 128
LANES = 128

epsilon = 1e-05

VMEM = pl.BlockSpec(memory_space=pltpu.VMEM)
SMEM = pl.BlockSpec(memory_space=pltpu.SMEM)
HBM = pl.BlockSpec(memory_space=pltpu.HBM)
MIB = 1024 * 1024
LIGHT = pl.CostEstimate(flops=1, bytes_accessed=1, transcendentals=0)


def ring_successors(count):
    order = [0] + list(range(1, count, 2)) + list(range(count - 2 + count % 2, 0, -2))
    return {order[i]: order[(i + 1) % count] for i in range(count)}


def lookup(table, index):
    value = jnp.int32(table[0])
    for place in range(1, len(table)):
        value = jnp.where(index == place, jnp.int32(table[place]), value)
    return value


def copy_all(pairs, sems):
    copies = [pltpu.make_async_copy(source, target, sems.at[i]) for i, (source, target) in enumerate(pairs)]
    for copy in copies:
        copy.start()
    return copies


def in_hbm(*values):
    return [pltpu.with_memory_space_constraint(value, pltpu.HBM) for value in values]


def pack_kernel(place_ref, rows_ref, query_ref, key_ref, value_ref, w_out_ref, sent_ref, piece_ref, all_ref, *refs):
    held_sent, held_piece, held, sems = refs
    depth, width = query_ref.shape
    count = rows_ref.shape[0]
    part, columns = piece_ref.shape
    first = pl.multiple_of(place_ref[0] * part, 16)
    pairs = [(rows_ref, held_sent.at[pl.ds(0, count), :]), (w_out_ref.at[pl.ds(first, part), :], held_piece)]
    for side in range(2):
        pairs.append((
            w_out_ref.at[pl.ds(first + side * part // 2, part // 2), :],
            held_sent.at[pl.ds(count, part // 2), pl.ds(side * columns, columns)],
        ))
    for place, source in enumerate((query_ref, key_ref, value_ref)):
        pairs.append((source, held.at[:, pl.ds(place * width, width)]))
    rows = w_out_ref.shape[0]
    for side in range(2):
        pairs.append((
            w_out_ref.at[:, pl.ds(side * width, width)],
            held.at[pl.ds(side * rows, rows), pl.ds(3 * width, width)],
        ))
    loads = copy_all(pairs, sems)
    for load in loads[:4]:
        load.wait()
    stores = copy_all([(held_sent, sent_ref), (held_piece, piece_ref)], sems.at[pl.ds(len(pairs), 2)])
    for load in loads[4:]:
        load.wait()
    stores += copy_all([(held, all_ref)], sems.at[pl.ds(len(pairs) + 2, 1)])
    for store in stores:
        store.wait()


def pack(place, rows, w_query, w_key, w_value, w_out, share):
    depth, width = w_query.shape
    part = w_out.shape[0] // share
    shapes = [
        (rows.shape[0] + part // 2, rows.shape[1]), (part, w_out.shape[1]), (depth, 4 * width)
    ]
    return pl.pallas_call(
        pack_kernel,
        out_shape=[pltpu.HBM(shape, jnp.bfloat16) for shape in shapes],
        in_specs=[SMEM] + [HBM] * 5,
        out_specs=[HBM] * 3,
        scratch_shapes=[pltpu.VMEM(shape, jnp.bfloat16) for shape in shapes] + [pltpu.SemaphoreType.DMA((12,))],
        compiler_params=pltpu.CompilerParams(vmem_limit_bytes=8 * MIB),
        cost_estimate=LIGHT,
        name="pack",
    )(place, *in_hbm(rows, w_query, w_key, w_value, w_out))


def join_kernel(skips, *refs):
    sources, (out, held, sems) = refs[:-3], refs[-3:]
    spans, parts, at = [], [], 0
    columns = held.shape[1]
    for skip, source in zip(skips, sources):
        rows = source.shape[0] - skip
        if source.shape[1] == columns:
            parts.append((source.at[pl.ds(skip, rows), :], held.at[pl.ds(at, rows), :]))
        else:
            rows //= 2
            for side in range(2):
                parts.append((
                    source.at[pl.ds(side * rows, rows), :],
                    held.at[pl.ds(at, rows), pl.ds(side * source.shape[1], source.shape[1])],
                ))
        spans.append(pl.ds(at, rows))
        at += rows
    for load in copy_all(parts, sems):
        load.wait()
    for store in copy_all([(held.at[span, :], out.at[span, :]) for span in spans], sems.at[pl.ds(len(parts), len(spans))]):
        store.wait()


def join(values, skips=None):
    skips = [0] * len(values) if skips is None else skips
    columns = max(value.shape[1] for value in values)
    rows = sum((value.shape[0] - skip) * value.shape[1] // columns for value, skip in zip(values, skips))
    return pl.pallas_call(
        functools.partial(join_kernel, tuple(skips)),
        out_shape=pltpu.HBM((rows, columns), jnp.bfloat16),
        in_specs=[HBM] * len(values),
        out_specs=HBM,
        scratch_shapes=[
            pltpu.VMEM((rows, columns), jnp.bfloat16), pltpu.SemaphoreType.DMA((3 * len(values),))
        ],
        compiler_params=pltpu.CompilerParams(vmem_limit_bytes=4 * MIB),
        cost_estimate=LIGHT,
        name="join",
    )(*values)


def project_kernel(blocks, count, gain_ref, weight_ref, *refs):
    rows = refs[:blocks]
    query_ref, pair_ref, held, weight, query_held, pair_held, sems = refs[blocks:]
    width = query_ref.shape[1]
    order = (1, 2, 0)
    loads = copy_all(
        [(rows[i].at[pl.ds(0, count), :], held.at[pl.ds(i * count, count), :]) for i in range(blocks)], sems
    )
    fetches = copy_all(
        [(weight_ref.at[:, pl.ds(place * width, width)], weight.at[place]) for place in order],
        sems.at[pl.ds(blocks, 3)],
    )
    gain = gain_ref[...]
    normalized = []
    for i in range(blocks):
        loads[i].wait()
        values = held[i * count:(i + 1) * count, :].astype(jnp.float32)
        center = values - jnp.mean(values, axis=-1, keepdims=True)
        spread = jnp.mean(center * center, axis=-1, keepdims=True)
        normalized.append((center * lax.rsqrt(spread + epsilon) * gain).astype(jnp.bfloat16))
    normalized = normalized[0] if blocks == 1 else jnp.concatenate(normalized, axis=0)
    stores = []
    for place, fetch in zip(order, fetches):
        fetch.wait()
        got = jnp.dot(normalized, weight[place], preferred_element_type=jnp.float32).astype(jnp.bfloat16)
        sem = sems.at[pl.ds(blocks + 3 + place, 1)]
        if place == 0:
            query_held[...] = (got.astype(jnp.float32) * (HD ** -0.5)).astype(jnp.bfloat16)
            stores += copy_all([(query_held, query_ref)], sem)
        else:
            part = pl.ds((place - 1) * width, width)
            pair_held[:, (place - 1) * width:place * width] = got
            stores += copy_all([(pair_held.at[:, part], pair_ref.at[:, part])], sem)
    for store in stores:
        store.wait()


def project(rows, count, width, gain, weight, cost):
    blocks, depth = len(rows), rows[0].shape[1]
    total = blocks * count
    return pl.pallas_call(
        functools.partial(project_kernel, blocks, count),
        out_shape=[pltpu.HBM((total, width), jnp.bfloat16), pltpu.HBM((total, 2 * width), jnp.bfloat16)],
        in_specs=[VMEM] + [HBM] * (blocks + 1),
        out_specs=[HBM, HBM],
        scratch_shapes=[
            pltpu.VMEM((total, depth), jnp.bfloat16),
            pltpu.VMEM((3, depth, width), jnp.bfloat16),
            pltpu.VMEM((total, width), jnp.bfloat16),
            pltpu.VMEM((total, 2 * width), jnp.bfloat16),
            pltpu.SemaphoreType.DMA((blocks + 6,)),
        ],
        compiler_params=pltpu.CompilerParams(vmem_limit_bytes=24 * MIB),
        cost_estimate=pl.CostEstimate(flops=cost, bytes_accessed=1, transcendentals=0),
        name="project",
    )(gain, *in_hbm(weight), *rows)


def window_kernel(shape, groups, place_ref, *refs):
    kinds = len(shape)
    queries, owns, sides = refs[:kinds], refs[kinds:2 * kinds], refs[2 * kinds:4 * kinds]
    q_all, kv_all, vt_all, sems = refs[4 * kinds:]
    block, width = q_all.shape
    rows = block // sum(shape)
    core = place_ref[0]
    chip_base = jnp.where(core == 0, 2 * block, 0)
    link_base = jnp.where(core == 0, 0, 2 * block)
    pairs, step = [], 0
    for kind in range(kinds):
        for inside in range(shape[kind]):
            at = place_ref[4 + step] * rows
            part = pl.ds(inside * rows, rows)
            pairs.append((queries[kind].at[part, :], q_all.at[pl.ds(pl.multiple_of(at, 64), rows), :]))
            for source, base in (
                (owns[kind], block), (sides[kind], chip_base), (sides[kinds + kind], link_base)
            ):
                to = pl.ds(pl.multiple_of(base + at, 64), rows)
                taken = source.at[1 - core, part, :] if len(source.shape) == 3 else source.at[part, :]
                pairs.append((taken, kv_all.at[to, :]))
            step += 1
    for copy in copy_all(pairs, sems):
        copy.wait()
    for index in range(3 * groups):
        for pair in range(width // LANES):
            columns = slice(width + pair * LANES, width + (pair + 1) * LANES)
            vt_all[pair, index] = kv_all[index * GROUP:(index + 1) * GROUP, columns].T


def window(place, groups, rows, queries, owns, chip_side, link_side):
    shape = [query.shape[0] // rows for query in queries]
    width, block = queries[0].shape[1], sum(shape) * rows
    pairs = width // LANES
    return pl.pallas_call(
        functools.partial(window_kernel, shape, groups),
        out_shape=(
            jax.ShapeDtypeStruct((block, width), jnp.bfloat16),
            jax.ShapeDtypeStruct((3 * block, 2 * width), jnp.bfloat16),
            jax.ShapeDtypeStruct((pairs, 3 * groups, LANES, GROUP), jnp.bfloat16),
        ),
        in_specs=[SMEM] + [HBM] * (4 * len(shape)),
        out_specs=(VMEM,) * 3,
        scratch_shapes=[pltpu.SemaphoreType.DMA((4 * sum(shape),))],
        compiler_params=pltpu.CompilerParams(vmem_limit_bytes=16 * MIB),
        cost_estimate=pl.CostEstimate(flops=0, bytes_accessed=2 * 14 * block * width, transcendentals=0),
        name="window",
    )(place, *in_hbm(*queries, *owns, *[side for side in chip_side if side.ndim == 3]),
      *[side for side in chip_side if side.ndim == 2], *link_side)


def attend_kernel(groups, reach, count_rows, place_ref, band_ref, turn_ref, q_all, kv_all, vt_all, *refs):
    outs, (score, ctx, chosen, limits, sems) = refs[:-5], refs[-5:]
    pairs, rows = vt_all.shape[0], outs[0].shape[0]
    first_group, total, length = (place_ref[i] for i in range(1, 4))
    first_row = turn_ref[0]
    slots = 2 * reach + 2
    half_mask = lax.broadcasted_iota(jnp.int32, (GROUP, LANES), 1) < HD
    row_ids = lax.broadcasted_iota(jnp.int32, (GROUP, 2 * GROUP), 0)
    part_group = lax.div(length, jnp.int32(GROUP))
    part_left = lax.rem(length, jnp.int32(GROUP))

    def one_group(place, carry):
        group = first_row // GROUP + place
        for slot in range(slots):
            chosen[slot] = groups + group
        offset = part_group - first_group - group
        column = jnp.clip(jnp.where(offset < 0, offset + reach, offset + reach - 1), 0, 2 * reach - 1)
        cut = (part_left > 0) & (offset != 0) & (jnp.abs(offset) <= reach) & (part_group < total)
        cut = cut & (band_ref[group, column] == 1)
        chosen[1] = jnp.where(cut, groups + group + offset, groups + group)
        limits[0] = jnp.where(cut, part_left, 0)
        count = 1 + cut.astype(jnp.int32)
        for column in range(2 * reach):
            offset = column - reach if column < reach else column - reach + 1
            there = first_group + group + offset
            good = (there >= 0) & (there < part_group) & (there < total) & (band_ref[group, column] == 1)
            chosen[count] = jnp.where(good, groups + group + offset, groups + group)
            limits[0] = jnp.where(good & (count == 1), GROUP, limits[0])
            count = count + good.astype(jnp.int32)
        query_at = pl.ds(pl.multiple_of(group * GROUP, GROUP), GROUP)
        out_at = pl.ds(pl.multiple_of(place * GROUP, GROUP), GROUP)

        def run(size):
            first_limit = limits[0]
            last_limit = jnp.where(count == size, GROUP, 0)
            indices = [chosen[slot] for slot in range(size)]
            best = []
            for pair in range(pairs):
                own = q_all[query_at, pair * LANES:(pair + 1) * LANES]
                zero = jnp.zeros_like(own)
                both = jnp.concatenate(
                    [jnp.where(half_mask, own, zero), jnp.where(half_mask, zero, own)], axis=0
                ).T
                top = None
                for slot in range(0, size, 2):
                    tiles = [
                        kv_all[pl.ds(pl.multiple_of(index * GROUP, GROUP), GROUP), pair * LANES:(pair + 1) * LANES]
                        for index in indices[slot:slot + 2]
                    ]
                    got = jnp.dot(jnp.concatenate(tiles, axis=0), both, preferred_element_type=jnp.float32)
                    for one in (slot, slot + 1):
                        part = got[(one - slot) * GROUP:(one - slot + 1) * GROUP]
                        if one == 1:
                            part = jnp.where(row_ids < first_limit, part, -jnp.inf)
                        elif one == size - 1:
                            part = jnp.where(row_ids < last_limit, part, -jnp.inf)
                        score[pair, one * GROUP:(one + 1) * GROUP, :] = part
                        high = jnp.max(part.reshape(GROUP // 8, 8, 2 * GROUP), axis=0)
                        top = high if top is None else jnp.maximum(top, high)
                best.append(jnp.max(top, axis=0, keepdims=True))
            for pair in range(pairs):
                total_sum = jnp.zeros((8, 2 * GROUP), jnp.float32)
                mixed = jnp.zeros((LANES, 2 * GROUP), jnp.float32)
                for slot in range(0, size, 2):
                    weights = jnp.exp(score[pair, slot * GROUP:(slot + 2) * GROUP, :] - best[pair])
                    total_sum += jnp.sum(weights.reshape(2 * GROUP // 8, 8, 2 * GROUP), axis=0)
                    tiles = [vt_all[pair, index] for index in indices[slot:slot + 2]]
                    mixed += jnp.dot(
                        jnp.concatenate(tiles, axis=1),
                        weights.astype(jnp.bfloat16),
                        preferred_element_type=jnp.float32,
                    )
                mixed = mixed / jnp.sum(total_sum, axis=0, keepdims=True)
                both_heads = jnp.concatenate([mixed[:HD, :GROUP], mixed[HD:, GROUP:]], axis=0)
                ctx[out_at, pair * LANES:(pair + 1) * LANES] = both_heads.T.astype(jnp.bfloat16)

        for size in range(2, slots + 1, 2):
            @pl.when((count == size) | (count == size - 1))
            def _():
                run(size)

        return carry

    lax.fori_loop(0, count_rows // GROUP, one_group, 0)
    stores = copy_all(
        [(ctx.at[pl.ds(pl.multiple_of(turn_ref[1 + i], 64), rows), :], out) for i, out in enumerate(outs)], sems
    )
    for store in stores:
        store.wait()


def attend(place, band, turn, outs, q_all, kv_all, vt_all):
    groups, reach = band.shape[0], band.shape[1] // 2
    pairs, block = vt_all.shape[0], q_all.shape[0]
    rows = block // (2 * outs)
    slots = 2 * reach + 2
    return pl.pallas_call(
        functools.partial(attend_kernel, groups, reach, block // 2),
        out_shape=[pltpu.HBM((rows, pairs * LANES), jnp.bfloat16)] * outs,
        in_specs=[SMEM, SMEM, SMEM] + [VMEM] * 3,
        out_specs=[HBM] * outs,
        scratch_shapes=[
            pltpu.VMEM((pairs, slots * GROUP, 2 * GROUP), jnp.float32),
            pltpu.VMEM((block // 2, pairs * LANES), jnp.bfloat16),
            pltpu.SMEM((slots + 2,), jnp.int32),
            pltpu.SMEM((1,), jnp.int32),
            pltpu.SemaphoreType.DMA((outs,)),
        ],
        compiler_params=pltpu.CompilerParams(vmem_limit_bytes=16 * MIB),
        cost_estimate=pl.CostEstimate(flops=1 << 32, bytes_accessed=1 << 20, transcendentals=0),
        name="attend",
    )(place, band, turn, q_all, kv_all, vt_all)


def place_kernel(share, place_ref, own_ref, far_ref, pieces_ref, out_ref, held, sems):
    core, layer, seq = (place_ref[i] for i in range(3))
    layers, _, depth, columns = out_ref.shape
    part = depth // share // 2
    half = columns // 2
    pairs = [(own_ref, held.at[layer, core])]
    far_rows = far_ref.shape[0] // 2
    for side in range(2):
        pairs.append((
            far_ref.at[
                pl.ds(pl.multiple_of((1 - core) * far_rows + side * depth, 16), depth),
                pl.ds(far_ref.shape[1] - half, half),
            ],
            held.at[layer, 1 - core, :, pl.ds(side * half, half)],
        ))
    for other in range(share):
        there = seq ^ other
        for holder in range(2):
            at = lax.rem(there // 2 * 2 + holder, share) * 2 * part
            for step in range(layers - 1):
                row = (other * (layers - 1) + step) * part
                for side in range(2):
                    to = pl.ds(pl.multiple_of(at + side * part, 16), part)
                    pairs.append((
                        pieces_ref.at[holder, pl.ds(row, part), pl.ds(side * columns, columns)],
                        held.at[place_ref[3 + step], lax.rem(there, 2), to, :],
                    ))
    for load in copy_all(pairs, sems):
        load.wait()
    store = pltpu.make_async_copy(held, out_ref, sems.at[len(pairs)])
    store.start()
    store.wait()


def place_weights(place, share, layers, own, far, pieces):
    shape = (layers, 2) + own.shape
    return pl.pallas_call(
        functools.partial(place_kernel, share),
        out_shape=pltpu.HBM(shape, jnp.bfloat16),
        in_specs=[SMEM] + [HBM] * 3,
        out_specs=HBM,
        scratch_shapes=[
            pltpu.VMEM(shape, jnp.bfloat16), pltpu.SemaphoreType.DMA((4 + 4 * share * (layers - 1),))
        ],
        compiler_params=pltpu.CompilerParams(vmem_limit_bytes=8 * MIB),
        cost_estimate=LIGHT,
        name="place",
    )(place, *in_hbm(own, far, pieces))


def output_kernel(layers, place_ref, weight_ref, *refs):
    contexts, out_ref, held, weight, sems = refs[:layers], *refs[layers:]
    columns = weight.shape[3]
    rows = contexts[0].shape[0]
    loads = []
    for step in range(layers):
        there = place_ref[step]
        loads.append(copy_all(
            [(contexts[step], held.at[pl.ds(step * rows, rows), :]), (weight_ref.at[there], weight.at[step])],
            sems.at[pl.ds(2 * step, 2)],
        ))
    totals = [None, None]
    for step in range(layers):
        for load in loads[step]:
            load.wait()
        for side in range(2):
            got = jnp.dot(
                held[step * rows:(step + 1) * rows, :], weight[step, side], preferred_element_type=jnp.float32
            )
            totals[side] = got if step == 0 else totals[side] + got
    for side in range(2):
        out_ref[0, :, side * columns:(side + 1) * columns] = totals[side].astype(jnp.bfloat16)


def output(place, weight, contexts):
    layers, _, depth, columns = weight.shape
    rows, width = contexts[0].shape
    return pl.pallas_call(
        functools.partial(output_kernel, layers),
        out_shape=jax.ShapeDtypeStruct((1, rows, 2 * columns), jnp.bfloat16),
        in_specs=[SMEM] + [HBM] * (1 + layers),
        out_specs=VMEM,
        scratch_shapes=[
            pltpu.VMEM((layers * rows, width), jnp.bfloat16),
            pltpu.VMEM(weight.shape, jnp.bfloat16),
            pltpu.SemaphoreType.DMA((2 * layers,)),
        ],
        compiler_params=pltpu.CompilerParams(vmem_limit_bytes=16 * MIB),
        cost_estimate=LIGHT,
        name="output",
    )(place, *in_hbm(weight), *contexts)


def hold_kernel(*refs):
    del refs


def hold(values):
    return pl.pallas_call(
        hold_kernel,
        out_shape=[jax.ShapeDtypeStruct(value.shape, value.dtype) for value in values],
        in_specs=[HBM] * len(values),
        out_specs=[HBM] * len(values),
        input_output_aliases={i: i for i in range(len(values))},
        compiler_params=pltpu.CompilerParams(vmem_limit_bytes=MIB),
        cost_estimate=pl.CostEstimate(flops=1 << 34, bytes_accessed=1, transcendentals=0),
        name="hold",
    )(*values)


def together(*values):
    return lax.optimization_barrier(values)


def numbers(*values):
    return jnp.stack([jnp.asarray(value, jnp.int32) for value in values])


def local(frames, norm_gain, w_query, w_key, w_value, w_out, group_band, lengths):
    cores, seqs, layers = lax.axis_size("dp"), lax.axis_size("seq"), lax.axis_size("head")
    core, seq, layer = lax.axis_index("dp"), lax.axis_index("seq"), lax.axis_index("head")
    groups = group_band.shape[1]
    width = w_query.shape[1]
    here = [(c, s) for c in range(cores) for s in range(seqs)]

    def home(c, s):
        return s % 2, s // 2 * 2 + c

    def flat(c, s, z=None):
        return c * seqs + s if z is None else (c * seqs + s) * layers + z

    def moved(value, shift):
        pairs = [(flat(c, s, z), flat(*home(c, s), shift(z))) for c, s in here for z in range(layers)]
        return lax.ppermute(value, ("dp", "seq", "head"), pairs)

    after = ring_successors(layers)
    before = {after[z]: z for z in after}
    swap = [(c, cores - 1 - c) for c in range(cores)]
    over_link = [(flat(1, s), flat(0, s + 2)) for s in range(seqs - 2)]
    over_link += [(flat(0, s + 2), flat(1, s)) for s in range(seqs - 2)]
    share = 4 if seqs % 4 == 0 else 2

    def shared(value):
        return [value] + [
            lax.ppermute(value, "seq", [(s, s ^ other) for s in range(seqs)]) for other in range(1, share)
        ]

    rows = frames[0]
    count = rows.shape[0]
    gain = norm_gain[None, :]

    sent, piece, own = pack(numbers(lax.rem(seq, share)), rows, w_query, w_key, w_value, w_out, share)
    first = moved(sent, lambda z: after[z])
    whole = moved(rows, lambda z: z)
    third = moved(sent, lambda z: before[z])
    piece = moved(piece, lambda z: after[after[z]])
    weights = lax.all_gather(own, "dp", axis=0, tiled=True)
    facts = jnp.concatenate([group_band[0], jnp.broadcast_to(lengths[:, None], (1, group_band.shape[2]))], axis=0)
    facts = lax.ppermute(facts, ("dp", "seq"), [(flat(c, s), flat(*home(c, s))) for c, s in here])
    first, whole, piece, facts = together(first, whole, piece, facts)
    second = lax.ppermute(first, "head", [(z, after[z]) for z in range(layers)])

    query_a, pair_a = project([whole, first, third], count, width, gain, weights, 1)
    link_a = lax.ppermute(pair_a, ("dp", "seq"), over_link)
    chip_a = lax.all_gather(pair_a, "dp", axis=0)
    shares = shared(join([first, third, piece], [count, count, 0]))
    query_c, pair_c = project([second], count, width, gain, weights, 1 << 33)
    pair_c, link_a = together(pair_c, link_a)
    link_c, chip_c = lax.ppermute(pair_c, ("dp", "seq"), over_link), lax.ppermute(pair_c, "dp", swap)

    back = {z: before[z] for z in range(layers)}
    ids = [layer, lookup([back[z] for z in range(layers)], layer)]
    ids.append(lookup([after[z] for z in range(layers)], layer))
    ids.append(lookup([back[back[z]] for z in range(layers)], layer))
    place = numbers(core, (seq // 2 * 2 + core) * groups, groups * seqs, facts[groups, 0], *ids)
    band = facts[:groups]
    q_all, kv_all, vt_all = window(
        place, groups, count, [query_a, query_c], [pair_a, pair_c], [chip_a, chip_c], [link_a, link_c]
    )
    *shares, q_all = together(*shares, q_all)
    pieces = join(shares)
    pieces, q_all = together(pieces, q_all)
    pieces = lax.all_gather(pieces, "dp", axis=0)
    half = layers // 2
    arrived, sources = [], []
    for near in (0, 1):
        side = layer // half if near else 1 - layer // half
        turn = numbers(side * half * count, *[lax.rem(layer + e, half) * count for e in range(half)])
        contexts = list(attend(place, band, turn, half, q_all, kv_all, vt_all))
        if not near:
            contexts[0], q_all = together(contexts[0], q_all)
        for e, context in enumerate(contexts):
            def target(z, e=e):
                return (z // half if near else 1 - z // half) * half + (z + e) % half

            arrived.append(moved(context, target))
            sources.append(side * half + lax.rem(layer + half - e, half))
    arrived = list(hold(arrived[:half])) + arrived[half:]
    froms = [before[z] for z in range(layers)], [after[z] for z in range(layers)], [back[back[z]] for z in range(layers)]
    weight = place_weights(
        numbers(core, layer, seq, *[lookup(table, layer) for table in froms]), share, layers, w_out, weights, pieces
    )
    return output(numbers(*sources), weight, arrived)


def solution(mesh):
    return jax.shard_map(
        local,
        mesh=mesh,
        in_specs=(
            P("dp", ("seq", "head"), None),
            P(),
            P("dp", "head"),
            P("dp", "head"),
            P("dp", "head"),
            P("head", "dp"),
            P("dp", "seq", None),
            P("dp"),
        ),
        out_specs=P("dp", ("seq", "head"), None),
        check_vma=False,
    )
```

time: 183 us -> 150 us (0.82)
  Pallas kernels: 77.4 us -> 40.7 us
  waiting for transfers between devices: 21.9 us -> 48.8 us
  starting transfers between devices: 51.4 us -> 35.2 us
  between operations: 1.01 us -> 14.1 us
  local copies, waits for them, and re-layouts: 18.9 us -> 8.6 us
  other arithmetic: 9.61 us -> 0.15 us
    pallas_call x6, Pallas kernels: 60.4 us -> 21.9 us  [the longest x2 9.31 us: project(): pl.pallas_call(functools.partial(project_kernel, blocks, count), out_shap...]
    ppermute x1, starting transfers between devices: 16.2 us -> 3.09 us  [local(): second = lax.ppermute(first, 'head', [(z, after[z]) for z in range(layers)])]
    ppermute x8 -> x3, waiting for transfers between devices: 3.84 us -> 16.8 us  [the longest x1 13.3 us: local(): link_a = lax.ppermute(pair_a, ('dp', 'seq'), over_link)]
    unnamed x51 -> x21, local copies, waits for them, and re-layouts: 17.5 us -> 7.38 us
    concatenate x1 -> x0, other arithmetic: 9.46 us -> none  [local(): jnp.concatenate([w_query, w_key, w_value, jnp.concatenate([weights_out[:,...]
    ppermute x1, waiting for transfers between devices: 2.07 us -> 7.86 us  [local(): lax.ppermute(facts, ('dp', 'seq'), [(flat(c, s), flat(*home(c, s))) for c...]
    ppermute x1, waiting for transfers between devices: 0.01 us -> 4.36 us  [local(): second = lax.ppermute(first, 'head', [(z, after[z]) for z in range(layers)])]
    ppermute x7 -> x8, waiting for transfers between devices: 16 us -> 19.7 us  [moved(): return lax.ppermute(value, ('dp', 'seq', 'head'), pairs)]
  transfers between devices with their start and end apart: 20 -> 19, of which waited for: 5 -> 6; matrix products, arithmetic and copies ran while one was open for 1% -> 1% of each run, Pallas kernels for 15% -> 20%
where the time goes in v4:
time: 150 us; the launch traced here: 147 us
  waiting for transfers between devices  48.8 us (33%)
  Pallas kernels  40.7 us (27%)
  starting transfers between devices  35.2 us (23%)
  between operations  14.1 us (9%)
  local copies, waits for them, and re-layouts  8.6 us (6%)
    ppermute x8, waiting for transfers between devices, moved(): return lax.ppermute(value, ('dp', 'seq', 'head'), pairs)  19.7 us
    ppermute x8, starting transfers between devices, moved(): return lax.ppermute(value, ('dp', 'seq', 'head'), pairs)  18.5 us
    ppermute x1, waiting for transfers between devices, local(): link_a = lax.ppermute(pair_a, ('dp', 'seq'), over_link)  13.3 us
    pallas_call x2, Pallas kernels, attend(): pl.pallas_call(functools.partial(attend_kernel, groups, reach, block // 2...  11 us
    pallas_call x2, Pallas kernels, project(): pl.pallas_call(functools.partial(project_kernel, blocks, count), out_shap...  9.31 us
    ppermute x1, waiting for transfers between devices, local(): lax.ppermute(facts, ('dp', 'seq'), [(flat(c, s), flat(*home(c, s))) for c...  7.86 us
    unnamed x21, local copies, waits for them, and re-layouts  7.38 us
    pallas_call x1, Pallas kernels, place_weights(): pl.pallas_call(functools.partial(place_kernel, share), out_shape=pltpu.HB...  5.54 us
  transfers between devices with their start and end apart: 19, of which 6 were waited for; matrix products, arithmetic and copies ran while one was open for 1% of the time, Pallas kernels for 20%

profile of v4, /device:TPU:1, one launch (start us, length us, event | category | flops | bytes accessed | tf_op | source)
XLA Modules:
  0.0 147.4 jit_solution(16751446598172946948)
XLA Ops:
  6.5 0.0 all-gather.6.cloned.1.call-start
  6.5 3.4 %pack.1 = (bf16[240,1536]{1,0:T(8,128)(2,1)}, bf16[96,768]{1,0:T(8,128)(2,1)}, bf16[768,1536]{1,0:T(8,128)(2,1)}) custom-call(s32[1]{0:T(128)} %bitcast.10.place_ref, bf16[192,1536]{1,0:T(8,128)(2,1)} %bitcast.30, bf16[768,384]{1,0:T(8,128)(2,1)} %query_ref.1, bf16[768,384]{1,0:T(8,128)(2,1)} %key_ref.1, bf16[768,384]{1,0:T(8,128)(2,1)} %value_ref.1, ...), custom_call_target="tpu_custom_call" | custom-call | flops 1 | bytes 1 | tf_op jit(solution)/shard_map/pack/pallas_call | solution.py:83
  10.0 0.0 all-gather.6.cloned.1.call-update
  10.0 0.0 all-gather.8.cloned.1.call-start
  10.1 3.7 %collective-permute-start = (bf16[240,1536]{1,0:T(8,128)(2,1)}, bf16[240,1536]{1,0:T(8,128)(2,1)S(1)}, u32[]{:S(2)}, u32[]{:S(2)}) collective-permute-start(bf16[240,1536]{1,0:T(8,128)(2,1)} %get-tuple-element.37), channel_id=1, source_target_pairs={{0,1},{1,3},{2,0},{3,2},{4,17},{5,19},{6,16},{7,18},{8,9},{9,11},{... | collective-permute-start | bytes 2211848 | tf_op jit(solution)/shard_map/ppermute | solution.py:492
  13.7 1.1 collective-permute-start.4
  14.8 0.0 copy-done.7
  14.8 3.4 %collective-permute-start.1 = (bf16[192,1536]{1,0:T(8,128)(2,1)S(1)}, bf16[192,1536]{1,0:T(8,128)(2,1)S(1)}, u32[]{:S(2)}, u32[]{:S(2)}) collective-permute-start(bf16[192,1536]{1,0:T(8,128)(2,1)S(1)} %bitcast.31), channel_id=1, source_target_pairs={{0,0},{1,1},{2,2},{3,3},{4,16},{5,17},{6,18},{7,19},{8,8},{9,9},{1... | collective-permute-start | bytes 1769480 | tf_op jit(solution)/shard_map/ppermute | solution.py:492
  18.2 3.1 %collective-permute-start.2 = (bf16[96,768]{1,0:T(8,128)(2,1)}, bf16[96,768]{1,0:T(8,128)(2,1)S(1)}, u32[]{:S(2)}, u32[]{:S(2)}) collective-permute-start(bf16[96,768]{1,0:T(8,128)(2,1)} %get-tuple-element.38), channel_id=1, source_target_pairs={{0,3},{1,2},{2,1},{3,0},{4,19},{5,18},{6,17},{7,16},{8,11},{9,10},... | collective-permute-start | bytes 442376 | tf_op jit(solution)/shard_map/ppermute | solution.py:492
  21.3 0.0 copy-done.9
  22.0 3.6 %collective-permute-start.3 = (s32[7,12]{1,0:T(8,128)S(1)}, s32[7,12]{1,0:T(8,128)S(1)}, u32[]{:S(2)}, u32[]{:S(2)}) collective-permute-start(s32[7,12]{1,0:T(8,128)S(1)} %concatenate.3), channel_id=1, source_target_pairs={{0,0},{4,16},{8,8},{12,24},{16,4},{20,20},{24,12},{28,28},{1,1},{5... | collective-permute-start | bytes 1016 | tf_op jit(solution)/shard_map/ppermute | solution.py:517
  25.6 7.9 %collective-permute-done.3 = s32[7,12]{1,0:T(8,128)S(1)} collective-permute-done((s32[7,12]{1,0:T(8,128)S(1)}, s32[7,12]{1,0:T(8,128)S(1)}, u32[]{:S(2)}, u32[]{:S(2)}) %collective-permute-start.3) | collective-permute-done | bytes 368 | tf_op jit(solution)/shard_map/ppermute | solution.py:517
  33.5 17.9 %collective-permute-done.2.refs_2_ = bf16[96,768]{1,0:T(8,128)(2,1)S(1)} collective-permute-done((bf16[96,768]{1,0:T(8,128)(2,1)}, bf16[96,768]{1,0:T(8,128)(2,1)S(1)}, u32[]{:S(2)}, u32[]{:S(2)}) %collective-permute-start.2) | collective-permute-done | bytes 147488 | tf_op jit(solution)/shard_map/ppermute | solution.py:492
  51.4 0.0 collective-permute-done.1.refs_0_
  51.4 0.0 collective-permute-done.refs_0_.refs_1_
  51.4 3.1 %collective-permute-start.8 = (bf16[240,1536]{1,0:T(8,128)(2,1)S(1)}, bf16[240,1536]{1,0:T(8,128)(2,1)}, u32[]{:S(2)}, u32[]{:S(2)}) collective-permute-start(bf16[240,1536]{1,0:T(8,128)(2,1)S(1)} %collective-permute-done.refs_0_.refs_1_), channel_id=1, source_target_pairs={{0,1},{1,3},{2,0},{3,2},{4,5},{5,7},{6,4},{7,6},{8,9},{9,11},{10,8... | collective-permute-start | bytes 2211848 | tf_op jit(solution)/shard_map/ppermute | solution.py:519
  54.5 0.0 collective-permute-done.4.refs_1_.refs_2_
  54.5 0.0 all-gather.6.cloned.1.call-done.weight_ref.far_ref
  54.5 5.7 %project.2 = (bf16[576,384]{1,0:T(8,128)(2,1)}, bf16[576,768]{1,0:T(8,128)(2,1)}) custom-call(f32[1,1536]{1,0:T(1,128)S(1)} %broadcast_in_dim.10.gain_ref, bf16[1536,1536]{1,0:T(8,128)(2,1)} %all-gather.6.cloned.1.call-done.weight_ref.far_ref, bf16[192,1536]{1,0:T(8,128)(2,1)S(1)} %collective-permute-done.1.refs_0_, ...), custom_call_target="tpu_custom_call" | custom-call | flops 1 | bytes 1 | tf_op jit(solution)/shard_map/project/pallas_call | solution.py:176
  60.2 0.0 all-gather.8.cloned.1.call-update
  60.3 0.0 all-gather.10.cloned.1.call-start
  60.3 3.5 %collective-permute-start.9 = (bf16[576,768]{1,0:T(8,128)(2,1)}, bf16[576,768]{1,0:T(8,128)(2,1)S(1)}, u32[]{:S(2)}, u32[]{:S(2)}) collective-permute-start(bf16[576,768]{1,0:T(8,128)(2,1)} %get-tuple-element.45.refs_2_), channel_id=1, source_target_pairs={{16,8},{20,12},{8,16},{12,20},{17,9},{21,13},{9,17},{13,21},{18,10... | collective-permute-start | bytes 2654216 | tf_op jit(solution)/shard_map/ppermute | solution.py:522
  63.8 1.3 join.2.refs_0_
  65.1 1.2 collective-permute-start.5
  66.2 0.0 collective-permute-start.6
  66.2 1.5 %collective-permute-start.7 = (bf16[144,1536]{1,0:T(8,128)(2,1)}, bf16[144,1536]{1,0:T(8,128)(2,1)S(1)}, u32[]{:S(2)}, u32[]{:S(2)}) collective-permute-start(bf16[144,1536]{1,0:T(8,128)(2,1)} %join.2.refs_0_), channel_id=1, source_target_pairs={{0,12},{4,8},{8,4},{12,0},{1,13},{5,9},{9,5},{13,1},{2,14},{6,10},... | collective-permute-start | bytes 1327112 | tf_op jit(solution)/shard_map/ppermute | solution.py:503
  67.8 4.4 %collective-permute-done.8.refs_0_ = bf16[240,1536]{1,0:T(8,128)(2,1)} collective-permute-done((bf16[240,1536]{1,0:T(8,128)(2,1)S(1)}, bf16[240,1536]{1,0:T(8,128)(2,1)}, u32[]{:S(2)}, u32[]{:S(2)}) %collective-permute-start.8) | collective-permute-done | bytes 737312 | tf_op jit(solution)/shard_map/ppermute | solution.py:519
  72.1 3.6 %project.3 = (bf16[192,384]{1,0:T(8,128)(2,1)}, bf16[192,768]{1,0:T(8,128)(2,1)}) custom-call(f32[1,1536]{1,0:T(1,128)S(1)} %broadcast_in_dim.10.gain_ref, bf16[1536,1536]{1,0:T(8,128)(2,1)} %all-gather.6.cloned.1.call-done.weight_ref.far_ref, bf16[240,1536]{1,0:T(8,128)(2,1)} %collective-permute-done.8.refs_0_), custom_call_target="tpu_custom_call" | custom-call | flops 8589934592 | bytes 1 | tf_op jit(solution)/shard_map/project/pallas_call | solution.py:176
  75.8 0.0 copy-start
  75.8 13.3 %collective-permute-done.9.refs_6_ = bf16[576,768]{1,0:T(8,128)(2,1)S(1)} collective-permute-done((bf16[576,768]{1,0:T(8,128)(2,1)}, bf16[576,768]{1,0:T(8,128)(2,1)S(1)}, u32[]{:S(2)}, u32[]{:S(2)}) %collective-permute-start.9) | collective-permute-done | bytes 884768 | tf_op jit(solution)/shard_map/ppermute | solution.py:522
  89.1 0.0 collective-permute-start.10
  89.1 3.6 %collective-permute-start.11 = (bf16[192,768]{1,0:T(8,128)(2,1)}, bf16[192,768]{1,0:T(8,128)(2,1)S(1)}, u32[]{:S(2)}, u32[]{:S(2)}) collective-permute-start(bf16[192,768]{1,0:T(8,128)(2,1)} %get-tuple-element.47.refs_3_), channel_id=1, source_target_pairs={{16,8},{20,12},{8,16},{12,20},{17,9},{21,13},{9,17},{13,21},{18,10... | collective-permute-start | bytes 884744 | tf_op jit(solution)/shard_map/ppermute | solution.py:527
  92.8 0.5 slice.6
  93.3 0.6 stack.84.place_ref
  93.9 0.0 collective-permute-done.10.refs_5_
  93.9 3.4 %collective-permute-done.11.refs_7_ = bf16[192,768]{1,0:T(8,128)(2,1)S(1)} collective-permute-done((bf16[192,768]{1,0:T(8,128)(2,1)}, bf16[192,768]{1,0:T(8,128)(2,1)S(1)}, u32[]{:S(2)}, u32[]{:S(2)}) %collective-permute-start.11) | collective-permute-done | bytes 294944 | tf_op jit(solution)/shard_map/ppermute | solution.py:527
  97.4 2.9 %window.1 = (bf16[768,384]{1,0:T(8,128)(2,1)S(1)}, bf16[2304,768]{1,0:T(8,128)(2,1)S(1)}, bf16[3,18,128,128]{3,2,1,0:T(8,128)(2,1)S(1)}) custom-call(s32[8]{0:T(128)S(1)} %stack.84.place_ref, bf16[576,384]{1,0:T(8,128)(2,1)} %get-tuple-element.43.refs_0_, bf16[192,384]{1,0:T(8,128)(2,1)} %get-tuple-element.44.refs_1_, ...), custom_call_target="tpu_custom_call" | custom-call | bytes 8257536 | tf_op jit(solution)/shard_map/window/pallas_call | solution.py:228
  100.3 1.9 %copy-done.1 = bf16[2304,768]{1,0:T(8,128)(2,1)} copy-done((bf16[2304,768]{1,0:T(8,128)(2,1)}, bf16[2304,768]{1,0:T(8,128)(2,1)S(1)}, u32[]{:S(2)}) %copy-start.1) | copy-done | bytes 3538968
  102.2 1.2 copy-done.3
  103.4 0.8 copy-done.5
  104.2 0.0 collective-permute-done.5.refs_1_
  104.2 0.0 collective-permute-done.6.refs_2_
  104.2 0.0 collective-permute-done.7.refs_3_
  104.2 0.0 copy-done
  104.2 2.4 %join.3 = bf16[576,1536]{1,0:T(8,128)(2,1)} custom-call(bf16[144,1536]{1,0:T(8,128)(2,1)S(1)} %copy-done, bf16[144,1536]{1,0:T(8,128)(2,1)S(1)} %collective-permute-done.5.refs_1_, bf16[144,1536]{1,0:T(8,128)(2,1)S(1)} %collective-permute-done.6.refs_2_, bf16[144,1536]{1,0:T(8,128)(2,1)S(1)} %collective-permute-done.7.refs_3_), custom_call_target="tpu_custom_call" | custom-call | flops 1 | bytes 1 | tf_op jit(solution)/shard_map/join/pallas_call | solution.py:122
  106.6 0.0 all-gather.10.cloned.1.call-update
  106.6 0.1 stack.81.place_ref
  106.7 0.1 pad_add_fusion.place_ref
  106.8 0.1 add_add_fusion
  106.9 0.0 copy-done.6
  106.9 2.0 %copy-done.2 = bf16[2304,768]{1,0:T(8,128)(2,1)S(1)} copy-done((bf16[2304,768]{1,0:T(8,128)(2,1)S(1)}, bf16[2304,768]{1,0:T(8,128)(2,1)}, u32[]{:S(2)}) %copy-start.2) | copy-done | bytes 3538968
  108.9 1.5 %copy-done.4 = bf16[3,18,128,128]{3,2,1,0:T(8,128)(2,1)S(1)} copy-done((bf16[3,18,128,128]{3,2,1,0:T(8,128)(2,1)S(1)}, bf16[3,18,128,128]{3,2,1,0:T(8,128)(2,1)}, u32[]{:S(2)}) %copy-start.4) | copy-done | bytes 1769496
  110.4 5.8 %attend.2 = (bf16[192,384]{1,0:T(8,128)(2,1)}, bf16[192,384]{1,0:T(8,128)(2,1)}) custom-call(s32[8]{0:T(128)S(1)} %stack.84.place_ref, s32[6,12]{1,0:T(8,128)S(1)} %bitcast.26, s32[3]{0:T(128)S(1)} %get-tuple-element.67.turn_ref, bf16[768,384]{1,0:T(8,128)(2,1)S(1)} %copy-done.6, bf16[2304,768]{1,0:T(8,128)(2,1)S(1)} %copy-done.2, ...), custom_call_target="tpu_custom_call" | custom-call | flops 4294967296 | bytes 1048576 | tf_op jit(solution)/shard_map/attend/pallas_call | solution.py:341
  116.2 0.1 collective-permute-start.12
  116.2 3.3 %collective-permute-start.13 = (bf16[192,384]{1,0:T(8,128)(2,1)}, bf16[192,384]{1,0:T(8,128)(2,1)S(1)}, u32[]{:S(2)}, u32[]{:S(2)}) collective-permute-start(bf16[192,384]{1,0:T(8,128)(2,1)} %get-tuple-element.61), channel_id=1, source_target_pairs={{0,3},{1,2},{2,1},{3,0},{4,19},{5,18},{6,17},{7,16},{8,11},{9,10},... | collective-permute-start | bytes 442376 | tf_op jit(solution)/shard_map/ppermute | solution.py:492
  119.5 5.2 %attend.3 = (bf16[192,384]{1,0:T(8,128)(2,1)}, bf16[192,384]{1,0:T(8,128)(2,1)}) custom-call(s32[8]{0:T(128)S(1)} %stack.84.place_ref, s32[6,12]{1,0:T(8,128)S(1)} %bitcast.27, s32[3]{0:T(128)S(1)} %get-tuple-element.68.turn_ref, bf16[768,384]{1,0:T(8,128)(2,1)S(1)} %copy-done.6, bf16[2304,768]{1,0:T(8,128)(2,1)S(1)} %copy-done.2, ...), custom_call_target="tpu_custom_call" | custom-call | flops 4294967296 | bytes 1048576 | tf_op jit(solution)/shard_map/attend/pallas_call | solution.py:341
  124.7 2.0 %collective-permute-start.14 = (bf16[192,384]{1,0:T(8,128)(2,1)}, bf16[192,384]{1,0:T(8,128)(2,1)S(1)}, u32[]{:S(2)}, u32[]{:S(2)}) collective-permute-start(bf16[192,384]{1,0:T(8,128)(2,1)} %get-tuple-element.65), channel_id=1, source_target_pairs={{0,0},{1,1},{2,2},{3,3},{4,16},{5,17},{6,18},{7,19},{8,8},{9,9},{1... | collective-permute-start | bytes 442376 | tf_op jit(solution)/shard_map/ppermute | solution.py:492
  126.8 1.9 %collective-permute-start.15 = (bf16[192,384]{1,0:T(8,128)(2,1)}, bf16[192,384]{1,0:T(8,128)(2,1)S(1)}, u32[]{:S(2)}, u32[]{:S(2)}) collective-permute-start(bf16[192,384]{1,0:T(8,128)(2,1)} %get-tuple-element.66), channel_id=1, source_target_pairs={{0,1},{1,0},{2,3},{3,2},{4,17},{5,16},{6,19},{7,18},{8,9},{9,8},{1... | collective-permute-start | bytes 442376 | tf_op jit(solution)/shard_map/ppermute | solution.py:492
  128.7 1.8 %collective-permute-done.12.refs_0_ = bf16[192,384]{1,0:T(8,128)(2,1)S(1)} collective-permute-done((bf16[192,384]{1,0:T(8,128)(2,1)}, bf16[192,384]{1,0:T(8,128)(2,1)S(1)}, u32[]{:S(2)}, u32[]{:S(2)}) %collective-permute-start.12) | collective-permute-done | bytes 147488 | tf_op jit(solution)/shard_map/ppermute | solution.py:492
  130.5 0.0 collective-permute-done.13.refs_1_
  130.5 5.5 %place.1.weight_ref = bf16[4,2,384,768]{3,2,1,0:T(8,128)(2,1)} custom-call(s32[6]{0:T(128)S(1)} %stack.81.place_ref, bf16[384,768]{1,0:T(8,128)(2,1)} %own_ref.1, bf16[1536,1536]{1,0:T(8,128)(2,1)} %all-gather.6.cloned.1.call-done.weight_ref.far_ref, bf16[2,576,1536]{2,1,0:T(8,128)(2,1)} %bitcast.28), custom_call_target="tpu_custom_call" | custom-call | flops 1 | bytes 1 | tf_op jit(solution)/shard_map/place/pallas_call | solution.py:395
  136.1 0.0 collective-permute-done.14.refs_2_
  136.1 0.0 collective-permute-done.15.refs_3_
  136.1 4.8 %output.1 = bf16[1,192,1536]{2,1,0:T(8,128)(2,1)} custom-call(s32[4]{0:T(128)S(1)} %pad_add_fusion.place_ref, bf16[4,2,384,768]{3,2,1,0:T(8,128)(2,1)} %place.1.weight_ref, bf16[192,384]{1,0:T(8,128)(2,1)S(1)} %get-tuple-element.62.refs_0_, bf16[192,384]{1,0:T(8,128)(2,1)S(1)} %get-tuple-element.63.refs_1_, ...), custom_call_target="tpu_custom_call" | custom-call | flops 1 | bytes 1 | tf_op jit(solution)/shard_map/output/pallas_call | solution.py:436
  (16 shorter events, 0.0 us)
Async XLA Ops:
  6.5 8.3 %copy-start.7 = (bf16[1,192,1536]{2,1,0:T(8,128)(2,1)S(1)}, bf16[1,192,1536]{2,1,0:T(8,128)(2,1)}, u32[]{:S(2)}) copy-start(bf16[1,192,1536]{2,1,0:T(8,128)(2,1)} %param.8) | copy-start | bytes 1769476
  6.5 14.7 %copy-start.9 = (s32[1,6,12]{2,0,1:T(1,128)S(1)}, s32[1,6,12]{2,0,1:T(1,128)}, u32[]{:S(2)}) copy-start(s32[1,6,12]{2,0,1:T(1,128)} %param.14) | copy-start | bytes 868
  6.5 47.9 %copy-start.8 = (f32[1536]{0:T(1024)S(1)}, f32[1536]{0:T(1024)}, u32[]{:S(2)}) copy-start(f32[1536]{0:T(1024)} %param.9) | copy-start | bytes 18436
  6.5 48.0 %all-gather.6.cloned.1.call-start = ((), (), s32[]{:S(2)}) async-start(), calls=%async_computation | async-start | bytes 7077888 | tf_op jit(solution)/shard_map/all_gather | solution.py:515
  10.0 87.4 %all-gather.8.cloned.1.call-start = ((), (), s32[]{:S(2)}) async-start(), calls=%async_computation.1 | async-start | bytes 2654208 | tf_op jit(solution)/shard_map/all_gather | solution.py:523
  10.1 41.3 %collective-permute-start = (bf16[240,1536]{1,0:T(8,128)(2,1)}, bf16[240,1536]{1,0:T(8,128)(2,1)S(1)}, u32[]{:S(2)}, u32[]{:S(2)}) collective-permute-start(bf16[240,1536]{1,0:T(8,128)(2,1)} %get-tuple-element.37), channel_id=1, source_target_pairs={{0,1},{1,3},{2,0},{3,2},{4,17},{5,19},{6,16},{7,18},{8,9},{9,11},{... | collective-permute-start | bytes 2211848 | tf_op jit(solution)/shard_map/ppermute | solution.py:492
  13.7 40.8 %collective-permute-start.4 = (bf16[240,1536]{1,0:T(8,128)(2,1)}, bf16[240,1536]{1,0:T(8,128)(2,1)S(1)}, u32[]{:S(2)}, u32[]{:S(2)}) collective-permute-start(bf16[240,1536]{1,0:T(8,128)(2,1)} %get-tuple-element.37), channel_id=1, source_target_pairs={{0,2},{1,0},{2,3},{3,1},{4,18},{5,16},{6,19},{7,17},{8,10},{9,8},{... | collective-permute-start | bytes 2211848 | tf_op jit(solution)/shard_map/ppermute | solution.py:492
  14.8 36.6 %collective-permute-start.1 = (bf16[192,1536]{1,0:T(8,128)(2,1)S(1)}, bf16[192,1536]{1,0:T(8,128)(2,1)S(1)}, u32[]{:S(2)}, u32[]{:S(2)}) collective-permute-start(bf16[192,1536]{1,0:T(8,128)(2,1)S(1)} %bitcast.31), channel_id=1, source_target_pairs={{0,0},{1,1},{2,2},{3,3},{4,16},{5,17},{6,18},{7,19},{8,8},{9,9},{1... | collective-permute-start | bytes 1769480 | tf_op jit(solution)/shard_map/ppermute | solution.py:492
  18.2 33.2 %collective-permute-start.2 = (bf16[96,768]{1,0:T(8,128)(2,1)}, bf16[96,768]{1,0:T(8,128)(2,1)S(1)}, u32[]{:S(2)}, u32[]{:S(2)}) collective-permute-start(bf16[96,768]{1,0:T(8,128)(2,1)} %get-tuple-element.38), channel_id=1, source_target_pairs={{0,3},{1,2},{2,1},{3,0},{4,19},{5,18},{6,17},{7,16},{8,11},{9,10},... | collective-permute-start | bytes 442376 | tf_op jit(solution)/shard_map/ppermute | solution.py:492
  22.0 11.5 %collective-permute-start.3 = (s32[7,12]{1,0:T(8,128)S(1)}, s32[7,12]{1,0:T(8,128)S(1)}, u32[]{:S(2)}, u32[]{:S(2)}) collective-permute-start(s32[7,12]{1,0:T(8,128)S(1)} %concatenate.3), channel_id=1, source_target_pairs={{0,0},{4,16},{8,8},{12,24},{16,4},{20,20},{24,12},{28,28},{1,1},{5... | collective-permute-start | bytes 1016 | tf_op jit(solution)/shard_map/ppermute | solution.py:517
  51.4 20.8 %collective-permute-start.8 = (bf16[240,1536]{1,0:T(8,128)(2,1)S(1)}, bf16[240,1536]{1,0:T(8,128)(2,1)}, u32[]{:S(2)}, u32[]{:S(2)}) collective-permute-start(bf16[240,1536]{1,0:T(8,128)(2,1)S(1)} %collective-permute-done.refs_0_.refs_1_), channel_id=1, source_target_pairs={{0,1},{1,3},{2,0},{3,2},{4,5},{5,7},{6,4},{7,6},{8,9},{9,11},{10,8... | collective-permute-start | bytes 2211848 | tf_op jit(solution)/shard_map/ppermute | solution.py:519
  60.3 70.2 %all-gather.10.cloned.1.call-start = ((), (), s32[]{:S(2)}) async-start(), calls=%async_computation.2 | async-start | bytes 5308416 | tf_op jit(solution)/shard_map/all_gather | solution.py:541
  60.3 28.8 %collective-permute-start.9 = (bf16[576,768]{1,0:T(8,128)(2,1)}, bf16[576,768]{1,0:T(8,128)(2,1)S(1)}, u32[]{:S(2)}, u32[]{:S(2)}) collective-permute-start(bf16[576,768]{1,0:T(8,128)(2,1)} %get-tuple-element.45.refs_2_), channel_id=1, source_target_pairs={{16,8},{20,12},{8,16},{12,20},{17,9},{21,13},{9,17},{13,21},{18,10... | collective-permute-start | bytes 2654216 | tf_op jit(solution)/shard_map/ppermute | solution.py:522
  65.1 39.1 %collective-permute-start.5 = (bf16[144,1536]{1,0:T(8,128)(2,1)}, bf16[144,1536]{1,0:T(8,128)(2,1)S(1)}, u32[]{:S(2)}, u32[]{:S(2)}) collective-permute-start(bf16[144,1536]{1,0:T(8,128)(2,1)} %join.2.refs_0_), channel_id=1, source_target_pairs={{0,4},{4,0},{8,12},{12,8},{1,5},{5,1},{9,13},{13,9},{2,6},{6,2},{1... | collective-permute-start | bytes 1327112 | tf_op jit(solution)/shard_map/ppermute | solution.py:503
  66.2 38.0 %collective-permute-start.6 = (bf16[144,1536]{1,0:T(8,128)(2,1)}, bf16[144,1536]{1,0:T(8,128)(2,1)S(1)}, u32[]{:S(2)}, u32[]{:S(2)}) collective-permute-start(bf16[144,1536]{1,0:T(8,128)(2,1)} %join.2.refs_0_), channel_id=1, source_target_pairs={{0,8},{4,12},{8,0},{12,4},{1,9},{5,13},{9,1},{13,5},{2,10},{6,14},... | collective-permute-start | bytes 1327112 | tf_op jit(solution)/shard_map/ppermute | solution.py:503
  66.2 38.0 %collective-permute-start.7 = (bf16[144,1536]{1,0:T(8,128)(2,1)}, bf16[144,1536]{1,0:T(8,128)(2,1)S(1)}, u32[]{:S(2)}, u32[]{:S(2)}) collective-permute-start(bf16[144,1536]{1,0:T(8,128)(2,1)} %join.2.refs_0_), channel_id=1, source_target_pairs={{0,12},{4,8},{8,4},{12,0},{1,13},{5,9},{9,5},{13,1},{2,14},{6,10},... | collective-permute-start | bytes 1327112 | tf_op jit(solution)/shard_map/ppermute | solution.py:503
  75.8 28.5 %copy-start = (bf16[144,1536]{1,0:T(8,128)(2,1)S(1)}, bf16[144,1536]{1,0:T(8,128)(2,1)}, u32[]{:S(2)}) copy-start(bf16[144,1536]{1,0:T(8,128)(2,1)} %join.2.refs_0_) | copy-start | bytes 1327108
  89.1 4.8 %collective-permute-start.10 = (bf16[192,768]{1,0:T(8,128)(2,1)}, bf16[192,768]{1,0:T(8,128)(2,1)S(1)}, u32[]{:S(2)}, u32[]{:S(2)}) collective-permute-start(bf16[192,768]{1,0:T(8,128)(2,1)} %get-tuple-element.47.refs_3_), channel_id=1, source_target_pairs={{0,16},{16,0},{1,17},{17,1},{2,18},{18,2},{3,19},{19,3},{4,20},{20... | collective-permute-start | bytes 884744 | tf_op jit(solution)/shard_map/ppermute | solution.py:527
  89.1 8.2 %collective-permute-start.11 = (bf16[192,768]{1,0:T(8,128)(2,1)}, bf16[192,768]{1,0:T(8,128)(2,1)S(1)}, u32[]{:S(2)}, u32[]{:S(2)}) collective-permute-start(bf16[192,768]{1,0:T(8,128)(2,1)} %get-tuple-element.47.refs_3_), channel_id=1, source_target_pairs={{16,8},{20,12},{8,16},{12,20},{17,9},{21,13},{9,17},{13,21},{18,10... | collective-permute-start | bytes 884744 | tf_op jit(solution)/shard_map/ppermute | solution.py:527
  100.3 1.9 %copy-start.1 = (bf16[2304,768]{1,0:T(8,128)(2,1)}, bf16[2304,768]{1,0:T(8,128)(2,1)S(1)}, u32[]{:S(2)}) copy-start(bf16[2304,768]{1,0:T(8,128)(2,1)S(1)} %get-tuple-element.57.kv_all) | copy-start | bytes 10616836
  102.2 1.2 copy-start.3
  103.4 0.8 copy-start.5
  104.2 2.7 %copy-start.6 = (bf16[768,384]{1,0:T(8,128)(2,1)S(1)}, bf16[768,384]{1,0:T(8,128)(2,1)}, u32[]{:S(2)}) copy-start(bf16[768,384]{1,0:T(8,128)(2,1)} %copy-done.5) | copy-start | bytes 1769476
  106.9 2.0 %copy-start.2 = (bf16[2304,768]{1,0:T(8,128)(2,1)S(1)}, bf16[2304,768]{1,0:T(8,128)(2,1)}, u32[]{:S(2)}) copy-start(bf16[2304,768]{1,0:T(8,128)(2,1)} %copy-done.1) | copy-start | bytes 10616836
  108.9 1.5 %copy-start.4 = (bf16[3,18,128,128]{3,2,1,0:T(8,128)(2,1)S(1)}, bf16[3,18,128,128]{3,2,1,0:T(8,128)(2,1)}, u32[]{:S(2)}) copy-start(bf16[3,18,128,128]{3,2,1,0:T(8,128)(2,1)} %copy-done.3) | copy-start | bytes 5308420
  116.2 14.3 %collective-permute-start.12 = (bf16[192,384]{1,0:T(8,128)(2,1)}, bf16[192,384]{1,0:T(8,128)(2,1)S(1)}, u32[]{:S(2)}, u32[]{:S(2)}) collective-permute-start(bf16[192,384]{1,0:T(8,128)(2,1)} %get-tuple-element.60), channel_id=1, source_target_pairs={{0,2},{1,3},{2,0},{3,1},{4,18},{5,19},{6,16},{7,17},{8,10},{9,11},... | collective-permute-start | bytes 442376 | tf_op jit(solution)/shard_map/ppermute | solution.py:492
  116.2 14.3 %collective-permute-start.13 = (bf16[192,384]{1,0:T(8,128)(2,1)}, bf16[192,384]{1,0:T(8,128)(2,1)S(1)}, u32[]{:S(2)}, u32[]{:S(2)}) collective-permute-start(bf16[192,384]{1,0:T(8,128)(2,1)} %get-tuple-element.61), channel_id=1, source_target_pairs={{0,3},{1,2},{2,1},{3,0},{4,19},{5,18},{6,17},{7,16},{8,11},{9,10},... | collective-permute-start | bytes 442376 | tf_op jit(solution)/shard_map/ppermute | solution.py:492
  124.7 11.3 %collective-permute-start.14 = (bf16[192,384]{1,0:T(8,128)(2,1)}, bf16[192,384]{1,0:T(8,128)(2,1)S(1)}, u32[]{:S(2)}, u32[]{:S(2)}) collective-permute-start(bf16[192,384]{1,0:T(8,128)(2,1)} %get-tuple-element.65), channel_id=1, source_target_pairs={{0,0},{1,1},{2,2},{3,3},{4,16},{5,17},{6,18},{7,19},{8,8},{9,9},{1... | collective-permute-start | bytes 442376 | tf_op jit(solution)/shard_map/ppermute | solution.py:492
  126.8 9.3 %collective-permute-start.15 = (bf16[192,384]{1,0:T(8,128)(2,1)}, bf16[192,384]{1,0:T(8,128)(2,1)S(1)}, u32[]{:S(2)}, u32[]{:S(2)}) collective-permute-start(bf16[192,384]{1,0:T(8,128)(2,1)} %get-tuple-element.66), channel_id=1, source_target_pairs={{0,1},{1,0},{2,3},{3,2},{4,17},{5,16},{6,19},{7,18},{8,9},{9,8},{1... | collective-permute-start | bytes 442376 | tf_op jit(solution)/shard_map/ppermute | solution.py:492
Sparse Core Ops, SparseCore 0:
  10.1 16.8 all-gather.5
  60.4 11.3 all-gather.7
  106.7 13.9 all-gather.9

commit v5 on v4

--- a/solution.py
+++ b/solution.py
@@ -43,18 +43,11 @@
     return [pltpu.with_memory_space_constraint(value, pltpu.HBM) for value in values]
 
 
-def pack_kernel(place_ref, rows_ref, query_ref, key_ref, value_ref, w_out_ref, sent_ref, piece_ref, all_ref, *refs):
-    held_sent, held_piece, held, sems = refs
+def bundle_kernel(place_ref, query_ref, key_ref, value_ref, w_out_ref, all_ref, piece_ref, held, held_piece, sems):
     depth, width = query_ref.shape
-    count = rows_ref.shape[0]
-    part, columns = piece_ref.shape
+    part = piece_ref.shape[0]
     first = pl.multiple_of(place_ref[0] * part, 16)
-    pairs = [(rows_ref, held_sent.at[pl.ds(0, count), :]), (w_out_ref.at[pl.ds(first, part), :], held_piece)]
-    for side in range(2):
-        pairs.append((
-            w_out_ref.at[pl.ds(first + side * part // 2, part // 2), :],
-            held_sent.at[pl.ds(count, part // 2), pl.ds(side * columns, columns)],
-        ))
+    pairs = [(w_out_ref.at[pl.ds(first, part), :], held_piece)]
     for place, source in enumerate((query_ref, key_ref, value_ref)):
         pairs.append((source, held.at[:, pl.ds(place * width, width)]))
     rows = w_out_ref.shape[0]
@@ -64,87 +57,74 @@
             held.at[pl.ds(side * rows, rows), pl.ds(3 * width, width)],
         ))
     loads = copy_all(pairs, sems)
-    for load in loads[:4]:
+    loads[0].wait()
+    stores = copy_all([(held_piece, piece_ref)], sems.at[pl.ds(len(pairs), 1)])
+    for load in loads[1:]:
         load.wait()
-    stores = copy_all([(held_sent, sent_ref), (held_piece, piece_ref)], sems.at[pl.ds(len(pairs), 2)])
-    for load in loads[4:]:
-        load.wait()
-    stores += copy_all([(held, all_ref)], sems.at[pl.ds(len(pairs) + 2, 1)])
+    stores += copy_all([(held, all_ref)], sems.at[pl.ds(len(pairs) + 1, 1)])
     for store in stores:
         store.wait()
 
 
-def pack(place, rows, w_query, w_key, w_value, w_out, share):
+def bundle(place, w_query, w_key, w_value, w_out, share):
     depth, width = w_query.shape
-    part = w_out.shape[0] // share
-    shapes = [
-        (rows.shape[0] + part // 2, rows.shape[1]), (part, w_out.shape[1]), (depth, 4 * width)
-    ]
-    return pl.pallas_call(
-        pack_kernel,
+    shapes = [(depth, 4 * width), (w_out.shape[0] // share, w_out.shape[1])]
+    return pl.pallas_call(
+        bundle_kernel,
         out_shape=[pltpu.HBM(shape, jnp.bfloat16) for shape in shapes],
-        in_specs=[SMEM] + [HBM] * 5,
-        out_specs=[HBM] * 3,
-        scratch_shapes=[pltpu.VMEM(shape, jnp.bfloat16) for shape in shapes] + [pltpu.SemaphoreType.DMA((12,))],
-        compiler_params=pltpu.CompilerParams(vmem_limit_bytes=8 * MIB),
+        in_specs=[SMEM] + [HBM] * 4,
+        out_specs=[HBM] * 2,
+        scratch_shapes=[pltpu.VMEM(shape, jnp.bfloat16) for shape in shapes] + [pltpu.SemaphoreType.DMA((8,))],
+        compiler_params=pltpu.CompilerParams(vmem_limit_bytes=4 * MIB),
         cost_estimate=LIGHT,
-        name="pack",
-    )(place, *in_hbm(rows, w_query, w_key, w_value, w_out))
-
-
-def join_kernel(skips, *refs):
+        name="bundle",
+    )(place, *in_hbm(w_query, w_key, w_value, w_out))
+
+
+def join_kernel(*refs):
     sources, (out, held, sems) = refs[:-3], refs[-3:]
-    spans, parts, at = [], [], 0
-    columns = held.shape[1]
-    for skip, source in zip(skips, sources):
-        rows = source.shape[0] - skip
-        if source.shape[1] == columns:
-            parts.append((source.at[pl.ds(skip, rows), :], held.at[pl.ds(at, rows), :]))
-        else:
-            rows //= 2
-            for side in range(2):
-                parts.append((
-                    source.at[pl.ds(side * rows, rows), :],
-                    held.at[pl.ds(at, rows), pl.ds(side * source.shape[1], source.shape[1])],
-                ))
-        spans.append(pl.ds(at, rows))
-        at += rows
-    for load in copy_all(parts, sems):
+    spans, at = [], 0
+    for source in sources:
+        spans.append(pl.ds(at, source.shape[0]))
+        at += source.shape[0]
+    loads = copy_all([(source, held.at[span, :]) for source, span in zip(sources, spans)], sems)
+    stores = []
+    for place, (load, span) in enumerate(zip(loads, spans)):
         load.wait()
-    for store in copy_all([(held.at[span, :], out.at[span, :]) for span in spans], sems.at[pl.ds(len(parts), len(spans))]):
+        stores += copy_all([(held.at[span, :], out.at[span, :])], sems.at[pl.ds(len(loads) + place, 1)])
+    for store in stores:
         store.wait()
 
 
-def join(values, skips=None):
-    skips = [0] * len(values) if skips is None else skips
-    columns = max(value.shape[1] for value in values)
-    rows = sum((value.shape[0] - skip) * value.shape[1] // columns for value, skip in zip(values, skips))
-    return pl.pallas_call(
-        functools.partial(join_kernel, tuple(skips)),
+def join(values, cost=1):
+    rows, columns = sum(value.shape[0] for value in values), values[0].shape[1]
+    return pl.pallas_call(
+        join_kernel,
         out_shape=pltpu.HBM((rows, columns), jnp.bfloat16),
         in_specs=[HBM] * len(values),
         out_specs=HBM,
         scratch_shapes=[
-            pltpu.VMEM((rows, columns), jnp.bfloat16), pltpu.SemaphoreType.DMA((3 * len(values),))
+            pltpu.VMEM((rows, columns), jnp.bfloat16), pltpu.SemaphoreType.DMA((2 * len(values),))
         ],
         compiler_params=pltpu.CompilerParams(vmem_limit_bytes=4 * MIB),
-        cost_estimate=LIGHT,
+        cost_estimate=pl.CostEstimate(flops=cost, bytes_accessed=1, transcendentals=0),
         name="join",
     )(*values)
 
 
-def project_kernel(blocks, count, gain_ref, weight_ref, *refs):
+def project_kernel(blocks, place_ref, gain_ref, own_ref, far_ref, *refs):
     rows = refs[:blocks]
     query_ref, pair_ref, held, weight, query_held, pair_held, sems = refs[blocks:]
-    width = query_ref.shape[1]
+    count, (depth, width) = rows[0].shape[0], (own_ref.shape[0], query_ref.shape[1])
+    core = place_ref[0]
     order = (1, 2, 0)
-    loads = copy_all(
-        [(rows[i].at[pl.ds(0, count), :], held.at[pl.ds(i * count, count), :]) for i in range(blocks)], sems
-    )
-    fetches = copy_all(
-        [(weight_ref.at[:, pl.ds(place * width, width)], weight.at[place]) for place in order],
-        sems.at[pl.ds(blocks, 3)],
-    )
+    loads = copy_all([(rows[i], held.at[pl.ds(i * count, count), :]) for i in range(blocks)], sems)
+    fetches = []
+    for place in order:
+        for source, owner in ((own_ref, core), (far_ref, 1 - core)):
+            to = weight.at[place, pl.ds(pl.multiple_of(owner * depth, 16), depth), :]
+            fetches.append((source.at[:, pl.ds(place * width, width)], to))
+    fetches = copy_all(fetches, sems.at[pl.ds(blocks, len(fetches))])
     gain = gain_ref[...]
     normalized = []
     for i in range(blocks):
@@ -155,10 +135,11 @@
         normalized.append((center * lax.rsqrt(spread + epsilon) * gain).astype(jnp.bfloat16))
     normalized = normalized[0] if blocks == 1 else jnp.concatenate(normalized, axis=0)
     stores = []
-    for place, fetch in zip(order, fetches):
-        fetch.wait()
+    for turn, place in enumerate(order):
+        for fetch in fetches[2 * turn:2 * turn + 2]:
+            fetch.wait()
         got = jnp.dot(normalized, weight[place], preferred_element_type=jnp.float32).astype(jnp.bfloat16)
-        sem = sems.at[pl.ds(blocks + 3 + place, 1)]
+        sem = sems.at[pl.ds(blocks + len(fetches) + place, 1)]
         if place == 0:
             query_held[...] = (got.astype(jnp.float32) * (HD ** -0.5)).astype(jnp.bfloat16)
             stores += copy_all([(query_held, query_ref)], sem)
@@ -170,25 +151,25 @@
         store.wait()
 
 
-def project(rows, count, width, gain, weight, cost):
-    blocks, depth = len(rows), rows[0].shape[1]
+def project(place, rows, width, gain, own, far, cost):
+    blocks, (count, depth) = len(rows), rows[0].shape
     total = blocks * count
     return pl.pallas_call(
-        functools.partial(project_kernel, blocks, count),
+        functools.partial(project_kernel, blocks),
         out_shape=[pltpu.HBM((total, width), jnp.bfloat16), pltpu.HBM((total, 2 * width), jnp.bfloat16)],
-        in_specs=[VMEM] + [HBM] * (blocks + 1),
+        in_specs=[SMEM, VMEM] + [HBM] * (blocks + 2),
         out_specs=[HBM, HBM],
         scratch_shapes=[
             pltpu.VMEM((total, depth), jnp.bfloat16),
             pltpu.VMEM((3, depth, width), jnp.bfloat16),
             pltpu.VMEM((total, width), jnp.bfloat16),
             pltpu.VMEM((total, 2 * width), jnp.bfloat16),
-            pltpu.SemaphoreType.DMA((blocks + 6,)),
+            pltpu.SemaphoreType.DMA((blocks + 9,)),
         ],
         compiler_params=pltpu.CompilerParams(vmem_limit_bytes=24 * MIB),
         cost_estimate=pl.CostEstimate(flops=cost, bytes_accessed=1, transcendentals=0),
         name="project",
-    )(gain, *in_hbm(weight), *rows)
+    )(place, gain, *in_hbm(own), far, *rows)
 
 
 def window_kernel(shape, groups, place_ref, *refs):
@@ -210,8 +191,7 @@
                 (owns[kind], block), (sides[kind], chip_base), (sides[kinds + kind], link_base)
             ):
                 to = pl.ds(pl.multiple_of(base + at, 64), rows)
-                taken = source.at[1 - core, part, :] if len(source.shape) == 3 else source.at[part, :]
-                pairs.append((taken, kv_all.at[to, :]))
+                pairs.append((source.at[part, :], kv_all.at[to, :]))
             step += 1
     for copy in copy_all(pairs, sems):
         copy.wait()
@@ -238,8 +218,7 @@
         compiler_params=pltpu.CompilerParams(vmem_limit_bytes=16 * MIB),
         cost_estimate=pl.CostEstimate(flops=0, bytes_accessed=2 * 14 * block * width, transcendentals=0),
         name="window",
-    )(place, *in_hbm(*queries, *owns, *[side for side in chip_side if side.ndim == 3]),
-      *[side for side in chip_side if side.ndim == 2], *link_side)
+    )(place, *in_hbm(*queries, *owns), *chip_side, *link_side)
 
 
 def attend_kernel(groups, reach, count_rows, place_ref, band_ref, turn_ref, q_all, kv_all, vt_all, *refs):
@@ -356,33 +335,24 @@
     )(place, band, turn, q_all, kv_all, vt_all)
 
 
-def place_kernel(share, place_ref, own_ref, far_ref, pieces_ref, out_ref, held, sems):
+def place_kernel(share, place_ref, own_ref, far_ref, pieces_ref, theirs_ref, out_ref, mark_ref, held, sems):
+    mark_ref[...] = jnp.zeros_like(mark_ref)
     core, layer, seq = (place_ref[i] for i in range(3))
     layers, _, depth, columns = out_ref.shape
-    part = depth // share // 2
+    part = depth // share
     half = columns // 2
     pairs = [(own_ref, held.at[layer, core])]
-    far_rows = far_ref.shape[0] // 2
     for side in range(2):
         pairs.append((
-            far_ref.at[
-                pl.ds(pl.multiple_of((1 - core) * far_rows + side * depth, 16), depth),
-                pl.ds(far_ref.shape[1] - half, half),
-            ],
+            far_ref.at[pl.ds(side * depth, depth), pl.ds(far_ref.shape[1] - half, half)],
             held.at[layer, 1 - core, :, pl.ds(side * half, half)],
         ))
     for other in range(share):
-        there = seq ^ other
-        for holder in range(2):
-            at = lax.rem(there // 2 * 2 + holder, share) * 2 * part
+        at = pl.ds(pl.multiple_of(lax.rem(seq ^ other, share) * part, 16), part)
+        for source, source_core in ((pieces_ref, core), (theirs_ref, 1 - core)):
             for step in range(layers - 1):
                 row = (other * (layers - 1) + step) * part
-                for side in range(2):
-                    to = pl.ds(pl.multiple_of(at + side * part, 16), part)
-                    pairs.append((
-                        pieces_ref.at[holder, pl.ds(row, part), pl.ds(side * columns, columns)],
-                        held.at[place_ref[3 + step], lax.rem(there, 2), to, :],
-                    ))
+                pairs.append((source.at[pl.ds(row, part), :], held.at[place_ref[3 + step], source_core, at, :]))
     for load in copy_all(pairs, sems):
         load.wait()
     store = pltpu.make_async_copy(held, out_ref, sems.at[len(pairs)])
@@ -390,20 +360,20 @@
     store.wait()
 
 
-def place_weights(place, share, layers, own, far, pieces):
+def place_weights(place, share, layers, own, far, mine, theirs):
     shape = (layers, 2) + own.shape
     return pl.pallas_call(
         functools.partial(place_kernel, share),
-        out_shape=pltpu.HBM(shape, jnp.bfloat16),
-        in_specs=[SMEM] + [HBM] * 3,
-        out_specs=HBM,
+        out_shape=[pltpu.HBM(shape, jnp.bfloat16), jax.ShapeDtypeStruct((8, LANES), jnp.float32)],
+        in_specs=[SMEM] + [HBM] * 4,
+        out_specs=[HBM, VMEM],
         scratch_shapes=[
-            pltpu.VMEM(shape, jnp.bfloat16), pltpu.SemaphoreType.DMA((4 + 4 * share * (layers - 1),))
+            pltpu.VMEM(shape, jnp.bfloat16), pltpu.SemaphoreType.DMA((4 + 2 * share * (layers - 1),))
         ],
         compiler_params=pltpu.CompilerParams(vmem_limit_bytes=8 * MIB),
         cost_estimate=LIGHT,
         name="place",
-    )(place, *in_hbm(own, far, pieces))
+    )(place, *in_hbm(own), far, *in_hbm(mine), theirs)
 
 
 def output_kernel(layers, place_ref, weight_ref, *refs):
@@ -496,49 +466,59 @@
     swap = [(c, cores - 1 - c) for c in range(cores)]
     over_link = [(flat(1, s), flat(0, s + 2)) for s in range(seqs - 2)]
     over_link += [(flat(0, s + 2), flat(1, s)) for s in range(seqs - 2)]
-    share = 4 if seqs % 4 == 0 else 2
+    share = 4
 
     def shared(value):
-        return [value] + [
-            lax.ppermute(value, "seq", [(s, s ^ other) for s in range(seqs)]) for other in range(1, share)
+        near = [lax.ppermute(value, "seq", [(s, s ^ step) for s in range(seqs)]) for step in (1, 2)]
+        middle = value.shape[0] // 2
+        halves = (near[1][:middle], near[0][middle:])
+        opposite = [
+            lax.ppermute(half, "seq", [(s, s ^ step) for s in range(seqs)]) for half, step in zip(halves, (1, 2))
         ]
+        return [value] + near + opposite
 
     rows = frames[0]
     count = rows.shape[0]
     gain = norm_gain[None, :]
 
-    sent, piece, own = pack(numbers(lax.rem(seq, share)), rows, w_query, w_key, w_value, w_out, share)
-    first = moved(sent, lambda z: after[z])
+    def ringed(value):
+        return lax.ppermute(value, "head", [(z, after[z]) for z in range(layers)])
+
+    first = moved(rows, lambda z: after[z])
+    second = ringed(first)
+    third = ringed(second)
+    own, piece = bundle(numbers(lax.rem(seq, share)), w_query, w_key, w_value, w_out, share)
+    far = lax.ppermute(own, "dp", swap)
     whole = moved(rows, lambda z: z)
-    third = moved(sent, lambda z: before[z])
-    piece = moved(piece, lambda z: after[after[z]])
-    weights = lax.all_gather(own, "dp", axis=0, tiled=True)
     facts = jnp.concatenate([group_band[0], jnp.broadcast_to(lengths[:, None], (1, group_band.shape[2]))], axis=0)
     facts = lax.ppermute(facts, ("dp", "seq"), [(flat(c, s), flat(*home(c, s))) for c, s in here])
-    first, whole, piece, facts = together(first, whole, piece, facts)
-    second = lax.ppermute(first, "head", [(z, after[z]) for z in range(layers)])
-
-    query_a, pair_a = project([whole, first, third], count, width, gain, weights, 1)
-    link_a = lax.ppermute(pair_a, ("dp", "seq"), over_link)
-    chip_a = lax.all_gather(pair_a, "dp", axis=0)
-    shares = shared(join([first, third, piece], [count, count, 0]))
-    query_c, pair_c = project([second], count, width, gain, weights, 1 << 33)
-    pair_c, link_a = together(pair_c, link_a)
+    pieces, held = [], piece
+    step = 1
+    while step < layers:
+        pieces.append(lax.ppermute(held, "head", [(z, z ^ step) for z in range(layers)]))
+        held = join([held, pieces[-1]], 1 << 33) if 2 * step < layers else held
+        step *= 2
+    shares = shared(join(pieces, 1 << 32))
+    whole, facts = together(whole, facts)
+
+    core_at = numbers(core)
+    query_a, pair_a = project(core_at, [whole, first, second], width, gain, own, far, 1)
+    link_a, chip_a = lax.ppermute(pair_a, ("dp", "seq"), over_link), lax.ppermute(pair_a, "dp", swap)
+    query_c, pair_c = project(core_at, [third], width, gain, own, far, 1 << 33)
     link_c, chip_c = lax.ppermute(pair_c, ("dp", "seq"), over_link), lax.ppermute(pair_c, "dp", swap)
+    _, *shares = together(query_a, *shares)
+    mine = join(shares)
+    theirs = lax.ppermute(mine, "dp", swap)
 
     back = {z: before[z] for z in range(layers)}
     ids = [layer, lookup([back[z] for z in range(layers)], layer)]
+    ids.append(lookup([back[back[z]] for z in range(layers)], layer))
     ids.append(lookup([after[z] for z in range(layers)], layer))
-    ids.append(lookup([back[back[z]] for z in range(layers)], layer))
     place = numbers(core, (seq // 2 * 2 + core) * groups, groups * seqs, facts[groups, 0], *ids)
     band = facts[:groups]
     q_all, kv_all, vt_all = window(
         place, groups, count, [query_a, query_c], [pair_a, pair_c], [chip_a, chip_c], [link_a, link_c]
     )
-    *shares, q_all = together(*shares, q_all)
-    pieces = join(shares)
-    pieces, q_all = together(pieces, q_all)
-    pieces = lax.all_gather(pieces, "dp", axis=0)
     half = layers // 2
     arrived, sources = [], []
     for near in (0, 1):
@@ -547,18 +527,20 @@
         contexts = list(attend(place, band, turn, half, q_all, kv_all, vt_all))
         if not near:
             contexts[0], q_all = together(contexts[0], q_all)
+        if near:
+            contexts[0], theirs = together(contexts[0], theirs)
         for e, context in enumerate(contexts):
             def target(z, e=e):
                 return (z // half if near else 1 - z // half) * half + (z + e) % half
 
             arrived.append(moved(context, target))
             sources.append(side * half + lax.rem(layer + half - e, half))
-    arrived = list(hold(arrived[:half])) + arrived[half:]
-    froms = [before[z] for z in range(layers)], [after[z] for z in range(layers)], [back[back[z]] for z in range(layers)]
-    weight = place_weights(
-        numbers(core, layer, seq, *[lookup(table, layer) for table in froms]), share, layers, w_out, weights, pieces
+    weight, mark = place_weights(
+        numbers(core, layer, seq, *[layer ^ step for step in range(1, layers)]),
+        share, layers, w_out, far, mine, theirs,
     )
-    return output(numbers(*sources), weight, arrived)
+    *held, _ = hold(arrived[:half] + [mark])
+    return output(numbers(*sources), weight, held + arrived[half:])
 
 
 def solution(mesh):

time: 150 us -> 122 us (0.81); the launches traced: 147 us -> 121 us
  waiting for transfers between devices: 48.8 us -> 20.6 us
  starting transfers between devices: 35.2 us -> 52.6 us
  between operations: 14.1 us -> 1.23 us
  local copies, waits for them, and re-layouts: 8.6 us -> 4.79 us
    ppermute x5 -> x12, starting transfers between devices: 9.27 us -> 29.5 us  [the longest x2 16.8 us: local(): lax.ppermute(held, 'head', [(z, z ^ step) for z in range(layers)])]
    ppermute x8 -> x6, waiting for transfers between devices: 19.7 us -> 0.02 us  [moved(): return lax.ppermute(value, ('dp', 'seq', 'head'), pairs)]
    ppermute x1, waiting for transfers between devices: 7.86 us -> 0.01 us  [local(): lax.ppermute(facts, ('dp', 'seq'), [(flat(c, s), flat(*home(c, s))) for c...]
    unnamed x21 -> x13, local copies, waits for them, and re-layouts: 7.38 us -> 1.99 us
    ppermute x8 -> x6, starting transfers between devices: 18.5 us -> 13.8 us  [moved(): return lax.ppermute(value, ('dp', 'seq', 'head'), pairs)]
    ppermute x1, starting transfers between devices: 3.64 us -> 6.1 us  [local(): lax.ppermute(facts, ('dp', 'seq'), [(flat(c, s), flat(*home(c, s))) for c...]
    ppermute x5 -> x12, waiting for transfers between devices: 17.7 us -> 16.6 us  [the longest x2 13.7 us: local(): lax.ppermute(held, 'head', [(z, z ^ step) for z in range(layers)])]
    pallas_call x6 -> x7, Pallas kernels: 21.9 us -> 22.8 us  [the longest x2 9.92 us: project(): pl.pallas_call(functools.partial(project_kernel, blocks), out_shape=[pltp...]
  transfers between devices with their start and end apart: 19 -> 21, of which waited for: 6 -> 4; matrix products, arithmetic and copies ran while one was open for 1% -> 2% of each run, Pallas kernels for 20% -> 28%
where the time goes in v5:
time: 122 us; the launch traced here: 121 us
  starting transfers between devices  52.6 us (43%)
  Pallas kernels  41.7 us (34%)
  waiting for transfers between devices  20.6 us (17%)
  local copies, waits for them, and re-layouts  4.79 us (4%)
  between operations  1.23 us (1%)
    ppermute x2, starting transfers between devices, local(): lax.ppermute(held, 'head', [(z, z ^ step) for z in range(layers)])  16.8 us
    ppermute x6, starting transfers between devices, moved(): return lax.ppermute(value, ('dp', 'seq', 'head'), pairs)  13.8 us
    ppermute x2, waiting for transfers between devices, local(): lax.ppermute(held, 'head', [(z, z ^ step) for z in range(layers)])  13.7 us
    pallas_call x2, Pallas kernels, attend(): pl.pallas_call(functools.partial(attend_kernel, groups, reach, block // 2...  10.9 us
    pallas_call x2, Pallas kernels, project(): pl.pallas_call(functools.partial(project_kernel, blocks), out_shape=[pltp...  9.92 us
    ppermute x1, starting transfers between devices, local(): lax.ppermute(facts, ('dp', 'seq'), [(flat(c, s), flat(*home(c, s))) for c...  6.1 us
    pallas_call x1, Pallas kernels, place_weights(): pl.pallas_call(functools.partial(place_kernel, share), out_shape=[pltpu.H...  5.07 us
    pallas_call x1, Pallas kernels, output(): pl.pallas_call(functools.partial(output_kernel, layers), out_shape=jax.Sh...  4.77 us
  transfers between devices with their start and end apart: 21, of which 4 were waited for; matrix products, arithmetic and copies ran while one was open for 2% of the time, Pallas kernels for 28%

profile of v5, /device:TPU:1, one launch (start us, length us, event | category | flops | bytes accessed | tf_op | source)
XLA Modules:
  0.0 121.1 jit_solution(315327573169419548)
XLA Ops:
  0.0 3.1 %bundle.1 = (bf16[768,1536]{1,0:T(8,128)(2,1)}, bf16[96,768]{1,0:T(8,128)(2,1)}) custom-call(s32[1]{0:T(128)} %bitcast.10.place_ref, bf16[768,384]{1,0:T(8,128)(2,1)} %query_ref.1, bf16[768,384]{1,0:T(8,128)(2,1)} %key_ref.1, bf16[768,384]{1,0:T(8,128)(2,1)} %value_ref.1, bf16[384,768]{1,0:T(8,128)(2,1)} %own_ref.1), custom_call_target="tpu_custom_call" | custom-call | flops 1 | bytes 1 | tf_op jit(solution)/shard_map/bundle/pallas_call | solution.py:72
  3.2 0.1 collective-permute-start
  3.3 2.8 %collective-permute-start.5 = (bf16[96,768]{1,0:T(8,128)(2,1)}, bf16[96,768]{1,0:T(8,128)(2,1)S(1)}, u32[]{:S(2)}, u32[]{:S(2)}) collective-permute-start(bf16[96,768]{1,0:T(8,128)(2,1)} %get-tuple-element.36.refs_0_), channel_id=1, source_target_pairs={{0,1},{1,0},{2,3},{3,2},{4,5},{5,4},{6,7},{7,6},{8,9},{9,8},{10,11... | collective-permute-start | bytes 442376 | tf_op jit(solution)/shard_map/ppermute | solution.py:498
  6.0 1.3 %collective-permute-start.3 = (bf16[192,1536]{1,0:T(8,128)(2,1)}, bf16[192,1536]{1,0:T(8,128)(2,1)S(1)}, u32[]{:S(2)}, u32[]{:S(2)}) collective-permute-start(bf16[192,1536]{1,0:T(8,128)(2,1)} %bitcast.11), channel_id=1, source_target_pairs={{0,1},{1,3},{2,0},{3,2},{4,17},{5,19},{6,16},{7,18},{8,9},{9,11},{... | collective-permute-start | bytes 1769480 | tf_op jit(solution)/shard_map/ppermute | solution.py:462
  7.4 3.0 %collective-permute-done.5.refs_1_.refs_0_ = bf16[96,768]{1,0:T(8,128)(2,1)S(1)} collective-permute-done((bf16[96,768]{1,0:T(8,128)(2,1)}, bf16[96,768]{1,0:T(8,128)(2,1)S(1)}, u32[]{:S(2)}, u32[]{:S(2)}) %collective-permute-start.5) | collective-permute-done | bytes 147488 | tf_op jit(solution)/shard_map/ppermute | solution.py:498
  10.4 0.9 copy-done.3
  11.3 1.1 join.3
  12.4 0.0 copy-start.5
  12.4 0.0 copy-start.4
  12.4 14.1 %collective-permute-start.6 = (bf16[192,768]{1,0:T(8,128)(2,1)}, bf16[192,768]{1,0:T(8,128)(2,1)S(1)}, u32[]{:S(2)}, u32[]{:S(2)}) collective-permute-start(bf16[192,768]{1,0:T(8,128)(2,1)} %join.3), channel_id=1, source_target_pairs={{0,2},{1,3},{2,0},{3,1},{4,6},{5,7},{6,4},{7,5},{8,10},{9,11},{10,... | collective-permute-start | bytes 884744 | tf_op jit(solution)/shard_map/ppermute | solution.py:498
  26.5 0.0 collective-permute-done.3.refs_1_
  26.5 2.2 %collective-permute-start.4 = (bf16[192,1536]{1,0:T(8,128)(2,1)S(1)}, bf16[192,1536]{1,0:T(8,128)(2,1)}, u32[]{:S(2)}, u32[]{:S(2)}) collective-permute-start(bf16[192,1536]{1,0:T(8,128)(2,1)S(1)} %collective-permute-done.3.refs_1_), channel_id=1, source_target_pairs={{0,1},{1,3},{2,0},{3,2},{4,5},{5,7},{6,4},{7,6},{8,9},{9,11},{10,8... | collective-permute-start | bytes 1769480 | tf_op jit(solution)/shard_map/ppermute | solution.py:485
  28.7 10.7 %collective-permute-done.6.refs_1_ = bf16[192,768]{1,0:T(8,128)(2,1)S(1)} collective-permute-done((bf16[192,768]{1,0:T(8,128)(2,1)}, bf16[192,768]{1,0:T(8,128)(2,1)S(1)}, u32[]{:S(2)}, u32[]{:S(2)}) %collective-permute-start.6) | collective-permute-done | bytes 294944 | tf_op jit(solution)/shard_map/ppermute | solution.py:498
  39.4 1.0 join.4.refs_0_
  40.4 2.4 %collective-permute-start.7 = (bf16[288,768]{1,0:T(8,128)(2,1)}, bf16[288,768]{1,0:T(8,128)(2,1)S(1)}, u32[]{:S(2)}, u32[]{:S(2)}) collective-permute-start(bf16[288,768]{1,0:T(8,128)(2,1)} %join.4.refs_0_), channel_id=1, source_target_pairs={{0,4},{4,0},{8,12},{12,8},{1,5},{5,1},{9,13},{13,9},{2,6},{6,2},{1... | collective-permute-start | bytes 1327112 | tf_op jit(solution)/shard_map/ppermute | solution.py:472
  42.8 1.2 %collective-permute-start.8 = (bf16[288,768]{1,0:T(8,128)(2,1)}, bf16[288,768]{1,0:T(8,128)(2,1)S(1)}, u32[]{:S(2)}, u32[]{:S(2)}) collective-permute-start(bf16[288,768]{1,0:T(8,128)(2,1)} %join.4.refs_0_), channel_id=1, source_target_pairs={{0,8},{4,12},{8,0},{12,4},{1,9},{5,13},{9,1},{13,5},{2,10},{6,14},... | collective-permute-start | bytes 1327112 | tf_op jit(solution)/shard_map/ppermute | solution.py:472
  44.0 5.2 %collective-permute-start.1 = (bf16[192,1536]{1,0:T(8,128)(2,1)}, bf16[192,1536]{1,0:T(8,128)(2,1)}, u32[]{:S(2)}, u32[]{:S(2)}) collective-permute-start(bf16[192,1536]{1,0:T(8,128)(2,1)} %bitcast.11), channel_id=1, source_target_pairs={{0,0},{1,1},{2,2},{3,3},{4,16},{5,17},{6,18},{7,19},{8,8},{9,9},{1... | collective-permute-start | bytes 1769480 | tf_op jit(solution)/shard_map/ppermute | solution.py:462
  49.3 2.9 %collective-permute-done.4.refs_2_ = bf16[192,1536]{1,0:T(8,128)(2,1)} collective-permute-done((bf16[192,1536]{1,0:T(8,128)(2,1)S(1)}, bf16[192,1536]{1,0:T(8,128)(2,1)}, u32[]{:S(2)}, u32[]{:S(2)}) %collective-permute-start.4) | collective-permute-done | bytes 589856 | tf_op jit(solution)/shard_map/ppermute | solution.py:485
  52.1 1.4 %collective-permute-start.11 = (bf16[192,1536]{1,0:T(8,128)(2,1)}, bf16[192,1536]{1,0:T(8,128)(2,1)}, u32[]{:S(2)}, u32[]{:S(2)}) collective-permute-start(bf16[192,1536]{1,0:T(8,128)(2,1)} %collective-permute-done.4.refs_2_), channel_id=1, source_target_pairs={{0,1},{1,3},{2,0},{3,2},{4,5},{5,7},{6,4},{7,6},{8,9},{9,11},{10,8... | collective-permute-start | bytes 1769480 | tf_op jit(solution)/shard_map/ppermute | solution.py:485
  54.2 0.0 collective-permute-done.7.refs_1_
  54.2 6.1 %collective-permute-start.2 = (s32[7,12]{1,0:T(8,128)S(1)}, s32[7,12]{1,0:T(8,128)S(1)}, u32[]{:S(2)}, u32[]{:S(2)}) collective-permute-start(s32[7,12]{1,0:T(8,128)S(1)} %concatenate.3), channel_id=1, source_target_pairs={{0,0},{4,16},{8,8},{12,24},{16,4},{20,20},{24,12},{28,28},{1,1},{5... | collective-permute-start | bytes 1016 | tf_op jit(solution)/shard_map/ppermute | solution.py:494
  60.4 0.7 slice.17
  61.1 0.0 collective-permute-done.8.refs_2_
  61.1 1.4 %collective-permute-start.10 = (bf16[144,768]{1,0:T(8,128)(2,1)}, bf16[144,768]{1,0:T(8,128)(2,1)S(1)}, u32[]{:S(2)}, u32[]{:S(2)}) collective-permute-start(bf16[144,768]{1,0:T(8,128)(2,1)} %slice.17), channel_id=1, source_target_pairs={{0,8},{4,12},{8,0},{12,4},{1,9},{5,13},{9,1},{13,5},{2,10},{6,14},... | collective-permute-start | bytes 663560 | tf_op jit(solution)/shard_map/ppermute | solution.py:476
  62.5 0.7 slice.16
  63.2 0.0 collective-permute-done.2
  63.2 0.0 collective-permute-start.9
  63.2 0.0 collective-permute-done.1.refs_0_
  63.2 0.0 collective-permute-done.far_ref
  63.2 0.0 copy-start.1
  63.3 1.1 copy-done.1
  64.3 6.3 %project.2 = (bf16[576,384]{1,0:T(8,128)(2,1)}, bf16[576,768]{1,0:T(8,128)(2,1)}) custom-call(s32[1]{0:T(128)} %bitcast.4.place_ref, f32[1,1536]{1,0:T(1,128)S(1)} %broadcast_in_dim.4.gain_ref, bf16[768,1536]{1,0:T(8,128)(2,1)} %get-tuple-element.33.own_ref, bf16[768,1536]{1,0:T(8,128)(2,1)S(1)} %collective-permute-done.far_ref, ...), custom_call_target="tpu_custom_call" | custom-call | flops 1 | bytes 1 | tf_op jit(solution)/shard_map/project/pallas_call | solution.py:157
  70.6 0.7 collective-permute-start.12
  71.4 3.1 %collective-permute-start.14 = (bf16[576,768]{1,0:T(8,128)(2,1)}, bf16[576,768]{1,0:T(8,128)(2,1)}, u32[]{:S(2)}, u32[]{:S(2)}) collective-permute-start(bf16[576,768]{1,0:T(8,128)(2,1)} %get-tuple-element.44.refs_2_), channel_id=1, source_target_pairs={{16,8},{20,12},{8,16},{12,20},{17,9},{21,13},{9,17},{13,21},{18,10... | collective-permute-start | bytes 2654216 | tf_op jit(solution)/shard_map/ppermute | solution.py:506
  74.4 0.0 collective-permute-done.10.refs_4_
  74.5 0.0 collective-permute-done.9.refs_3_
  74.5 2.5 %join.5.pieces_ref = bf16[1152,768]{1,0:T(8,128)(2,1)} custom-call(bf16[288,768]{1,0:T(8,128)(2,1)S(1)} %copy-done.2, bf16[288,768]{1,0:T(8,128)(2,1)S(1)} %collective-permute-done.7.refs_1_, bf16[288,768]{1,0:T(8,128)(2,1)S(1)} %collective-permute-done.8.refs_2_, bf16[144,768]{1,0:T(8,128)(2,1)} %collective-permute-done.9.refs_3_, ...), custom_call_target="tpu_custom_call" | custom-call | flops 1 | bytes 1 | tf_op jit(solution)/shard_map/join/pallas_call | solution.py:101
  77.0 0.1 collective-permute-start.16
  77.1 0.0 collective-permute-done.11.refs_0_
  77.1 3.6 %project.3 = (bf16[192,384]{1,0:T(8,128)(2,1)}, bf16[192,768]{1,0:T(8,128)(2,1)}) custom-call(s32[1]{0:T(128)} %bitcast.4.place_ref, f32[1,1536]{1,0:T(1,128)S(1)} %broadcast_in_dim.4.gain_ref, bf16[768,1536]{1,0:T(8,128)(2,1)} %get-tuple-element.33.own_ref, bf16[768,1536]{1,0:T(8,128)(2,1)S(1)} %collective-permute-done.far_ref, ...), custom_call_target="tpu_custom_call" | custom-call | flops 8589934592 | bytes 1 | tf_op jit(solution)/shard_map/project/pallas_call | solution.py:157
  80.8 0.6 collective-permute-start.13
  81.3 2.6 %collective-permute-start.15 = (bf16[192,768]{1,0:T(8,128)(2,1)}, bf16[192,768]{1,0:T(8,128)(2,1)S(1)}, u32[]{:S(2)}, u32[]{:S(2)}) collective-permute-start(bf16[192,768]{1,0:T(8,128)(2,1)} %get-tuple-element.45.refs_3_), channel_id=1, source_target_pairs={{16,8},{20,12},{8,16},{12,20},{17,9},{21,13},{9,17},{13,21},{18,10... | collective-permute-start | bytes 884744 | tf_op jit(solution)/shard_map/ppermute | solution.py:508
  84.0 0.1 stack.88.place_ref
  84.1 0.1 pad_add_fusion.place_ref
  84.2 0.1 add_add_fusion
  84.3 0.5 slice.14
  84.8 0.7 stack.94.place_ref
  85.5 0.0 collective-permute-done.13.refs_5_
  85.5 4.0 %collective-permute-done.15.refs_7_ = bf16[192,768]{1,0:T(8,128)(2,1)S(1)} collective-permute-done((bf16[192,768]{1,0:T(8,128)(2,1)}, bf16[192,768]{1,0:T(8,128)(2,1)S(1)}, u32[]{:S(2)}, u32[]{:S(2)}) %collective-permute-start.15) | collective-permute-done | bytes 294944 | tf_op jit(solution)/shard_map/ppermute | solution.py:508
  89.5 0.0 collective-permute-done.12.refs_4_
  89.5 0.0 collective-permute-done.14.refs_6_
  89.5 3.2 %window.1 = (bf16[768,384]{1,0:T(8,128)(2,1)S(1)}, bf16[2304,768]{1,0:T(8,128)(2,1)S(1)}, bf16[3,18,128,128]{3,2,1,0:T(8,128)(2,1)S(1)}) custom-call(s32[8]{0:T(128)S(1)} %stack.94.place_ref, bf16[576,384]{1,0:T(8,128)(2,1)} %get-tuple-element.35.refs_0_, bf16[192,384]{1,0:T(8,128)(2,1)} %get-tuple-element.43.refs_1_, ...), custom_call_target="tpu_custom_call" | custom-call | bytes 8257536 | tf_op jit(solution)/shard_map/window/pallas_call | solution.py:208
  92.7 5.5 %attend.2 = (bf16[192,384]{1,0:T(8,128)(2,1)}, bf16[192,384]{1,0:T(8,128)(2,1)}) custom-call(s32[8]{0:T(128)S(1)} %stack.94.place_ref, s32[6,12]{1,0:T(8,128)S(1)} %bitcast.27, s32[3]{0:T(128)S(1)} %get-tuple-element.62.turn_ref, bf16[768,384]{1,0:T(8,128)(2,1)S(1)} %get-tuple-element.50.q_all, bf16[2304,768]{1,0:T(8,128)(2,1)S(1)} %get-tuple-element.47.kv_all, ...), custom_call_target="tpu_custom_call" | custom-call | flops 4294967296 | bytes 1048576 | tf_op jit(solution)/shard_map/attend/pallas_call | solution.py:320
  98.3 0.1 collective-permute-start.17
  98.4 4.1 %collective-permute-start.18 = (bf16[192,384]{1,0:T(8,128)(2,1)}, bf16[192,384]{1,0:T(8,128)(2,1)S(1)}, u32[]{:S(2)}, u32[]{:S(2)}) collective-permute-start(bf16[192,384]{1,0:T(8,128)(2,1)} %get-tuple-element.55), channel_id=1, source_target_pairs={{0,3},{1,2},{2,1},{3,0},{4,19},{5,18},{6,17},{7,16},{8,11},{9,10},... | collective-permute-start | bytes 442376 | tf_op jit(solution)/shard_map/ppermute | solution.py:462
  102.5 5.4 %attend.3 = (bf16[192,384]{1,0:T(8,128)(2,1)}, bf16[192,384]{1,0:T(8,128)(2,1)}) custom-call(s32[8]{0:T(128)S(1)} %stack.94.place_ref, s32[6,12]{1,0:T(8,128)S(1)} %bitcast.28, s32[3]{0:T(128)S(1)} %get-tuple-element.61.turn_ref, bf16[768,384]{1,0:T(8,128)(2,1)S(1)} %get-tuple-element.50.q_all, bf16[2304,768]{1,0:T(8,128)(2,1)S(1)} %get-tuple-element.47.kv_all, ...), custom_call_target="tpu_custom_call" | custom-call | flops 4294967296 | bytes 1048576 | tf_op jit(solution)/shard_map/attend/pallas_call | solution.py:320
  107.9 0.1 collective-permute-start.20
  108.0 0.0 collective-permute-done.16.theirs_ref
  108.0 3.0 %collective-permute-start.19 = (bf16[192,384]{1,0:T(8,128)(2,1)}, bf16[192,384]{1,0:T(8,128)(2,1)S(1)}, u32[]{:S(2)}, u32[]{:S(2)}) collective-permute-start(bf16[192,384]{1,0:T(8,128)(2,1)} %get-tuple-element.59), channel_id=1, source_target_pairs={{0,0},{1,1},{2,2},{3,3},{4,16},{5,17},{6,18},{7,19},{8,8},{9,9},{1... | collective-permute-start | bytes 442376 | tf_op jit(solution)/shard_map/ppermute | solution.py:462
  111.0 5.1 %place.1 = (bf16[4,2,384,768]{3,2,1,0:T(8,128)(2,1)}, f32[8,128]{1,0:T(8,128)S(1)}) custom-call(s32[6]{0:T(128)S(1)} %stack.88.place_ref, bf16[384,768]{1,0:T(8,128)(2,1)} %own_ref.1, bf16[768,1536]{1,0:T(8,128)(2,1)S(1)} %collective-permute-done.far_ref, bf16[1152,768]{1,0:T(8,128)(2,1)} %join.5.pieces_ref, bf16[1152,768]{1,0:T(8,128)(2,1)} %collective-permute-done.16.theirs_ref), custom_call_target="tpu_custom_call" | custom-call | flops 1 | bytes 1 | tf_op jit(solution)/shard_map/place/pallas_call | solution.py:365
  116.1 0.0 collective-permute-done.17.refs_0_
  116.1 0.0 collective-permute-done.18.refs_1_
  116.1 0.0 collective-permute-done.19.refs_2_
  116.1 4.8 %output.1 = bf16[1,192,1536]{2,1,0:T(8,128)(2,1)} custom-call(s32[4]{0:T(128)S(1)} %pad_add_fusion.place_ref, bf16[4,2,384,768]{3,2,1,0:T(8,128)(2,1)} %get-tuple-element.53.weight_ref, bf16[192,384]{1,0:T(8,128)(2,1)S(1)} %get-tuple-element.57.refs_0_, bf16[192,384]{1,0:T(8,128)(2,1)S(1)} %get-tuple-element.58.refs_1_, ...), custom_call_target="tpu_custom_call" | custom-call | flops 1 | bytes 1 | tf_op jit(solution)/shard_map/output/pallas_call | solution.py:406
  (12 shorter events, 0.0 us)
Async XLA Ops:
  3.2 60.1 %collective-permute-start = (bf16[768,1536]{1,0:T(8,128)(2,1)}, bf16[768,1536]{1,0:T(8,128)(2,1)S(1)}, u32[]{:S(2)}, u32[]{:S(2)}) collective-permute-start(bf16[768,1536]{1,0:T(8,128)(2,1)} %get-tuple-element.33.own_ref), channel_id=1, source_target_pairs={{0,16},{16,0},{1,17},{17,1},{2,18},{18,2},{3,19},{19,3},{4,20},{20... | collective-permute-start | bytes 7077896 | tf_op jit(solution)/shard_map/ppermute | solution.py:491
  3.3 7.1 %collective-permute-start.5 = (bf16[96,768]{1,0:T(8,128)(2,1)}, bf16[96,768]{1,0:T(8,128)(2,1)S(1)}, u32[]{:S(2)}, u32[]{:S(2)}) collective-permute-start(bf16[96,768]{1,0:T(8,128)(2,1)} %get-tuple-element.36.refs_0_), channel_id=1, source_target_pairs={{0,1},{1,0},{2,3},{3,2},{4,5},{5,4},{6,7},{7,6},{8,9},{9,8},{10,11... | collective-permute-start | bytes 442376 | tf_op jit(solution)/shard_map/ppermute | solution.py:498
  6.0 20.5 %collective-permute-start.3 = (bf16[192,1536]{1,0:T(8,128)(2,1)}, bf16[192,1536]{1,0:T(8,128)(2,1)S(1)}, u32[]{:S(2)}, u32[]{:S(2)}) collective-permute-start(bf16[192,1536]{1,0:T(8,128)(2,1)} %bitcast.11), channel_id=1, source_target_pairs={{0,1},{1,3},{2,0},{3,2},{4,17},{5,19},{6,16},{7,18},{8,9},{9,11},{... | collective-permute-start | bytes 1769480 | tf_op jit(solution)/shard_map/ppermute | solution.py:462
  10.4 0.9 copy-start.3
  12.4 41.2 %copy-start.5 = (s32[1,6,12]{2,0,1:T(1,128)S(1)}, s32[1,6,12]{2,0,1:T(1,128)}, u32[]{:S(2)}) copy-start(s32[1,6,12]{2,0,1:T(1,128)} %param.14) | copy-start | bytes 868
  12.4 50.8 %copy-start.4 = (f32[1536]{0:T(1024)S(1)}, f32[1536]{0:T(1024)}, u32[]{:S(2)}) copy-start(f32[1536]{0:T(1024)} %param.9) | copy-start | bytes 18436
  12.4 27.0 %collective-permute-start.6 = (bf16[192,768]{1,0:T(8,128)(2,1)}, bf16[192,768]{1,0:T(8,128)(2,1)S(1)}, u32[]{:S(2)}, u32[]{:S(2)}) collective-permute-start(bf16[192,768]{1,0:T(8,128)(2,1)} %join.3), channel_id=1, source_target_pairs={{0,2},{1,3},{2,0},{3,1},{4,6},{5,7},{6,4},{7,5},{8,10},{9,11},{10,... | collective-permute-start | bytes 884744 | tf_op jit(solution)/shard_map/ppermute | solution.py:498
  26.5 13.9 %copy-start = (bf16[192,1536]{1,0:T(8,128)(2,1)}, bf16[192,1536]{1,0:T(8,128)(2,1)S(1)}, u32[]{:S(2)}) copy-start(bf16[192,1536]{1,0:T(8,128)(2,1)S(1)} %collective-permute-done.3.refs_1_) | copy-start | bytes 1769476
  26.5 25.6 %collective-permute-start.4 = (bf16[192,1536]{1,0:T(8,128)(2,1)S(1)}, bf16[192,1536]{1,0:T(8,128)(2,1)}, u32[]{:S(2)}, u32[]{:S(2)}) collective-permute-start(bf16[192,1536]{1,0:T(8,128)(2,1)S(1)} %collective-permute-done.3.refs_1_), channel_id=1, source_target_pairs={{0,1},{1,3},{2,0},{3,2},{4,5},{5,7},{6,4},{7,6},{8,9},{9,11},{10,8... | collective-permute-start | bytes 1769480 | tf_op jit(solution)/shard_map/ppermute | solution.py:485
  40.4 13.8 %collective-permute-start.7 = (bf16[288,768]{1,0:T(8,128)(2,1)}, bf16[288,768]{1,0:T(8,128)(2,1)S(1)}, u32[]{:S(2)}, u32[]{:S(2)}) collective-permute-start(bf16[288,768]{1,0:T(8,128)(2,1)} %join.4.refs_0_), channel_id=1, source_target_pairs={{0,4},{4,0},{8,12},{12,8},{1,5},{5,1},{9,13},{13,9},{2,6},{6,2},{1... | collective-permute-start | bytes 1327112 | tf_op jit(solution)/shard_map/ppermute | solution.py:472
  42.8 18.3 %collective-permute-start.8 = (bf16[288,768]{1,0:T(8,128)(2,1)}, bf16[288,768]{1,0:T(8,128)(2,1)S(1)}, u32[]{:S(2)}, u32[]{:S(2)}) collective-permute-start(bf16[288,768]{1,0:T(8,128)(2,1)} %join.4.refs_0_), channel_id=1, source_target_pairs={{0,8},{4,12},{8,0},{12,4},{1,9},{5,13},{9,1},{13,5},{2,10},{6,14},... | collective-permute-start | bytes 1327112 | tf_op jit(solution)/shard_map/ppermute | solution.py:472
  44.0 19.2 %collective-permute-start.1 = (bf16[192,1536]{1,0:T(8,128)(2,1)}, bf16[192,1536]{1,0:T(8,128)(2,1)}, u32[]{:S(2)}, u32[]{:S(2)}) collective-permute-start(bf16[192,1536]{1,0:T(8,128)(2,1)} %bitcast.11), channel_id=1, source_target_pairs={{0,0},{1,1},{2,2},{3,3},{4,16},{5,17},{6,18},{7,19},{8,8},{9,9},{1... | collective-permute-start | bytes 1769480 | tf_op jit(solution)/shard_map/ppermute | solution.py:462
  52.1 25.0 %collective-permute-start.11 = (bf16[192,1536]{1,0:T(8,128)(2,1)}, bf16[192,1536]{1,0:T(8,128)(2,1)}, u32[]{:S(2)}, u32[]{:S(2)}) collective-permute-start(bf16[192,1536]{1,0:T(8,128)(2,1)} %collective-permute-done.4.refs_2_), channel_id=1, source_target_pairs={{0,1},{1,3},{2,0},{3,2},{4,5},{5,7},{6,4},{7,6},{8,9},{9,11},{10,8... | collective-permute-start | bytes 1769480 | tf_op jit(solution)/shard_map/ppermute | solution.py:485
  54.2 8.9 %collective-permute-start.2 = (s32[7,12]{1,0:T(8,128)S(1)}, s32[7,12]{1,0:T(8,128)S(1)}, u32[]{:S(2)}, u32[]{:S(2)}) collective-permute-start(s32[7,12]{1,0:T(8,128)S(1)} %concatenate.3), channel_id=1, source_target_pairs={{0,0},{4,16},{8,8},{12,24},{16,4},{20,20},{24,12},{28,28},{1,1},{5... | collective-permute-start | bytes 1016 | tf_op jit(solution)/shard_map/ppermute | solution.py:494
  61.1 13.4 %collective-permute-start.10 = (bf16[144,768]{1,0:T(8,128)(2,1)}, bf16[144,768]{1,0:T(8,128)(2,1)S(1)}, u32[]{:S(2)}, u32[]{:S(2)}) collective-permute-start(bf16[144,768]{1,0:T(8,128)(2,1)} %slice.17), channel_id=1, source_target_pairs={{0,8},{4,12},{8,0},{12,4},{1,9},{5,13},{9,1},{13,5},{2,10},{6,14},... | collective-permute-start | bytes 663560 | tf_op jit(solution)/shard_map/ppermute | solution.py:476
  63.2 11.3 %collective-permute-start.9 = (bf16[144,768]{1,0:T(8,128)(2,1)}, bf16[144,768]{1,0:T(8,128)(2,1)}, u32[]{:S(2)}, u32[]{:S(2)}) collective-permute-start(bf16[144,768]{1,0:T(8,128)(2,1)} %slice.16), channel_id=1, source_target_pairs={{0,4},{4,0},{8,12},{12,8},{1,5},{5,1},{9,13},{13,9},{2,6},{6,2},{1... | collective-permute-start | bytes 663560 | tf_op jit(solution)/shard_map/ppermute | solution.py:476
  63.2 1.1 copy-start.1
  64.3 10.2 %copy-start.2 = (bf16[288,768]{1,0:T(8,128)(2,1)S(1)}, bf16[288,768]{1,0:T(8,128)(2,1)}, u32[]{:S(2)}) copy-start(bf16[288,768]{1,0:T(8,128)(2,1)} %join.4.refs_0_) | copy-start | bytes 1327108
  70.6 18.9 %collective-permute-start.12 = (bf16[576,768]{1,0:T(8,128)(2,1)}, bf16[576,768]{1,0:T(8,128)(2,1)}, u32[]{:S(2)}, u32[]{:S(2)}) collective-permute-start(bf16[576,768]{1,0:T(8,128)(2,1)} %get-tuple-element.44.refs_2_), channel_id=1, source_target_pairs={{0,16},{16,0},{1,17},{17,1},{2,18},{18,2},{3,19},{19,3},{4,20},{20... | collective-permute-start | bytes 2654216 | tf_op jit(solution)/shard_map/ppermute | solution.py:506
  71.4 18.2 %collective-permute-start.14 = (bf16[576,768]{1,0:T(8,128)(2,1)}, bf16[576,768]{1,0:T(8,128)(2,1)}, u32[]{:S(2)}, u32[]{:S(2)}) collective-permute-start(bf16[576,768]{1,0:T(8,128)(2,1)} %get-tuple-element.44.refs_2_), channel_id=1, source_target_pairs={{16,8},{20,12},{8,16},{12,20},{17,9},{21,13},{9,17},{13,21},{18,10... | collective-permute-start | bytes 2654216 | tf_op jit(solution)/shard_map/ppermute | solution.py:506
  77.0 30.9 %collective-permute-start.16 = (bf16[1152,768]{1,0:T(8,128)(2,1)}, bf16[1152,768]{1,0:T(8,128)(2,1)}, u32[]{:S(2)}, u32[]{:S(2)}) collective-permute-start(bf16[1152,768]{1,0:T(8,128)(2,1)} %join.5.pieces_ref), channel_id=1, source_target_pairs={{0,16},{16,0},{1,17},{17,1},{2,18},{18,2},{3,19},{19,3},{4,20},{20... | collective-permute-start | bytes 5308424 | tf_op jit(solution)/shard_map/ppermute | solution.py:511
  80.8 4.8 %collective-permute-start.13 = (bf16[192,768]{1,0:T(8,128)(2,1)}, bf16[192,768]{1,0:T(8,128)(2,1)S(1)}, u32[]{:S(2)}, u32[]{:S(2)}) collective-permute-start(bf16[192,768]{1,0:T(8,128)(2,1)} %get-tuple-element.45.refs_3_), channel_id=1, source_target_pairs={{0,16},{16,0},{1,17},{17,1},{2,18},{18,2},{3,19},{19,3},{4,20},{20... | collective-permute-start | bytes 884744 | tf_op jit(solution)/shard_map/ppermute | solution.py:508
  81.3 8.2 %collective-permute-start.15 = (bf16[192,768]{1,0:T(8,128)(2,1)}, bf16[192,768]{1,0:T(8,128)(2,1)S(1)}, u32[]{:S(2)}, u32[]{:S(2)}) collective-permute-start(bf16[192,768]{1,0:T(8,128)(2,1)} %get-tuple-element.45.refs_3_), channel_id=1, source_target_pairs={{16,8},{20,12},{8,16},{12,20},{17,9},{21,13},{9,17},{13,21},{18,10... | collective-permute-start | bytes 884744 | tf_op jit(solution)/shard_map/ppermute | solution.py:508
  98.3 17.8 %collective-permute-start.17 = (bf16[192,384]{1,0:T(8,128)(2,1)}, bf16[192,384]{1,0:T(8,128)(2,1)S(1)}, u32[]{:S(2)}, u32[]{:S(2)}) collective-permute-start(bf16[192,384]{1,0:T(8,128)(2,1)} %get-tuple-element.54), channel_id=1, source_target_pairs={{0,2},{1,3},{2,0},{3,1},{4,18},{5,19},{6,16},{7,17},{8,10},{9,11},... | collective-permute-start | bytes 442376 | tf_op jit(solution)/shard_map/ppermute | solution.py:462
  98.4 17.7 %collective-permute-start.18 = (bf16[192,384]{1,0:T(8,128)(2,1)}, bf16[192,384]{1,0:T(8,128)(2,1)S(1)}, u32[]{:S(2)}, u32[]{:S(2)}) collective-permute-start(bf16[192,384]{1,0:T(8,128)(2,1)} %get-tuple-element.55), channel_id=1, source_target_pairs={{0,3},{1,2},{2,1},{3,0},{4,19},{5,18},{6,17},{7,16},{8,11},{9,10},... | collective-permute-start | bytes 442376 | tf_op jit(solution)/shard_map/ppermute | solution.py:462
  107.9 8.2 %collective-permute-start.20 = (bf16[192,384]{1,0:T(8,128)(2,1)}, bf16[192,384]{1,0:T(8,128)(2,1)S(1)}, u32[]{:S(2)}, u32[]{:S(2)}) collective-permute-start(bf16[192,384]{1,0:T(8,128)(2,1)} %get-tuple-element.60), channel_id=1, source_target_pairs={{0,1},{1,0},{2,3},{3,2},{4,17},{5,16},{6,19},{7,18},{8,9},{9,8},{1... | collective-permute-start | bytes 442376 | tf_op jit(solution)/shard_map/ppermute | solution.py:462
  108.0 8.2 %collective-permute-start.19 = (bf16[192,384]{1,0:T(8,128)(2,1)}, bf16[192,384]{1,0:T(8,128)(2,1)S(1)}, u32[]{:S(2)}, u32[]{:S(2)}) collective-permute-start(bf16[192,384]{1,0:T(8,128)(2,1)} %get-tuple-element.59), channel_id=1, source_target_pairs={{0,0},{1,1},{2,2},{3,3},{4,16},{5,17},{6,18},{7,19},{8,8},{9,9},{1... | collective-permute-start | bytes 442376 | tf_op jit(solution)/shard_map/ppermute | solution.py:462

commit v6 on v5

--- a/solution.py
+++ b/solution.py
@@ -43,88 +43,124 @@
     return [pltpu.with_memory_space_constraint(value, pltpu.HBM) for value in values]
 
 
-def bundle_kernel(place_ref, query_ref, key_ref, value_ref, w_out_ref, all_ref, piece_ref, held, held_piece, sems):
-    depth, width = query_ref.shape
-    part = piece_ref.shape[0]
+def run_copies(loads, stores, sems):
+    for copy in copy_all(loads, sems):
+        copy.wait()
+    for copy in copy_all(stores, sems):
+        copy.wait()
+
+
+def pack_kernel(place_ref, rows_ref, w_out_ref, sent_ref, piece_ref, held, held_piece, sems):
+    count = rows_ref.shape[0]
+    part, columns = piece_ref.shape
     first = pl.multiple_of(place_ref[0] * part, 16)
-    pairs = [(w_out_ref.at[pl.ds(first, part), :], held_piece)]
-    for place, source in enumerate((query_ref, key_ref, value_ref)):
-        pairs.append((source, held.at[:, pl.ds(place * width, width)]))
-    rows = w_out_ref.shape[0]
+    loads = [(w_out_ref.at[pl.ds(first, part), :], held_piece), (rows_ref, held.at[pl.ds(0, count), :])]
     for side in range(2):
-        pairs.append((
+        loads.append((
+            w_out_ref.at[pl.ds(first + side * (part // 2), part // 2), :],
+            held.at[pl.ds(count, part // 2), pl.ds(side * columns, columns)],
+        ))
+    run_copies(loads, [(held, sent_ref), (held_piece, piece_ref)], sems)
+
+
+def pack(place, rows, w_out, share):
+    part = w_out.shape[0] // share
+    shapes = [(rows.shape[0] + part // 2, rows.shape[1]), (part, w_out.shape[1])]
+    return pl.pallas_call(
+        pack_kernel,
+        out_shape=[pltpu.HBM(shape, jnp.bfloat16) for shape in shapes],
+        in_specs=[SMEM] + [HBM] * 2,
+        out_specs=[HBM] * 2,
+        scratch_shapes=[pltpu.VMEM(shape, jnp.bfloat16) for shape in shapes] + [pltpu.SemaphoreType.DMA((4,))],
+        compiler_params=pltpu.CompilerParams(vmem_limit_bytes=4 * MIB),
+        cost_estimate=LIGHT,
+        name="pack",
+    )(place, *in_hbm(rows, w_out))
+
+
+def bundle_kernel(query_ref, key_ref, value_ref, w_out_ref, front_ref, back_ref, held, held_back, sems):
+    width, rows = query_ref.shape[1], w_out_ref.shape[0]
+    loads = [
+        (query_ref, held.at[:, pl.ds(0, width)]),
+        (key_ref, held.at[:, pl.ds(width, width)]),
+        (value_ref, held_back.at[:, pl.ds(0, width)]),
+    ]
+    for side in range(2):
+        loads.append((
             w_out_ref.at[:, pl.ds(side * width, width)],
-            held.at[pl.ds(side * rows, rows), pl.ds(3 * width, width)],
+            held_back.at[pl.ds(side * rows, rows), pl.ds(width, width)],
         ))
-    loads = copy_all(pairs, sems)
-    loads[0].wait()
-    stores = copy_all([(held_piece, piece_ref)], sems.at[pl.ds(len(pairs), 1)])
-    for load in loads[1:]:
-        load.wait()
-    stores += copy_all([(held, all_ref)], sems.at[pl.ds(len(pairs) + 1, 1)])
-    for store in stores:
-        store.wait()
-
-
-def bundle(place, w_query, w_key, w_value, w_out, share):
-    depth, width = w_query.shape
-    shapes = [(depth, 4 * width), (w_out.shape[0] // share, w_out.shape[1])]
+    run_copies(loads, [(held, front_ref), (held_back, back_ref)], sems)
+
+
+def bundle(w_query, w_key, w_value, w_out):
+    shape = (w_query.shape[0], 2 * w_query.shape[1])
     return pl.pallas_call(
         bundle_kernel,
-        out_shape=[pltpu.HBM(shape, jnp.bfloat16) for shape in shapes],
-        in_specs=[SMEM] + [HBM] * 4,
+        out_shape=[pltpu.HBM(shape, jnp.bfloat16)] * 2,
+        in_specs=[HBM] * 4,
         out_specs=[HBM] * 2,
-        scratch_shapes=[pltpu.VMEM(shape, jnp.bfloat16) for shape in shapes] + [pltpu.SemaphoreType.DMA((8,))],
+        scratch_shapes=[pltpu.VMEM(shape, jnp.bfloat16)] * 2 + [pltpu.SemaphoreType.DMA((5,))],
         compiler_params=pltpu.CompilerParams(vmem_limit_bytes=4 * MIB),
         cost_estimate=LIGHT,
         name="bundle",
-    )(place, *in_hbm(w_query, w_key, w_value, w_out))
-
-
-def join_kernel(*refs):
-    sources, (out, held, sems) = refs[:-3], refs[-3:]
-    spans, at = [], 0
-    for source in sources:
-        spans.append(pl.ds(at, source.shape[0]))
-        at += source.shape[0]
-    loads = copy_all([(source, held.at[span, :]) for source, span in zip(sources, spans)], sems)
-    stores = []
-    for place, (load, span) in enumerate(zip(loads, spans)):
-        load.wait()
-        stores += copy_all([(held.at[span, :], out.at[span, :])], sems.at[pl.ds(len(loads) + place, 1)])
-    for store in stores:
-        store.wait()
-
-
-def join(values, cost=1):
-    rows, columns = sum(value.shape[0] for value in values), values[0].shape[1]
-    return pl.pallas_call(
-        join_kernel,
-        out_shape=pltpu.HBM((rows, columns), jnp.bfloat16),
-        in_specs=[HBM] * len(values),
+    )(*in_hbm(w_query, w_key, w_value, w_out))
+
+
+def join_kernel(count, first_ref, second_ref, piece_ref, out_ref, held, sems):
+    part, columns = piece_ref.shape[0] // 2, piece_ref.shape[1]
+    loads = [
+        (source.at[pl.ds(count, part), :], held.at[pl.ds(place * part, part), :])
+        for place, source in enumerate((first_ref, second_ref))
+    ]
+    for side in range(2):
+        loads.append((
+            piece_ref.at[pl.ds(side * part, part), :],
+            held.at[pl.ds(2 * part, part), pl.ds(side * columns, columns)],
+        ))
+    run_copies(loads, [(held, out_ref)], sems)
+
+
+def join(count, first, second, piece):
+    shape = (3 * piece.shape[0] // 2, first.shape[1])
+    return pl.pallas_call(
+        functools.partial(join_kernel, count),
+        out_shape=pltpu.HBM(shape, jnp.bfloat16),
+        in_specs=[HBM] * 3,
         out_specs=HBM,
-        scratch_shapes=[
-            pltpu.VMEM((rows, columns), jnp.bfloat16), pltpu.SemaphoreType.DMA((2 * len(values),))
-        ],
+        scratch_shapes=[pltpu.VMEM(shape, jnp.bfloat16), pltpu.SemaphoreType.DMA((4,))],
         compiler_params=pltpu.CompilerParams(vmem_limit_bytes=4 * MIB),
-        cost_estimate=pl.CostEstimate(flops=cost, bytes_accessed=1, transcendentals=0),
+        cost_estimate=LIGHT,
         name="join",
-    )(*values)
-
-
-def project_kernel(blocks, place_ref, gain_ref, own_ref, far_ref, *refs):
-    rows = refs[:blocks]
-    query_ref, pair_ref, held, weight, query_held, pair_held, sems = refs[blocks:]
-    count, (depth, width) = rows[0].shape[0], (own_ref.shape[0], query_ref.shape[1])
+    )(first, second, piece)
+
+
+def project_kernel(blocks, joined, count, place_ref, gain_ref, own_front, own_back, far_front, far_back, *refs):
+    rows, sources = refs[:blocks], refs[blocks:blocks + joined]
+    refs = refs[blocks + joined:]
+    if joined:
+        query_ref, pair_ref, join_ref, held, weight, query_held, pair_held, join_held, sems = refs
+    else:
+        query_ref, pair_ref, held, weight, query_held, pair_held, sems = refs[-7:]
+    depth, width = own_front.shape[0], query_ref.shape[1]
+    to_rows = pl.ds(query_ref.shape[0] - blocks * count if len(refs) > 8 and not joined else 0, blocks * count)
     core = place_ref[0]
     order = (1, 2, 0)
-    loads = copy_all([(rows[i], held.at[pl.ds(i * count, count), :]) for i in range(blocks)], sems)
+    loads = copy_all(
+        [(rows[i].at[pl.ds(0, count), :], held.at[pl.ds(i * count, count), :]) for i in range(blocks)], sems
+    )
     fetches = []
     for place in order:
-        for source, owner in ((own_ref, core), (far_ref, 1 - core)):
+        for pair, owner in (((own_front, own_back), core), ((far_front, far_back), 1 - core)):
             to = weight.at[place, pl.ds(pl.multiple_of(owner * depth, 16), depth), :]
-            fetches.append((source.at[:, pl.ds(place * width, width)], to))
+            fetches.append((pair[place // 2].at[:, pl.ds(place % 2 * width, width)], to))
     fetches = copy_all(fetches, sems.at[pl.ds(blocks, len(fetches))])
+    parts, at = [], 0
+    for source in sources:
+        parts.append((source, join_held.at[pl.ds(at, source.shape[0]), :]))
+        at += source.shape[0]
+    used = blocks + len(fetches) + 3
+    parts = copy_all(parts, sems.at[pl.ds(used, max(1, joined))])
     gain = gain_ref[...]
     normalized = []
     for i in range(blocks):
@@ -142,34 +178,46 @@
         sem = sems.at[pl.ds(blocks + len(fetches) + place, 1)]
         if place == 0:
             query_held[...] = (got.astype(jnp.float32) * (HD ** -0.5)).astype(jnp.bfloat16)
-            stores += copy_all([(query_held, query_ref)], sem)
+            stores += copy_all([(query_held, query_ref.at[to_rows, :])], sem)
         else:
             part = pl.ds((place - 1) * width, width)
             pair_held[:, (place - 1) * width:place * width] = got
-            stores += copy_all([(pair_held.at[:, part], pair_ref.at[:, part])], sem)
+            stores += copy_all([(pair_held.at[:, part], pair_ref.at[to_rows, part])], sem)
+        if turn == 0 and joined:
+            for part in parts:
+                part.wait()
+            stores += copy_all([(join_held, join_ref)], sems.at[pl.ds(used + joined, 1)])
     for store in stores:
         store.wait()
 
 
-def project(place, rows, width, gain, own, far, cost):
-    blocks, (count, depth) = len(rows), rows[0].shape
+def project(place, rows, count, width, gain, own, far, cost, room=0, into=(), joined=()):
+    blocks, depth = len(rows), rows[0].shape[1]
     total = blocks * count
-    return pl.pallas_call(
-        functools.partial(project_kernel, blocks),
-        out_shape=[pltpu.HBM((total, width), jnp.bfloat16), pltpu.HBM((total, 2 * width), jnp.bfloat16)],
-        in_specs=[SMEM, VMEM] + [HBM] * (blocks + 2),
-        out_specs=[HBM, HBM],
-        scratch_shapes=[
-            pltpu.VMEM((total, depth), jnp.bfloat16),
-            pltpu.VMEM((3, depth, width), jnp.bfloat16),
-            pltpu.VMEM((total, width), jnp.bfloat16),
-            pltpu.VMEM((total, 2 * width), jnp.bfloat16),
-            pltpu.SemaphoreType.DMA((blocks + 9,)),
-        ],
+    full = into[0].shape[0] if into else total + room
+    out_shape = [pltpu.HBM((full, width), jnp.bfloat16), pltpu.HBM((full, 2 * width), jnp.bfloat16)]
+    scratch = [
+        pltpu.VMEM((total, depth), jnp.bfloat16),
+        pltpu.VMEM((3, depth, width), jnp.bfloat16),
+        pltpu.VMEM((total, width), jnp.bfloat16),
+        pltpu.VMEM((total, 2 * width), jnp.bfloat16),
+    ]
+    if joined:
+        shape = (sum(value.shape[0] for value in joined), joined[0].shape[1])
+        out_shape.append(pltpu.HBM(shape, jnp.bfloat16))
+        scratch.append(pltpu.VMEM(shape, jnp.bfloat16))
+    inputs = 6 + blocks + len(joined)
+    return pl.pallas_call(
+        functools.partial(project_kernel, blocks, len(joined), count),
+        out_shape=out_shape,
+        in_specs=[SMEM, VMEM] + [HBM] * (inputs - 2 + len(into)),
+        out_specs=[HBM] * len(out_shape),
+        scratch_shapes=scratch + [pltpu.SemaphoreType.DMA((blocks + 10 + max(1, len(joined)),))],
+        input_output_aliases={inputs + i: i for i in range(len(into))},
         compiler_params=pltpu.CompilerParams(vmem_limit_bytes=24 * MIB),
         cost_estimate=pl.CostEstimate(flops=cost, bytes_accessed=1, transcendentals=0),
         name="project",
-    )(place, gain, *in_hbm(own), far, *rows)
+    )(place, gain, *in_hbm(*own), *far, *rows, *joined, *in_hbm(*into))
 
 
 def window_kernel(shape, groups, place_ref, *refs):
@@ -221,7 +269,38 @@
     )(place, *in_hbm(*queries, *owns), *chip_side, *link_side)
 
 
-def attend_kernel(groups, reach, count_rows, place_ref, band_ref, turn_ref, q_all, kv_all, vt_all, *refs):
+def weight_copies(share, place_ref, own_ref, far_ref, pieces_ref, theirs_ref, weight_ref):
+    core, layer, seq = (place_ref[i] for i in range(3))
+    layers, _, depth, columns = weight_ref.shape
+    part = depth // share // 2
+    half = columns // 2
+    pairs = [(own_ref, weight_ref.at[layer, core])]
+    for side in range(2):
+        pairs.append((
+            far_ref.at[pl.ds(side * depth, depth), pl.ds(far_ref.shape[1] - half, half)],
+            weight_ref.at[layer, 1 - core, :, pl.ds(side * half, half)],
+        ))
+    for other in range(share):
+        there = seq ^ other
+        for source, holder in ((pieces_ref, core), (theirs_ref, 1 - core)):
+            at = lax.rem(there // 2 * 2 + holder, share) * 2 * part
+            for step in range(layers - 1):
+                row = (other * (layers - 1) + step) * part
+                for side in range(2):
+                    to = pl.ds(pl.multiple_of(at + side * part, 16), part)
+                    pairs.append((
+                        source.at[pl.ds(row, part), pl.ds(side * columns, columns)],
+                        weight_ref.at[place_ref[3 + step], lax.rem(there, 2), to, :],
+                    ))
+    return pairs
+
+
+def attend_kernel(groups, reach, count_rows, share, place_ref, band_ref, turn_ref, q_all, kv_all, vt_all, *refs):
+    loads = []
+    if share:
+        sources, refs = refs[:5], refs[5:]
+        weight, load_sems, refs = refs[-7], refs[-1], refs[:-7] + refs[-6:-1]
+        loads = copy_all(weight_copies(share, *sources, weight), load_sems)
     outs, (score, ctx, chosen, limits, sems) = refs[:-5], refs[-5:]
     pairs, rows = vt_all.shape[0], outs[0].shape[0]
     first_group, total, length = (place_ref[i] for i in range(1, 4))
@@ -308,96 +387,56 @@
     stores = copy_all(
         [(ctx.at[pl.ds(pl.multiple_of(turn_ref[1 + i], 64), rows), :], out) for i, out in enumerate(outs)], sems
     )
-    for store in stores:
-        store.wait()
-
-
-def attend(place, band, turn, outs, q_all, kv_all, vt_all):
+    for copy in stores + loads:
+        copy.wait()
+
+
+def attend(place, band, turn, outs, q_all, kv_all, vt_all, share=0, layers=0, parts=()):
     groups, reach = band.shape[0], band.shape[1] // 2
     pairs, block = vt_all.shape[0], q_all.shape[0]
     rows = block // (2 * outs)
     slots = 2 * reach + 2
-    return pl.pallas_call(
-        functools.partial(attend_kernel, groups, reach, block // 2),
-        out_shape=[pltpu.HBM((rows, pairs * LANES), jnp.bfloat16)] * outs,
-        in_specs=[SMEM, SMEM, SMEM] + [VMEM] * 3,
-        out_specs=[HBM] * outs,
-        scratch_shapes=[
-            pltpu.VMEM((pairs, slots * GROUP, 2 * GROUP), jnp.float32),
-            pltpu.VMEM((block // 2, pairs * LANES), jnp.bfloat16),
-            pltpu.SMEM((slots + 2,), jnp.int32),
-            pltpu.SMEM((1,), jnp.int32),
-            pltpu.SemaphoreType.DMA((outs,)),
-        ],
+    out_shape = [pltpu.HBM((rows, pairs * LANES), jnp.bfloat16)] * outs
+    scratch = [
+        pltpu.VMEM((pairs, slots * GROUP, 2 * GROUP), jnp.float32),
+        pltpu.VMEM((block // 2, pairs * LANES), jnp.bfloat16),
+        pltpu.SMEM((slots + 2,), jnp.int32),
+        pltpu.SMEM((1,), jnp.int32),
+        pltpu.SemaphoreType.DMA((outs,)),
+    ]
+    if parts:
+        depth, columns = parts[1].shape
+        out_shape.append(jax.ShapeDtypeStruct((layers, 2, depth, columns), jnp.bfloat16))
+        scratch.append(pltpu.SemaphoreType.DMA((3 + 4 * share * (layers - 1),)))
+        parts = [parts[0], *in_hbm(parts[1]), parts[2], *in_hbm(parts[3]), parts[4]]
+    return pl.pallas_call(
+        functools.partial(attend_kernel, groups, reach, block // 2, share),
+        out_shape=out_shape,
+        in_specs=[SMEM, SMEM, SMEM] + [VMEM] * 3 + ([SMEM] + [HBM] * 4 if parts else []),
+        out_specs=[HBM] * outs + ([VMEM] if parts else []),
+        scratch_shapes=scratch,
         compiler_params=pltpu.CompilerParams(vmem_limit_bytes=16 * MIB),
-        cost_estimate=pl.CostEstimate(flops=1 << 32, bytes_accessed=1 << 20, transcendentals=0),
+        cost_estimate=pl.CostEstimate(flops=1 << 34, bytes_accessed=1 << 20, transcendentals=0),
         name="attend",
-    )(place, band, turn, q_all, kv_all, vt_all)
-
-
-def place_kernel(share, place_ref, own_ref, far_ref, pieces_ref, theirs_ref, out_ref, mark_ref, held, sems):
-    mark_ref[...] = jnp.zeros_like(mark_ref)
-    core, layer, seq = (place_ref[i] for i in range(3))
-    layers, _, depth, columns = out_ref.shape
-    part = depth // share
-    half = columns // 2
-    pairs = [(own_ref, held.at[layer, core])]
-    for side in range(2):
-        pairs.append((
-            far_ref.at[pl.ds(side * depth, depth), pl.ds(far_ref.shape[1] - half, half)],
-            held.at[layer, 1 - core, :, pl.ds(side * half, half)],
-        ))
-    for other in range(share):
-        at = pl.ds(pl.multiple_of(lax.rem(seq ^ other, share) * part, 16), part)
-        for source, source_core in ((pieces_ref, core), (theirs_ref, 1 - core)):
-            for step in range(layers - 1):
-                row = (other * (layers - 1) + step) * part
-                pairs.append((source.at[pl.ds(row, part), :], held.at[place_ref[3 + step], source_core, at, :]))
-    for load in copy_all(pairs, sems):
-        load.wait()
-    store = pltpu.make_async_copy(held, out_ref, sems.at[len(pairs)])
-    store.start()
-    store.wait()
-
-
-def place_weights(place, share, layers, own, far, mine, theirs):
-    shape = (layers, 2) + own.shape
-    return pl.pallas_call(
-        functools.partial(place_kernel, share),
-        out_shape=[pltpu.HBM(shape, jnp.bfloat16), jax.ShapeDtypeStruct((8, LANES), jnp.float32)],
-        in_specs=[SMEM] + [HBM] * 4,
-        out_specs=[HBM, VMEM],
-        scratch_shapes=[
-            pltpu.VMEM(shape, jnp.bfloat16), pltpu.SemaphoreType.DMA((4 + 2 * share * (layers - 1),))
-        ],
-        compiler_params=pltpu.CompilerParams(vmem_limit_bytes=8 * MIB),
-        cost_estimate=LIGHT,
-        name="place",
-    )(place, *in_hbm(own), far, *in_hbm(mine), theirs)
-
-
-def output_kernel(layers, place_ref, weight_ref, *refs):
-    contexts, out_ref, held, weight, sems = refs[:layers], *refs[layers:]
+    )(place, band, turn, q_all, kv_all, vt_all, *parts)
+
+
+def output_kernel(layers, place_ref, weight, *refs):
+    contexts, out_ref, held, sems = refs[:layers], *refs[layers:]
     columns = weight.shape[3]
     rows = contexts[0].shape[0]
-    loads = []
-    for step in range(layers):
-        there = place_ref[step]
-        loads.append(copy_all(
-            [(contexts[step], held.at[pl.ds(step * rows, rows), :]), (weight_ref.at[there], weight.at[step])],
-            sems.at[pl.ds(2 * step, 2)],
-        ))
-    totals = [None, None]
-    for step in range(layers):
-        for load in loads[step]:
-            load.wait()
-        for side in range(2):
+    loads = copy_all([(contexts[step], held.at[pl.ds(step * rows, rows), :]) for step in range(layers)], sems)
+    for load in loads:
+        load.wait()
+    for side in range(2):
+        total = None
+        for step in range(layers):
             got = jnp.dot(
-                held[step * rows:(step + 1) * rows, :], weight[step, side], preferred_element_type=jnp.float32
+                held[step * rows:(step + 1) * rows, :], weight[place_ref[step], side],
+                preferred_element_type=jnp.float32,
             )
-            totals[side] = got if step == 0 else totals[side] + got
-    for side in range(2):
-        out_ref[0, :, side * columns:(side + 1) * columns] = totals[side].astype(jnp.bfloat16)
+            total = got if step == 0 else total + got
+        out_ref[0, :, side * columns:(side + 1) * columns] = total.astype(jnp.bfloat16)
 
 
 def output(place, weight, contexts):
@@ -406,24 +445,20 @@
     return pl.pallas_call(
         functools.partial(output_kernel, layers),
         out_shape=jax.ShapeDtypeStruct((1, rows, 2 * columns), jnp.bfloat16),
-        in_specs=[SMEM] + [HBM] * (1 + layers),
+        in_specs=[SMEM, VMEM] + [HBM] * layers,
         out_specs=VMEM,
-        scratch_shapes=[
-            pltpu.VMEM((layers * rows, width), jnp.bfloat16),
-            pltpu.VMEM(weight.shape, jnp.bfloat16),
-            pltpu.SemaphoreType.DMA((2 * layers,)),
-        ],
-        compiler_params=pltpu.CompilerParams(vmem_limit_bytes=16 * MIB),
+        scratch_shapes=[pltpu.VMEM((layers * rows, width), jnp.bfloat16), pltpu.SemaphoreType.DMA((layers,))],
+        compiler_params=pltpu.CompilerParams(vmem_limit_bytes=8 * MIB),
         cost_estimate=LIGHT,
         name="output",
-    )(place, *in_hbm(weight), *contexts)
+    )(place, weight, *contexts)
 
 
 def hold_kernel(*refs):
     del refs
 
 
-def hold(values):
+def hold(values, cost=1 << 34):
     return pl.pallas_call(
         hold_kernel,
         out_shape=[jax.ShapeDtypeStruct(value.shape, value.dtype) for value in values],
@@ -431,7 +466,7 @@
         out_specs=[HBM] * len(values),
         input_output_aliases={i: i for i in range(len(values))},
         compiler_params=pltpu.CompilerParams(vmem_limit_bytes=MIB),
-        cost_estimate=pl.CostEstimate(flops=1 << 34, bytes_accessed=1, transcendentals=0),
+        cost_estimate=pl.CostEstimate(flops=cost, bytes_accessed=1, transcendentals=0),
         name="hold",
     )(*values)
 
@@ -470,7 +505,7 @@
 
     def shared(value):
         near = [lax.ppermute(value, "seq", [(s, s ^ step) for s in range(seqs)]) for step in (1, 2)]
-        middle = value.shape[0] // 2
+        middle = (value.shape[0] // 2 + 15) // 16 * 16
         halves = (near[1][:middle], near[0][middle:])
         opposite = [
             lax.ppermute(half, "seq", [(s, s ^ step) for s in range(seqs)]) for half, step in zip(halves, (1, 2))
@@ -484,63 +519,62 @@
     def ringed(value):
         return lax.ppermute(value, "head", [(z, after[z]) for z in range(layers)])
 
-    first = moved(rows, lambda z: after[z])
+    sent, piece = pack(numbers(lax.rem(seq, share)), rows, w_out, share)
+    piece = moved(piece, lambda z: before[z])
+    first = moved(sent, lambda z: after[z])
     second = ringed(first)
-    third = ringed(second)
-    own, piece = bundle(numbers(lax.rem(seq, share)), w_query, w_key, w_value, w_out, share)
-    far = lax.ppermute(own, "dp", swap)
+    own = bundle(w_query, w_key, w_value, w_out)
     whole = moved(rows, lambda z: z)
     facts = jnp.concatenate([group_band[0], jnp.broadcast_to(lengths[:, None], (1, group_band.shape[2]))], axis=0)
     facts = lax.ppermute(facts, ("dp", "seq"), [(flat(c, s), flat(*home(c, s))) for c, s in here])
-    pieces, held = [], piece
-    step = 1
-    while step < layers:
-        pieces.append(lax.ppermute(held, "head", [(z, z ^ step) for z in range(layers)]))
-        held = join([held, pieces[-1]], 1 << 33) if 2 * step < layers else held
-        step *= 2
-    shares = shared(join(pieces, 1 << 32))
-    whole, facts = together(whole, facts)
-
-    core_at = numbers(core)
-    query_a, pair_a = project(core_at, [whole, first, second], width, gain, own, far, 1)
-    link_a, chip_a = lax.ppermute(pair_a, ("dp", "seq"), over_link), lax.ppermute(pair_a, "dp", swap)
-    query_c, pair_c = project(core_at, [third], width, gain, own, far, 1 << 33)
-    link_c, chip_c = lax.ppermute(pair_c, ("dp", "seq"), over_link), lax.ppermute(pair_c, "dp", swap)
-    _, *shares = together(query_a, *shares)
-    mine = join(shares)
-    theirs = lax.ppermute(mine, "dp", swap)
-
+    *own, facts = together(*own, facts)
+    far = [lax.ppermute(value, "dp", swap) for value in own]
     back = {z: before[z] for z in range(layers)}
     ids = [layer, lookup([back[z] for z in range(layers)], layer)]
     ids.append(lookup([back[back[z]] for z in range(layers)], layer))
     ids.append(lookup([after[z] for z in range(layers)], layer))
     place = numbers(core, (seq // 2 * 2 + core) * groups, groups * seqs, facts[groups, 0], *ids)
     band = facts[:groups]
+    piece, = hold([piece], 1 << 33)
+    whole, place, band, piece = together(whole, place, band, piece)
+
+    core_at = numbers(core)
+    done = project(core_at, [whole, first], count, width, gain, own, far, 1, room=count)
+    *done, second = together(*done, second)
+    third = ringed(second)
+    shares = shared(join(count, first, second, piece))
+    done = project(core_at, [second], count, width, gain, own, far, 1, into=done)
+    query_a, pair_a = done
+    link_a, chip_a = lax.ppermute(pair_a, ("dp", "seq"), over_link), lax.ppermute(pair_a, "dp", swap)
+    query_c, pair_c, mine = project(core_at, [third], count, width, gain, own, far, 1 << 33, joined=shares)
+    link_c, chip_c = lax.ppermute(pair_c, ("dp", "seq"), over_link), lax.ppermute(pair_c, "dp", swap)
+    theirs = lax.ppermute(mine, "dp", swap)
     q_all, kv_all, vt_all = window(
         place, groups, count, [query_a, query_c], [pair_a, pair_c], [chip_a, chip_c], [link_a, link_c]
     )
+
     half = layers // 2
     arrived, sources = [], []
     for near in (0, 1):
         side = layer // half if near else 1 - layer // half
         turn = numbers(side * half * count, *[lax.rem(layer + e, half) * count for e in range(half)])
-        contexts = list(attend(place, band, turn, half, q_all, kv_all, vt_all))
-        if not near:
+        if near:
+            weight_place = numbers(core, layer, seq, ids[1], ids[2], ids[3])
+            *contexts, weight = attend(
+                place, band, turn, half, q_all, kv_all, vt_all, share, layers,
+                [weight_place, w_out, far[1], mine, theirs],
+            )
+        else:
+            contexts = list(attend(place, band, turn, half, q_all, kv_all, vt_all))
             contexts[0], q_all = together(contexts[0], q_all)
-        if near:
-            contexts[0], theirs = together(contexts[0], theirs)
         for e, context in enumerate(contexts):
             def target(z, e=e):
                 return (z // half if near else 1 - z // half) * half + (z + e) % half
 
             arrived.append(moved(context, target))
             sources.append(side * half + lax.rem(layer + half - e, half))
-    weight, mark = place_weights(
-        numbers(core, layer, seq, *[layer ^ step for step in range(1, layers)]),
-        share, layers, w_out, far, mine, theirs,
-    )
-    *held, _ = hold(arrived[:half] + [mark])
-    return output(numbers(*sources), weight, held + arrived[half:])
+    arrived = list(hold(arrived[:half])) + arrived[half:]
+    return output(numbers(*sources), weight, arrived)
 
 
 def solution(mesh):

time: 122 us -> 118 us (0.967)
  waiting for transfers between devices: 20.6 us -> 38.8 us
  starting transfers between devices: 52.6 us -> 34.5 us
  Pallas kernels: 41.7 us -> 37 us
    ppermute x3 -> x2, starting transfers between devices: 16.9 us -> 0.51 us  [local(): far = [lax.ppermute(value, 'dp', swap) for value in own]]
    ppermute x6 -> x7, waiting for transfers between devices: 0.02 us -> 13.8 us  [moved(): return lax.ppermute(value, ('dp', 'seq', 'head'), pairs)]
    ppermute x3 -> x2, waiting for transfers between devices: 13.7 us -> 0.01 us  [local(): far = [lax.ppermute(value, 'dp', swap) for value in own]]
    ppermute x2, waiting for transfers between devices: 0.01 us -> 9.27 us  [shared(): lax.ppermute(value, 'seq', [(s, s ^ step) for s in range(seqs)])]
    ppermute x2, waiting for transfers between devices: 2.86 us -> 8.48 us  [ringed(): return lax.ppermute(value, 'head', [(z, after[z]) for z in range(layers)])]
    ppermute x1, starting transfers between devices: 6.1 us -> 1.91 us  [local(): lax.ppermute(facts, ('dp', 'seq'), [(flat(c, s), flat(*home(c, s))) for c...]
    ppermute x1, waiting for transfers between devices: 0.01 us -> 3.73 us  [local(): lax.ppermute(pair_a, ('dp', 'seq'), over_link)]
    pallas_call x7 -> x6, Pallas kernels: 22.8 us -> 19.7 us  [the longest x3 12.7 us: project(): pl.pallas_call(functools.partial(project_kernel, blocks, len(joined), cou...]
  transfers between devices with their start and end apart: 21 -> 21, of which waited for: 4 -> 8; matrix products, arithmetic and copies ran while one was open for 2% -> 3% of each run, Pallas kernels for 28% -> 27%
where the time goes in v6:
time: 118 us; the launch traced here: 117 us
  waiting for transfers between devices  38.8 us (33%)
  Pallas kernels  37 us (31%)
  starting transfers between devices  34.5 us (29%)
  local copies, waits for them, and re-layouts  5.1 us (4%)
    ppermute x7, starting transfers between devices, moved(): return lax.ppermute(value, ('dp', 'seq', 'head'), pairs)  16.4 us
    ppermute x7, waiting for transfers between devices, moved(): return lax.ppermute(value, ('dp', 'seq', 'head'), pairs)  13.8 us
    pallas_call x3, Pallas kernels, project(): pl.pallas_call(functools.partial(project_kernel, blocks, len(joined), cou...  12.7 us
    pallas_call x2, Pallas kernels, attend(): pl.pallas_call(functools.partial(attend_kernel, groups, reach, block // 2...  10.8 us
    ppermute x2, waiting for transfers between devices, shared(): lax.ppermute(value, 'seq', [(s, s ^ step) for s in range(seqs)])  9.27 us
    ppermute x2, waiting for transfers between devices, ringed(): return lax.ppermute(value, 'head', [(z, after[z]) for z in range(layers)])  8.48 us
    ppermute x2, starting transfers between devices, ringed(): return lax.ppermute(value, 'head', [(z, after[z]) for z in range(layers)])  5.83 us
    ppermute x1, starting transfers between devices, local(): lax.ppermute(pair_a, ('dp', 'seq'), over_link)  4.58 us
  transfers between devices with their start and end apart: 21, of which 8 were waited for; matrix products, arithmetic and copies ran while one was open for 3% of the time, Pallas kernels for 27%

profile of v6, /device:TPU:1, one launch (start us, length us, event | category | flops | bytes accessed | tf_op | source)
XLA Modules:
  0.0 116.7 jit_solution(3882999591951640120)
XLA Ops:
  0.0 2.1 %pack.1 = (bf16[240,1536]{1,0:T(8,128)(2,1)}, bf16[96,768]{1,0:T(8,128)(2,1)}) custom-call(s32[1]{0:T(128)} %bitcast.13.place_ref, bf16[192,1536]{1,0:T(8,128)(2,1)} %bitcast.4.rows_ref, bf16[384,768]{1,0:T(8,128)(2,1)} %refs_1_.1), custom_call_target="tpu_custom_call" | custom-call | flops 1 | bytes 1 | tf_op jit(solution)/shard_map/pack/pallas_call | solution.py:69
  2.1 0.0 copy-start.6
  2.1 3.7 %collective-permute-start.5 = (bf16[240,1536]{1,0:T(8,128)(2,1)}, bf16[240,1536]{1,0:T(8,128)(2,1)S(1)}, u32[]{:S(2)}, u32[]{:S(2)}) collective-permute-start(bf16[240,1536]{1,0:T(8,128)(2,1)} %get-tuple-element.47), channel_id=1, source_target_pairs={{0,1},{1,3},{2,0},{3,2},{4,17},{5,19},{6,16},{7,18},{8,9},{9,11},{... | collective-permute-start | bytes 2211848 | tf_op jit(solution)/shard_map/ppermute | solution.py:497
  6.4 0.7 copy.16
  7.1 1.9 %collective-permute-start.1 = (s32[7,12]{1,0:T(8,128)S(1)}, s32[7,12]{1,0:T(8,128)S(1)}, u32[]{:S(2)}, u32[]{:S(2)}) collective-permute-start(s32[7,12]{1,0:T(8,128)S(1)} %concatenate.3), channel_id=1, source_target_pairs={{0,0},{4,16},{8,8},{12,24},{16,4},{20,20},{24,12},{28,28},{1,1},{5... | collective-permute-start | bytes 1016 | tf_op jit(solution)/shard_map/ppermute | solution.py:529
  9.1 3.0 %bundle.1 = (bf16[768,768]{1,0:T(8,128)(2,1)}, bf16[768,768]{1,0:T(8,128)(2,1)}) custom-call(bf16[768,384]{1,0:T(8,128)(2,1)} %query_ref.1, bf16[768,384]{1,0:T(8,128)(2,1)} %key_ref.1, bf16[768,384]{1,0:T(8,128)(2,1)} %value_ref.1, bf16[384,768]{1,0:T(8,128)(2,1)} %refs_1_.1), custom_call_target="tpu_custom_call" | custom-call | flops 1 | bytes 1 | tf_op jit(solution)/shard_map/bundle/pallas_call | solution.py:98
  12.1 0.3 collective-permute-done.1
  12.4 0.0 collective-permute-start.3
  12.4 0.5 collective-permute-start.4
  12.9 2.3 %collective-permute-start.2 = (bf16[96,768]{1,0:T(8,128)(2,1)S(1)}, bf16[96,768]{1,0:T(8,128)(2,1)S(1)}, u32[]{:S(2)}, u32[]{:S(2)}) collective-permute-start(bf16[96,768]{1,0:T(8,128)(2,1)S(1)} %copy-done.6), channel_id=1, source_target_pairs={{0,2},{1,0},{2,3},{3,1},{4,18},{5,16},{6,19},{7,17},{8,10},{9,8},{... | collective-permute-start | bytes 442376 | tf_op jit(solution)/shard_map/ppermute | solution.py:497
  15.2 2.2 %collective-permute-start = (bf16[192,1536]{1,0:T(8,128)(2,1)}, bf16[192,1536]{1,0:T(8,128)(2,1)}, u32[]{:S(2)}, u32[]{:S(2)}) collective-permute-start(bf16[192,1536]{1,0:T(8,128)(2,1)} %bitcast.4.rows_ref), channel_id=1, source_target_pairs={{0,0},{1,1},{2,2},{3,3},{4,16},{5,17},{6,18},{7,19},{8,8},{9,9},{1... | collective-permute-start | bytes 1769480 | tf_op jit(solution)/shard_map/ppermute | solution.py:497
  17.5 0.6 slice.12
  18.0 0.8 stack.82.place_ref
  18.8 4.7 %collective-permute-done.5.refs_1_.first_ref = bf16[240,1536]{1,0:T(8,128)(2,1)S(1)} collective-permute-done((bf16[240,1536]{1,0:T(8,128)(2,1)}, bf16[240,1536]{1,0:T(8,128)(2,1)S(1)}, u32[]{:S(2)}, u32[]{:S(2)}) %collective-permute-start.5) | collective-permute-done | bytes 737312 | tf_op jit(solution)/shard_map/ppermute | solution.py:497
  23.5 4.1 %collective-permute-start.6 = (bf16[240,1536]{1,0:T(8,128)(2,1)S(1)}, bf16[240,1536]{1,0:T(8,128)(2,1)}, u32[]{:S(2)}, u32[]{:S(2)}) collective-permute-start(bf16[240,1536]{1,0:T(8,128)(2,1)S(1)} %collective-permute-done.5.refs_1_.first_ref), channel_id=1, source_target_pairs={{0,1},{1,3},{2,0},{3,2},{4,5},{5,7},{6,4},{7,6},{8,9},{9,11},{10,8... | collective-permute-start | bytes 2211848 | tf_op jit(solution)/shard_map/ppermute | solution.py:520
  27.6 0.0 collective-permute-done.2.refs_0_
  27.6 2.9 %collective-permute-done.refs_0_ = bf16[192,1536]{1,0:T(8,128)(2,1)} collective-permute-done((bf16[192,1536]{1,0:T(8,128)(2,1)}, bf16[192,1536]{1,0:T(8,128)(2,1)}, u32[]{:S(2)}, u32[]{:S(2)}) %collective-permute-start) | collective-permute-done | bytes 589856 | tf_op jit(solution)/shard_map/ppermute | solution.py:497
  30.5 0.0 collective-permute-done.3.far_front
  30.5 0.0 collective-permute-done.4.far_back.refs_2_
  30.5 4.9 %project.3 = (bf16[576,384]{1,0:T(8,128)(2,1)}, bf16[576,768]{1,0:T(8,128)(2,1)}) custom-call(s32[1]{0:T(128)} %bitcast.5.place_ref, f32[1,1536]{1,0:T(1,128)S(1)} %broadcast_in_dim.10.gain_ref, bf16[768,768]{1,0:T(8,128)(2,1)} %get-tuple-element.44.own_front, bf16[768,768]{1,0:T(8,128)(2,1)} %get-tuple-element.45.own_back, ...), custom_call_target="tpu_custom_call" | custom-call | flops 1 | bytes 1 | tf_op jit(solution)/shard_map/project/pallas_call | solution.py:210
  35.4 8.5 %collective-permute-done.6.refs_0_.second_ref = bf16[240,1536]{1,0:T(8,128)(2,1)} collective-permute-done((bf16[240,1536]{1,0:T(8,128)(2,1)S(1)}, bf16[240,1536]{1,0:T(8,128)(2,1)}, u32[]{:S(2)}, u32[]{:S(2)}) %collective-permute-start.6) | collective-permute-done | bytes 737312 | tf_op jit(solution)/shard_map/ppermute | solution.py:520
  43.9 1.7 %collective-permute-start.7 = (bf16[240,1536]{1,0:T(8,128)(2,1)}, bf16[240,1536]{1,0:T(8,128)(2,1)}, u32[]{:S(2)}, u32[]{:S(2)}) collective-permute-start(bf16[240,1536]{1,0:T(8,128)(2,1)} %collective-permute-done.6.refs_0_.second_ref), channel_id=1, source_target_pairs={{0,1},{1,3},{2,0},{3,2},{4,5},{5,7},{6,4},{7,6},{8,9},{9,11},{10,8... | collective-permute-start | bytes 2211848 | tf_op jit(solution)/shard_map/ppermute | solution.py:520
  45.6 1.9 %join.1.refs_1_ = bf16[144,1536]{1,0:T(8,128)(2,1)} custom-call(bf16[240,1536]{1,0:T(8,128)(2,1)S(1)} %collective-permute-done.5.refs_1_.first_ref, bf16[240,1536]{1,0:T(8,128)(2,1)} %collective-permute-done.6.refs_0_.second_ref, bf16[96,768]{1,0:T(8,128)(2,1)S(1)} %hold.2.piece_ref), custom_call_target="tpu_custom_call" | custom-call | flops 1 | bytes 1 | tf_op jit(solution)/shard_map/join/pallas_call | solution.py:126
  47.5 1.3 %collective-permute-start.9 = (bf16[144,1536]{1,0:T(8,128)(2,1)}, bf16[144,1536]{1,0:T(8,128)(2,1)S(1)}, u32[]{:S(2)}, u32[]{:S(2)}) collective-permute-start(bf16[144,1536]{1,0:T(8,128)(2,1)} %join.1.refs_1_), channel_id=1, source_target_pairs={{0,8},{4,12},{8,0},{12,4},{1,9},{5,13},{9,1},{13,5},{2,10},{6,14},... | collective-permute-start | bytes 1327112 | tf_op jit(solution)/shard_map/ppermute | solution.py:507
  48.8 0.0 collective-permute-start.8
  48.8 9.3 %collective-permute-done.9.refs_3_ = bf16[144,1536]{1,0:T(8,128)(2,1)S(1)} collective-permute-done((bf16[144,1536]{1,0:T(8,128)(2,1)}, bf16[144,1536]{1,0:T(8,128)(2,1)S(1)}, u32[]{:S(2)}, u32[]{:S(2)}) %collective-permute-start.9) | collective-permute-done | bytes 442400 | tf_op jit(solution)/shard_map/ppermute | solution.py:507
  58.1 0.7 slice.16
  58.8 0.8 copy-done.1
  59.6 0.0 collective-permute-start.10
  59.6 0.0 collective-permute-done.8.refs_2_
  59.6 0.7 slice.17
  60.3 0.8 copy-done.3
  61.1 1.2 %collective-permute-start.11 = (bf16[64,1536]{1,0:T(8,128)(2,1)}, bf16[64,1536]{1,0:T(8,128)(2,1)}, u32[]{:S(2)}, u32[]{:S(2)}) collective-permute-start(bf16[64,1536]{1,0:T(8,128)(2,1)} %slice.17), channel_id=1, source_target_pairs={{0,8},{4,12},{8,0},{12,4},{1,9},{5,13},{9,1},{13,5},{2,10},{6,14},... | collective-permute-start | bytes 589832 | tf_op jit(solution)/shard_map/ppermute | solution.py:511
  62.3 3.7 %project.4 = (bf16[576,384]{1,0:T(8,128)(2,1)}, bf16[576,768]{1,0:T(8,128)(2,1)}) custom-call(s32[1]{0:T(128)} %bitcast.5.place_ref, f32[1,1536]{1,0:T(1,128)S(1)} %broadcast_in_dim.10.gain_ref, bf16[768,768]{1,0:T(8,128)(2,1)} %get-tuple-element.44.own_front, ...), custom_call_target="tpu_custom_call", output_to_operand_aliasing={{0}: (7, {}), {1}: (8, {})} | custom-call | flops 1 | bytes 1 | tf_op jit(solution)/shard_map/project/pallas_call | solution.py:210
  66.1 4.6 %collective-permute-start.14 = (bf16[576,768]{1,0:T(8,128)(2,1)}, bf16[576,768]{1,0:T(8,128)(2,1)S(1)}, u32[]{:S(2)}, u32[]{:S(2)}) collective-permute-start(bf16[576,768]{1,0:T(8,128)(2,1)} %get-tuple-element.56.refs_2_), channel_id=1, source_target_pairs={{16,8},{20,12},{8,16},{12,20},{17,9},{21,13},{9,17},{13,21},{18,10... | collective-permute-start | bytes 2654216 | tf_op jit(solution)/shard_map/ppermute | solution.py:548
  70.6 0.1 collective-permute-start.12
  70.7 0.0 collective-permute-done.11.refs_5_
  70.7 0.0 collective-permute-done.10.refs_4_
  70.7 0.0 collective-permute-done.7.refs_0_
  70.8 4.0 %project.5 = (bf16[192,384]{1,0:T(8,128)(2,1)}, bf16[192,768]{1,0:T(8,128)(2,1)}, bf16[576,1536]{1,0:T(8,128)(2,1)}) custom-call(s32[1]{0:T(128)} %bitcast.5.place_ref, f32[1,1536]{1,0:T(1,128)S(1)} %broadcast_in_dim.10.gain_ref, bf16[768,768]{1,0:T(8,128)(2,1)} %get-tuple-element.44.own_front, bf16[768,768]{1,0:T(8,128)(2,1)} %get-tuple-element.45.own_back, ...), custom_call_target="tpu_custom_call" | custom-call | flops 8589934592 | bytes 1 | tf_op jit(solution)/shard_map/project/pallas_call | solution.py:210
  74.8 2.1 %collective-permute-start.15 = (bf16[192,768]{1,0:T(8,128)(2,1)}, bf16[192,768]{1,0:T(8,128)(2,1)S(1)}, u32[]{:S(2)}, u32[]{:S(2)}) collective-permute-start(bf16[192,768]{1,0:T(8,128)(2,1)} %get-tuple-element.57.refs_3_), channel_id=1, source_target_pairs={{16,8},{20,12},{8,16},{12,20},{17,9},{21,13},{9,17},{13,21},{18,10... | collective-permute-start | bytes 884744 | tf_op jit(solution)/shard_map/ppermute | solution.py:550
  76.9 0.1 collective-permute-start.13
  77.0 0.1 add_add_fusion.1.turn_ref
  77.1 0.5 collective-permute-start.16
  77.6 0.1 add_add_fusion.turn_ref
  77.7 0.1 stack.91.refs_0_
  77.8 0.1 pad_add_fusion.place_ref
  77.8 3.7 %collective-permute-done.14.refs_6_ = bf16[576,768]{1,0:T(8,128)(2,1)S(1)} collective-permute-done((bf16[576,768]{1,0:T(8,128)(2,1)}, bf16[576,768]{1,0:T(8,128)(2,1)S(1)}, u32[]{:S(2)}, u32[]{:S(2)}) %collective-permute-start.14) | collective-permute-done | bytes 884768 | tf_op jit(solution)/shard_map/ppermute | solution.py:548
  81.6 0.0 collective-permute-done.12.refs_4_
  81.6 3.2 %collective-permute-done.15.refs_7_ = bf16[192,768]{1,0:T(8,128)(2,1)S(1)} collective-permute-done((bf16[192,768]{1,0:T(8,128)(2,1)}, bf16[192,768]{1,0:T(8,128)(2,1)S(1)}, u32[]{:S(2)}, u32[]{:S(2)}) %collective-permute-start.15) | collective-permute-done | bytes 294944 | tf_op jit(solution)/shard_map/ppermute | solution.py:550
  84.7 0.0 collective-permute-done.13.refs_5_
  84.7 2.9 %window.1 = (bf16[768,384]{1,0:T(8,128)(2,1)S(1)}, bf16[2304,768]{1,0:T(8,128)(2,1)S(1)}, bf16[3,18,128,128]{3,2,1,0:T(8,128)(2,1)S(1)}) custom-call(s32[8]{0:T(128)S(1)} %stack.82.place_ref, bf16[576,384]{1,0:T(8,128)(2,1)} %get-tuple-element.53.refs_0_, bf16[192,384]{1,0:T(8,128)(2,1)} %get-tuple-element.55.refs_1_, ...), custom_call_target="tpu_custom_call" | custom-call | bytes 8257536 | tf_op jit(solution)/shard_map/window/pallas_call | solution.py:256
  87.7 4.6 %attend.2 = (bf16[192,384]{1,0:T(8,128)(2,1)}, bf16[192,384]{1,0:T(8,128)(2,1)}) custom-call(s32[8]{0:T(128)S(1)} %stack.82.place_ref, s32[6,12]{1,0:T(8,128)S(1)} %bitcast.24, s32[3]{0:T(128)S(1)} %add_add_fusion.1.turn_ref, bf16[768,384]{1,0:T(8,128)(2,1)S(1)} %get-tuple-element.62.q_all, bf16[2304,768]{1,0:T(8,128)(2,1)S(1)} %get-tuple-element.59.kv_all, ...), custom_call_target="tpu_custom_call" | custom-call | flops 17179869184 | bytes 1048576 | tf_op jit(solution)/shard_map/attend/pallas_call | solution.py:412
  92.3 0.1 collective-permute-start.17
  92.3 6.2 %collective-permute-start.18 = (bf16[192,384]{1,0:T(8,128)(2,1)}, bf16[192,384]{1,0:T(8,128)(2,1)S(1)}, u32[]{:S(2)}, u32[]{:S(2)}) collective-permute-start(bf16[192,384]{1,0:T(8,128)(2,1)} %get-tuple-element.66), channel_id=1, source_target_pairs={{0,3},{1,2},{2,1},{3,0},{4,19},{5,18},{6,17},{7,16},{8,11},{9,10},... | collective-permute-start | bytes 442376 | tf_op jit(solution)/shard_map/ppermute | solution.py:497
  98.5 0.0 collective-permute-done.16.refs_4_
  98.6 6.2 %attend.3 = (bf16[192,384]{1,0:T(8,128)(2,1)}, bf16[192,384]{1,0:T(8,128)(2,1)}, bf16[4,2,384,768]{3,2,1,0:T(8,128)(2,1)S(1)}) custom-call(s32[8]{0:T(128)S(1)} %stack.82.place_ref, s32[6,12]{1,0:T(8,128)S(1)} %bitcast.25, s32[3]{0:T(128)S(1)} %add_add_fusion.turn_ref, bf16[768,384]{1,0:T(8,128)(2,1)S(1)} %get-tuple-element.62.q_all, ...), custom_call_target="tpu_custom_call" | custom-call | flops 17179869184 | bytes 1048576 | tf_op jit(solution)/shard_map/attend/pallas_call | solution.py:412
  104.8 1.9 %collective-permute-start.19 = (bf16[192,384]{1,0:T(8,128)(2,1)}, bf16[192,384]{1,0:T(8,128)(2,1)S(1)}, u32[]{:S(2)}, u32[]{:S(2)}) collective-permute-start(bf16[192,384]{1,0:T(8,128)(2,1)} %get-tuple-element.69), channel_id=1, source_target_pairs={{0,0},{1,1},{2,2},{3,3},{4,16},{5,17},{6,18},{7,19},{8,8},{9,9},{1... | collective-permute-start | bytes 442376 | tf_op jit(solution)/shard_map/ppermute | solution.py:497
  106.7 0.1 collective-permute-start.20
  106.8 0.0 collective-permute-done.17.refs_0_
  106.8 0.0 collective-permute-done.18.refs_1_
  106.8 6.2 %collective-permute-done.19.refs_2_ = bf16[192,384]{1,0:T(8,128)(2,1)S(1)} collective-permute-done((bf16[192,384]{1,0:T(8,128)(2,1)}, bf16[192,384]{1,0:T(8,128)(2,1)S(1)}, u32[]{:S(2)}, u32[]{:S(2)}) %collective-permute-start.19) | collective-permute-done | bytes 147488 | tf_op jit(solution)/shard_map/ppermute | solution.py:497
  113.0 0.0 collective-permute-done.20.refs_3_
  113.0 3.5 %output.1 = bf16[1,192,1536]{2,1,0:T(8,128)(2,1)} custom-call(s32[4]{0:T(128)S(1)} %pad_add_fusion.place_ref, bf16[4,2,384,768]{3,2,1,0:T(8,128)(2,1)S(1)} %get-tuple-element.64.weight, bf16[192,384]{1,0:T(8,128)(2,1)S(1)} %get-tuple-element.67.refs_0_, bf16[192,384]{1,0:T(8,128)(2,1)S(1)} %get-tuple-element.68.refs_1_, ...), custom_call_target="tpu_custom_call" | custom-call | flops 1 | bytes 1 | tf_op jit(solution)/shard_map/output/pallas_call | solution.py:445
  (15 shorter events, 0.0 us)
Async XLA Ops:
  0.0 17.4 %copy-start.5 = (f32[1536]{0:T(1024)S(1)}, f32[1536]{0:T(1024)}, u32[]{:S(2)}) copy-start(f32[1536]{0:T(1024)} %param.9) | copy-start | bytes 18436
  2.1 10.8 %copy-start.6 = (bf16[96,768]{1,0:T(8,128)(2,1)S(1)}, bf16[96,768]{1,0:T(8,128)(2,1)}, u32[]{:S(2)}) copy-start(bf16[96,768]{1,0:T(8,128)(2,1)} %get-tuple-element.41) | copy-start | bytes 442372
  2.1 21.3 %collective-permute-start.5 = (bf16[240,1536]{1,0:T(8,128)(2,1)}, bf16[240,1536]{1,0:T(8,128)(2,1)S(1)}, u32[]{:S(2)}, u32[]{:S(2)}) collective-permute-start(bf16[240,1536]{1,0:T(8,128)(2,1)} %get-tuple-element.47), channel_id=1, source_target_pairs={{0,1},{1,3},{2,0},{3,2},{4,17},{5,19},{6,16},{7,18},{8,9},{9,11},{... | collective-permute-start | bytes 2211848 | tf_op jit(solution)/shard_map/ppermute | solution.py:497
  7.1 5.2 %collective-permute-start.1 = (s32[7,12]{1,0:T(8,128)S(1)}, s32[7,12]{1,0:T(8,128)S(1)}, u32[]{:S(2)}, u32[]{:S(2)}) collective-permute-start(s32[7,12]{1,0:T(8,128)S(1)} %concatenate.3), channel_id=1, source_target_pairs={{0,0},{4,16},{8,8},{12,24},{16,4},{20,20},{24,12},{28,28},{1,1},{5... | collective-permute-start | bytes 1016 | tf_op jit(solution)/shard_map/ppermute | solution.py:529
  12.4 18.1 %collective-permute-start.3 = (bf16[768,768]{1,0:T(8,128)(2,1)}, bf16[768,768]{1,0:T(8,128)(2,1)S(1)}, u32[]{:S(2)}, u32[]{:S(2)}) collective-permute-start(bf16[768,768]{1,0:T(8,128)(2,1)} %get-tuple-element.44.own_front), channel_id=1, source_target_pairs={{0,16},{16,0},{1,17},{17,1},{2,18},{18,2},{3,19},{19,3},{4,20},{20... | collective-permute-start | bytes 3538952 | tf_op jit(solution)/shard_map/ppermute | solution.py:531
  12.4 18.1 %collective-permute-start.4 = (bf16[768,768]{1,0:T(8,128)(2,1)}, bf16[768,768]{1,0:T(8,128)(2,1)S(1)}, u32[]{:S(2)}, u32[]{:S(2)}) collective-permute-start(bf16[768,768]{1,0:T(8,128)(2,1)} %get-tuple-element.45.own_back), channel_id=1, source_target_pairs={{0,16},{16,0},{1,17},{17,1},{2,18},{18,2},{3,19},{19,3},{4,20},{20... | collective-permute-start | bytes 3538952 | tf_op jit(solution)/shard_map/ppermute | solution.py:531
  12.9 14.7 %collective-permute-start.2 = (bf16[96,768]{1,0:T(8,128)(2,1)S(1)}, bf16[96,768]{1,0:T(8,128)(2,1)S(1)}, u32[]{:S(2)}, u32[]{:S(2)}) collective-permute-start(bf16[96,768]{1,0:T(8,128)(2,1)S(1)} %copy-done.6), channel_id=1, source_target_pairs={{0,2},{1,0},{2,3},{3,1},{4,18},{5,16},{6,19},{7,17},{8,10},{9,8},{... | collective-permute-start | bytes 442376 | tf_op jit(solution)/shard_map/ppermute | solution.py:497
  15.2 15.3 %collective-permute-start = (bf16[192,1536]{1,0:T(8,128)(2,1)}, bf16[192,1536]{1,0:T(8,128)(2,1)}, u32[]{:S(2)}, u32[]{:S(2)}) collective-permute-start(bf16[192,1536]{1,0:T(8,128)(2,1)} %bitcast.4.rows_ref), channel_id=1, source_target_pairs={{0,0},{1,1},{2,2},{3,3},{4,16},{5,17},{6,18},{7,19},{8,8},{9,9},{1... | collective-permute-start | bytes 1769480 | tf_op jit(solution)/shard_map/ppermute | solution.py:497
  23.5 20.5 %collective-permute-start.6 = (bf16[240,1536]{1,0:T(8,128)(2,1)S(1)}, bf16[240,1536]{1,0:T(8,128)(2,1)}, u32[]{:S(2)}, u32[]{:S(2)}) collective-permute-start(bf16[240,1536]{1,0:T(8,128)(2,1)S(1)} %collective-permute-done.5.refs_1_.first_ref), channel_id=1, source_target_pairs={{0,1},{1,3},{2,0},{3,2},{4,5},{5,7},{6,4},{7,6},{8,9},{9,11},{10,8... | collective-permute-start | bytes 2211848 | tf_op jit(solution)/shard_map/ppermute | solution.py:520
  43.9 26.8 %collective-permute-start.7 = (bf16[240,1536]{1,0:T(8,128)(2,1)}, bf16[240,1536]{1,0:T(8,128)(2,1)}, u32[]{:S(2)}, u32[]{:S(2)}) collective-permute-start(bf16[240,1536]{1,0:T(8,128)(2,1)} %collective-permute-done.6.refs_0_.second_ref), channel_id=1, source_target_pairs={{0,1},{1,3},{2,0},{3,2},{4,5},{5,7},{6,4},{7,6},{8,9},{9,11},{10,8... | collective-permute-start | bytes 2211848 | tf_op jit(solution)/shard_map/ppermute | solution.py:520
  47.5 10.6 %collective-permute-start.9 = (bf16[144,1536]{1,0:T(8,128)(2,1)}, bf16[144,1536]{1,0:T(8,128)(2,1)S(1)}, u32[]{:S(2)}, u32[]{:S(2)}) collective-permute-start(bf16[144,1536]{1,0:T(8,128)(2,1)} %join.1.refs_1_), channel_id=1, source_target_pairs={{0,8},{4,12},{8,0},{12,4},{1,9},{5,13},{9,1},{13,5},{2,10},{6,14},... | collective-permute-start | bytes 1327112 | tf_op jit(solution)/shard_map/ppermute | solution.py:507
  48.8 10.8 %collective-permute-start.8 = (bf16[144,1536]{1,0:T(8,128)(2,1)}, bf16[144,1536]{1,0:T(8,128)(2,1)S(1)}, u32[]{:S(2)}, u32[]{:S(2)}) collective-permute-start(bf16[144,1536]{1,0:T(8,128)(2,1)} %join.1.refs_1_), channel_id=1, source_target_pairs={{0,4},{4,0},{8,12},{12,8},{1,5},{5,1},{9,13},{13,9},{2,6},{6,2},{1... | collective-permute-start | bytes 1327112 | tf_op jit(solution)/shard_map/ppermute | solution.py:507
  58.8 0.8 copy-start.1
  59.6 11.1 %collective-permute-start.10 = (bf16[80,1536]{1,0:T(8,128)(2,1)}, bf16[80,1536]{1,0:T(8,128)(2,1)S(1)}, u32[]{:S(2)}, u32[]{:S(2)}) collective-permute-start(bf16[80,1536]{1,0:T(8,128)(2,1)} %slice.16), channel_id=1, source_target_pairs={{0,4},{4,0},{8,12},{12,8},{1,5},{5,1},{9,13},{13,9},{2,6},{6,2},{1... | collective-permute-start | bytes 737288 | tf_op jit(solution)/shard_map/ppermute | solution.py:511
  60.3 0.8 copy-start.3
  61.1 9.7 %collective-permute-start.11 = (bf16[64,1536]{1,0:T(8,128)(2,1)}, bf16[64,1536]{1,0:T(8,128)(2,1)}, u32[]{:S(2)}, u32[]{:S(2)}) collective-permute-start(bf16[64,1536]{1,0:T(8,128)(2,1)} %slice.17), channel_id=1, source_target_pairs={{0,8},{4,12},{8,0},{12,4},{1,9},{5,13},{9,1},{13,5},{2,10},{6,14},... | collective-permute-start | bytes 589832 | tf_op jit(solution)/shard_map/ppermute | solution.py:511
  62.3 8.4 %copy-start = (bf16[144,1536]{1,0:T(8,128)(2,1)S(1)}, bf16[144,1536]{1,0:T(8,128)(2,1)}, u32[]{:S(2)}) copy-start(bf16[144,1536]{1,0:T(8,128)(2,1)} %join.1.refs_1_) | copy-start | bytes 1327108
  62.3 8.5 %copy-start.2 = (bf16[144,1536]{1,0:T(8,128)(2,1)S(1)}, bf16[144,1536]{1,0:T(8,128)(2,1)}, u32[]{:S(2)}) copy-start(bf16[144,1536]{1,0:T(8,128)(2,1)} %copy-done.1) | copy-start | bytes 1327108
  62.3 8.5 %copy-start.4 = (bf16[144,1536]{1,0:T(8,128)(2,1)S(1)}, bf16[144,1536]{1,0:T(8,128)(2,1)}, u32[]{:S(2)}) copy-start(bf16[144,1536]{1,0:T(8,128)(2,1)} %copy-done.3) | copy-start | bytes 1327108
  66.1 15.5 %collective-permute-start.14 = (bf16[576,768]{1,0:T(8,128)(2,1)}, bf16[576,768]{1,0:T(8,128)(2,1)S(1)}, u32[]{:S(2)}, u32[]{:S(2)}) collective-permute-start(bf16[576,768]{1,0:T(8,128)(2,1)} %get-tuple-element.56.refs_2_), channel_id=1, source_target_pairs={{16,8},{20,12},{8,16},{12,20},{17,9},{21,13},{9,17},{13,21},{18,10... | collective-permute-start | bytes 2654216 | tf_op jit(solution)/shard_map/ppermute | solution.py:548
  70.6 10.9 %collective-permute-start.12 = (bf16[576,768]{1,0:T(8,128)(2,1)}, bf16[576,768]{1,0:T(8,128)(2,1)}, u32[]{:S(2)}, u32[]{:S(2)}) collective-permute-start(bf16[576,768]{1,0:T(8,128)(2,1)} %get-tuple-element.56.refs_2_), channel_id=1, source_target_pairs={{0,16},{16,0},{1,17},{17,1},{2,18},{18,2},{3,19},{19,3},{4,20},{20... | collective-permute-start | bytes 2654216 | tf_op jit(solution)/shard_map/ppermute | solution.py:548
  74.8 9.9 %collective-permute-start.15 = (bf16[192,768]{1,0:T(8,128)(2,1)}, bf16[192,768]{1,0:T(8,128)(2,1)S(1)}, u32[]{:S(2)}, u32[]{:S(2)}) collective-permute-start(bf16[192,768]{1,0:T(8,128)(2,1)} %get-tuple-element.57.refs_3_), channel_id=1, source_target_pairs={{16,8},{20,12},{8,16},{12,20},{17,9},{21,13},{9,17},{13,21},{18,10... | collective-permute-start | bytes 884744 | tf_op jit(solution)/shard_map/ppermute | solution.py:550
  76.9 7.8 %collective-permute-start.13 = (bf16[192,768]{1,0:T(8,128)(2,1)}, bf16[192,768]{1,0:T(8,128)(2,1)S(1)}, u32[]{:S(2)}, u32[]{:S(2)}) collective-permute-start(bf16[192,768]{1,0:T(8,128)(2,1)} %get-tuple-element.57.refs_3_), channel_id=1, source_target_pairs={{0,16},{16,0},{1,17},{17,1},{2,18},{18,2},{3,19},{19,3},{4,20},{20... | collective-permute-start | bytes 884744 | tf_op jit(solution)/shard_map/ppermute | solution.py:550
  77.1 21.4 %collective-permute-start.16 = (bf16[576,1536]{1,0:T(8,128)(2,1)}, bf16[576,1536]{1,0:T(8,128)(2,1)}, u32[]{:S(2)}, u32[]{:S(2)}) collective-permute-start(bf16[576,1536]{1,0:T(8,128)(2,1)} %get-tuple-element.63.refs_3_), channel_id=1, source_target_pairs={{0,16},{16,0},{1,17},{17,1},{2,18},{18,2},{3,19},{19,3},{4,20},{20... | collective-permute-start | bytes 5308424 | tf_op jit(solution)/shard_map/ppermute | solution.py:551
  92.3 14.5 %collective-permute-start.17 = (bf16[192,384]{1,0:T(8,128)(2,1)}, bf16[192,384]{1,0:T(8,128)(2,1)S(1)}, u32[]{:S(2)}, u32[]{:S(2)}) collective-permute-start(bf16[192,384]{1,0:T(8,128)(2,1)} %get-tuple-element.65), channel_id=1, source_target_pairs={{0,2},{1,3},{2,0},{3,1},{4,18},{5,19},{6,16},{7,17},{8,10},{9,11},... | collective-permute-start | bytes 442376 | tf_op jit(solution)/shard_map/ppermute | solution.py:497
  92.3 14.4 %collective-permute-start.18 = (bf16[192,384]{1,0:T(8,128)(2,1)}, bf16[192,384]{1,0:T(8,128)(2,1)S(1)}, u32[]{:S(2)}, u32[]{:S(2)}) collective-permute-start(bf16[192,384]{1,0:T(8,128)(2,1)} %get-tuple-element.66), channel_id=1, source_target_pairs={{0,3},{1,2},{2,1},{3,0},{4,19},{5,18},{6,17},{7,16},{8,11},{9,10},... | collective-permute-start | bytes 442376 | tf_op jit(solution)/shard_map/ppermute | solution.py:497
  104.8 8.3 %collective-permute-start.19 = (bf16[192,384]{1,0:T(8,128)(2,1)}, bf16[192,384]{1,0:T(8,128)(2,1)S(1)}, u32[]{:S(2)}, u32[]{:S(2)}) collective-permute-start(bf16[192,384]{1,0:T(8,128)(2,1)} %get-tuple-element.69), channel_id=1, source_target_pairs={{0,0},{1,1},{2,2},{3,3},{4,16},{5,17},{6,18},{7,19},{8,8},{9,9},{1... | collective-permute-start | bytes 442376 | tf_op jit(solution)/shard_map/ppermute | solution.py:497
  106.7 6.3 %collective-permute-start.20 = (bf16[192,384]{1,0:T(8,128)(2,1)}, bf16[192,384]{1,0:T(8,128)(2,1)S(1)}, u32[]{:S(2)}, u32[]{:S(2)}) collective-permute-start(bf16[192,384]{1,0:T(8,128)(2,1)} %get-tuple-element.70), channel_id=1, source_target_pairs={{0,1},{1,0},{2,3},{3,2},{4,17},{5,16},{6,19},{7,18},{8,9},{9,8},{1... | collective-permute-start | bytes 442376 | tf_op jit(solution)/shard_map/ppermute | solution.py:497

commit v7 on v6

--- a/solution.py
+++ b/solution.py
@@ -135,15 +135,10 @@
     )(first, second, piece)
 
 
-def project_kernel(blocks, joined, count, place_ref, gain_ref, own_front, own_back, far_front, far_back, *refs):
-    rows, sources = refs[:blocks], refs[blocks:blocks + joined]
-    refs = refs[blocks + joined:]
-    if joined:
-        query_ref, pair_ref, join_ref, held, weight, query_held, pair_held, join_held, sems = refs
-    else:
-        query_ref, pair_ref, held, weight, query_held, pair_held, sems = refs[-7:]
+def project_kernel(blocks, count, place_ref, gain_ref, own_front, own_back, far_front, far_back, *refs):
+    rows = refs[:blocks]
+    query_ref, pair_ref, held, weight, query_held, pair_held, sems = refs[blocks:]
     depth, width = own_front.shape[0], query_ref.shape[1]
-    to_rows = pl.ds(query_ref.shape[0] - blocks * count if len(refs) > 8 and not joined else 0, blocks * count)
     core = place_ref[0]
     order = (1, 2, 0)
     loads = copy_all(
@@ -155,12 +150,6 @@
             to = weight.at[place, pl.ds(pl.multiple_of(owner * depth, 16), depth), :]
             fetches.append((pair[place // 2].at[:, pl.ds(place % 2 * width, width)], to))
     fetches = copy_all(fetches, sems.at[pl.ds(blocks, len(fetches))])
-    parts, at = [], 0
-    for source in sources:
-        parts.append((source, join_held.at[pl.ds(at, source.shape[0]), :]))
-        at += source.shape[0]
-    used = blocks + len(fetches) + 3
-    parts = copy_all(parts, sems.at[pl.ds(used, max(1, joined))])
     gain = gain_ref[...]
     normalized = []
     for i in range(blocks):
@@ -178,52 +167,41 @@
         sem = sems.at[pl.ds(blocks + len(fetches) + place, 1)]
         if place == 0:
             query_held[...] = (got.astype(jnp.float32) * (HD ** -0.5)).astype(jnp.bfloat16)
-            stores += copy_all([(query_held, query_ref.at[to_rows, :])], sem)
+            stores += copy_all([(query_held, query_ref)], sem)
         else:
             part = pl.ds((place - 1) * width, width)
             pair_held[:, (place - 1) * width:place * width] = got
-            stores += copy_all([(pair_held.at[:, part], pair_ref.at[to_rows, part])], sem)
-        if turn == 0 and joined:
-            for part in parts:
-                part.wait()
-            stores += copy_all([(join_held, join_ref)], sems.at[pl.ds(used + joined, 1)])
+            stores += copy_all([(pair_held.at[:, part], pair_ref.at[:, part])], sem)
     for store in stores:
         store.wait()
 
 
-def project(place, rows, count, width, gain, own, far, cost, room=0, into=(), joined=()):
+def project(place, rows, count, width, gain, own, far, cost):
     blocks, depth = len(rows), rows[0].shape[1]
     total = blocks * count
-    full = into[0].shape[0] if into else total + room
-    out_shape = [pltpu.HBM((full, width), jnp.bfloat16), pltpu.HBM((full, 2 * width), jnp.bfloat16)]
-    scratch = [
-        pltpu.VMEM((total, depth), jnp.bfloat16),
-        pltpu.VMEM((3, depth, width), jnp.bfloat16),
-        pltpu.VMEM((total, width), jnp.bfloat16),
-        pltpu.VMEM((total, 2 * width), jnp.bfloat16),
-    ]
-    if joined:
-        shape = (sum(value.shape[0] for value in joined), joined[0].shape[1])
-        out_shape.append(pltpu.HBM(shape, jnp.bfloat16))
-        scratch.append(pltpu.VMEM(shape, jnp.bfloat16))
-    inputs = 6 + blocks + len(joined)
-    return pl.pallas_call(
-        functools.partial(project_kernel, blocks, len(joined), count),
-        out_shape=out_shape,
-        in_specs=[SMEM, VMEM] + [HBM] * (inputs - 2 + len(into)),
-        out_specs=[HBM] * len(out_shape),
-        scratch_shapes=scratch + [pltpu.SemaphoreType.DMA((blocks + 10 + max(1, len(joined)),))],
-        input_output_aliases={inputs + i: i for i in range(len(into))},
-        compiler_params=pltpu.CompilerParams(vmem_limit_bytes=24 * MIB),
+    return pl.pallas_call(
+        functools.partial(project_kernel, blocks, count),
+        out_shape=[pltpu.HBM((total, width), jnp.bfloat16), pltpu.HBM((total, 2 * width), jnp.bfloat16)],
+        in_specs=[SMEM, VMEM] + [HBM] * (4 + blocks),
+        out_specs=[HBM, HBM],
+        scratch_shapes=[
+            pltpu.VMEM((total, depth), jnp.bfloat16),
+            pltpu.VMEM((3, depth, width), jnp.bfloat16),
+            pltpu.VMEM((total, width), jnp.bfloat16),
+            pltpu.VMEM((total, 2 * width), jnp.bfloat16),
+            pltpu.SemaphoreType.DMA((blocks + 9,)),
+        ],
+        compiler_params=pltpu.CompilerParams(vmem_limit_bytes=16 * MIB),
         cost_estimate=pl.CostEstimate(flops=cost, bytes_accessed=1, transcendentals=0),
         name="project",
-    )(place, gain, *in_hbm(*own), *far, *rows, *joined, *in_hbm(*into))
-
-
-def window_kernel(shape, groups, place_ref, *refs):
+    )(place, gain, *in_hbm(*own), *far, *rows)
+
+
+def window_kernel(shape, groups, joined, place_ref, *refs):
     kinds = len(shape)
     queries, owns, sides = refs[:kinds], refs[kinds:2 * kinds], refs[2 * kinds:4 * kinds]
-    q_all, kv_all, vt_all, sems = refs[4 * kinds:]
+    sources = refs[4 * kinds:4 * kinds + joined]
+    q_all, kv_all, vt_all, join_ref, join_held, sems = refs[4 * kinds + joined:]
     block, width = q_all.shape
     rows = block // sum(shape)
     core = place_ref[0]
@@ -241,32 +219,45 @@
                 to = pl.ds(pl.multiple_of(base + at, 64), rows)
                 pairs.append((source.at[part, :], kv_all.at[to, :]))
             step += 1
-    for copy in copy_all(pairs, sems):
-        copy.wait()
+    loads = copy_all(pairs, sems)
+    parts, at = [], 0
+    for source in sources:
+        parts.append((source, join_held.at[pl.ds(at, source.shape[0]), :]))
+        at += source.shape[0]
+    parts = copy_all(parts, sems.at[pl.ds(len(loads), joined)])
+    for load in loads + parts:
+        load.wait()
+    stores = copy_all([(join_held, join_ref)], sems.at[pl.ds(len(loads) + joined, 1)])
     for index in range(3 * groups):
         for pair in range(width // LANES):
             columns = slice(width + pair * LANES, width + (pair + 1) * LANES)
             vt_all[pair, index] = kv_all[index * GROUP:(index + 1) * GROUP, columns].T
-
-
-def window(place, groups, rows, queries, owns, chip_side, link_side):
+    for store in stores:
+        store.wait()
+
+
+def window(place, groups, rows, queries, owns, chip_side, link_side, joined):
     shape = [query.shape[0] // rows for query in queries]
     width, block = queries[0].shape[1], sum(shape) * rows
     pairs = width // LANES
-    return pl.pallas_call(
-        functools.partial(window_kernel, shape, groups),
+    join_shape = (sum(value.shape[0] for value in joined), joined[0].shape[1])
+    return pl.pallas_call(
+        functools.partial(window_kernel, shape, groups, len(joined)),
         out_shape=(
             jax.ShapeDtypeStruct((block, width), jnp.bfloat16),
             jax.ShapeDtypeStruct((3 * block, 2 * width), jnp.bfloat16),
             jax.ShapeDtypeStruct((pairs, 3 * groups, LANES, GROUP), jnp.bfloat16),
+            pltpu.HBM(join_shape, jnp.bfloat16),
         ),
-        in_specs=[SMEM] + [HBM] * (4 * len(shape)),
-        out_specs=(VMEM,) * 3,
-        scratch_shapes=[pltpu.SemaphoreType.DMA((4 * sum(shape),))],
+        in_specs=[SMEM] + [HBM] * (4 * len(shape) + len(joined)),
+        out_specs=(VMEM,) * 3 + (HBM,),
+        scratch_shapes=[
+            pltpu.VMEM(join_shape, jnp.bfloat16), pltpu.SemaphoreType.DMA((4 * sum(shape) + len(joined) + 1,))
+        ],
         compiler_params=pltpu.CompilerParams(vmem_limit_bytes=16 * MIB),
         cost_estimate=pl.CostEstimate(flops=0, bytes_accessed=2 * 14 * block * width, transcendentals=0),
         name="window",
-    )(place, *in_hbm(*queries, *owns), *chip_side, *link_side)
+    )(place, *in_hbm(*queries, *owns), *chip_side, *link_side, *in_hbm(joined[0]), *joined[1:])
 
 
 def weight_copies(share, place_ref, own_ref, far_ref, pieces_ref, theirs_ref, weight_ref):
@@ -503,18 +494,17 @@
     over_link += [(flat(0, s + 2), flat(1, s)) for s in range(seqs - 2)]
     share = 4
 
-    def shared(value):
+    def shared(value, behind):
         near = [lax.ppermute(value, "seq", [(s, s ^ step) for s in range(seqs)]) for step in (1, 2)]
-        middle = (value.shape[0] // 2 + 15) // 16 * 16
-        halves = (near[1][:middle], near[0][middle:])
-        opposite = [
-            lax.ppermute(half, "seq", [(s, s ^ step) for s in range(seqs)]) for half, step in zip(halves, (1, 2))
-        ]
-        return [value] + near + opposite
+        *near, _ = together(*near, behind)
+        return [value] + near + [lax.ppermute(near[1], "seq", [(s, s ^ 1) for s in range(seqs)])]
 
     rows = frames[0]
     count = rows.shape[0]
     gain = norm_gain[None, :]
+
+    def halos(pair):
+        return lax.ppermute(pair, ("dp", "seq"), over_link), lax.ppermute(pair, "dp", swap)
 
     def ringed(value):
         return lax.ppermute(value, "head", [(z, after[z]) for z in range(layers)])
@@ -539,41 +529,48 @@
     whole, place, band, piece = together(whole, place, band, piece)
 
     core_at = numbers(core)
-    done = project(core_at, [whole, first], count, width, gain, own, far, 1, room=count)
-    *done, second = together(*done, second)
+    query_a, pair_a = project(core_at, [whole, first], count, width, gain, own, far, 1)
+    link_a, chip_a = halos(pair_a)
+    second, link_a, chip_a = together(second, link_a, chip_a)
     third = ringed(second)
-    shares = shared(join(count, first, second, piece))
-    done = project(core_at, [second], count, width, gain, own, far, 1, into=done)
-    query_a, pair_a = done
-    link_a, chip_a = lax.ppermute(pair_a, ("dp", "seq"), over_link), lax.ppermute(pair_a, "dp", swap)
-    query_c, pair_c, mine = project(core_at, [third], count, width, gain, own, far, 1 << 33, joined=shares)
-    link_c, chip_c = lax.ppermute(pair_c, ("dp", "seq"), over_link), lax.ppermute(pair_c, "dp", swap)
+    query_b, pair_b = project(core_at, [second], count, width, gain, own, far, 1)
+    shares = shared(join(count, first, second, piece), query_b)
+    link_b, chip_b = halos(pair_b)
+    third, link_b, chip_b = together(third, link_b, chip_b)
+    query_c, pair_c = project(core_at, [third], count, width, gain, own, far, 1)
+    link_c, chip_c = halos(pair_c)
+    q_all, kv_all, vt_all, mine = window(
+        place, groups, count, [query_a, query_b, query_c], [pair_a, pair_b, pair_c],
+        [chip_a, chip_b, chip_c], [link_a, link_b, link_c], shares,
+    )
     theirs = lax.ppermute(mine, "dp", swap)
-    q_all, kv_all, vt_all = window(
-        place, groups, count, [query_a, query_c], [pair_a, pair_c], [chip_a, chip_c], [link_a, link_c]
-    )
 
     half = layers // 2
-    arrived, sources = [], []
+    contexts, arrived, sources = [], [], []
     for near in (0, 1):
         side = layer // half if near else 1 - layer // half
         turn = numbers(side * half * count, *[lax.rem(layer + e, half) * count for e in range(half)])
         if near:
             weight_place = numbers(core, layer, seq, ids[1], ids[2], ids[3])
-            *contexts, weight = attend(
+            *got, weight = attend(
                 place, band, turn, half, q_all, kv_all, vt_all, share, layers,
                 [weight_place, w_out, far[1], mine, theirs],
             )
         else:
-            contexts = list(attend(place, band, turn, half, q_all, kv_all, vt_all))
-            contexts[0], q_all = together(contexts[0], q_all)
-        for e, context in enumerate(contexts):
-            def target(z, e=e):
-                return (z // half if near else 1 - z // half) * half + (z + e) % half
-
-            arrived.append(moved(context, target))
-            sources.append(side * half + lax.rem(layer + half - e, half))
-    arrived = list(hold(arrived[:half])) + arrived[half:]
+            got = list(attend(place, band, turn, half, q_all, kv_all, vt_all))
+            got[0], q_all = together(got[0], q_all)
+        contexts += got
+    *contexts[1:half], contexts[half] = together(*contexts[1:half], contexts[half])
+    for index, context in enumerate(contexts):
+        near, e = divmod(index, half)
+
+        def target(z, near=near, e=e):
+            return (z // half if near else 1 - z // half) * half + (z + e) % half
+
+        side = layer // half if near else 1 - layer // half
+        arrived.append(moved(context, target))
+        sources.append(side * half + lax.rem(layer + half - e, half))
+    arrived = list(hold(arrived[:1])) + arrived[1:]
     return output(numbers(*sources), weight, arrived)
 
 

time: 118 us -> 124 us (1.051)
  local copies, waits for them, and re-layouts: 5.1 us -> 16.3 us
  waiting for transfers between devices: 38.8 us -> 29.6 us
  starting transfers between devices: 34.5 us -> 38.7 us
    unnamed x15 -> x43, local copies, waits for them, and re-layouts: 2.25 us -> 15.1 us
    ppermute x2, waiting for transfers between devices: 9.27 us -> 2.59 us  [shared(): lax.ppermute(value, 'seq', [(s, s ^ step) for s in range(seqs)])]
    ppermute x6 -> x7, starting transfers between devices: 8.07 us -> 13 us  [the longest x3 8.56 us: halos(): lax.ppermute(pair, ('dp', 'seq'), over_link)]
    ppermute x2, waiting for transfers between devices: 8.48 us -> 5.29 us  [ringed(): return lax.ppermute(value, 'head', [(z, after[z]) for z in range(layers)])]
    slice x2 -> x0, local copies, waits for them, and re-layouts: 1.41 us -> none  [shared(): halves = (near[1][:middle], near[0][middle:])]
    ppermute x6 -> x7, waiting for transfers between devices: 6.9 us -> 8.17 us  [the longest x3 7.85 us: halos(): lax.ppermute(pair, ('dp', 'seq'), over_link)]
  transfers between devices with their start and end apart: 21 -> 22, of which waited for: 8 -> 13; matrix products, arithmetic and copies ran while one was open for 3% -> 2% of each run, Pallas kernels for 27% -> 22%
where the time goes in v7:
time: 124 us; the launch traced here: 123 us
  starting transfers between devices  38.7 us (31%)
  Pallas kernels  36.9 us (30%)
  waiting for transfers between devices  29.6 us (24%)
  local copies, waits for them, and re-layouts  16.3 us (13%)
    ppermute x7, starting transfers between devices, moved(): return lax.ppermute(value, ('dp', 'seq', 'head'), pairs)  16.9 us
    unnamed x43, local copies, waits for them, and re-layouts  15.1 us
    ppermute x7, waiting for transfers between devices, moved(): return lax.ppermute(value, ('dp', 'seq', 'head'), pairs)  13.2 us
    pallas_call x3, Pallas kernels, project(): pl.pallas_call(functools.partial(project_kernel, blocks, count), out_shap...  11.7 us
    pallas_call x2, Pallas kernels, attend(): pl.pallas_call(functools.partial(attend_kernel, groups, reach, block // 2...  11.2 us
    ppermute x3, starting transfers between devices, halos(): lax.ppermute(pair, ('dp', 'seq'), over_link)  8.56 us
    ppermute x3, waiting for transfers between devices, halos(): lax.ppermute(pair, ('dp', 'seq'), over_link)  7.85 us
    ppermute x2, waiting for transfers between devices, ringed(): return lax.ppermute(value, 'head', [(z, after[z]) for z in range(layers)])  5.29 us
  transfers between devices with their start and end apart: 22, of which 13 were waited for; matrix products, arithmetic and copies ran while one was open for 2% of the time, Pallas kernels for 22%

profile of v7, /device:TPU:1, one launch (start us, length us, event | category | flops | bytes accessed | tf_op | source)
XLA Modules:
  0.0 122.9 jit_solution(13398440960657913737)
XLA Ops:
  0.0 2.1 %pack.1 = (bf16[240,1536]{1,0:T(8,128)(2,1)}, bf16[96,768]{1,0:T(8,128)(2,1)}) custom-call(s32[1]{0:T(128)} %bitcast.13.place_ref, bf16[192,1536]{1,0:T(8,128)(2,1)} %bitcast.4.rows_ref, bf16[384,768]{1,0:T(8,128)(2,1)} %refs_1_.1), custom_call_target="tpu_custom_call" | custom-call | flops 1 | bytes 1 | tf_op jit(solution)/shard_map/pack/pallas_call | solution.py:69
  2.1 0.0 copy-start.19
  2.1 3.7 %collective-permute-start.5 = (bf16[240,1536]{1,0:T(8,128)(2,1)}, bf16[240,1536]{1,0:T(8,128)(2,1)S(1)}, u32[]{:S(2)}, u32[]{:S(2)}) collective-permute-start(bf16[240,1536]{1,0:T(8,128)(2,1)} %get-tuple-element.52), channel_id=1, source_target_pairs={{0,1},{1,3},{2,0},{3,2},{4,17},{5,19},{6,16},{7,18},{8,9},{9,11},{... | collective-permute-start | bytes 2211848 | tf_op jit(solution)/shard_map/ppermute | solution.py:488
  6.4 0.7 copy.13
  7.1 1.9 %collective-permute-start.1 = (s32[7,12]{1,0:T(8,128)S(1)}, s32[7,12]{1,0:T(8,128)S(1)}, u32[]{:S(2)}, u32[]{:S(2)}) collective-permute-start(s32[7,12]{1,0:T(8,128)S(1)} %concatenate.3), channel_id=1, source_target_pairs={{0,0},{4,16},{8,8},{12,24},{16,4},{20,20},{24,12},{28,28},{1,1},{5... | collective-permute-start | bytes 1016 | tf_op jit(solution)/shard_map/ppermute | solution.py:519
  9.1 3.0 %bundle.1 = (bf16[768,768]{1,0:T(8,128)(2,1)}, bf16[768,768]{1,0:T(8,128)(2,1)}) custom-call(bf16[768,384]{1,0:T(8,128)(2,1)} %query_ref.1, bf16[768,384]{1,0:T(8,128)(2,1)} %key_ref.1, bf16[768,384]{1,0:T(8,128)(2,1)} %value_ref.1, bf16[384,768]{1,0:T(8,128)(2,1)} %refs_1_.1), custom_call_target="tpu_custom_call" | custom-call | flops 1 | bytes 1 | tf_op jit(solution)/shard_map/bundle/pallas_call | solution.py:98
  12.1 0.3 collective-permute-done.1
  12.4 0.5 collective-permute-start.4
  12.9 2.3 %collective-permute-start.2 = (bf16[96,768]{1,0:T(8,128)(2,1)S(1)}, bf16[96,768]{1,0:T(8,128)(2,1)S(1)}, u32[]{:S(2)}, u32[]{:S(2)}) collective-permute-start(bf16[96,768]{1,0:T(8,128)(2,1)S(1)} %copy-done.19), channel_id=1, source_target_pairs={{0,2},{1,0},{2,3},{3,1},{4,18},{5,16},{6,19},{7,17},{8,10},{9,8},{... | collective-permute-start | bytes 442376 | tf_op jit(solution)/shard_map/ppermute | solution.py:488
  15.2 2.2 %collective-permute-start = (bf16[192,1536]{1,0:T(8,128)(2,1)}, bf16[192,1536]{1,0:T(8,128)(2,1)}, u32[]{:S(2)}, u32[]{:S(2)}) collective-permute-start(bf16[192,1536]{1,0:T(8,128)(2,1)} %bitcast.4.rows_ref), channel_id=1, source_target_pairs={{0,0},{1,1},{2,2},{3,3},{4,16},{5,17},{6,18},{7,19},{8,8},{9,9},{1... | collective-permute-start | bytes 1769480 | tf_op jit(solution)/shard_map/ppermute | solution.py:488
  17.4 0.5 slice.6
  17.9 0.6 stack.82.place_ref
  18.5 4.9 %collective-permute-done.5.refs_1_.first_ref = bf16[240,1536]{1,0:T(8,128)(2,1)S(1)} collective-permute-done((bf16[240,1536]{1,0:T(8,128)(2,1)}, bf16[240,1536]{1,0:T(8,128)(2,1)S(1)}, u32[]{:S(2)}, u32[]{:S(2)}) %collective-permute-start.5) | collective-permute-done | bytes 737312 | tf_op jit(solution)/shard_map/ppermute | solution.py:488
  23.5 4.1 %collective-permute-start.6 = (bf16[240,1536]{1,0:T(8,128)(2,1)S(1)}, bf16[240,1536]{1,0:T(8,128)(2,1)S(1)}, u32[]{:S(2)}, u32[]{:S(2)}) collective-permute-start(bf16[240,1536]{1,0:T(8,128)(2,1)S(1)} %collective-permute-done.5.refs_1_.first_ref), channel_id=1, source_target_pairs={{0,1},{1,3},{2,0},{3,2},{4,5},{5,7},{6,4},{7,6},{8,9},{9,11},{10,8... | collective-permute-start | bytes 2211848 | tf_op jit(solution)/shard_map/ppermute | solution.py:510
  27.6 2.8 %collective-permute-done.refs_0_ = bf16[192,1536]{1,0:T(8,128)(2,1)} collective-permute-done((bf16[192,1536]{1,0:T(8,128)(2,1)}, bf16[192,1536]{1,0:T(8,128)(2,1)}, u32[]{:S(2)}, u32[]{:S(2)}) %collective-permute-start) | collective-permute-done | bytes 589856 | tf_op jit(solution)/shard_map/ppermute | solution.py:488
  30.4 4.9 %project.3 = (bf16[384,384]{1,0:T(8,128)(2,1)}, bf16[384,768]{1,0:T(8,128)(2,1)}) custom-call(s32[1]{0:T(128)} %bitcast.5.place_ref, f32[1,1536]{1,0:T(1,128)S(1)} %broadcast_in_dim.10.gain_ref, bf16[768,768]{1,0:T(8,128)(2,1)} %get-tuple-element.49.own_front, bf16[768,768]{1,0:T(8,128)(2,1)} %get-tuple-element.50.own_back, ...), custom_call_target="tpu_custom_call" | custom-call | flops 1 | bytes 1 | tf_op jit(solution)/shard_map/project/pallas_call | solution.py:182
  35.3 0.1 collective-permute-start.8
  35.4 3.5 %collective-permute-start.7 = (bf16[384,768]{1,0:T(8,128)(2,1)}, bf16[384,768]{1,0:T(8,128)(2,1)S(1)}, u32[]{:S(2)}, u32[]{:S(2)}) collective-permute-start(bf16[384,768]{1,0:T(8,128)(2,1)} %get-tuple-element.54.refs_3_), channel_id=1, source_target_pairs={{16,8},{20,12},{8,16},{12,20},{17,9},{21,13},{9,17},{13,21},{18,10... | collective-permute-start | bytes 1769480 | tf_op jit(solution)/shard_map/ppermute | solution.py:507
  38.9 4.9 %collective-permute-done.6.refs_0_.second_ref = bf16[240,1536]{1,0:T(8,128)(2,1)S(1)} collective-permute-done((bf16[240,1536]{1,0:T(8,128)(2,1)S(1)}, bf16[240,1536]{1,0:T(8,128)(2,1)S(1)}, u32[]{:S(2)}, u32[]{:S(2)}) %collective-permute-start.6) | collective-permute-done | bytes 737312 | tf_op jit(solution)/shard_map/ppermute | solution.py:510
  43.8 0.8 copy-done
  44.6 2.2 %collective-permute-done.7.refs_9_ = bf16[384,768]{1,0:T(8,128)(2,1)S(1)} collective-permute-done((bf16[384,768]{1,0:T(8,128)(2,1)}, bf16[384,768]{1,0:T(8,128)(2,1)S(1)}, u32[]{:S(2)}, u32[]{:S(2)}) %collective-permute-start.7) | collective-permute-done | bytes 589856 | tf_op jit(solution)/shard_map/ppermute | solution.py:507
  46.8 0.8 copy-done.2
  47.6 0.6 collective-permute-start.9
  48.2 1.2 join.1.refs_12_
  49.4 0.3 collective-permute-start.15
  49.7 1.4 %collective-permute-start.14 = (bf16[144,1536]{1,0:T(8,128)(2,1)}, bf16[144,1536]{1,0:T(8,128)(2,1)S(1)}, u32[]{:S(2)}, u32[]{:S(2)}) collective-permute-start(bf16[144,1536]{1,0:T(8,128)(2,1)} %join.1.refs_12_), channel_id=1, source_target_pairs={{0,4},{4,0},{8,12},{12,8},{1,5},{5,1},{9,13},{13,9},{2,6},{6,2},{1... | collective-permute-start | bytes 1327112 | tf_op jit(solution)/shard_map/ppermute | solution.py:498
  51.0 3.4 %project.4 = (bf16[192,384]{1,0:T(8,128)(2,1)}, bf16[192,768]{1,0:T(8,128)(2,1)}) custom-call(s32[1]{0:T(128)} %bitcast.5.place_ref, f32[1,1536]{1,0:T(1,128)S(1)} %broadcast_in_dim.10.gain_ref, bf16[768,768]{1,0:T(8,128)(2,1)} %get-tuple-element.49.own_front, bf16[768,768]{1,0:T(8,128)(2,1)} %get-tuple-element.50.own_back, ...), custom_call_target="tpu_custom_call" | custom-call | flops 1 | bytes 1 | tf_op jit(solution)/shard_map/project/pallas_call | solution.py:182
  54.4 2.1 %collective-permute-start.11 = (bf16[192,768]{1,0:T(8,128)(2,1)}, bf16[192,768]{1,0:T(8,128)(2,1)S(1)}, u32[]{:S(2)}, u32[]{:S(2)}) collective-permute-start(bf16[192,768]{1,0:T(8,128)(2,1)} %get-tuple-element.57.refs_4_), channel_id=1, source_target_pairs={{0,16},{16,0},{1,17},{17,1},{2,18},{18,2},{3,19},{19,3},{4,20},{20... | collective-permute-start | bytes 884744 | tf_op jit(solution)/shard_map/ppermute | solution.py:507
  56.5 1.9 %collective-permute-start.10 = (bf16[192,768]{1,0:T(8,128)(2,1)}, bf16[192,768]{1,0:T(8,128)(2,1)S(1)}, u32[]{:S(2)}, u32[]{:S(2)}) collective-permute-start(bf16[192,768]{1,0:T(8,128)(2,1)} %get-tuple-element.57.refs_4_), channel_id=1, source_target_pairs={{16,8},{20,12},{8,16},{12,20},{17,9},{21,13},{9,17},{13,21},{18,10... | collective-permute-start | bytes 884744 | tf_op jit(solution)/shard_map/ppermute | solution.py:507
  58.4 2.6 %collective-permute-done.15.refs_14_ = bf16[144,1536]{1,0:T(8,128)(2,1)} collective-permute-done((bf16[144,1536]{1,0:T(8,128)(2,1)}, bf16[144,1536]{1,0:T(8,128)(2,1)}, u32[]{:S(2)}, u32[]{:S(2)}) %collective-permute-start.15) | collective-permute-done | bytes 442400 | tf_op jit(solution)/shard_map/ppermute | solution.py:498
  61.0 2.2 %collective-permute-start.16 = (bf16[144,1536]{1,0:T(8,128)(2,1)}, bf16[144,1536]{1,0:T(8,128)(2,1)}, u32[]{:S(2)}, u32[]{:S(2)}) collective-permute-start(bf16[144,1536]{1,0:T(8,128)(2,1)} %collective-permute-done.15.refs_14_), channel_id=1, source_target_pairs={{0,4},{4,0},{8,12},{12,8},{1,5},{5,1},{9,13},{13,9},{2,6},{6,2},{1... | collective-permute-start | bytes 1327112 | tf_op jit(solution)/shard_map/ppermute | solution.py:500
  63.3 0.7 copy-done.6
  64.0 1.1 collective-permute-done.10.refs_10_
  65.0 0.7 copy-done.8
  65.8 0.4 collective-permute-done.9.refs_0_
  66.1 3.4 %project.5 = (bf16[192,384]{1,0:T(8,128)(2,1)}, bf16[192,768]{1,0:T(8,128)(2,1)}) custom-call(s32[1]{0:T(128)} %bitcast.5.place_ref, f32[1,1536]{1,0:T(1,128)S(1)} %broadcast_in_dim.10.gain_ref, bf16[768,768]{1,0:T(8,128)(2,1)} %get-tuple-element.49.own_front, bf16[768,768]{1,0:T(8,128)(2,1)} %get-tuple-element.50.own_back, ...), custom_call_target="tpu_custom_call" | custom-call | flops 1 | bytes 1 | tf_op jit(solution)/shard_map/project/pallas_call | solution.py:182
  69.5 3.1 %collective-permute-start.13 = (bf16[192,768]{1,0:T(8,128)(2,1)}, bf16[192,768]{1,0:T(8,128)(2,1)S(1)}, u32[]{:S(2)}, u32[]{:S(2)}) collective-permute-start(bf16[192,768]{1,0:T(8,128)(2,1)} %get-tuple-element.60.refs_5_), channel_id=1, source_target_pairs={{16,8},{20,12},{8,16},{12,20},{17,9},{21,13},{9,17},{13,21},{18,10... | collective-permute-start | bytes 884744 | tf_op jit(solution)/shard_map/ppermute | solution.py:507
  72.7 0.1 collective-permute-start.12
  72.8 0.1 add_add_fusion.1.turn_ref
  72.8 0.3 collective-permute-done.16.refs_15_
  73.2 4.6 %collective-permute-done.13.refs_11_ = bf16[192,768]{1,0:T(8,128)(2,1)S(1)} collective-permute-done((bf16[192,768]{1,0:T(8,128)(2,1)}, bf16[192,768]{1,0:T(8,128)(2,1)S(1)}, u32[]{:S(2)}, u32[]{:S(2)}) %collective-permute-start.13) | collective-permute-done | bytes 294944 | tf_op jit(solution)/shard_map/ppermute | solution.py:507
  77.8 1.0 copy-done.5
  78.8 1.0 copy-done.7
  79.8 1.0 copy-done.9
  80.7 4.1 %window.1 = (bf16[768,384]{1,0:T(8,128)(2,1)S(1)}, bf16[2304,768]{1,0:T(8,128)(2,1)S(1)}, bf16[3,18,128,128]{3,2,1,0:T(8,128)(2,1)S(1)}, bf16[576,1536]{1,0:T(8,128)(2,1)}) custom-call(s32[8]{0:T(128)S(1)} %stack.82.place_ref, bf16[384,384]{1,0:T(8,128)(2,1)} %get-tuple-element.53.refs_0_, bf16[192,384]{1,0:T(8,128)(2,1)} %get-tuple-element.56.refs_1_, ...), custom_call_target="tpu_custom_call" | custom-call | bytes 8257536 | tf_op jit(solution)/shard_map/window/pallas_call | solution.py:244
  84.9 1.8 %copy-done.10 = bf16[2304,768]{1,0:T(8,128)(2,1)} copy-done((bf16[2304,768]{1,0:T(8,128)(2,1)}, bf16[2304,768]{1,0:T(8,128)(2,1)S(1)}, u32[]{:S(2)}) %copy-start.10) | copy-done | bytes 3538968
  86.7 1.2 copy-done.13
  87.9 0.8 copy-done.15
  88.7 0.1 add_add_fusion.turn_ref
  88.8 0.1 stack.91.refs_0_
  88.9 0.1 pad_add_fusion.place_ref
  89.0 2.0 %copy-done.11 = bf16[2304,768]{1,0:T(8,128)(2,1)S(1)} copy-done((bf16[2304,768]{1,0:T(8,128)(2,1)S(1)}, bf16[2304,768]{1,0:T(8,128)(2,1)}, u32[]{:S(2)}) %copy-start.11) | copy-done | bytes 3538968
  91.0 1.5 %copy-done.14 = bf16[3,18,128,128]{3,2,1,0:T(8,128)(2,1)S(1)} copy-done((bf16[3,18,128,128]{3,2,1,0:T(8,128)(2,1)S(1)}, bf16[3,18,128,128]{3,2,1,0:T(8,128)(2,1)}, u32[]{:S(2)}) %copy-start.14) | copy-done | bytes 1769496
  92.5 1.1 copy-done.16
  93.5 4.4 %attend.2 = (bf16[192,384]{1,0:T(8,128)(2,1)}, bf16[192,384]{1,0:T(8,128)(2,1)}) custom-call(s32[8]{0:T(128)S(1)} %stack.82.place_ref, s32[6,12]{1,0:T(8,128)S(1)} %bitcast.24, s32[3]{0:T(128)S(1)} %add_add_fusion.1.turn_ref, bf16[768,384]{1,0:T(8,128)(2,1)S(1)} %copy-done.16, bf16[2304,768]{1,0:T(8,128)(2,1)S(1)} %copy-done.11, ...), custom_call_target="tpu_custom_call" | custom-call | flops 17179869184 | bytes 1048576 | tf_op jit(solution)/shard_map/attend/pallas_call | solution.py:403
  98.0 3.0 %collective-permute-start.18 = (bf16[192,384]{1,0:T(8,128)(2,1)}, bf16[192,384]{1,0:T(8,128)(2,1)S(1)}, u32[]{:S(2)}, u32[]{:S(2)}) collective-permute-start(bf16[192,384]{1,0:T(8,128)(2,1)} %get-tuple-element.75), channel_id=1, source_target_pairs={{0,2},{1,3},{2,0},{3,1},{4,18},{5,19},{6,16},{7,17},{8,10},{9,11},... | collective-permute-start | bytes 442376 | tf_op jit(solution)/shard_map/ppermute | solution.py:488
  100.9 6.8 %attend.3 = (bf16[192,384]{1,0:T(8,128)(2,1)}, bf16[192,384]{1,0:T(8,128)(2,1)}, bf16[4,2,384,768]{3,2,1,0:T(8,128)(2,1)S(1)}) custom-call(s32[8]{0:T(128)S(1)} %stack.82.place_ref, s32[6,12]{1,0:T(8,128)S(1)} %bitcast.25, s32[3]{0:T(128)S(1)} %add_add_fusion.turn_ref, bf16[768,384]{1,0:T(8,128)(2,1)S(1)} %copy-done.17, bf16[2304,768]{1,0:T(8,128)(2,1)S(1)} %copy-done.12, ...), custom_call_target="tpu_custom_call" | custom-call | flops 17179869184 | bytes 1048576 | tf_op jit(solution)/shard_map/attend/pallas_call | solution.py:403
  107.8 2.3 %collective-permute-start.19 = (bf16[192,384]{1,0:T(8,128)(2,1)S(1)}, bf16[192,384]{1,0:T(8,128)(2,1)S(1)}, u32[]{:S(2)}, u32[]{:S(2)}) collective-permute-start(bf16[192,384]{1,0:T(8,128)(2,1)S(1)} %copy-done.20), channel_id=1, source_target_pairs={{0,3},{1,2},{2,1},{3,0},{4,19},{5,18},{6,17},{7,16},{8,11},{9,10},... | collective-permute-start | bytes 442376 | tf_op jit(solution)/shard_map/ppermute | solution.py:488
  110.0 3.4 %collective-permute-start.20 = (bf16[192,384]{1,0:T(8,128)(2,1)}, bf16[192,384]{1,0:T(8,128)(2,1)S(1)}, u32[]{:S(2)}, u32[]{:S(2)}) collective-permute-start(bf16[192,384]{1,0:T(8,128)(2,1)} %get-tuple-element.79), channel_id=1, source_target_pairs={{0,0},{1,1},{2,2},{3,3},{4,16},{5,17},{6,18},{7,19},{8,8},{9,9},{1... | collective-permute-start | bytes 442376 | tf_op jit(solution)/shard_map/ppermute | solution.py:488
  113.5 0.2 collective-permute-start.21
  113.7 2.5 %collective-permute-done.19.refs_1_ = bf16[192,384]{1,0:T(8,128)(2,1)S(1)} collective-permute-done((bf16[192,384]{1,0:T(8,128)(2,1)S(1)}, bf16[192,384]{1,0:T(8,128)(2,1)S(1)}, u32[]{:S(2)}, u32[]{:S(2)}) %collective-permute-start.19) | collective-permute-done | bytes 147488 | tf_op jit(solution)/shard_map/ppermute | solution.py:488
  116.1 1.4 %collective-permute-done.20.refs_2_ = bf16[192,384]{1,0:T(8,128)(2,1)S(1)} collective-permute-done((bf16[192,384]{1,0:T(8,128)(2,1)}, bf16[192,384]{1,0:T(8,128)(2,1)S(1)}, u32[]{:S(2)}, u32[]{:S(2)}) %collective-permute-start.20) | collective-permute-done | bytes 147488 | tf_op jit(solution)/shard_map/ppermute | solution.py:488
  117.6 1.6 %collective-permute-done.21.refs_3_ = bf16[192,384]{1,0:T(8,128)(2,1)S(1)} collective-permute-done((bf16[192,384]{1,0:T(8,128)(2,1)}, bf16[192,384]{1,0:T(8,128)(2,1)S(1)}, u32[]{:S(2)}, u32[]{:S(2)}) %collective-permute-start.21) | collective-permute-done | bytes 147488 | tf_op jit(solution)/shard_map/ppermute | solution.py:488
  119.2 3.5 %output.1 = bf16[1,192,1536]{2,1,0:T(8,128)(2,1)} custom-call(s32[4]{0:T(128)S(1)} %pad_add_fusion.place_ref, bf16[4,2,384,768]{3,2,1,0:T(8,128)(2,1)S(1)} %get-tuple-element.74.weight, bf16[192,384]{1,0:T(8,128)(2,1)S(1)} %hold.3.refs_0_, bf16[192,384]{1,0:T(8,128)(2,1)S(1)} %collective-permute-done.19.refs_1_, ...), custom_call_target="tpu_custom_call" | custom-call | flops 1 | bytes 1 | tf_op jit(solution)/shard_map/output/pallas_call | solution.py:436
  (43 shorter events, 0.1 us)
Async XLA Ops:
  0.0 17.4 %copy-start.18 = (f32[1536]{0:T(1024)S(1)}, f32[1536]{0:T(1024)}, u32[]{:S(2)}) copy-start(f32[1536]{0:T(1024)} %param.9) | copy-start | bytes 18436
  2.1 10.8 %copy-start.19 = (bf16[96,768]{1,0:T(8,128)(2,1)S(1)}, bf16[96,768]{1,0:T(8,128)(2,1)}, u32[]{:S(2)}) copy-start(bf16[96,768]{1,0:T(8,128)(2,1)} %get-tuple-element.46) | copy-start | bytes 442372
  2.1 21.3 %collective-permute-start.5 = (bf16[240,1536]{1,0:T(8,128)(2,1)}, bf16[240,1536]{1,0:T(8,128)(2,1)S(1)}, u32[]{:S(2)}, u32[]{:S(2)}) collective-permute-start(bf16[240,1536]{1,0:T(8,128)(2,1)} %get-tuple-element.52), channel_id=1, source_target_pairs={{0,1},{1,3},{2,0},{3,2},{4,17},{5,19},{6,16},{7,18},{8,9},{9,11},{... | collective-permute-start | bytes 2211848 | tf_op jit(solution)/shard_map/ppermute | solution.py:488
  7.1 5.2 %collective-permute-start.1 = (s32[7,12]{1,0:T(8,128)S(1)}, s32[7,12]{1,0:T(8,128)S(1)}, u32[]{:S(2)}, u32[]{:S(2)}) collective-permute-start(s32[7,12]{1,0:T(8,128)S(1)} %concatenate.3), channel_id=1, source_target_pairs={{0,0},{4,16},{8,8},{12,24},{16,4},{20,20},{24,12},{28,28},{1,1},{5... | collective-permute-start | bytes 1016 | tf_op jit(solution)/shard_map/ppermute | solution.py:519
  12.4 18.0 %collective-permute-start.3 = (bf16[768,768]{1,0:T(8,128)(2,1)}, bf16[768,768]{1,0:T(8,128)(2,1)S(1)}, u32[]{:S(2)}, u32[]{:S(2)}) collective-permute-start(bf16[768,768]{1,0:T(8,128)(2,1)} %get-tuple-element.49.own_front), channel_id=1, source_target_pairs={{0,16},{16,0},{1,17},{17,1},{2,18},{18,2},{3,19},{19,3},{4,20},{20... | collective-permute-start | bytes 3538952 | tf_op jit(solution)/shard_map/ppermute | solution.py:521
  12.4 18.0 %collective-permute-start.4 = (bf16[768,768]{1,0:T(8,128)(2,1)}, bf16[768,768]{1,0:T(8,128)(2,1)S(1)}, u32[]{:S(2)}, u32[]{:S(2)}) collective-permute-start(bf16[768,768]{1,0:T(8,128)(2,1)} %get-tuple-element.50.own_back), channel_id=1, source_target_pairs={{0,16},{16,0},{1,17},{17,1},{2,18},{18,2},{3,19},{19,3},{4,20},{20... | collective-permute-start | bytes 3538952 | tf_op jit(solution)/shard_map/ppermute | solution.py:521
  12.9 14.7 %collective-permute-start.2 = (bf16[96,768]{1,0:T(8,128)(2,1)S(1)}, bf16[96,768]{1,0:T(8,128)(2,1)S(1)}, u32[]{:S(2)}, u32[]{:S(2)}) collective-permute-start(bf16[96,768]{1,0:T(8,128)(2,1)S(1)} %copy-done.19), channel_id=1, source_target_pairs={{0,2},{1,0},{2,3},{3,1},{4,18},{5,16},{6,19},{7,17},{8,10},{9,8},{... | collective-permute-start | bytes 442376 | tf_op jit(solution)/shard_map/ppermute | solution.py:488
  15.2 15.2 %collective-permute-start = (bf16[192,1536]{1,0:T(8,128)(2,1)}, bf16[192,1536]{1,0:T(8,128)(2,1)}, u32[]{:S(2)}, u32[]{:S(2)}) collective-permute-start(bf16[192,1536]{1,0:T(8,128)(2,1)} %bitcast.4.rows_ref), channel_id=1, source_target_pairs={{0,0},{1,1},{2,2},{3,3},{4,16},{5,17},{6,18},{7,19},{8,8},{9,9},{1... | collective-permute-start | bytes 1769480 | tf_op jit(solution)/shard_map/ppermute | solution.py:488
  23.5 20.4 %collective-permute-start.6 = (bf16[240,1536]{1,0:T(8,128)(2,1)S(1)}, bf16[240,1536]{1,0:T(8,128)(2,1)S(1)}, u32[]{:S(2)}, u32[]{:S(2)}) collective-permute-start(bf16[240,1536]{1,0:T(8,128)(2,1)S(1)} %collective-permute-done.5.refs_1_.first_ref), channel_id=1, source_target_pairs={{0,1},{1,3},{2,0},{3,2},{4,5},{5,7},{6,4},{7,6},{8,9},{9,11},{10,8... | collective-permute-start | bytes 2211848 | tf_op jit(solution)/shard_map/ppermute | solution.py:510
  35.3 8.5 %collective-permute-start.8 = (bf16[384,768]{1,0:T(8,128)(2,1)}, bf16[384,768]{1,0:T(8,128)(2,1)S(1)}, u32[]{:S(2)}, u32[]{:S(2)}) collective-permute-start(bf16[384,768]{1,0:T(8,128)(2,1)} %get-tuple-element.54.refs_3_), channel_id=1, source_target_pairs={{0,16},{16,0},{1,17},{17,1},{2,18},{18,2},{3,19},{19,3},{4,20},{20... | collective-permute-start | bytes 1769480 | tf_op jit(solution)/shard_map/ppermute | solution.py:507
  35.4 11.4 %collective-permute-start.7 = (bf16[384,768]{1,0:T(8,128)(2,1)}, bf16[384,768]{1,0:T(8,128)(2,1)S(1)}, u32[]{:S(2)}, u32[]{:S(2)}) collective-permute-start(bf16[384,768]{1,0:T(8,128)(2,1)} %get-tuple-element.54.refs_3_), channel_id=1, source_target_pairs={{16,8},{20,12},{8,16},{12,20},{17,9},{21,13},{9,17},{13,21},{18,10... | collective-permute-start | bytes 1769480 | tf_op jit(solution)/shard_map/ppermute | solution.py:507
  43.8 0.8 copy-start
  46.8 0.8 copy-start.2
  47.6 18.5 %collective-permute-start.9 = (bf16[240,1536]{1,0:T(8,128)(2,1)S(1)}, bf16[240,1536]{1,0:T(8,128)(2,1)S(1)}, u32[]{:S(2)}, u32[]{:S(2)}) collective-permute-start(bf16[240,1536]{1,0:T(8,128)(2,1)S(1)} %collective-permute-done.6.refs_0_.second_ref), channel_id=1, source_target_pairs={{0,1},{1,3},{2,0},{3,2},{4,5},{5,7},{6,4},{7,6},{8,9},{9,11},{10,8... | collective-permute-start | bytes 2211848 | tf_op jit(solution)/shard_map/ppermute | solution.py:510
  49.4 11.6 %collective-permute-start.15 = (bf16[144,1536]{1,0:T(8,128)(2,1)}, bf16[144,1536]{1,0:T(8,128)(2,1)}, u32[]{:S(2)}, u32[]{:S(2)}) collective-permute-start(bf16[144,1536]{1,0:T(8,128)(2,1)} %join.1.refs_12_), channel_id=1, source_target_pairs={{0,8},{4,12},{8,0},{12,4},{1,9},{5,13},{9,1},{13,5},{2,10},{6,14},... | collective-permute-start | bytes 1327112 | tf_op jit(solution)/shard_map/ppermute | solution.py:498
  49.7 11.3 %collective-permute-start.14 = (bf16[144,1536]{1,0:T(8,128)(2,1)}, bf16[144,1536]{1,0:T(8,128)(2,1)S(1)}, u32[]{:S(2)}, u32[]{:S(2)}) collective-permute-start(bf16[144,1536]{1,0:T(8,128)(2,1)} %join.1.refs_12_), channel_id=1, source_target_pairs={{0,4},{4,0},{8,12},{12,8},{1,5},{5,1},{9,13},{13,9},{2,6},{6,2},{1... | collective-permute-start | bytes 1327112 | tf_op jit(solution)/shard_map/ppermute | solution.py:498
  54.4 8.9 %collective-permute-start.11 = (bf16[192,768]{1,0:T(8,128)(2,1)}, bf16[192,768]{1,0:T(8,128)(2,1)S(1)}, u32[]{:S(2)}, u32[]{:S(2)}) collective-permute-start(bf16[192,768]{1,0:T(8,128)(2,1)} %get-tuple-element.57.refs_4_), channel_id=1, source_target_pairs={{0,16},{16,0},{1,17},{17,1},{2,18},{18,2},{3,19},{19,3},{4,20},{20... | collective-permute-start | bytes 884744 | tf_op jit(solution)/shard_map/ppermute | solution.py:507
  56.5 8.5 %collective-permute-start.10 = (bf16[192,768]{1,0:T(8,128)(2,1)}, bf16[192,768]{1,0:T(8,128)(2,1)S(1)}, u32[]{:S(2)}, u32[]{:S(2)}) collective-permute-start(bf16[192,768]{1,0:T(8,128)(2,1)} %get-tuple-element.57.refs_4_), channel_id=1, source_target_pairs={{16,8},{20,12},{8,16},{12,20},{17,9},{21,13},{9,17},{13,21},{18,10... | collective-permute-start | bytes 884744 | tf_op jit(solution)/shard_map/ppermute | solution.py:507
  61.0 8.5 %copy-start.4 = (bf16[144,1536]{1,0:T(8,128)(2,1)}, bf16[144,1536]{1,0:T(8,128)(2,1)S(1)}, u32[]{:S(2)}) copy-start(bf16[144,1536]{1,0:T(8,128)(2,1)S(1)} %collective-permute-done.14.refs_13_) | copy-start | bytes 1327108
  61.0 16.8 %copy-start.1 = (bf16[384,768]{1,0:T(8,128)(2,1)S(1)}, bf16[384,768]{1,0:T(8,128)(2,1)}, u32[]{:S(2)}) copy-start(bf16[384,768]{1,0:T(8,128)(2,1)} %copy-done) | copy-start | bytes 1769476
  61.0 16.8 %copy-start.3 = (bf16[384,768]{1,0:T(8,128)(2,1)S(1)}, bf16[384,768]{1,0:T(8,128)(2,1)}, u32[]{:S(2)}) copy-start(bf16[384,768]{1,0:T(8,128)(2,1)} %copy-done.2) | copy-start | bytes 1769476
  61.0 12.1 %collective-permute-start.16 = (bf16[144,1536]{1,0:T(8,128)(2,1)}, bf16[144,1536]{1,0:T(8,128)(2,1)}, u32[]{:S(2)}, u32[]{:S(2)}) collective-permute-start(bf16[144,1536]{1,0:T(8,128)(2,1)} %collective-permute-done.15.refs_14_), channel_id=1, source_target_pairs={{0,4},{4,0},{8,12},{12,8},{1,5},{5,1},{9,13},{13,9},{2,6},{6,2},{1... | collective-permute-start | bytes 1327112 | tf_op jit(solution)/shard_map/ppermute | solution.py:500
  63.3 0.7 copy-start.6
  65.0 0.7 copy-start.8
  69.5 8.3 %collective-permute-start.13 = (bf16[192,768]{1,0:T(8,128)(2,1)}, bf16[192,768]{1,0:T(8,128)(2,1)S(1)}, u32[]{:S(2)}, u32[]{:S(2)}) collective-permute-start(bf16[192,768]{1,0:T(8,128)(2,1)} %get-tuple-element.60.refs_5_), channel_id=1, source_target_pairs={{16,8},{20,12},{8,16},{12,20},{17,9},{21,13},{9,17},{13,21},{18,10... | collective-permute-start | bytes 884744 | tf_op jit(solution)/shard_map/ppermute | solution.py:507
  72.7 5.1 %collective-permute-start.12 = (bf16[192,768]{1,0:T(8,128)(2,1)}, bf16[192,768]{1,0:T(8,128)(2,1)S(1)}, u32[]{:S(2)}, u32[]{:S(2)}) collective-permute-start(bf16[192,768]{1,0:T(8,128)(2,1)} %get-tuple-element.60.refs_5_), channel_id=1, source_target_pairs={{0,16},{16,0},{1,17},{17,1},{2,18},{18,2},{3,19},{19,3},{4,20},{20... | collective-permute-start | bytes 884744 | tf_op jit(solution)/shard_map/ppermute | solution.py:507
  77.8 1.0 copy-start.5
  78.8 1.0 copy-start.7
  79.8 1.0 copy-start.9
  84.9 1.8 %copy-start.10 = (bf16[2304,768]{1,0:T(8,128)(2,1)}, bf16[2304,768]{1,0:T(8,128)(2,1)S(1)}, u32[]{:S(2)}) copy-start(bf16[2304,768]{1,0:T(8,128)(2,1)S(1)} %get-tuple-element.69.kv_all) | copy-start | bytes 10616836
  86.7 1.2 copy-start.13
  87.9 0.8 copy-start.15
  88.7 12.2 %collective-permute-start.17 = (bf16[576,1536]{1,0:T(8,128)(2,1)}, bf16[576,1536]{1,0:T(8,128)(2,1)S(1)}, u32[]{:S(2)}, u32[]{:S(2)}) collective-permute-start(bf16[576,1536]{1,0:T(8,128)(2,1)} %get-tuple-element.73.refs_3_), channel_id=1, source_target_pairs={{0,16},{16,0},{1,17},{17,1},{2,18},{18,2},{3,19},{19,3},{4,20},{20... | collective-permute-start | bytes 5308424 | tf_op jit(solution)/shard_map/ppermute | solution.py:546
  89.0 2.0 %copy-start.11 = (bf16[2304,768]{1,0:T(8,128)(2,1)S(1)}, bf16[2304,768]{1,0:T(8,128)(2,1)}, u32[]{:S(2)}) copy-start(bf16[2304,768]{1,0:T(8,128)(2,1)} %copy-done.10) | copy-start | bytes 10616836
  91.0 1.5 %copy-start.14 = (bf16[3,18,128,128]{3,2,1,0:T(8,128)(2,1)S(1)}, bf16[3,18,128,128]{3,2,1,0:T(8,128)(2,1)}, u32[]{:S(2)}) copy-start(bf16[3,18,128,128]{3,2,1,0:T(8,128)(2,1)} %copy-done.13) | copy-start | bytes 5308420
  92.5 1.1 copy-start.16
  93.5 7.4 %copy-start.12 = (bf16[2304,768]{1,0:T(8,128)(2,1)S(1)}, bf16[2304,768]{1,0:T(8,128)(2,1)}, u32[]{:S(2)}) copy-start(bf16[2304,768]{1,0:T(8,128)(2,1)} %copy-done.10) | copy-start | bytes 10616836
  93.5 7.4 %copy-start.17 = (bf16[768,384]{1,0:T(8,128)(2,1)S(1)}, bf16[768,384]{1,0:T(8,128)(2,1)}, u32[]{:S(2)}) copy-start(bf16[768,384]{1,0:T(8,128)(2,1)} %copy-done.15) | copy-start | bytes 1769476
  98.0 9.8 %copy-start.20 = (bf16[192,384]{1,0:T(8,128)(2,1)S(1)}, bf16[192,384]{1,0:T(8,128)(2,1)}, u32[]{:S(2)}) copy-start(bf16[192,384]{1,0:T(8,128)(2,1)} %get-tuple-element.78) | copy-start | bytes 442372
  98.0 15.7 %collective-permute-start.18 = (bf16[192,384]{1,0:T(8,128)(2,1)}, bf16[192,384]{1,0:T(8,128)(2,1)S(1)}, u32[]{:S(2)}, u32[]{:S(2)}) collective-permute-start(bf16[192,384]{1,0:T(8,128)(2,1)} %get-tuple-element.75), channel_id=1, source_target_pairs={{0,2},{1,3},{2,0},{3,1},{4,18},{5,19},{6,16},{7,17},{8,10},{9,11},... | collective-permute-start | bytes 442376 | tf_op jit(solution)/shard_map/ppermute | solution.py:488
  107.8 8.3 %collective-permute-start.19 = (bf16[192,384]{1,0:T(8,128)(2,1)S(1)}, bf16[192,384]{1,0:T(8,128)(2,1)S(1)}, u32[]{:S(2)}, u32[]{:S(2)}) collective-permute-start(bf16[192,384]{1,0:T(8,128)(2,1)S(1)} %copy-done.20), channel_id=1, source_target_pairs={{0,3},{1,2},{2,1},{3,0},{4,19},{5,18},{6,17},{7,16},{8,11},{9,10},... | collective-permute-start | bytes 442376 | tf_op jit(solution)/shard_map/ppermute | solution.py:488
  110.0 7.5 %collective-permute-start.20 = (bf16[192,384]{1,0:T(8,128)(2,1)}, bf16[192,384]{1,0:T(8,128)(2,1)S(1)}, u32[]{:S(2)}, u32[]{:S(2)}) collective-permute-start(bf16[192,384]{1,0:T(8,128)(2,1)} %get-tuple-element.79), channel_id=1, source_target_pairs={{0,0},{1,1},{2,2},{3,3},{4,16},{5,17},{6,18},{7,19},{8,8},{9,9},{1... | collective-permute-start | bytes 442376 | tf_op jit(solution)/shard_map/ppermute | solution.py:488
  113.5 5.7 %collective-permute-start.21 = (bf16[192,384]{1,0:T(8,128)(2,1)}, bf16[192,384]{1,0:T(8,128)(2,1)S(1)}, u32[]{:S(2)}, u32[]{:S(2)}) collective-permute-start(bf16[192,384]{1,0:T(8,128)(2,1)} %get-tuple-element.80), channel_id=1, source_target_pairs={{0,1},{1,0},{2,3},{3,2},{4,17},{5,16},{6,19},{7,18},{8,9},{9,8},{1... | collective-permute-start | bytes 442376 | tf_op jit(solution)/shard_map/ppermute | solution.py:488

commit v8 on v7

--- a/solution.py
+++ b/solution.py
@@ -526,9 +526,18 @@
     place = numbers(core, (seq // 2 * 2 + core) * groups, groups * seqs, facts[groups, 0], *ids)
     band = facts[:groups]
     piece, = hold([piece], 1 << 33)
-    whole, place, band, piece = together(whole, place, band, piece)
-
+    half = layers // 2
+    sides = (1 - layer // half, layer // half)
+    turns = [
+        numbers(side * half * count, *[lax.rem(layer + e, half) * count for e in range(half)]) for side in sides
+    ]
+    weight_place = numbers(core, layer, seq, ids[1], ids[2], ids[3])
+    sources = numbers(*[side * half + lax.rem(layer + half - e, half) for side in sides for e in range(half)])
     core_at = numbers(core)
+    whole, place, band, piece, weight_place, sources, core_at, *turns = together(
+        whole, place, band, piece, weight_place, sources, core_at, *turns
+    )
+
     query_a, pair_a = project(core_at, [whole, first], count, width, gain, own, far, 1)
     link_a, chip_a = halos(pair_a)
     second, link_a, chip_a = together(second, link_a, chip_a)
@@ -545,19 +554,15 @@
     )
     theirs = lax.ppermute(mine, "dp", swap)
 
-    half = layers // 2
-    contexts, arrived, sources = [], [], []
+    contexts, arrived = [], []
     for near in (0, 1):
-        side = layer // half if near else 1 - layer // half
-        turn = numbers(side * half * count, *[lax.rem(layer + e, half) * count for e in range(half)])
         if near:
-            weight_place = numbers(core, layer, seq, ids[1], ids[2], ids[3])
             *got, weight = attend(
-                place, band, turn, half, q_all, kv_all, vt_all, share, layers,
+                place, band, turns[near], half, q_all, kv_all, vt_all, share, layers,
                 [weight_place, w_out, far[1], mine, theirs],
             )
         else:
-            got = list(attend(place, band, turn, half, q_all, kv_all, vt_all))
+            got = list(attend(place, band, turns[near], half, q_all, kv_all, vt_all))
             got[0], q_all = together(got[0], q_all)
         contexts += got
     *contexts[1:half], contexts[half] = together(*contexts[1:half], contexts[half])
@@ -567,11 +572,9 @@
         def target(z, near=near, e=e):
             return (z // half if near else 1 - z // half) * half + (z + e) % half
 
-        side = layer // half if near else 1 - layer // half
         arrived.append(moved(context, target))
-        sources.append(side * half + lax.rem(layer + half - e, half))
     arrived = list(hold(arrived[:1])) + arrived[1:]
-    return output(numbers(*sources), weight, arrived)
+    return output(sources, weight, arrived)
 
 
 def solution(mesh):

time: 124 us -> 110 us (0.89)
  local copies, waits for them, and re-layouts: 16.3 us -> 1.96 us
    unnamed x43 -> x7, local copies, waits for them, and re-layouts: 15.1 us -> 0.7 us
    ppermute x7, waiting for transfers between devices: 13.2 us -> 11.4 us  [moved(): return lax.ppermute(value, ('dp', 'seq', 'head'), pairs)]
  transfers between devices with their start and end apart: 22 -> 22, of which waited for: 13 -> 13; matrix products, arithmetic and copies ran while one was open for 2% -> 2% of each run, Pallas kernels for 22% -> 25%
where the time goes in v8:
time: 110 us; the launch traced here: 109 us
  starting transfers between devices  38.1 us (35%)
  Pallas kernels  36.8 us (33%)
  waiting for transfers between devices  30.5 us (28%)
  local copies, waits for them, and re-layouts  1.96 us (2%)
    ppermute x7, starting transfers between devices, moved(): return lax.ppermute(value, ('dp', 'seq', 'head'), pairs)  16.3 us
    pallas_call x3, Pallas kernels, project(): pl.pallas_call(functools.partial(project_kernel, blocks, count), out_shap...  11.6 us
    pallas_call x2, Pallas kernels, attend(): pl.pallas_call(functools.partial(attend_kernel, groups, reach, block // 2...  11.6 us
    ppermute x7, waiting for transfers between devices, moved(): return lax.ppermute(value, ('dp', 'seq', 'head'), pairs)  11.4 us
    ppermute x3, waiting for transfers between devices, halos(): lax.ppermute(pair, ('dp', 'seq'), over_link)  8.14 us
    ppermute x3, starting transfers between devices, halos(): lax.ppermute(pair, ('dp', 'seq'), over_link)  8.09 us
    ppermute x2, waiting for transfers between devices, ringed(): return lax.ppermute(value, 'head', [(z, after[z]) for z in range(layers)])  6.4 us
    ppermute x2, starting transfers between devices, ringed(): return lax.ppermute(value, 'head', [(z, after[z]) for z in range(layers)])  5.93 us
  transfers between devices with their start and end apart: 22, of which 13 were waited for; matrix products, arithmetic and copies ran while one was open for 2% of the time, Pallas kernels for 25%

profile of v8, /device:TPU:1, one launch (start us, length us, event | category | flops | bytes accessed | tf_op | source)
XLA Modules:
  0.0 108.6 jit_solution(5512350563068261427)
XLA Ops:
  0.0 2.1 %pack.1 = (bf16[240,1536]{1,0:T(8,128)(2,1)}, bf16[96,768]{1,0:T(8,128)(2,1)}) custom-call(s32[1]{0:T(128)} %bitcast.9.place_ref, bf16[192,1536]{1,0:T(8,128)(2,1)} %bitcast.rows_ref, bf16[384,768]{1,0:T(8,128)(2,1)} %refs_1_.1), custom_call_target="tpu_custom_call" | custom-call | flops 1 | bytes 1 | tf_op jit(solution)/shard_map/pack/pallas_call | solution.py:69
  2.1 0.0 copy-start.1
  2.1 3.7 %collective-permute-start.5 = (bf16[240,1536]{1,0:T(8,128)(2,1)}, bf16[240,1536]{1,0:T(8,128)(2,1)S(1)}, u32[]{:S(2)}, u32[]{:S(2)}) collective-permute-start(bf16[240,1536]{1,0:T(8,128)(2,1)} %get-tuple-element.61), channel_id=1, source_target_pairs={{0,1},{1,3},{2,0},{3,2},{4,17},{5,19},{6,16},{7,18},{8,9},{9,11},{... | collective-permute-start | bytes 2211848 | tf_op jit(solution)/shard_map/ppermute | solution.py:488
  6.4 0.7 copy.13
  7.1 1.9 %collective-permute-start.1 = (s32[7,12]{1,0:T(8,128)S(1)}, s32[7,12]{1,0:T(8,128)S(1)}, u32[]{:S(2)}, u32[]{:S(2)}) collective-permute-start(s32[7,12]{1,0:T(8,128)S(1)} %concatenate.3), channel_id=1, source_target_pairs={{0,0},{4,16},{8,8},{12,24},{16,4},{20,20},{24,12},{28,28},{1,1},{5... | collective-permute-start | bytes 1016 | tf_op jit(solution)/shard_map/ppermute | solution.py:519
  9.1 3.0 %bundle.1 = (bf16[768,768]{1,0:T(8,128)(2,1)}, bf16[768,768]{1,0:T(8,128)(2,1)}) custom-call(bf16[768,384]{1,0:T(8,128)(2,1)} %query_ref.1, bf16[768,384]{1,0:T(8,128)(2,1)} %key_ref.1, bf16[768,384]{1,0:T(8,128)(2,1)} %value_ref.1, bf16[384,768]{1,0:T(8,128)(2,1)} %refs_1_.1), custom_call_target="tpu_custom_call" | custom-call | flops 1 | bytes 1 | tf_op jit(solution)/shard_map/bundle/pallas_call | solution.py:98
  12.1 0.3 collective-permute-done.1
  12.4 0.0 collective-permute-start.3
  12.4 0.5 collective-permute-start.4
  12.9 3.4 %collective-permute-start = (bf16[192,1536]{1,0:T(8,128)(2,1)}, bf16[192,1536]{1,0:T(8,128)(2,1)}, u32[]{:S(2)}, u32[]{:S(2)}) collective-permute-start(bf16[192,1536]{1,0:T(8,128)(2,1)} %bitcast.rows_ref), channel_id=1, source_target_pairs={{0,0},{1,1},{2,2},{3,3},{4,16},{5,17},{6,18},{7,19},{8,8},{9,9},{1... | collective-permute-start | bytes 1769480 | tf_op jit(solution)/shard_map/ppermute | solution.py:488
  16.3 0.0 copy-done.1
  16.3 1.1 %collective-permute-start.2 = (bf16[96,768]{1,0:T(8,128)(2,1)S(1)}, bf16[96,768]{1,0:T(8,128)(2,1)S(1)}, u32[]{:S(2)}, u32[]{:S(2)}) collective-permute-start(bf16[96,768]{1,0:T(8,128)(2,1)S(1)} %copy-done.1), channel_id=1, source_target_pairs={{0,2},{1,0},{2,3},{3,1},{4,18},{5,16},{6,19},{7,17},{8,10},{9,8},{... | collective-permute-start | bytes 442376 | tf_op jit(solution)/shard_map/ppermute | solution.py:488
  17.4 0.1 pad_add_fusion.place_ref
  17.5 0.1 stack.80.refs_0_
  17.6 0.1 add_add_fusion
  17.7 0.5 slice.6
  18.2 0.6 stack.77.place_ref
  18.9 4.6 %collective-permute-done.5.refs_1_.first_ref = bf16[240,1536]{1,0:T(8,128)(2,1)S(1)} collective-permute-done((bf16[240,1536]{1,0:T(8,128)(2,1)}, bf16[240,1536]{1,0:T(8,128)(2,1)S(1)}, u32[]{:S(2)}, u32[]{:S(2)}) %collective-permute-start.5) | collective-permute-done | bytes 737312 | tf_op jit(solution)/shard_map/ppermute | solution.py:488
  23.4 4.2 %collective-permute-start.6 = (bf16[240,1536]{1,0:T(8,128)(2,1)S(1)}, bf16[240,1536]{1,0:T(8,128)(2,1)S(1)}, u32[]{:S(2)}, u32[]{:S(2)}) collective-permute-start(bf16[240,1536]{1,0:T(8,128)(2,1)S(1)} %collective-permute-done.5.refs_1_.first_ref), channel_id=1, source_target_pairs={{0,1},{1,3},{2,0},{3,2},{4,5},{5,7},{6,4},{7,6},{8,9},{9,11},{10,8... | collective-permute-start | bytes 2211848 | tf_op jit(solution)/shard_map/ppermute | solution.py:510
  27.6 0.0 collective-permute-done.2.refs_0_
  27.6 1.6 %collective-permute-done.refs_0_ = bf16[192,1536]{1,0:T(8,128)(2,1)} collective-permute-done((bf16[192,1536]{1,0:T(8,128)(2,1)}, bf16[192,1536]{1,0:T(8,128)(2,1)}, u32[]{:S(2)}, u32[]{:S(2)}) %collective-permute-start) | collective-permute-done | bytes 589856 | tf_op jit(solution)/shard_map/ppermute | solution.py:488
  29.2 0.0 collective-permute-done.3.far_front
  29.2 0.0 collective-permute-done.4.far_back.refs_2_
  29.2 4.9 %project.3 = (bf16[384,384]{1,0:T(8,128)(2,1)}, bf16[384,768]{1,0:T(8,128)(2,1)}) custom-call(s32[1]{0:T(128)} %bitcast.1.place_ref, f32[1,1536]{1,0:T(1,128)S(1)} %broadcast_in_dim.10.gain_ref, bf16[768,768]{1,0:T(8,128)(2,1)} %get-tuple-element.58.own_front, bf16[768,768]{1,0:T(8,128)(2,1)} %get-tuple-element.59.own_back, ...), custom_call_target="tpu_custom_call" | custom-call | flops 1 | bytes 1 | tf_op jit(solution)/shard_map/project/pallas_call | solution.py:182
  34.1 0.1 collective-permute-start.8
  34.2 3.5 %collective-permute-start.7 = (bf16[384,768]{1,0:T(8,128)(2,1)}, bf16[384,768]{1,0:T(8,128)(2,1)S(1)}, u32[]{:S(2)}, u32[]{:S(2)}) collective-permute-start(bf16[384,768]{1,0:T(8,128)(2,1)} %get-tuple-element.63.refs_3_), channel_id=1, source_target_pairs={{16,8},{20,12},{8,16},{12,20},{17,9},{21,13},{9,17},{13,21},{18,10... | collective-permute-start | bytes 1769480 | tf_op jit(solution)/shard_map/ppermute | solution.py:507
  37.7 6.1 %collective-permute-done.6.refs_0_.second_ref = bf16[240,1536]{1,0:T(8,128)(2,1)S(1)} collective-permute-done((bf16[240,1536]{1,0:T(8,128)(2,1)S(1)}, bf16[240,1536]{1,0:T(8,128)(2,1)S(1)}, u32[]{:S(2)}, u32[]{:S(2)}) %collective-permute-start.6) | collective-permute-done | bytes 737312 | tf_op jit(solution)/shard_map/ppermute | solution.py:510
  43.8 0.0 collective-permute-done.8.refs_6_
  43.8 1.8 %collective-permute-done.7.refs_9_ = bf16[384,768]{1,0:T(8,128)(2,1)S(1)} collective-permute-done((bf16[384,768]{1,0:T(8,128)(2,1)}, bf16[384,768]{1,0:T(8,128)(2,1)S(1)}, u32[]{:S(2)}, u32[]{:S(2)}) %collective-permute-start.7) | collective-permute-done | bytes 589856 | tf_op jit(solution)/shard_map/ppermute | solution.py:507
  45.6 1.8 %collective-permute-start.9 = (bf16[240,1536]{1,0:T(8,128)(2,1)S(1)}, bf16[240,1536]{1,0:T(8,128)(2,1)S(1)}, u32[]{:S(2)}, u32[]{:S(2)}) collective-permute-start(bf16[240,1536]{1,0:T(8,128)(2,1)S(1)} %collective-permute-done.6.refs_0_.second_ref), channel_id=1, source_target_pairs={{0,1},{1,3},{2,0},{3,2},{4,5},{5,7},{6,4},{7,6},{8,9},{9,11},{10,8... | collective-permute-start | bytes 2211848 | tf_op jit(solution)/shard_map/ppermute | solution.py:510
  47.4 1.2 %join.1.refs_12_ = bf16[144,1536]{1,0:T(8,128)(2,1)} custom-call(bf16[240,1536]{1,0:T(8,128)(2,1)S(1)} %collective-permute-done.5.refs_1_.first_ref, bf16[240,1536]{1,0:T(8,128)(2,1)S(1)} %collective-permute-done.6.refs_0_.second_ref, bf16[96,768]{1,0:T(8,128)(2,1)S(1)} %hold.2.piece_ref), custom_call_target="tpu_custom_call" | custom-call | flops 1 | bytes 1 | tf_op jit(solution)/shard_map/join/pallas_call | solution.py:126
  48.6 0.1 collective-permute-start.15
  48.7 1.5 %collective-permute-start.14 = (bf16[144,1536]{1,0:T(8,128)(2,1)}, bf16[144,1536]{1,0:T(8,128)(2,1)S(1)}, u32[]{:S(2)}, u32[]{:S(2)}) collective-permute-start(bf16[144,1536]{1,0:T(8,128)(2,1)} %join.1.refs_12_), channel_id=1, source_target_pairs={{0,4},{4,0},{8,12},{12,8},{1,5},{5,1},{9,13},{13,9},{2,6},{6,2},{1... | collective-permute-start | bytes 1327112 | tf_op jit(solution)/shard_map/ppermute | solution.py:498
  50.2 3.4 %project.4 = (bf16[192,384]{1,0:T(8,128)(2,1)}, bf16[192,768]{1,0:T(8,128)(2,1)}) custom-call(s32[1]{0:T(128)} %bitcast.1.place_ref, f32[1,1536]{1,0:T(1,128)S(1)} %broadcast_in_dim.10.gain_ref, bf16[768,768]{1,0:T(8,128)(2,1)} %get-tuple-element.58.own_front, bf16[768,768]{1,0:T(8,128)(2,1)} %get-tuple-element.59.own_back, ...), custom_call_target="tpu_custom_call" | custom-call | flops 1 | bytes 1 | tf_op jit(solution)/shard_map/project/pallas_call | solution.py:182
  53.6 2.1 %collective-permute-start.11 = (bf16[192,768]{1,0:T(8,128)(2,1)}, bf16[192,768]{1,0:T(8,128)(2,1)S(1)}, u32[]{:S(2)}, u32[]{:S(2)}) collective-permute-start(bf16[192,768]{1,0:T(8,128)(2,1)} %get-tuple-element.66.refs_4_), channel_id=1, source_target_pairs={{0,16},{16,0},{1,17},{17,1},{2,18},{18,2},{3,19},{19,3},{4,20},{20... | collective-permute-start | bytes 884744 | tf_op jit(solution)/shard_map/ppermute | solution.py:507
  55.7 1.9 %collective-permute-start.10 = (bf16[192,768]{1,0:T(8,128)(2,1)}, bf16[192,768]{1,0:T(8,128)(2,1)S(1)}, u32[]{:S(2)}, u32[]{:S(2)}) collective-permute-start(bf16[192,768]{1,0:T(8,128)(2,1)} %get-tuple-element.66.refs_4_), channel_id=1, source_target_pairs={{16,8},{20,12},{8,16},{12,20},{17,9},{21,13},{9,17},{13,21},{18,10... | collective-permute-start | bytes 884744 | tf_op jit(solution)/shard_map/ppermute | solution.py:507
  57.6 3.2 %collective-permute-done.15.refs_14_ = bf16[144,1536]{1,0:T(8,128)(2,1)S(1)} collective-permute-done((bf16[144,1536]{1,0:T(8,128)(2,1)}, bf16[144,1536]{1,0:T(8,128)(2,1)S(1)}, u32[]{:S(2)}, u32[]{:S(2)}) %collective-permute-start.15) | collective-permute-done | bytes 442400 | tf_op jit(solution)/shard_map/ppermute | solution.py:498
  60.8 0.0 collective-permute-done.14.refs_13_
  60.8 1.5 %collective-permute-start.16 = (bf16[144,1536]{1,0:T(8,128)(2,1)S(1)}, bf16[144,1536]{1,0:T(8,128)(2,1)S(1)}, u32[]{:S(2)}, u32[]{:S(2)}) collective-permute-start(bf16[144,1536]{1,0:T(8,128)(2,1)S(1)} %collective-permute-done.15.refs_14_), channel_id=1, source_target_pairs={{0,4},{4,0},{8,12},{12,8},{1,5},{5,1},{9,13},{13,9},{2,6},{6,2},{1... | collective-permute-start | bytes 1327112 | tf_op jit(solution)/shard_map/ppermute | solution.py:500
  62.3 0.0 collective-permute-done.11.refs_7_
  62.3 1.9 %collective-permute-done.10.refs_10_ = bf16[192,768]{1,0:T(8,128)(2,1)S(1)} collective-permute-done((bf16[192,768]{1,0:T(8,128)(2,1)}, bf16[192,768]{1,0:T(8,128)(2,1)S(1)}, u32[]{:S(2)}, u32[]{:S(2)}) %collective-permute-start.10) | collective-permute-done | bytes 294944 | tf_op jit(solution)/shard_map/ppermute | solution.py:507
  64.2 0.3 collective-permute-done.9.refs_0_
  64.6 3.4 %project.5 = (bf16[192,384]{1,0:T(8,128)(2,1)}, bf16[192,768]{1,0:T(8,128)(2,1)}) custom-call(s32[1]{0:T(128)} %bitcast.1.place_ref, f32[1,1536]{1,0:T(1,128)S(1)} %broadcast_in_dim.10.gain_ref, bf16[768,768]{1,0:T(8,128)(2,1)} %get-tuple-element.58.own_front, bf16[768,768]{1,0:T(8,128)(2,1)} %get-tuple-element.59.own_back, ...), custom_call_target="tpu_custom_call" | custom-call | flops 1 | bytes 1 | tf_op jit(solution)/shard_map/project/pallas_call | solution.py:182
  67.9 2.7 %collective-permute-start.13 = (bf16[192,768]{1,0:T(8,128)(2,1)}, bf16[192,768]{1,0:T(8,128)(2,1)S(1)}, u32[]{:S(2)}, u32[]{:S(2)}) collective-permute-start(bf16[192,768]{1,0:T(8,128)(2,1)} %get-tuple-element.69.refs_5_), channel_id=1, source_target_pairs={{16,8},{20,12},{8,16},{12,20},{17,9},{21,13},{9,17},{13,21},{18,10... | collective-permute-start | bytes 884744 | tf_op jit(solution)/shard_map/ppermute | solution.py:507
  70.6 0.1 collective-permute-start.12
  70.7 1.1 %collective-permute-done.16.refs_15_ = bf16[144,1536]{1,0:T(8,128)(2,1)S(1)} collective-permute-done((bf16[144,1536]{1,0:T(8,128)(2,1)S(1)}, bf16[144,1536]{1,0:T(8,128)(2,1)S(1)}, u32[]{:S(2)}, u32[]{:S(2)}) %collective-permute-start.16) | collective-permute-done | bytes 442400 | tf_op jit(solution)/shard_map/ppermute | solution.py:500
  71.8 4.4 %collective-permute-done.13.refs_11_ = bf16[192,768]{1,0:T(8,128)(2,1)S(1)} collective-permute-done((bf16[192,768]{1,0:T(8,128)(2,1)}, bf16[192,768]{1,0:T(8,128)(2,1)S(1)}, u32[]{:S(2)}, u32[]{:S(2)}) %collective-permute-start.13) | collective-permute-done | bytes 294944 | tf_op jit(solution)/shard_map/ppermute | solution.py:507
  76.2 0.0 collective-permute-done.12.refs_8_
  76.2 3.7 %window.1 = (bf16[768,384]{1,0:T(8,128)(2,1)S(1)}, bf16[2304,768]{1,0:T(8,128)(2,1)S(1)}, bf16[3,18,128,128]{3,2,1,0:T(8,128)(2,1)S(1)}, bf16[576,1536]{1,0:T(8,128)(2,1)}) custom-call(s32[8]{0:T(128)S(1)} %stack.77.place_ref, bf16[384,384]{1,0:T(8,128)(2,1)} %get-tuple-element.62.refs_0_, bf16[192,384]{1,0:T(8,128)(2,1)} %get-tuple-element.65.refs_1_, ...), custom_call_target="tpu_custom_call" | custom-call | bytes 8257536 | tf_op jit(solution)/shard_map/window/pallas_call | solution.py:244
  79.9 0.1 collective-permute-start.17
  80.0 5.0 %attend.2 = (bf16[192,384]{1,0:T(8,128)(2,1)}, bf16[192,384]{1,0:T(8,128)(2,1)}) custom-call(s32[8]{0:T(128)S(1)} %stack.77.place_ref, s32[6,12]{1,0:T(8,128)S(1)} %bitcast.24, s32[3]{0:T(128)S(1)} %get-tuple-element.56.turn_ref, bf16[768,384]{1,0:T(8,128)(2,1)S(1)} %get-tuple-element.81.q_all, bf16[2304,768]{1,0:T(8,128)(2,1)S(1)} %get-tuple-element.78.kv_all, ...), custom_call_target="tpu_custom_call" | custom-call | flops 17179869184 | bytes 1048576 | tf_op jit(solution)/shard_map/attend/pallas_call | solution.py:403
  85.0 0.0 copy-start.2
  85.0 2.4 %collective-permute-start.18 = (bf16[192,384]{1,0:T(8,128)(2,1)}, bf16[192,384]{1,0:T(8,128)(2,1)S(1)}, u32[]{:S(2)}, u32[]{:S(2)}) collective-permute-start(bf16[192,384]{1,0:T(8,128)(2,1)} %get-tuple-element.85), channel_id=1, source_target_pairs={{0,2},{1,3},{2,0},{3,1},{4,18},{5,19},{6,16},{7,17},{8,10},{9,11},... | collective-permute-start | bytes 442376 | tf_op jit(solution)/shard_map/ppermute | solution.py:488
  87.3 0.0 collective-permute-done.17.refs_4_
  87.4 6.6 %attend.3 = (bf16[192,384]{1,0:T(8,128)(2,1)}, bf16[192,384]{1,0:T(8,128)(2,1)}, bf16[4,2,384,768]{3,2,1,0:T(8,128)(2,1)S(1)}) custom-call(s32[8]{0:T(128)S(1)} %stack.77.place_ref, s32[6,12]{1,0:T(8,128)S(1)} %bitcast.25, s32[3]{0:T(128)S(1)} %get-tuple-element.55.turn_ref, bf16[768,384]{1,0:T(8,128)(2,1)S(1)} %get-tuple-element.81.q_all, ...), custom_call_target="tpu_custom_call" | custom-call | flops 17179869184 | bytes 1048576 | tf_op jit(solution)/shard_map/attend/pallas_call | solution.py:403
  94.0 0.0 copy-done.2
  94.0 2.0 %collective-permute-start.19 = (bf16[192,384]{1,0:T(8,128)(2,1)S(1)}, bf16[192,384]{1,0:T(8,128)(2,1)S(1)}, u32[]{:S(2)}, u32[]{:S(2)}) collective-permute-start(bf16[192,384]{1,0:T(8,128)(2,1)S(1)} %copy-done.2), channel_id=1, source_target_pairs={{0,3},{1,2},{2,1},{3,0},{4,19},{5,18},{6,17},{7,16},{8,11},{9,10},... | collective-permute-start | bytes 442376 | tf_op jit(solution)/shard_map/ppermute | solution.py:488
  96.0 3.2 %collective-permute-start.20 = (bf16[192,384]{1,0:T(8,128)(2,1)}, bf16[192,384]{1,0:T(8,128)(2,1)S(1)}, u32[]{:S(2)}, u32[]{:S(2)}) collective-permute-start(bf16[192,384]{1,0:T(8,128)(2,1)} %get-tuple-element.89), channel_id=1, source_target_pairs={{0,0},{1,1},{2,2},{3,3},{4,16},{5,17},{6,18},{7,19},{8,8},{9,9},{1... | collective-permute-start | bytes 442376 | tf_op jit(solution)/shard_map/ppermute | solution.py:488
  99.2 0.5 collective-permute-start.21
  99.7 0.0 collective-permute-done.18.refs_0_
  99.7 2.1 %collective-permute-done.19.refs_1_ = bf16[192,384]{1,0:T(8,128)(2,1)S(1)} collective-permute-done((bf16[192,384]{1,0:T(8,128)(2,1)S(1)}, bf16[192,384]{1,0:T(8,128)(2,1)S(1)}, u32[]{:S(2)}, u32[]{:S(2)}) %collective-permute-start.19) | collective-permute-done | bytes 147488 | tf_op jit(solution)/shard_map/ppermute | solution.py:488
  101.7 1.5 %collective-permute-done.20.refs_2_ = bf16[192,384]{1,0:T(8,128)(2,1)S(1)} collective-permute-done((bf16[192,384]{1,0:T(8,128)(2,1)}, bf16[192,384]{1,0:T(8,128)(2,1)S(1)}, u32[]{:S(2)}, u32[]{:S(2)}) %collective-permute-start.20) | collective-permute-done | bytes 147488 | tf_op jit(solution)/shard_map/ppermute | solution.py:488
  103.2 1.7 %collective-permute-done.21.refs_3_ = bf16[192,384]{1,0:T(8,128)(2,1)S(1)} collective-permute-done((bf16[192,384]{1,0:T(8,128)(2,1)}, bf16[192,384]{1,0:T(8,128)(2,1)S(1)}, u32[]{:S(2)}, u32[]{:S(2)}) %collective-permute-start.21) | collective-permute-done | bytes 147488 | tf_op jit(solution)/shard_map/ppermute | solution.py:488
  104.9 3.6 %output.1 = bf16[1,192,1536]{2,1,0:T(8,128)(2,1)} custom-call(s32[4]{0:T(128)S(1)} %pad_add_fusion.place_ref, bf16[4,2,384,768]{3,2,1,0:T(8,128)(2,1)S(1)} %get-tuple-element.84.weight, bf16[192,384]{1,0:T(8,128)(2,1)S(1)} %hold.3.refs_0_, bf16[192,384]{1,0:T(8,128)(2,1)S(1)} %collective-permute-done.19.refs_1_, ...), custom_call_target="tpu_custom_call" | custom-call | flops 1 | bytes 1 | tf_op jit(solution)/shard_map/output/pallas_call | solution.py:436
  (6 shorter events, 0.0 us)
Async XLA Ops:
  0.0 17.5 %copy-start = (f32[1536]{0:T(1024)S(1)}, f32[1536]{0:T(1024)}, u32[]{:S(2)}) copy-start(f32[1536]{0:T(1024)} %param.9) | copy-start | bytes 18436
  2.1 14.2 %copy-start.1 = (bf16[96,768]{1,0:T(8,128)(2,1)S(1)}, bf16[96,768]{1,0:T(8,128)(2,1)}, u32[]{:S(2)}) copy-start(bf16[96,768]{1,0:T(8,128)(2,1)} %get-tuple-element.51) | copy-start | bytes 442372
  2.1 21.3 %collective-permute-start.5 = (bf16[240,1536]{1,0:T(8,128)(2,1)}, bf16[240,1536]{1,0:T(8,128)(2,1)S(1)}, u32[]{:S(2)}, u32[]{:S(2)}) collective-permute-start(bf16[240,1536]{1,0:T(8,128)(2,1)} %get-tuple-element.61), channel_id=1, source_target_pairs={{0,1},{1,3},{2,0},{3,2},{4,17},{5,19},{6,16},{7,18},{8,9},{9,11},{... | collective-permute-start | bytes 2211848 | tf_op jit(solution)/shard_map/ppermute | solution.py:488
  7.1 5.2 %collective-permute-start.1 = (s32[7,12]{1,0:T(8,128)S(1)}, s32[7,12]{1,0:T(8,128)S(1)}, u32[]{:S(2)}, u32[]{:S(2)}) collective-permute-start(s32[7,12]{1,0:T(8,128)S(1)} %concatenate.3), channel_id=1, source_target_pairs={{0,0},{4,16},{8,8},{12,24},{16,4},{20,20},{24,12},{28,28},{1,1},{5... | collective-permute-start | bytes 1016 | tf_op jit(solution)/shard_map/ppermute | solution.py:519
  12.4 16.8 %collective-permute-start.3 = (bf16[768,768]{1,0:T(8,128)(2,1)}, bf16[768,768]{1,0:T(8,128)(2,1)S(1)}, u32[]{:S(2)}, u32[]{:S(2)}) collective-permute-start(bf16[768,768]{1,0:T(8,128)(2,1)} %get-tuple-element.58.own_front), channel_id=1, source_target_pairs={{0,16},{16,0},{1,17},{17,1},{2,18},{18,2},{3,19},{19,3},{4,20},{20... | collective-permute-start | bytes 3538952 | tf_op jit(solution)/shard_map/ppermute | solution.py:521
  12.4 16.8 %collective-permute-start.4 = (bf16[768,768]{1,0:T(8,128)(2,1)}, bf16[768,768]{1,0:T(8,128)(2,1)S(1)}, u32[]{:S(2)}, u32[]{:S(2)}) collective-permute-start(bf16[768,768]{1,0:T(8,128)(2,1)} %get-tuple-element.59.own_back), channel_id=1, source_target_pairs={{0,16},{16,0},{1,17},{17,1},{2,18},{18,2},{3,19},{19,3},{4,20},{20... | collective-permute-start | bytes 3538952 | tf_op jit(solution)/shard_map/ppermute | solution.py:521
  12.9 16.3 %collective-permute-start = (bf16[192,1536]{1,0:T(8,128)(2,1)}, bf16[192,1536]{1,0:T(8,128)(2,1)}, u32[]{:S(2)}, u32[]{:S(2)}) collective-permute-start(bf16[192,1536]{1,0:T(8,128)(2,1)} %bitcast.rows_ref), channel_id=1, source_target_pairs={{0,0},{1,1},{2,2},{3,3},{4,16},{5,17},{6,18},{7,19},{8,8},{9,9},{1... | collective-permute-start | bytes 1769480 | tf_op jit(solution)/shard_map/ppermute | solution.py:488
  16.3 11.2 %collective-permute-start.2 = (bf16[96,768]{1,0:T(8,128)(2,1)S(1)}, bf16[96,768]{1,0:T(8,128)(2,1)S(1)}, u32[]{:S(2)}, u32[]{:S(2)}) collective-permute-start(bf16[96,768]{1,0:T(8,128)(2,1)S(1)} %copy-done.1), channel_id=1, source_target_pairs={{0,2},{1,0},{2,3},{3,1},{4,18},{5,16},{6,19},{7,17},{8,10},{9,8},{... | collective-permute-start | bytes 442376 | tf_op jit(solution)/shard_map/ppermute | solution.py:488
  23.4 20.4 %collective-permute-start.6 = (bf16[240,1536]{1,0:T(8,128)(2,1)S(1)}, bf16[240,1536]{1,0:T(8,128)(2,1)S(1)}, u32[]{:S(2)}, u32[]{:S(2)}) collective-permute-start(bf16[240,1536]{1,0:T(8,128)(2,1)S(1)} %collective-permute-done.5.refs_1_.first_ref), channel_id=1, source_target_pairs={{0,1},{1,3},{2,0},{3,2},{4,5},{5,7},{6,4},{7,6},{8,9},{9,11},{10,8... | collective-permute-start | bytes 2211848 | tf_op jit(solution)/shard_map/ppermute | solution.py:510
  34.1 9.7 %collective-permute-start.8 = (bf16[384,768]{1,0:T(8,128)(2,1)}, bf16[384,768]{1,0:T(8,128)(2,1)S(1)}, u32[]{:S(2)}, u32[]{:S(2)}) collective-permute-start(bf16[384,768]{1,0:T(8,128)(2,1)} %get-tuple-element.63.refs_3_), channel_id=1, source_target_pairs={{0,16},{16,0},{1,17},{17,1},{2,18},{18,2},{3,19},{19,3},{4,20},{20... | collective-permute-start | bytes 1769480 | tf_op jit(solution)/shard_map/ppermute | solution.py:507
  34.2 11.4 %collective-permute-start.7 = (bf16[384,768]{1,0:T(8,128)(2,1)}, bf16[384,768]{1,0:T(8,128)(2,1)S(1)}, u32[]{:S(2)}, u32[]{:S(2)}) collective-permute-start(bf16[384,768]{1,0:T(8,128)(2,1)} %get-tuple-element.63.refs_3_), channel_id=1, source_target_pairs={{16,8},{20,12},{8,16},{12,20},{17,9},{21,13},{9,17},{13,21},{18,10... | collective-permute-start | bytes 1769480 | tf_op jit(solution)/shard_map/ppermute | solution.py:507
  45.6 18.9 %collective-permute-start.9 = (bf16[240,1536]{1,0:T(8,128)(2,1)S(1)}, bf16[240,1536]{1,0:T(8,128)(2,1)S(1)}, u32[]{:S(2)}, u32[]{:S(2)}) collective-permute-start(bf16[240,1536]{1,0:T(8,128)(2,1)S(1)} %collective-permute-done.6.refs_0_.second_ref), channel_id=1, source_target_pairs={{0,1},{1,3},{2,0},{3,2},{4,5},{5,7},{6,4},{7,6},{8,9},{9,11},{10,8... | collective-permute-start | bytes 2211848 | tf_op jit(solution)/shard_map/ppermute | solution.py:510
  48.6 12.2 %collective-permute-start.15 = (bf16[144,1536]{1,0:T(8,128)(2,1)}, bf16[144,1536]{1,0:T(8,128)(2,1)S(1)}, u32[]{:S(2)}, u32[]{:S(2)}) collective-permute-start(bf16[144,1536]{1,0:T(8,128)(2,1)} %join.1.refs_12_), channel_id=1, source_target_pairs={{0,8},{4,12},{8,0},{12,4},{1,9},{5,13},{9,1},{13,5},{2,10},{6,14},... | collective-permute-start | bytes 1327112 | tf_op jit(solution)/shard_map/ppermute | solution.py:498
  48.7 12.1 %collective-permute-start.14 = (bf16[144,1536]{1,0:T(8,128)(2,1)}, bf16[144,1536]{1,0:T(8,128)(2,1)S(1)}, u32[]{:S(2)}, u32[]{:S(2)}) collective-permute-start(bf16[144,1536]{1,0:T(8,128)(2,1)} %join.1.refs_12_), channel_id=1, source_target_pairs={{0,4},{4,0},{8,12},{12,8},{1,5},{5,1},{9,13},{13,9},{2,6},{6,2},{1... | collective-permute-start | bytes 1327112 | tf_op jit(solution)/shard_map/ppermute | solution.py:498
  53.6 8.7 %collective-permute-start.11 = (bf16[192,768]{1,0:T(8,128)(2,1)}, bf16[192,768]{1,0:T(8,128)(2,1)S(1)}, u32[]{:S(2)}, u32[]{:S(2)}) collective-permute-start(bf16[192,768]{1,0:T(8,128)(2,1)} %get-tuple-element.66.refs_4_), channel_id=1, source_target_pairs={{0,16},{16,0},{1,17},{17,1},{2,18},{18,2},{3,19},{19,3},{4,20},{20... | collective-permute-start | bytes 884744 | tf_op jit(solution)/shard_map/ppermute | solution.py:507
  55.7 8.5 %collective-permute-start.10 = (bf16[192,768]{1,0:T(8,128)(2,1)}, bf16[192,768]{1,0:T(8,128)(2,1)S(1)}, u32[]{:S(2)}, u32[]{:S(2)}) collective-permute-start(bf16[192,768]{1,0:T(8,128)(2,1)} %get-tuple-element.66.refs_4_), channel_id=1, source_target_pairs={{16,8},{20,12},{8,16},{12,20},{17,9},{21,13},{9,17},{13,21},{18,10... | collective-permute-start | bytes 884744 | tf_op jit(solution)/shard_map/ppermute | solution.py:507
  60.8 11.0 %collective-permute-start.16 = (bf16[144,1536]{1,0:T(8,128)(2,1)S(1)}, bf16[144,1536]{1,0:T(8,128)(2,1)S(1)}, u32[]{:S(2)}, u32[]{:S(2)}) collective-permute-start(bf16[144,1536]{1,0:T(8,128)(2,1)S(1)} %collective-permute-done.15.refs_14_), channel_id=1, source_target_pairs={{0,4},{4,0},{8,12},{12,8},{1,5},{5,1},{9,13},{13,9},{2,6},{6,2},{1... | collective-permute-start | bytes 1327112 | tf_op jit(solution)/shard_map/ppermute | solution.py:500
  67.9 8.3 %collective-permute-start.13 = (bf16[192,768]{1,0:T(8,128)(2,1)}, bf16[192,768]{1,0:T(8,128)(2,1)S(1)}, u32[]{:S(2)}, u32[]{:S(2)}) collective-permute-start(bf16[192,768]{1,0:T(8,128)(2,1)} %get-tuple-element.69.refs_5_), channel_id=1, source_target_pairs={{16,8},{20,12},{8,16},{12,20},{17,9},{21,13},{9,17},{13,21},{18,10... | collective-permute-start | bytes 884744 | tf_op jit(solution)/shard_map/ppermute | solution.py:507
  70.6 5.6 %collective-permute-start.12 = (bf16[192,768]{1,0:T(8,128)(2,1)}, bf16[192,768]{1,0:T(8,128)(2,1)S(1)}, u32[]{:S(2)}, u32[]{:S(2)}) collective-permute-start(bf16[192,768]{1,0:T(8,128)(2,1)} %get-tuple-element.69.refs_5_), channel_id=1, source_target_pairs={{0,16},{16,0},{1,17},{17,1},{2,18},{18,2},{3,19},{19,3},{4,20},{20... | collective-permute-start | bytes 884744 | tf_op jit(solution)/shard_map/ppermute | solution.py:507
  79.9 7.5 %collective-permute-start.17 = (bf16[576,1536]{1,0:T(8,128)(2,1)}, bf16[576,1536]{1,0:T(8,128)(2,1)S(1)}, u32[]{:S(2)}, u32[]{:S(2)}) collective-permute-start(bf16[576,1536]{1,0:T(8,128)(2,1)} %get-tuple-element.83.refs_3_), channel_id=1, source_target_pairs={{0,16},{16,0},{1,17},{17,1},{2,18},{18,2},{3,19},{19,3},{4,20},{20... | collective-permute-start | bytes 5308424 | tf_op jit(solution)/shard_map/ppermute | solution.py:555
  85.0 9.0 %copy-start.2 = (bf16[192,384]{1,0:T(8,128)(2,1)S(1)}, bf16[192,384]{1,0:T(8,128)(2,1)}, u32[]{:S(2)}) copy-start(bf16[192,384]{1,0:T(8,128)(2,1)} %get-tuple-element.88) | copy-start | bytes 442372
  85.0 14.7 %collective-permute-start.18 = (bf16[192,384]{1,0:T(8,128)(2,1)}, bf16[192,384]{1,0:T(8,128)(2,1)S(1)}, u32[]{:S(2)}, u32[]{:S(2)}) collective-permute-start(bf16[192,384]{1,0:T(8,128)(2,1)} %get-tuple-element.85), channel_id=1, source_target_pairs={{0,2},{1,3},{2,0},{3,1},{4,18},{5,19},{6,16},{7,17},{8,10},{9,11},... | collective-permute-start | bytes 442376 | tf_op jit(solution)/shard_map/ppermute | solution.py:488
  94.0 7.8 %collective-permute-start.19 = (bf16[192,384]{1,0:T(8,128)(2,1)S(1)}, bf16[192,384]{1,0:T(8,128)(2,1)S(1)}, u32[]{:S(2)}, u32[]{:S(2)}) collective-permute-start(bf16[192,384]{1,0:T(8,128)(2,1)S(1)} %copy-done.2), channel_id=1, source_target_pairs={{0,3},{1,2},{2,1},{3,0},{4,19},{5,18},{6,17},{7,16},{8,11},{9,10},... | collective-permute-start | bytes 442376 | tf_op jit(solution)/shard_map/ppermute | solution.py:488
  96.0 7.2 %collective-permute-start.20 = (bf16[192,384]{1,0:T(8,128)(2,1)}, bf16[192,384]{1,0:T(8,128)(2,1)S(1)}, u32[]{:S(2)}, u32[]{:S(2)}) collective-permute-start(bf16[192,384]{1,0:T(8,128)(2,1)} %get-tuple-element.89), channel_id=1, source_target_pairs={{0,0},{1,1},{2,2},{3,3},{4,16},{5,17},{6,18},{7,19},{8,8},{9,9},{1... | collective-permute-start | bytes 442376 | tf_op jit(solution)/shard_map/ppermute | solution.py:488
  99.2 5.7 %collective-permute-start.21 = (bf16[192,384]{1,0:T(8,128)(2,1)}, bf16[192,384]{1,0:T(8,128)(2,1)S(1)}, u32[]{:S(2)}, u32[]{:S(2)}) collective-permute-start(bf16[192,384]{1,0:T(8,128)(2,1)} %get-tuple-element.90), channel_id=1, source_target_pairs={{0,1},{1,0},{2,3},{3,2},{4,17},{5,16},{6,19},{7,18},{8,9},{9,8},{1... | collective-permute-start | bytes 442376 | tf_op jit(solution)/shard_map/ppermute | solution.py:488

commit v9 on v8

--- a/solution.py
+++ b/solution.py
@@ -78,29 +78,30 @@
     )(place, *in_hbm(rows, w_out))
 
 
-def bundle_kernel(query_ref, key_ref, value_ref, w_out_ref, front_ref, back_ref, held, held_back, sems):
+def bundle_kernel(query_ref, key_ref, value_ref, w_out_ref, front_ref, back_ref, sems):
     width, rows = query_ref.shape[1], w_out_ref.shape[0]
     loads = [
-        (query_ref, held.at[:, pl.ds(0, width)]),
-        (key_ref, held.at[:, pl.ds(width, width)]),
-        (value_ref, held_back.at[:, pl.ds(0, width)]),
+        (query_ref, front_ref.at[:, pl.ds(0, width)]),
+        (key_ref, front_ref.at[:, pl.ds(width, width)]),
+        (value_ref, back_ref.at[:, pl.ds(0, width)]),
     ]
     for side in range(2):
         loads.append((
             w_out_ref.at[:, pl.ds(side * width, width)],
-            held_back.at[pl.ds(side * rows, rows), pl.ds(width, width)],
+            back_ref.at[pl.ds(side * rows, rows), pl.ds(width, width)],
         ))
-    run_copies(loads, [(held, front_ref), (held_back, back_ref)], sems)
+    for load in copy_all(loads, sems):
+        load.wait()
 
 
 def bundle(w_query, w_key, w_value, w_out):
     shape = (w_query.shape[0], 2 * w_query.shape[1])
     return pl.pallas_call(
         bundle_kernel,
-        out_shape=[pltpu.HBM(shape, jnp.bfloat16)] * 2,
+        out_shape=[jax.ShapeDtypeStruct(shape, jnp.bfloat16)] * 2,
         in_specs=[HBM] * 4,
-        out_specs=[HBM] * 2,
-        scratch_shapes=[pltpu.VMEM(shape, jnp.bfloat16)] * 2 + [pltpu.SemaphoreType.DMA((5,))],
+        out_specs=[VMEM] * 2,
+        scratch_shapes=[pltpu.SemaphoreType.DMA((5,))],
         compiler_params=pltpu.CompilerParams(vmem_limit_bytes=4 * MIB),
         cost_estimate=LIGHT,
         name="bundle",
@@ -137,34 +138,32 @@
 
 def project_kernel(blocks, count, place_ref, gain_ref, own_front, own_back, far_front, far_back, *refs):
     rows = refs[:blocks]
-    query_ref, pair_ref, held, weight, query_held, pair_held, sems = refs[blocks:]
+    query_ref, pair_ref, held, query_held, pair_held, sems = refs[blocks:]
     depth, width = own_front.shape[0], query_ref.shape[1]
-    core = place_ref[0]
-    order = (1, 2, 0)
+    first = place_ref[0] == 0
     loads = copy_all(
         [(rows[i].at[pl.ds(0, count), :], held.at[pl.ds(i * count, count), :]) for i in range(blocks)], sems
     )
-    fetches = []
-    for place in order:
-        for pair, owner in (((own_front, own_back), core), ((far_front, far_back), 1 - core)):
-            to = weight.at[place, pl.ds(pl.multiple_of(owner * depth, 16), depth), :]
-            fetches.append((pair[place // 2].at[:, pl.ds(place % 2 * width, width)], to))
-    fetches = copy_all(fetches, sems.at[pl.ds(blocks, len(fetches))])
     gain = gain_ref[...]
-    normalized = []
+    mine, theirs = [], []
     for i in range(blocks):
         loads[i].wait()
         values = held[i * count:(i + 1) * count, :].astype(jnp.float32)
         center = values - jnp.mean(values, axis=-1, keepdims=True)
         spread = jnp.mean(center * center, axis=-1, keepdims=True)
-        normalized.append((center * lax.rsqrt(spread + epsilon) * gain).astype(jnp.bfloat16))
-    normalized = normalized[0] if blocks == 1 else jnp.concatenate(normalized, axis=0)
+        normalized = (center * lax.rsqrt(spread + epsilon) * gain).astype(jnp.bfloat16)
+        low, high = normalized[:, :depth], normalized[:, depth:]
+        mine.append(jnp.where(first, low, high))
+        theirs.append(jnp.where(first, high, low))
+    mine = mine[0] if blocks == 1 else jnp.concatenate(mine, axis=0)
+    theirs = theirs[0] if blocks == 1 else jnp.concatenate(theirs, axis=0)
     stores = []
-    for turn, place in enumerate(order):
-        for fetch in fetches[2 * turn:2 * turn + 2]:
-            fetch.wait()
-        got = jnp.dot(normalized, weight[place], preferred_element_type=jnp.float32).astype(jnp.bfloat16)
-        sem = sems.at[pl.ds(blocks + len(fetches) + place, 1)]
+    for place in (1, 2, 0):
+        own, far = ((own_front, far_front), (own_back, far_back))[place // 2]
+        columns = slice(place % 2 * width, (place % 2 + 1) * width)
+        got = jnp.dot(mine, own[:, columns], preferred_element_type=jnp.float32)
+        got = (got + jnp.dot(theirs, far[:, columns], preferred_element_type=jnp.float32)).astype(jnp.bfloat16)
+        sem = sems.at[pl.ds(blocks + place, 1)]
         if place == 0:
             query_held[...] = (got.astype(jnp.float32) * (HD ** -0.5)).astype(jnp.bfloat16)
             stores += copy_all([(query_held, query_ref)], sem)
@@ -182,19 +181,18 @@
     return pl.pallas_call(
         functools.partial(project_kernel, blocks, count),
         out_shape=[pltpu.HBM((total, width), jnp.bfloat16), pltpu.HBM((total, 2 * width), jnp.bfloat16)],
-        in_specs=[SMEM, VMEM] + [HBM] * (4 + blocks),
+        in_specs=[SMEM] + [VMEM] * 5 + [HBM] * blocks,
         out_specs=[HBM, HBM],
         scratch_shapes=[
             pltpu.VMEM((total, depth), jnp.bfloat16),
-            pltpu.VMEM((3, depth, width), jnp.bfloat16),
             pltpu.VMEM((total, width), jnp.bfloat16),
             pltpu.VMEM((total, 2 * width), jnp.bfloat16),
-            pltpu.SemaphoreType.DMA((blocks + 9,)),
+            pltpu.SemaphoreType.DMA((blocks + 3,)),
         ],
         compiler_params=pltpu.CompilerParams(vmem_limit_bytes=16 * MIB),
         cost_estimate=pl.CostEstimate(flops=cost, bytes_accessed=1, transcendentals=0),
         name="project",
-    )(place, gain, *in_hbm(*own), *far, *rows)
+    )(place, gain, *own, *far, *rows)
 
 
 def window_kernel(shape, groups, joined, place_ref, *refs):
@@ -413,32 +411,24 @@
 
 
 def output_kernel(layers, place_ref, weight, *refs):
-    contexts, out_ref, held, sems = refs[:layers], *refs[layers:]
+    contexts, out_ref = refs[:layers], refs[layers]
     columns = weight.shape[3]
-    rows = contexts[0].shape[0]
-    loads = copy_all([(contexts[step], held.at[pl.ds(step * rows, rows), :]) for step in range(layers)], sems)
-    for load in loads:
-        load.wait()
     for side in range(2):
         total = None
         for step in range(layers):
-            got = jnp.dot(
-                held[step * rows:(step + 1) * rows, :], weight[place_ref[step], side],
-                preferred_element_type=jnp.float32,
-            )
+            got = jnp.dot(contexts[step][...], weight[place_ref[step], side], preferred_element_type=jnp.float32)
             total = got if step == 0 else total + got
         out_ref[0, :, side * columns:(side + 1) * columns] = total.astype(jnp.bfloat16)
 
 
 def output(place, weight, contexts):
     layers, _, depth, columns = weight.shape
-    rows, width = contexts[0].shape
+    rows = contexts[0].shape[0]
     return pl.pallas_call(
         functools.partial(output_kernel, layers),
         out_shape=jax.ShapeDtypeStruct((1, rows, 2 * columns), jnp.bfloat16),
-        in_specs=[SMEM, VMEM] + [HBM] * layers,
+        in_specs=[SMEM] + [VMEM] * (1 + layers),
         out_specs=VMEM,
-        scratch_shapes=[pltpu.VMEM((layers * rows, width), jnp.bfloat16), pltpu.SemaphoreType.DMA((layers,))],
         compiler_params=pltpu.CompilerParams(vmem_limit_bytes=8 * MIB),
         cost_estimate=LIGHT,
         name="output",
@@ -541,12 +531,12 @@
     query_a, pair_a = project(core_at, [whole, first], count, width, gain, own, far, 1)
     link_a, chip_a = halos(pair_a)
     second, link_a, chip_a = together(second, link_a, chip_a)
-    third = ringed(second)
+    third = ringed(second[:count])
     query_b, pair_b = project(core_at, [second], count, width, gain, own, far, 1)
     shares = shared(join(count, first, second, piece), query_b)
     link_b, chip_b = halos(pair_b)
     third, link_b, chip_b = together(third, link_b, chip_b)
-    query_c, pair_c = project(core_at, [third], count, width, gain, own, far, 1)
+    query_c, pair_c = project(core_at, [third], count, width, gain, own, far, 1 << 32)
     link_c, chip_c = halos(pair_c)
     q_all, kv_all, vt_all, mine = window(
         place, groups, count, [query_a, query_b, query_c], [pair_a, pair_b, pair_c],

time: 110 us -> 109 us (level)
  local copies, waits for them, and re-layouts: 1.96 us -> 3.37 us
    ppermute x1, waiting for transfers between devices: 0.28 us -> 1.8 us  [local(): lax.ppermute(facts, ('dp', 'seq'), [(flat(c, s), flat(*home(c, s))) for c...]
    pallas_call x1, Pallas kernels: 3.04 us -> 1.63 us  [bundle(): pl.pallas_call(bundle_kernel, out_shape=[jax.ShapeDtypeStruct(shape, jnp....]
    ppermute x7, waiting for transfers between devices: 11.4 us -> 9.99 us  [moved(): return lax.ppermute(value, ('dp', 'seq', 'head'), pairs)]
    ppermute x7, starting transfers between devices: 16.3 us -> 15.1 us  [moved(): return lax.ppermute(value, ('dp', 'seq', 'head'), pairs)]
    ppermute x2, waiting for transfers between devices: 6.4 us -> 5.22 us  [ringed(): return lax.ppermute(value, 'head', [(z, after[z]) for z in range(layers)])]
  transfers between devices with their start and end apart: 22 -> 22, of which waited for: 13 -> 12; matrix products, arithmetic and copies ran while one was open for 2% -> 4% of each run, Pallas kernels for 25% -> 26%
where the time goes in v9:
time: 109 us; the launch traced here: 108 us
  starting transfers between devices  37.4 us (34%)
  Pallas kernels  36.1 us (33%)
  waiting for transfers between devices  29.6 us (27%)
  local copies, waits for them, and re-layouts  3.37 us (3%)
    ppermute x7, starting transfers between devices, moved(): return lax.ppermute(value, ('dp', 'seq', 'head'), pairs)  15.1 us
    pallas_call x3, Pallas kernels, project(): pl.pallas_call(functools.partial(project_kernel, blocks, count), out_shap...  12.6 us
    pallas_call x2, Pallas kernels, attend(): pl.pallas_call(functools.partial(attend_kernel, groups, reach, block // 2...  11.5 us
    ppermute x7, waiting for transfers between devices, moved(): return lax.ppermute(value, ('dp', 'seq', 'head'), pairs)  9.99 us
    ppermute x3, starting transfers between devices, halos(): lax.ppermute(pair, ('dp', 'seq'), over_link)  8.56 us
    ppermute x3, waiting for transfers between devices, halos(): lax.ppermute(pair, ('dp', 'seq'), over_link)  8.29 us
    ppermute x2, starting transfers between devices, ringed(): return lax.ppermute(value, 'head', [(z, after[z]) for z in range(layers)])  5.92 us
    ppermute x2, waiting for transfers between devices, ringed(): return lax.ppermute(value, 'head', [(z, after[z]) for z in range(layers)])  5.22 us
  transfers between devices with their start and end apart: 22, of which 12 were waited for; matrix products, arithmetic and copies ran while one was open for 4% of the time, Pallas kernels for 26%

profile of v9, /device:TPU:1, one launch (start us, length us, event | category | flops | bytes accessed | tf_op | source)
XLA Modules:
  0.0 108.1 jit_solution(10879452158018695200)
XLA Ops:
  0.0 2.1 %pack.1 = (bf16[240,1536]{1,0:T(8,128)(2,1)}, bf16[96,768]{1,0:T(8,128)(2,1)}) custom-call(s32[1]{0:T(128)} %bitcast.9.place_ref, bf16[192,1536]{1,0:T(8,128)(2,1)} %bitcast.rows_ref, bf16[384,768]{1,0:T(8,128)(2,1)} %refs_1_.1), custom_call_target="tpu_custom_call" | custom-call | flops 1 | bytes 1 | tf_op jit(solution)/shard_map/pack/pallas_call | solution.py:69
  2.1 3.7 %collective-permute-start.5 = (bf16[240,1536]{1,0:T(8,128)(2,1)}, bf16[240,1536]{1,0:T(8,128)(2,1)}, u32[]{:S(2)}, u32[]{:S(2)}) collective-permute-start(bf16[240,1536]{1,0:T(8,128)(2,1)} %get-tuple-element.61), channel_id=1, source_target_pairs={{0,1},{1,3},{2,0},{3,2},{4,17},{5,19},{6,16},{7,18},{8,9},{9,11},{... | collective-permute-start | bytes 2211848 | tf_op jit(solution)/shard_map/ppermute | solution.py:478
  6.4 0.7 copy.13
  7.1 1.9 %collective-permute-start.1 = (s32[7,12]{1,0:T(8,128)S(1)}, s32[7,12]{1,0:T(8,128)S(1)}, u32[]{:S(2)}, u32[]{:S(2)}) collective-permute-start(s32[7,12]{1,0:T(8,128)S(1)} %concatenate.3), channel_id=1, source_target_pairs={{0,0},{4,16},{8,8},{12,24},{16,4},{20,20},{24,12},{28,28},{1,1},{5... | collective-permute-start | bytes 1016 | tf_op jit(solution)/shard_map/ppermute | solution.py:509
  9.0 1.6 %bundle.1 = (bf16[768,768]{1,0:T(8,128)(2,1)S(1)}, bf16[768,768]{1,0:T(8,128)(2,1)S(1)}) custom-call(bf16[768,384]{1,0:T(8,128)(2,1)} %query_ref.1, bf16[768,384]{1,0:T(8,128)(2,1)} %key_ref.1, bf16[768,384]{1,0:T(8,128)(2,1)} %value_ref.1, bf16[384,768]{1,0:T(8,128)(2,1)} %refs_1_.1), custom_call_target="tpu_custom_call" | custom-call | flops 1 | bytes 1 | tf_op jit(solution)/shard_map/bundle/pallas_call | solution.py:99
  10.7 1.8 %collective-permute-done.1 = s32[7,12]{1,0:T(8,128)S(1)} collective-permute-done((s32[7,12]{1,0:T(8,128)S(1)}, s32[7,12]{1,0:T(8,128)S(1)}, u32[]{:S(2)}, u32[]{:S(2)}) %collective-permute-start.1) | collective-permute-done | bytes 368 | tf_op jit(solution)/shard_map/ppermute | solution.py:509
  12.5 0.0 collective-permute-start.3
  12.5 0.5 collective-permute-start.4
  13.0 1.9 %collective-permute-start = (bf16[192,1536]{1,0:T(8,128)(2,1)}, bf16[192,1536]{1,0:T(8,128)(2,1)}, u32[]{:S(2)}, u32[]{:S(2)}) collective-permute-start(bf16[192,1536]{1,0:T(8,128)(2,1)} %bitcast.rows_ref), channel_id=1, source_target_pairs={{0,0},{1,1},{2,2},{3,3},{4,16},{5,17},{6,18},{7,19},{8,8},{9,9},{1... | collective-permute-start | bytes 1769480 | tf_op jit(solution)/shard_map/ppermute | solution.py:478
  14.9 2.6 %collective-permute-start.2 = (bf16[96,768]{1,0:T(8,128)(2,1)}, bf16[96,768]{1,0:T(8,128)(2,1)}, u32[]{:S(2)}, u32[]{:S(2)}) collective-permute-start(bf16[96,768]{1,0:T(8,128)(2,1)} %get-tuple-element.51), channel_id=1, source_target_pairs={{0,2},{1,0},{2,3},{3,1},{4,18},{5,16},{6,19},{7,17},{8,10},{9,8},{... | collective-permute-start | bytes 442376 | tf_op jit(solution)/shard_map/ppermute | solution.py:478
  17.5 0.1 pad_add_fusion.place_ref
  17.6 0.7 broadcast_in_dim.10.gain_ref
  18.3 0.7 stack.80.refs_0_
  18.9 0.7 add_add_fusion
  19.6 0.5 slice.9
  20.1 0.0 copy-done.3
  20.1 0.7 stack.77.place_ref
  20.8 2.7 %collective-permute-done.5.refs_1_.first_ref = bf16[240,1536]{1,0:T(8,128)(2,1)} collective-permute-done((bf16[240,1536]{1,0:T(8,128)(2,1)}, bf16[240,1536]{1,0:T(8,128)(2,1)}, u32[]{:S(2)}, u32[]{:S(2)}) %collective-permute-start.5) | collective-permute-done | bytes 737312 | tf_op jit(solution)/shard_map/ppermute | solution.py:478
  23.5 4.1 %collective-permute-start.6 = (bf16[240,1536]{1,0:T(8,128)(2,1)}, bf16[240,1536]{1,0:T(8,128)(2,1)S(1)}, u32[]{:S(2)}, u32[]{:S(2)}) collective-permute-start(bf16[240,1536]{1,0:T(8,128)(2,1)} %collective-permute-done.5.refs_1_.first_ref), channel_id=1, source_target_pairs={{0,1},{1,3},{2,0},{3,2},{4,5},{5,7},{6,4},{7,6},{8,9},{9,11},{10,8... | collective-permute-start | bytes 2211848 | tf_op jit(solution)/shard_map/ppermute | solution.py:500
  27.6 0.0 collective-permute-done.2.refs_0_
  27.6 1.7 %collective-permute-done.refs_0_ = bf16[192,1536]{1,0:T(8,128)(2,1)} collective-permute-done((bf16[192,1536]{1,0:T(8,128)(2,1)}, bf16[192,1536]{1,0:T(8,128)(2,1)}, u32[]{:S(2)}, u32[]{:S(2)}) %collective-permute-start) | collective-permute-done | bytes 589856 | tf_op jit(solution)/shard_map/ppermute | solution.py:478
  29.2 0.0 collective-permute-done.3.far_front
  29.2 0.0 collective-permute-done.4.far_back.refs_2_
  29.2 5.7 %project.3 = (bf16[384,384]{1,0:T(8,128)(2,1)}, bf16[384,768]{1,0:T(8,128)(2,1)}) custom-call(s32[1]{0:T(128)} %bitcast.1.place_ref, f32[1,1536]{1,0:T(1,128)S(1)} %broadcast_in_dim.10.gain_ref, bf16[768,768]{1,0:T(8,128)(2,1)S(1)} %get-tuple-element.58.own_front, bf16[768,768]{1,0:T(8,128)(2,1)S(1)} %get-tuple-element.59.own_back, ...), custom_call_target="tpu_custom_call" | custom-call | flops 1 | bytes 1 | tf_op jit(solution)/shard_map/project/pallas_call | solution.py:181
  34.9 0.1 collective-permute-start.8
  35.0 3.5 %collective-permute-start.7 = (bf16[384,768]{1,0:T(8,128)(2,1)}, bf16[384,768]{1,0:T(8,128)(2,1)S(1)}, u32[]{:S(2)}, u32[]{:S(2)}) collective-permute-start(bf16[384,768]{1,0:T(8,128)(2,1)} %get-tuple-element.63.refs_3_), channel_id=1, source_target_pairs={{16,8},{20,12},{8,16},{12,20},{17,9},{21,13},{9,17},{13,21},{18,10... | collective-permute-start | bytes 1769480 | tf_op jit(solution)/shard_map/ppermute | solution.py:497
  38.5 5.2 %collective-permute-done.6.refs_0_.second_ref = bf16[240,1536]{1,0:T(8,128)(2,1)S(1)} collective-permute-done((bf16[240,1536]{1,0:T(8,128)(2,1)}, bf16[240,1536]{1,0:T(8,128)(2,1)S(1)}, u32[]{:S(2)}, u32[]{:S(2)}) %collective-permute-start.6) | collective-permute-done | bytes 737312 | tf_op jit(solution)/shard_map/ppermute | solution.py:500
  43.8 0.0 collective-permute-done.8.refs_6_
  43.8 2.7 %collective-permute-done.7.refs_9_ = bf16[384,768]{1,0:T(8,128)(2,1)S(1)} collective-permute-done((bf16[384,768]{1,0:T(8,128)(2,1)}, bf16[384,768]{1,0:T(8,128)(2,1)S(1)}, u32[]{:S(2)}, u32[]{:S(2)}) %collective-permute-start.7) | collective-permute-done | bytes 589856 | tf_op jit(solution)/shard_map/ppermute | solution.py:497
  46.5 1.9 %collective-permute-start.9 = (bf16[192,1536]{1,0:T(8,128)(2,1)S(1)}, bf16[192,1536]{1,0:T(8,128)(2,1)S(1)}, u32[]{:S(2)}, u32[]{:S(2)}) collective-permute-start(bf16[192,1536]{1,0:T(8,128)(2,1)S(1)} %slice.11), channel_id=1, source_target_pairs={{0,1},{1,3},{2,0},{3,2},{4,5},{5,7},{6,4},{7,6},{8,9},{9,11},{10,8... | collective-permute-start | bytes 1769480 | tf_op jit(solution)/shard_map/ppermute | solution.py:500
  48.3 1.9 %join.1.refs_12_ = bf16[144,1536]{1,0:T(8,128)(2,1)} custom-call(bf16[240,1536]{1,0:T(8,128)(2,1)} %collective-permute-done.5.refs_1_.first_ref, bf16[240,1536]{1,0:T(8,128)(2,1)S(1)} %collective-permute-done.6.refs_0_.second_ref, bf16[96,768]{1,0:T(8,128)(2,1)} %hold.2.piece_ref), custom_call_target="tpu_custom_call" | custom-call | flops 1 | bytes 1 | tf_op jit(solution)/shard_map/join/pallas_call | solution.py:127
  50.2 0.1 collective-permute-start.15
  50.3 1.5 %collective-permute-start.14 = (bf16[144,1536]{1,0:T(8,128)(2,1)}, bf16[144,1536]{1,0:T(8,128)(2,1)S(1)}, u32[]{:S(2)}, u32[]{:S(2)}) collective-permute-start(bf16[144,1536]{1,0:T(8,128)(2,1)} %join.1.refs_12_), channel_id=1, source_target_pairs={{0,4},{4,0},{8,12},{12,8},{1,5},{5,1},{9,13},{13,9},{2,6},{6,2},{1... | collective-permute-start | bytes 1327112 | tf_op jit(solution)/shard_map/ppermute | solution.py:488
  51.9 3.4 %project.4 = (bf16[192,384]{1,0:T(8,128)(2,1)}, bf16[192,768]{1,0:T(8,128)(2,1)}) custom-call(s32[1]{0:T(128)} %bitcast.1.place_ref, f32[1,1536]{1,0:T(1,128)S(1)} %broadcast_in_dim.10.gain_ref, bf16[768,768]{1,0:T(8,128)(2,1)S(1)} %get-tuple-element.58.own_front, bf16[768,768]{1,0:T(8,128)(2,1)S(1)} %get-tuple-element.59.own_back, ...), custom_call_target="tpu_custom_call" | custom-call | flops 1 | bytes 1 | tf_op jit(solution)/shard_map/project/pallas_call | solution.py:181
  55.3 2.1 %collective-permute-start.11 = (bf16[192,768]{1,0:T(8,128)(2,1)}, bf16[192,768]{1,0:T(8,128)(2,1)S(1)}, u32[]{:S(2)}, u32[]{:S(2)}) collective-permute-start(bf16[192,768]{1,0:T(8,128)(2,1)} %get-tuple-element.66.refs_4_), channel_id=1, source_target_pairs={{0,16},{16,0},{1,17},{17,1},{2,18},{18,2},{3,19},{19,3},{4,20},{20... | collective-permute-start | bytes 884744 | tf_op jit(solution)/shard_map/ppermute | solution.py:497
  57.4 1.9 %collective-permute-start.10 = (bf16[192,768]{1,0:T(8,128)(2,1)}, bf16[192,768]{1,0:T(8,128)(2,1)S(1)}, u32[]{:S(2)}, u32[]{:S(2)}) collective-permute-start(bf16[192,768]{1,0:T(8,128)(2,1)} %get-tuple-element.66.refs_4_), channel_id=1, source_target_pairs={{16,8},{20,12},{8,16},{12,20},{17,9},{21,13},{9,17},{13,21},{18,10... | collective-permute-start | bytes 884744 | tf_op jit(solution)/shard_map/ppermute | solution.py:497
  59.3 3.1 %collective-permute-done.15.refs_14_ = bf16[144,1536]{1,0:T(8,128)(2,1)S(1)} collective-permute-done((bf16[144,1536]{1,0:T(8,128)(2,1)}, bf16[144,1536]{1,0:T(8,128)(2,1)S(1)}, u32[]{:S(2)}, u32[]{:S(2)}) %collective-permute-start.15) | collective-permute-done | bytes 442400 | tf_op jit(solution)/shard_map/ppermute | solution.py:488
  62.4 0.0 collective-permute-done.14.refs_13_
  62.4 1.5 %collective-permute-start.16 = (bf16[144,1536]{1,0:T(8,128)(2,1)S(1)}, bf16[144,1536]{1,0:T(8,128)(2,1)S(1)}, u32[]{:S(2)}, u32[]{:S(2)}) collective-permute-start(bf16[144,1536]{1,0:T(8,128)(2,1)S(1)} %collective-permute-done.15.refs_14_), channel_id=1, source_target_pairs={{0,4},{4,0},{8,12},{12,8},{1,5},{5,1},{9,13},{13,9},{2,6},{6,2},{1... | collective-permute-start | bytes 1327112 | tf_op jit(solution)/shard_map/ppermute | solution.py:490
  63.9 0.0 collective-permute-done.11.refs_7_
  63.9 1.7 %collective-permute-done.10.refs_10_ = bf16[192,768]{1,0:T(8,128)(2,1)S(1)} collective-permute-done((bf16[192,768]{1,0:T(8,128)(2,1)}, bf16[192,768]{1,0:T(8,128)(2,1)S(1)}, u32[]{:S(2)}, u32[]{:S(2)}) %collective-permute-start.10) | collective-permute-done | bytes 294944 | tf_op jit(solution)/shard_map/ppermute | solution.py:497
  65.6 0.0 collective-permute-done.9.refs_0_
  65.6 3.4 %project.5 = (bf16[192,384]{1,0:T(8,128)(2,1)}, bf16[192,768]{1,0:T(8,128)(2,1)}) custom-call(s32[1]{0:T(128)} %bitcast.1.place_ref, f32[1,1536]{1,0:T(1,128)S(1)} %broadcast_in_dim.10.gain_ref, bf16[768,768]{1,0:T(8,128)(2,1)S(1)} %get-tuple-element.58.own_front, bf16[768,768]{1,0:T(8,128)(2,1)S(1)} %get-tuple-element.59.own_back, ...), custom_call_target="tpu_custom_call" | custom-call | flops 4294967296 | bytes 1 | tf_op jit(solution)/shard_map/project/pallas_call | solution.py:181
  69.1 3.1 %collective-permute-start.13 = (bf16[192,768]{1,0:T(8,128)(2,1)}, bf16[192,768]{1,0:T(8,128)(2,1)S(1)}, u32[]{:S(2)}, u32[]{:S(2)}) collective-permute-start(bf16[192,768]{1,0:T(8,128)(2,1)} %get-tuple-element.69.refs_5_), channel_id=1, source_target_pairs={{16,8},{20,12},{8,16},{12,20},{17,9},{21,13},{9,17},{13,21},{18,10... | collective-permute-start | bytes 884744 | tf_op jit(solution)/shard_map/ppermute | solution.py:497
  72.2 0.1 collective-permute-start.12
  72.3 1.1 %collective-permute-done.16.refs_15_ = bf16[144,1536]{1,0:T(8,128)(2,1)S(1)} collective-permute-done((bf16[144,1536]{1,0:T(8,128)(2,1)S(1)}, bf16[144,1536]{1,0:T(8,128)(2,1)S(1)}, u32[]{:S(2)}, u32[]{:S(2)}) %collective-permute-start.16) | collective-permute-done | bytes 442400 | tf_op jit(solution)/shard_map/ppermute | solution.py:490
  73.4 3.9 %collective-permute-done.13.refs_11_ = bf16[192,768]{1,0:T(8,128)(2,1)S(1)} collective-permute-done((bf16[192,768]{1,0:T(8,128)(2,1)}, bf16[192,768]{1,0:T(8,128)(2,1)S(1)}, u32[]{:S(2)}, u32[]{:S(2)}) %collective-permute-start.13) | collective-permute-done | bytes 294944 | tf_op jit(solution)/shard_map/ppermute | solution.py:497
  77.3 0.0 collective-permute-done.12.refs_8_
  77.3 3.7 %window.1 = (bf16[768,384]{1,0:T(8,128)(2,1)S(1)}, bf16[2304,768]{1,0:T(8,128)(2,1)S(1)}, bf16[3,18,128,128]{3,2,1,0:T(8,128)(2,1)S(1)}, bf16[576,1536]{1,0:T(8,128)(2,1)}) custom-call(s32[8]{0:T(128)S(1)} %stack.77.place_ref, bf16[384,384]{1,0:T(8,128)(2,1)} %get-tuple-element.62.refs_0_, bf16[192,384]{1,0:T(8,128)(2,1)} %get-tuple-element.65.refs_1_, ...), custom_call_target="tpu_custom_call" | custom-call | bytes 8257536 | tf_op jit(solution)/shard_map/window/pallas_call | solution.py:242
  81.1 0.1 collective-permute-start.17
  81.1 0.0 copy-done.2
  81.1 0.0 copy-done.4
  81.2 4.7 %attend.2 = (bf16[192,384]{1,0:T(8,128)(2,1)}, bf16[192,384]{1,0:T(8,128)(2,1)}) custom-call(s32[8]{0:T(128)S(1)} %stack.77.place_ref, s32[6,12]{1,0:T(8,128)S(1)} %bitcast.24, s32[3]{0:T(128)S(1)} %copy-done.2, bf16[768,384]{1,0:T(8,128)(2,1)S(1)} %get-tuple-element.81.q_all, bf16[2304,768]{1,0:T(8,128)(2,1)S(1)} %get-tuple-element.78.kv_all, ...), custom_call_target="tpu_custom_call" | custom-call | flops 17179869184 | bytes 1048576 | tf_op jit(solution)/shard_map/attend/pallas_call | solution.py:401
  85.9 1.1 %collective-permute-start.18 = (bf16[192,384]{1,0:T(8,128)(2,1)}, bf16[192,384]{1,0:T(8,128)(2,1)S(1)}, u32[]{:S(2)}, u32[]{:S(2)}) collective-permute-start(bf16[192,384]{1,0:T(8,128)(2,1)} %get-tuple-element.85), channel_id=1, source_target_pairs={{0,2},{1,3},{2,0},{3,1},{4,18},{5,19},{6,16},{7,17},{8,10},{9,11},... | collective-permute-start | bytes 442376 | tf_op jit(solution)/shard_map/ppermute | solution.py:478
  87.0 0.0 collective-permute-done.17.refs_4_
  87.0 6.8 %attend.3 = (bf16[192,384]{1,0:T(8,128)(2,1)}, bf16[192,384]{1,0:T(8,128)(2,1)}, bf16[4,2,384,768]{3,2,1,0:T(8,128)(2,1)S(1)}) custom-call(s32[8]{0:T(128)S(1)} %stack.77.place_ref, s32[6,12]{1,0:T(8,128)S(1)} %bitcast.25, s32[3]{0:T(128)S(1)} %copy-done.1, bf16[768,384]{1,0:T(8,128)(2,1)S(1)} %get-tuple-element.81.q_all, ...), custom_call_target="tpu_custom_call" | custom-call | flops 17179869184 | bytes 1048576 | tf_op jit(solution)/shard_map/attend/pallas_call | solution.py:401
  93.8 2.7 %collective-permute-start.19 = (bf16[192,384]{1,0:T(8,128)(2,1)S(1)}, bf16[192,384]{1,0:T(8,128)(2,1)S(1)}, u32[]{:S(2)}, u32[]{:S(2)}) collective-permute-start(bf16[192,384]{1,0:T(8,128)(2,1)S(1)} %copy-done.5), channel_id=1, source_target_pairs={{0,3},{1,2},{2,1},{3,0},{4,19},{5,18},{6,17},{7,16},{8,11},{9,10},... | collective-permute-start | bytes 442376 | tf_op jit(solution)/shard_map/ppermute | solution.py:478
  96.5 3.1 %collective-permute-start.20 = (bf16[192,384]{1,0:T(8,128)(2,1)}, bf16[192,384]{1,0:T(8,128)(2,1)S(1)}, u32[]{:S(2)}, u32[]{:S(2)}) collective-permute-start(bf16[192,384]{1,0:T(8,128)(2,1)} %get-tuple-element.89), channel_id=1, source_target_pairs={{0,0},{1,1},{2,2},{3,3},{4,16},{5,17},{6,18},{7,19},{8,8},{9,9},{1... | collective-permute-start | bytes 442376 | tf_op jit(solution)/shard_map/ppermute | solution.py:478
  99.6 0.1 collective-permute-start.21
  99.7 0.0 collective-permute-done.18.refs_0_
  99.7 3.1 %collective-permute-done.19.refs_1_ = bf16[192,384]{1,0:T(8,128)(2,1)S(1)} collective-permute-done((bf16[192,384]{1,0:T(8,128)(2,1)S(1)}, bf16[192,384]{1,0:T(8,128)(2,1)S(1)}, u32[]{:S(2)}, u32[]{:S(2)}) %collective-permute-start.19) | collective-permute-done | bytes 147488 | tf_op jit(solution)/shard_map/ppermute | solution.py:478
  102.7 1.3 %collective-permute-done.20.refs_2_ = bf16[192,384]{1,0:T(8,128)(2,1)S(1)} collective-permute-done((bf16[192,384]{1,0:T(8,128)(2,1)}, bf16[192,384]{1,0:T(8,128)(2,1)S(1)}, u32[]{:S(2)}, u32[]{:S(2)}) %collective-permute-start.20) | collective-permute-done | bytes 147488 | tf_op jit(solution)/shard_map/ppermute | solution.py:478
  104.0 1.3 %collective-permute-done.21.refs_3_ = bf16[192,384]{1,0:T(8,128)(2,1)S(1)} collective-permute-done((bf16[192,384]{1,0:T(8,128)(2,1)}, bf16[192,384]{1,0:T(8,128)(2,1)S(1)}, u32[]{:S(2)}, u32[]{:S(2)}) %collective-permute-start.21) | collective-permute-done | bytes 147488 | tf_op jit(solution)/shard_map/ppermute | solution.py:478
  105.3 2.7 %output.1 = bf16[1,192,1536]{2,1,0:T(8,128)(2,1)} custom-call(s32[4]{0:T(128)S(1)} %pad_add_fusion.place_ref, bf16[4,2,384,768]{3,2,1,0:T(8,128)(2,1)S(1)} %get-tuple-element.84.weight, bf16[192,384]{1,0:T(8,128)(2,1)S(1)} %hold.3.refs_0_, bf16[192,384]{1,0:T(8,128)(2,1)S(1)} %collective-permute-done.19.refs_1_, ...), custom_call_target="tpu_custom_call" | custom-call | flops 1 | bytes 1 | tf_op jit(solution)/shard_map/output/pallas_call | solution.py:427
  (13 shorter events, 0.1 us)
Async XLA Ops:
  2.1 21.4 %collective-permute-start.5 = (bf16[240,1536]{1,0:T(8,128)(2,1)}, bf16[240,1536]{1,0:T(8,128)(2,1)}, u32[]{:S(2)}, u32[]{:S(2)}) collective-permute-start(bf16[240,1536]{1,0:T(8,128)(2,1)} %get-tuple-element.61), channel_id=1, source_target_pairs={{0,1},{1,3},{2,0},{3,2},{4,17},{5,19},{6,16},{7,18},{8,9},{9,11},{... | collective-permute-start | bytes 2211848 | tf_op jit(solution)/shard_map/ppermute | solution.py:478
  7.1 5.4 %collective-permute-start.1 = (s32[7,12]{1,0:T(8,128)S(1)}, s32[7,12]{1,0:T(8,128)S(1)}, u32[]{:S(2)}, u32[]{:S(2)}) collective-permute-start(s32[7,12]{1,0:T(8,128)S(1)} %concatenate.3), channel_id=1, source_target_pairs={{0,0},{4,16},{8,8},{12,24},{16,4},{20,20},{24,12},{28,28},{1,1},{5... | collective-permute-start | bytes 1016 | tf_op jit(solution)/shard_map/ppermute | solution.py:509
  12.5 7.6 %copy-start.3 = (s32[7,12]{1,0:T(8,128)}, s32[7,12]{1,0:T(8,128)S(1)}, u32[]{:S(2)}) copy-start(s32[7,12]{1,0:T(8,128)S(1)} %collective-permute-done.1) | copy-start | bytes 1012
  12.5 16.8 %collective-permute-start.3 = (bf16[768,768]{1,0:T(8,128)(2,1)S(1)}, bf16[768,768]{1,0:T(8,128)(2,1)}, u32[]{:S(2)}, u32[]{:S(2)}) collective-permute-start(bf16[768,768]{1,0:T(8,128)(2,1)S(1)} %get-tuple-element.58.own_front), channel_id=1, source_target_pairs={{0,16},{16,0},{1,17},{17,1},{2,18},{18,2},{3,19},{19,3},{4,20},{20... | collective-permute-start | bytes 3538952 | tf_op jit(solution)/shard_map/ppermute | solution.py:511
  12.5 16.8 %collective-permute-start.4 = (bf16[768,768]{1,0:T(8,128)(2,1)S(1)}, bf16[768,768]{1,0:T(8,128)(2,1)S(1)}, u32[]{:S(2)}, u32[]{:S(2)}) collective-permute-start(bf16[768,768]{1,0:T(8,128)(2,1)S(1)} %get-tuple-element.59.own_back), channel_id=1, source_target_pairs={{0,16},{16,0},{1,17},{17,1},{2,18},{18,2},{3,19},{19,3},{4,20},{20... | collective-permute-start | bytes 3538952 | tf_op jit(solution)/shard_map/ppermute | solution.py:511
  13.0 16.3 %collective-permute-start = (bf16[192,1536]{1,0:T(8,128)(2,1)}, bf16[192,1536]{1,0:T(8,128)(2,1)}, u32[]{:S(2)}, u32[]{:S(2)}) collective-permute-start(bf16[192,1536]{1,0:T(8,128)(2,1)} %bitcast.rows_ref), channel_id=1, source_target_pairs={{0,0},{1,1},{2,2},{3,3},{4,16},{5,17},{6,18},{7,19},{8,8},{9,9},{1... | collective-permute-start | bytes 1769480 | tf_op jit(solution)/shard_map/ppermute | solution.py:478
  14.9 12.6 %collective-permute-start.2 = (bf16[96,768]{1,0:T(8,128)(2,1)}, bf16[96,768]{1,0:T(8,128)(2,1)}, u32[]{:S(2)}, u32[]{:S(2)}) collective-permute-start(bf16[96,768]{1,0:T(8,128)(2,1)} %get-tuple-element.51), channel_id=1, source_target_pairs={{0,2},{1,0},{2,3},{3,1},{4,18},{5,16},{6,19},{7,17},{8,10},{9,8},{... | collective-permute-start | bytes 442376 | tf_op jit(solution)/shard_map/ppermute | solution.py:478
  23.5 20.3 %collective-permute-start.6 = (bf16[240,1536]{1,0:T(8,128)(2,1)}, bf16[240,1536]{1,0:T(8,128)(2,1)S(1)}, u32[]{:S(2)}, u32[]{:S(2)}) collective-permute-start(bf16[240,1536]{1,0:T(8,128)(2,1)} %collective-permute-done.5.refs_1_.first_ref), channel_id=1, source_target_pairs={{0,1},{1,3},{2,0},{3,2},{4,5},{5,7},{6,4},{7,6},{8,9},{9,11},{10,8... | collective-permute-start | bytes 2211848 | tf_op jit(solution)/shard_map/ppermute | solution.py:500
  34.9 8.8 %collective-permute-start.8 = (bf16[384,768]{1,0:T(8,128)(2,1)}, bf16[384,768]{1,0:T(8,128)(2,1)S(1)}, u32[]{:S(2)}, u32[]{:S(2)}) collective-permute-start(bf16[384,768]{1,0:T(8,128)(2,1)} %get-tuple-element.63.refs_3_), channel_id=1, source_target_pairs={{0,16},{16,0},{1,17},{17,1},{2,18},{18,2},{3,19},{19,3},{4,20},{20... | collective-permute-start | bytes 1769480 | tf_op jit(solution)/shard_map/ppermute | solution.py:497
  35.0 11.4 %collective-permute-start.7 = (bf16[384,768]{1,0:T(8,128)(2,1)}, bf16[384,768]{1,0:T(8,128)(2,1)S(1)}, u32[]{:S(2)}, u32[]{:S(2)}) collective-permute-start(bf16[384,768]{1,0:T(8,128)(2,1)} %get-tuple-element.63.refs_3_), channel_id=1, source_target_pairs={{16,8},{20,12},{8,16},{12,20},{17,9},{21,13},{9,17},{13,21},{18,10... | collective-permute-start | bytes 1769480 | tf_op jit(solution)/shard_map/ppermute | solution.py:497
  46.5 19.2 %collective-permute-start.9 = (bf16[192,1536]{1,0:T(8,128)(2,1)S(1)}, bf16[192,1536]{1,0:T(8,128)(2,1)S(1)}, u32[]{:S(2)}, u32[]{:S(2)}) collective-permute-start(bf16[192,1536]{1,0:T(8,128)(2,1)S(1)} %slice.11), channel_id=1, source_target_pairs={{0,1},{1,3},{2,0},{3,2},{4,5},{5,7},{6,4},{7,6},{8,9},{9,11},{10,8... | collective-permute-start | bytes 1769480 | tf_op jit(solution)/shard_map/ppermute | solution.py:500
  50.2 12.2 %collective-permute-start.15 = (bf16[144,1536]{1,0:T(8,128)(2,1)}, bf16[144,1536]{1,0:T(8,128)(2,1)S(1)}, u32[]{:S(2)}, u32[]{:S(2)}) collective-permute-start(bf16[144,1536]{1,0:T(8,128)(2,1)} %join.1.refs_12_), channel_id=1, source_target_pairs={{0,8},{4,12},{8,0},{12,4},{1,9},{5,13},{9,1},{13,5},{2,10},{6,14},... | collective-permute-start | bytes 1327112 | tf_op jit(solution)/shard_map/ppermute | solution.py:488
  50.3 12.1 %collective-permute-start.14 = (bf16[144,1536]{1,0:T(8,128)(2,1)}, bf16[144,1536]{1,0:T(8,128)(2,1)S(1)}, u32[]{:S(2)}, u32[]{:S(2)}) collective-permute-start(bf16[144,1536]{1,0:T(8,128)(2,1)} %join.1.refs_12_), channel_id=1, source_target_pairs={{0,4},{4,0},{8,12},{12,8},{1,5},{5,1},{9,13},{13,9},{2,6},{6,2},{1... | collective-permute-start | bytes 1327112 | tf_op jit(solution)/shard_map/ppermute | solution.py:488
  55.3 8.6 %collective-permute-start.11 = (bf16[192,768]{1,0:T(8,128)(2,1)}, bf16[192,768]{1,0:T(8,128)(2,1)S(1)}, u32[]{:S(2)}, u32[]{:S(2)}) collective-permute-start(bf16[192,768]{1,0:T(8,128)(2,1)} %get-tuple-element.66.refs_4_), channel_id=1, source_target_pairs={{0,16},{16,0},{1,17},{17,1},{2,18},{18,2},{3,19},{19,3},{4,20},{20... | collective-permute-start | bytes 884744 | tf_op jit(solution)/shard_map/ppermute | solution.py:497
  57.4 8.2 %collective-permute-start.10 = (bf16[192,768]{1,0:T(8,128)(2,1)}, bf16[192,768]{1,0:T(8,128)(2,1)S(1)}, u32[]{:S(2)}, u32[]{:S(2)}) collective-permute-start(bf16[192,768]{1,0:T(8,128)(2,1)} %get-tuple-element.66.refs_4_), channel_id=1, source_target_pairs={{16,8},{20,12},{8,16},{12,20},{17,9},{21,13},{9,17},{13,21},{18,10... | collective-permute-start | bytes 884744 | tf_op jit(solution)/shard_map/ppermute | solution.py:497
  62.4 11.0 %collective-permute-start.16 = (bf16[144,1536]{1,0:T(8,128)(2,1)S(1)}, bf16[144,1536]{1,0:T(8,128)(2,1)S(1)}, u32[]{:S(2)}, u32[]{:S(2)}) collective-permute-start(bf16[144,1536]{1,0:T(8,128)(2,1)S(1)} %collective-permute-done.15.refs_14_), channel_id=1, source_target_pairs={{0,4},{4,0},{8,12},{12,8},{1,5},{5,1},{9,13},{13,9},{2,6},{6,2},{1... | collective-permute-start | bytes 1327112 | tf_op jit(solution)/shard_map/ppermute | solution.py:490
  69.1 8.3 %collective-permute-start.13 = (bf16[192,768]{1,0:T(8,128)(2,1)}, bf16[192,768]{1,0:T(8,128)(2,1)S(1)}, u32[]{:S(2)}, u32[]{:S(2)}) collective-permute-start(bf16[192,768]{1,0:T(8,128)(2,1)} %get-tuple-element.69.refs_5_), channel_id=1, source_target_pairs={{16,8},{20,12},{8,16},{12,20},{17,9},{21,13},{9,17},{13,21},{18,10... | collective-permute-start | bytes 884744 | tf_op jit(solution)/shard_map/ppermute | solution.py:497
  72.2 5.1 %collective-permute-start.12 = (bf16[192,768]{1,0:T(8,128)(2,1)}, bf16[192,768]{1,0:T(8,128)(2,1)S(1)}, u32[]{:S(2)}, u32[]{:S(2)}) collective-permute-start(bf16[192,768]{1,0:T(8,128)(2,1)} %get-tuple-element.69.refs_5_), channel_id=1, source_target_pairs={{0,16},{16,0},{1,17},{17,1},{2,18},{18,2},{3,19},{19,3},{4,20},{20... | collective-permute-start | bytes 884744 | tf_op jit(solution)/shard_map/ppermute | solution.py:497
  77.3 3.8 %copy-start.2 = (s32[3]{0:T(128)S(1)}, s32[3]{0:T(128)}, u32[]{:S(2)}) copy-start(s32[3]{0:T(128)} %get-tuple-element.56.turn_ref) | copy-start | bytes 40
  77.3 3.8 %copy-start.4 = (s32[7,12]{1,0:T(8,128)S(1)}, s32[7,12]{1,0:T(8,128)}, u32[]{:S(2)}) copy-start(s32[7,12]{1,0:T(8,128)} %copy-done.3) | copy-start | bytes 1012
  81.1 6.0 %collective-permute-start.17 = (bf16[576,1536]{1,0:T(8,128)(2,1)}, bf16[576,1536]{1,0:T(8,128)(2,1)S(1)}, u32[]{:S(2)}, u32[]{:S(2)}) collective-permute-start(bf16[576,1536]{1,0:T(8,128)(2,1)} %get-tuple-element.83.refs_3_), channel_id=1, source_target_pairs={{0,16},{16,0},{1,17},{17,1},{2,18},{18,2},{3,19},{19,3},{4,20},{20... | collective-permute-start | bytes 5308424 | tf_op jit(solution)/shard_map/ppermute | solution.py:545
  81.2 5.9 %copy-start = (s32[6]{0:T(128)S(1)}, s32[6]{0:T(128)}, u32[]{:S(2)}) copy-start(s32[6]{0:T(128)} %stack.80.refs_0_) | copy-start | bytes 76
  81.2 5.9 %copy-start.1 = (s32[3]{0:T(128)S(1)}, s32[3]{0:T(128)}, u32[]{:S(2)}) copy-start(s32[3]{0:T(128)} %get-tuple-element.55.turn_ref) | copy-start | bytes 40
  85.9 7.9 %copy-start.5 = (bf16[192,384]{1,0:T(8,128)(2,1)S(1)}, bf16[192,384]{1,0:T(8,128)(2,1)}, u32[]{:S(2)}) copy-start(bf16[192,384]{1,0:T(8,128)(2,1)} %get-tuple-element.88) | copy-start | bytes 442372
  85.9 13.7 %collective-permute-start.18 = (bf16[192,384]{1,0:T(8,128)(2,1)}, bf16[192,384]{1,0:T(8,128)(2,1)S(1)}, u32[]{:S(2)}, u32[]{:S(2)}) collective-permute-start(bf16[192,384]{1,0:T(8,128)(2,1)} %get-tuple-element.85), channel_id=1, source_target_pairs={{0,2},{1,3},{2,0},{3,1},{4,18},{5,19},{6,16},{7,17},{8,10},{9,11},... | collective-permute-start | bytes 442376 | tf_op jit(solution)/shard_map/ppermute | solution.py:478
  93.8 8.9 %collective-permute-start.19 = (bf16[192,384]{1,0:T(8,128)(2,1)S(1)}, bf16[192,384]{1,0:T(8,128)(2,1)S(1)}, u32[]{:S(2)}, u32[]{:S(2)}) collective-permute-start(bf16[192,384]{1,0:T(8,128)(2,1)S(1)} %copy-done.5), channel_id=1, source_target_pairs={{0,3},{1,2},{2,1},{3,0},{4,19},{5,18},{6,17},{7,16},{8,11},{9,10},... | collective-permute-start | bytes 442376 | tf_op jit(solution)/shard_map/ppermute | solution.py:478
  96.5 7.5 %collective-permute-start.20 = (bf16[192,384]{1,0:T(8,128)(2,1)}, bf16[192,384]{1,0:T(8,128)(2,1)S(1)}, u32[]{:S(2)}, u32[]{:S(2)}) collective-permute-start(bf16[192,384]{1,0:T(8,128)(2,1)} %get-tuple-element.89), channel_id=1, source_target_pairs={{0,0},{1,1},{2,2},{3,3},{4,16},{5,17},{6,18},{7,19},{8,8},{9,9},{1... | collective-permute-start | bytes 442376 | tf_op jit(solution)/shard_map/ppermute | solution.py:478
  99.6 5.7 %collective-permute-start.21 = (bf16[192,384]{1,0:T(8,128)(2,1)}, bf16[192,384]{1,0:T(8,128)(2,1)S(1)}, u32[]{:S(2)}, u32[]{:S(2)}) collective-permute-start(bf16[192,384]{1,0:T(8,128)(2,1)} %get-tuple-element.90), channel_id=1, source_target_pairs={{0,1},{1,0},{2,3},{3,2},{4,17},{5,16},{6,19},{7,18},{8,9},{9,8},{1... | collective-permute-start | bytes 442376 | tf_op jit(solution)/shard_map/ppermute | solution.py:478

commit v10 on v9

--- a/solution.py
+++ b/solution.py
@@ -500,7 +500,6 @@
         return lax.ppermute(value, "head", [(z, after[z]) for z in range(layers)])
 
     sent, piece = pack(numbers(lax.rem(seq, share)), rows, w_out, share)
-    piece = moved(piece, lambda z: before[z])
     first = moved(sent, lambda z: after[z])
     second = ringed(first)
     own = bundle(w_query, w_key, w_value, w_out)
@@ -515,7 +514,7 @@
     ids.append(lookup([after[z] for z in range(layers)], layer))
     place = numbers(core, (seq // 2 * 2 + core) * groups, groups * seqs, facts[groups, 0], *ids)
     band = facts[:groups]
-    piece, = hold([piece], 1 << 33)
+    whole, = hold([whole], 1 << 33)
     half = layers // 2
     sides = (1 - layer // half, layer // half)
     turns = [
@@ -524,19 +523,22 @@
     weight_place = numbers(core, layer, seq, ids[1], ids[2], ids[3])
     sources = numbers(*[side * half + lax.rem(layer + half - e, half) for side in sides for e in range(half)])
     core_at = numbers(core)
-    whole, place, band, piece, weight_place, sources, core_at, *turns = together(
-        whole, place, band, piece, weight_place, sources, core_at, *turns
+    whole, place, band, weight_place, sources, core_at, *turns = together(
+        whole, place, band, weight_place, sources, core_at, *turns
     )
 
     query_a, pair_a = project(core_at, [whole, first], count, width, gain, own, far, 1)
     link_a, chip_a = halos(pair_a)
-    second, link_a, chip_a = together(second, link_a, chip_a)
+    piece, pair_a = together(piece, pair_a)
+    piece = moved(piece, lambda z: before[z])
+    second, piece = together(second, piece)
     third = ringed(second[:count])
+    piece, link_a, chip_a = together(piece, link_a, chip_a)
     query_b, pair_b = project(core_at, [second], count, width, gain, own, far, 1)
     shares = shared(join(count, first, second, piece), query_b)
     link_b, chip_b = halos(pair_b)
     third, link_b, chip_b = together(third, link_b, chip_b)
-    query_c, pair_c = project(core_at, [third], count, width, gain, own, far, 1 << 32)
+    query_c, pair_c = project(core_at, [third], count, width, gain, own, far, 1 << 30)
     link_c, chip_c = halos(pair_c)
     q_all, kv_all, vt_all, mine = window(
         place, groups, count, [query_a, query_b, query_c], [pair_a, pair_b, pair_c],

time: 109 us -> 112 us (1.028)
  waiting for transfers between devices: 29.6 us -> 38.1 us
  starting transfers between devices: 37.4 us -> 32.1 us
    ppermute x1, waiting for transfers between devices: 1.8 us -> 9.55 us  [local(): lax.ppermute(facts, ('dp', 'seq'), [(flat(c, s), flat(*home(c, s))) for c...]
    ppermute x7, waiting for transfers between devices: 9.99 us -> 17.3 us  [moved(): return lax.ppermute(value, ('dp', 'seq', 'head'), pairs)]
    ppermute x2, waiting for transfers between devices: 5.22 us -> 0.01 us  [ringed(): return lax.ppermute(value, 'head', [(z, after[z]) for z in range(layers)])]
    ppermute x2, starting transfers between devices: 5.92 us -> 1.77 us  [ringed(): return lax.ppermute(value, 'head', [(z, after[z]) for z in range(layers)])]
    ppermute x7, starting transfers between devices: 15.1 us -> 13 us  [moved(): return lax.ppermute(value, ('dp', 'seq', 'head'), pairs)]
    ppermute x2, waiting for transfers between devices: 3.12 us -> 1.22 us  [shared(): lax.ppermute(value, 'seq', [(s, s ^ step) for s in range(seqs)])]
    ppermute x3, waiting for transfers between devices: 8.29 us -> 10 us  [halos(): lax.ppermute(pair, ('dp', 'seq'), over_link)]
    ppermute x1, starting transfers between devices: 1.91 us -> 3.63 us  [local(): lax.ppermute(facts, ('dp', 'seq'), [(flat(c, s), flat(*home(c, s))) for c...]
  transfers between devices with their start and end apart: 22 -> 22, of which waited for: 12 -> 8; matrix products, arithmetic and copies ran while one was open for 4% -> 4% of each run, Pallas kernels for 26% -> 25%
where the time goes in v10:
time: 112 us
  waiting for transfers between devices  38.1 us (34%)
  Pallas kernels  36.4 us (32%)
  starting transfers between devices  32.1 us (29%)
  local copies, waits for them, and re-layouts  3.24 us (3%)
    ppermute x7, waiting for transfers between devices, moved(): return lax.ppermute(value, ('dp', 'seq', 'head'), pairs)  17.3 us
    ppermute x7, starting transfers between devices, moved(): return lax.ppermute(value, ('dp', 'seq', 'head'), pairs)  13 us
    pallas_call x3, Pallas kernels, project(): pl.pallas_call(functools.partial(project_kernel, blocks, count), out_shap...  12.6 us
    pallas_call x2, Pallas kernels, attend(): pl.pallas_call(functools.partial(attend_kernel, groups, reach, block // 2...  11.9 us
    ppermute x3, waiting for transfers between devices, halos(): lax.ppermute(pair, ('dp', 'seq'), over_link)  10 us
    ppermute x1, waiting for transfers between devices, local(): lax.ppermute(facts, ('dp', 'seq'), [(flat(c, s), flat(*home(c, s))) for c...  9.55 us
    ppermute x3, starting transfers between devices, halos(): lax.ppermute(pair, ('dp', 'seq'), over_link)  8.38 us
    pallas_call x1, Pallas kernels, window(): pl.pallas_call(functools.partial(window_kernel, shape, groups, len(joined...  3.72 us
  transfers between devices with their start and end apart: 22, of which 8 were waited for; matrix products, arithmetic and copies ran while one was open for 4% of the time, Pallas kernels for 25%

profile of v10, /device:TPU:1, one launch (start us, length us, event | category | flops | bytes accessed | tf_op | source)
XLA Modules:
  0.0 111.5 jit_solution(1920102436384764132)
XLA Ops:
  0.0 2.1 %pack.1 = (bf16[240,1536]{1,0:T(8,128)(2,1)}, bf16[96,768]{1,0:T(8,128)(2,1)}) custom-call(s32[1]{0:T(128)} %bitcast.18.place_ref, bf16[192,1536]{1,0:T(8,128)(2,1)} %bitcast.26, bf16[384,768]{1,0:T(8,128)(2,1)} %refs_1_.1), custom_call_target="tpu_custom_call" | custom-call | flops 1 | bytes 1 | tf_op jit(solution)/shard_map/pack/pallas_call | solution.py:69
  2.1 3.7 %collective-permute-start.4 = (bf16[240,1536]{1,0:T(8,128)(2,1)}, bf16[240,1536]{1,0:T(8,128)(2,1)}, u32[]{:S(2)}, u32[]{:S(2)}) collective-permute-start(bf16[240,1536]{1,0:T(8,128)(2,1)} %get-tuple-element.63), channel_id=1, source_target_pairs={{0,1},{1,3},{2,0},{3,2},{4,17},{5,19},{6,16},{7,18},{8,9},{9,11},{... | collective-permute-start | bytes 2211848 | tf_op jit(solution)/shard_map/ppermute | solution.py:478
  5.8 1.9 %collective-permute-start = (bf16[192,1536]{1,0:T(8,128)(2,1)}, bf16[192,1536]{1,0:T(8,128)(2,1)}, u32[]{:S(2)}, u32[]{:S(2)}) collective-permute-start(bf16[192,1536]{1,0:T(8,128)(2,1)} %bitcast.27), channel_id=1, source_target_pairs={{0,0},{1,1},{2,2},{3,3},{4,16},{5,17},{6,18},{7,19},{8,8},{9,9},{1... | collective-permute-start | bytes 1769480 | tf_op jit(solution)/shard_map/ppermute | solution.py:478
  8.4 0.7 copy.13
  9.1 3.6 %collective-permute-start.1 = (s32[7,12]{1,0:T(8,128)S(1)}, s32[7,12]{1,0:T(8,128)S(1)}, u32[]{:S(2)}, u32[]{:S(2)}) collective-permute-start(s32[7,12]{1,0:T(8,128)S(1)} %concatenate.3), channel_id=1, source_target_pairs={{0,0},{4,16},{8,8},{12,24},{16,4},{20,20},{24,12},{28,28},{1,1},{5... | collective-permute-start | bytes 1016 | tf_op jit(solution)/shard_map/ppermute | solution.py:508
  12.7 1.6 %bundle.1 = (bf16[768,768]{1,0:T(8,128)(2,1)S(1)}, bf16[768,768]{1,0:T(8,128)(2,1)S(1)}) custom-call(bf16[768,384]{1,0:T(8,128)(2,1)} %query_ref.1, bf16[768,384]{1,0:T(8,128)(2,1)} %key_ref.1, bf16[768,384]{1,0:T(8,128)(2,1)} %value_ref.1, bf16[384,768]{1,0:T(8,128)(2,1)} %refs_1_.1), custom_call_target="tpu_custom_call" | custom-call | flops 1 | bytes 1 | tf_op jit(solution)/shard_map/bundle/pallas_call | solution.py:99
  14.3 9.5 %collective-permute-done.1 = s32[7,12]{1,0:T(8,128)S(1)} collective-permute-done((s32[7,12]{1,0:T(8,128)S(1)}, s32[7,12]{1,0:T(8,128)S(1)}, u32[]{:S(2)}, u32[]{:S(2)}) %collective-permute-start.1) | collective-permute-done | bytes 368 | tf_op jit(solution)/shard_map/ppermute | solution.py:508
  23.9 0.0 collective-permute-start.2
  23.9 0.5 collective-permute-start.3
  24.4 0.7 broadcast_in_dim.10.gain_ref
  25.1 0.7 stack.79.refs_0_
  25.8 0.1 pad_add_fusion.place_ref
  25.8 0.6 add_add_fusion
  26.5 0.5 slice.9
  27.0 0.0 copy-done.3
  27.0 0.6 stack.77.place_ref
  27.6 0.0 collective-permute-done.4.refs_1_.first_ref
  27.6 1.3 %collective-permute-start.5 = (bf16[240,1536]{1,0:T(8,128)(2,1)}, bf16[240,1536]{1,0:T(8,128)(2,1)S(1)}, u32[]{:S(2)}, u32[]{:S(2)}) collective-permute-start(bf16[240,1536]{1,0:T(8,128)(2,1)} %collective-permute-done.4.refs_1_.first_ref), channel_id=1, source_target_pairs={{0,1},{1,3},{2,0},{3,2},{4,5},{5,7},{6,4},{7,6},{8,9},{9,11},{10,8... | collective-permute-start | bytes 2211848 | tf_op jit(solution)/shard_map/ppermute | solution.py:500
  28.9 0.0 collective-permute-done.refs_0_
  28.9 0.0 collective-permute-done.2.far_front
  28.9 0.0 collective-permute-done.3.far_back.refs_2_
  28.9 5.7 %project.3 = (bf16[384,384]{1,0:T(8,128)(2,1)}, bf16[384,768]{1,0:T(8,128)(2,1)}) custom-call(s32[1]{0:T(128)} %bitcast.1.place_ref, f32[1,1536]{1,0:T(1,128)S(1)} %broadcast_in_dim.10.gain_ref, bf16[768,768]{1,0:T(8,128)(2,1)S(1)} %get-tuple-element.60.own_front, bf16[768,768]{1,0:T(8,128)(2,1)S(1)} %get-tuple-element.61.own_back, ...), custom_call_target="tpu_custom_call" | custom-call | flops 1 | bytes 1 | tf_op jit(solution)/shard_map/project/pallas_call | solution.py:181
  34.6 0.4 collective-permute-start.11
  35.0 3.2 %collective-permute-start.10 = (bf16[384,768]{1,0:T(8,128)(2,1)}, bf16[384,768]{1,0:T(8,128)(2,1)S(1)}, u32[]{:S(2)}, u32[]{:S(2)}) collective-permute-start(bf16[384,768]{1,0:T(8,128)(2,1)} %get-tuple-element.73.refs_3_), channel_id=1, source_target_pairs={{16,8},{20,12},{8,16},{12,20},{17,9},{21,13},{9,17},{13,21},{18,10... | collective-permute-start | bytes 1769480 | tf_op jit(solution)/shard_map/ppermute | solution.py:497
  38.2 0.0 copy-done.5
  38.2 0.1 collective-permute-start.6
  38.3 11.0 %collective-permute-done.6.piece_ref = bf16[96,768]{1,0:T(8,128)(2,1)S(1)} collective-permute-done((bf16[96,768]{1,0:T(8,128)(2,1)S(1)}, bf16[96,768]{1,0:T(8,128)(2,1)S(1)}, u32[]{:S(2)}, u32[]{:S(2)}) %collective-permute-start.6) | collective-permute-done | bytes 147488 | tf_op jit(solution)/shard_map/ppermute | solution.py:478
  49.3 0.0 collective-permute-done.5.refs_0_.second_ref
  49.4 0.5 collective-permute-start.7
  49.9 0.0 collective-permute-done.11.refs_6_
  49.9 0.0 collective-permute-done.10.refs_9_
  49.9 1.7 %join.1.refs_12_ = bf16[144,1536]{1,0:T(8,128)(2,1)} custom-call(bf16[240,1536]{1,0:T(8,128)(2,1)} %collective-permute-done.4.refs_1_.first_ref, bf16[240,1536]{1,0:T(8,128)(2,1)S(1)} %collective-permute-done.5.refs_0_.second_ref, bf16[96,768]{1,0:T(8,128)(2,1)S(1)} %collective-permute-done.6.piece_ref), custom_call_target="tpu_custom_call" | custom-call | flops 1 | bytes 1 | tf_op jit(solution)/shard_map/join/pallas_call | solution.py:127
  51.6 1.2 %collective-permute-start.15 = (bf16[144,1536]{1,0:T(8,128)(2,1)}, bf16[144,1536]{1,0:T(8,128)(2,1)S(1)}, u32[]{:S(2)}, u32[]{:S(2)}) collective-permute-start(bf16[144,1536]{1,0:T(8,128)(2,1)} %join.1.refs_12_), channel_id=1, source_target_pairs={{0,8},{4,12},{8,0},{12,4},{1,9},{5,13},{9,1},{13,5},{2,10},{6,14},... | collective-permute-start | bytes 1327112 | tf_op jit(solution)/shard_map/ppermute | solution.py:488
  52.8 0.1 collective-permute-start.14
  53.0 3.4 %project.4 = (bf16[192,384]{1,0:T(8,128)(2,1)}, bf16[192,768]{1,0:T(8,128)(2,1)}) custom-call(s32[1]{0:T(128)} %bitcast.1.place_ref, f32[1,1536]{1,0:T(1,128)S(1)} %broadcast_in_dim.10.gain_ref, bf16[768,768]{1,0:T(8,128)(2,1)S(1)} %get-tuple-element.60.own_front, bf16[768,768]{1,0:T(8,128)(2,1)S(1)} %get-tuple-element.61.own_back, ...), custom_call_target="tpu_custom_call" | custom-call | flops 1 | bytes 1 | tf_op jit(solution)/shard_map/project/pallas_call | solution.py:181
  56.4 3.0 %collective-permute-start.9 = (bf16[192,768]{1,0:T(8,128)(2,1)}, bf16[192,768]{1,0:T(8,128)(2,1)S(1)}, u32[]{:S(2)}, u32[]{:S(2)}) collective-permute-start(bf16[192,768]{1,0:T(8,128)(2,1)} %get-tuple-element.70.refs_4_), channel_id=1, source_target_pairs={{0,16},{16,0},{1,17},{17,1},{2,18},{18,2},{3,19},{19,3},{4,20},{20... | collective-permute-start | bytes 884744 | tf_op jit(solution)/shard_map/ppermute | solution.py:497
  59.4 2.0 %collective-permute-start.8 = (bf16[192,768]{1,0:T(8,128)(2,1)}, bf16[192,768]{1,0:T(8,128)(2,1)S(1)}, u32[]{:S(2)}, u32[]{:S(2)}) collective-permute-start(bf16[192,768]{1,0:T(8,128)(2,1)} %get-tuple-element.70.refs_4_), channel_id=1, source_target_pairs={{16,8},{20,12},{8,16},{12,20},{17,9},{21,13},{9,17},{13,21},{18,10... | collective-permute-start | bytes 884744 | tf_op jit(solution)/shard_map/ppermute | solution.py:497
  61.5 0.4 collective-permute-done.15.refs_14_
  61.9 0.8 collective-permute-done.14.refs_13_
  62.7 0.0 collective-permute-start.16
  62.7 0.0 collective-permute-done.9.refs_7_
  62.7 5.0 %collective-permute-done.8.refs_10_ = bf16[192,768]{1,0:T(8,128)(2,1)S(1)} collective-permute-done((bf16[192,768]{1,0:T(8,128)(2,1)}, bf16[192,768]{1,0:T(8,128)(2,1)S(1)}, u32[]{:S(2)}, u32[]{:S(2)}) %collective-permute-start.8) | collective-permute-done | bytes 294944 | tf_op jit(solution)/shard_map/ppermute | solution.py:497
  67.7 0.0 collective-permute-done.7.refs_0_
  67.7 3.4 %project.5 = (bf16[192,384]{1,0:T(8,128)(2,1)}, bf16[192,768]{1,0:T(8,128)(2,1)}) custom-call(s32[1]{0:T(128)} %bitcast.1.place_ref, f32[1,1536]{1,0:T(1,128)S(1)} %broadcast_in_dim.10.gain_ref, bf16[768,768]{1,0:T(8,128)(2,1)S(1)} %get-tuple-element.60.own_front, bf16[768,768]{1,0:T(8,128)(2,1)S(1)} %get-tuple-element.61.own_back, ...), custom_call_target="tpu_custom_call" | custom-call | flops 1073741824 | bytes 1 | tf_op jit(solution)/shard_map/project/pallas_call | solution.py:181
  71.1 3.1 %collective-permute-start.13 = (bf16[192,768]{1,0:T(8,128)(2,1)}, bf16[192,768]{1,0:T(8,128)(2,1)S(1)}, u32[]{:S(2)}, u32[]{:S(2)}) collective-permute-start(bf16[192,768]{1,0:T(8,128)(2,1)} %get-tuple-element.74.refs_5_), channel_id=1, source_target_pairs={{16,8},{20,12},{8,16},{12,20},{17,9},{21,13},{9,17},{13,21},{18,10... | collective-permute-start | bytes 884744 | tf_op jit(solution)/shard_map/ppermute | solution.py:497
  74.2 0.1 collective-permute-start.12
  74.3 5.1 %collective-permute-done.13.refs_11_ = bf16[192,768]{1,0:T(8,128)(2,1)S(1)} collective-permute-done((bf16[192,768]{1,0:T(8,128)(2,1)}, bf16[192,768]{1,0:T(8,128)(2,1)S(1)}, u32[]{:S(2)}, u32[]{:S(2)}) %collective-permute-start.13) | collective-permute-done | bytes 294944 | tf_op jit(solution)/shard_map/ppermute | solution.py:497
  79.4 0.0 collective-permute-done.12.refs_8_
  79.4 0.0 collective-permute-done.16.refs_15_
  79.4 0.0 copy-start.4
  79.4 3.7 %window.1 = (bf16[768,384]{1,0:T(8,128)(2,1)S(1)}, bf16[2304,768]{1,0:T(8,128)(2,1)S(1)}, bf16[3,18,128,128]{3,2,1,0:T(8,128)(2,1)S(1)}, bf16[576,1536]{1,0:T(8,128)(2,1)}) custom-call(s32[8]{0:T(128)S(1)} %stack.77.place_ref, bf16[384,384]{1,0:T(8,128)(2,1)} %get-tuple-element.64.refs_0_, bf16[192,384]{1,0:T(8,128)(2,1)} %get-tuple-element.69.refs_1_, ...), custom_call_target="tpu_custom_call" | custom-call | bytes 8257536 | tf_op jit(solution)/shard_map/window/pallas_call | solution.py:242
  83.1 0.1 collective-permute-start.17
  83.2 4.6 %attend.2 = (bf16[192,384]{1,0:T(8,128)(2,1)}, bf16[192,384]{1,0:T(8,128)(2,1)}) custom-call(s32[8]{0:T(128)S(1)} %stack.77.place_ref, s32[6,12]{1,0:T(8,128)S(1)} %bitcast.24, s32[3]{0:T(128)S(1)} %copy-done.2, bf16[768,384]{1,0:T(8,128)(2,1)S(1)} %get-tuple-element.87.q_all, bf16[2304,768]{1,0:T(8,128)(2,1)S(1)} %get-tuple-element.84.kv_all, ...), custom_call_target="tpu_custom_call" | custom-call | flops 17179869184 | bytes 1048576 | tf_op jit(solution)/shard_map/attend/pallas_call | solution.py:401
  87.8 2.4 %collective-permute-start.18 = (bf16[192,384]{1,0:T(8,128)(2,1)}, bf16[192,384]{1,0:T(8,128)(2,1)S(1)}, u32[]{:S(2)}, u32[]{:S(2)}) collective-permute-start(bf16[192,384]{1,0:T(8,128)(2,1)} %get-tuple-element.91), channel_id=1, source_target_pairs={{0,2},{1,3},{2,0},{3,1},{4,18},{5,19},{6,16},{7,17},{8,10},{9,11},... | collective-permute-start | bytes 442376 | tf_op jit(solution)/shard_map/ppermute | solution.py:478
  90.2 0.0 collective-permute-done.17.refs_4_
  90.2 7.3 %attend.3 = (bf16[192,384]{1,0:T(8,128)(2,1)}, bf16[192,384]{1,0:T(8,128)(2,1)}, bf16[4,2,384,768]{3,2,1,0:T(8,128)(2,1)S(1)}) custom-call(s32[8]{0:T(128)S(1)} %stack.77.place_ref, s32[6,12]{1,0:T(8,128)S(1)} %bitcast.25, s32[3]{0:T(128)S(1)} %copy-done.1, bf16[768,384]{1,0:T(8,128)(2,1)S(1)} %get-tuple-element.87.q_all, ...), custom_call_target="tpu_custom_call" | custom-call | flops 17179869184 | bytes 1048576 | tf_op jit(solution)/shard_map/attend/pallas_call | solution.py:401
  97.6 2.0 %collective-permute-start.19 = (bf16[192,384]{1,0:T(8,128)(2,1)S(1)}, bf16[192,384]{1,0:T(8,128)(2,1)S(1)}, u32[]{:S(2)}, u32[]{:S(2)}) collective-permute-start(bf16[192,384]{1,0:T(8,128)(2,1)S(1)} %copy-done.6), channel_id=1, source_target_pairs={{0,3},{1,2},{2,1},{3,0},{4,19},{5,18},{6,17},{7,16},{8,11},{9,10},... | collective-permute-start | bytes 442376 | tf_op jit(solution)/shard_map/ppermute | solution.py:478
  99.6 2.8 %collective-permute-start.20 = (bf16[192,384]{1,0:T(8,128)(2,1)}, bf16[192,384]{1,0:T(8,128)(2,1)S(1)}, u32[]{:S(2)}, u32[]{:S(2)}) collective-permute-start(bf16[192,384]{1,0:T(8,128)(2,1)} %get-tuple-element.95), channel_id=1, source_target_pairs={{0,0},{1,1},{2,2},{3,3},{4,16},{5,17},{6,18},{7,19},{8,8},{9,9},{1... | collective-permute-start | bytes 442376 | tf_op jit(solution)/shard_map/ppermute | solution.py:478
  102.5 0.1 collective-permute-start.21
  102.5 0.0 collective-permute-done.18.refs_0_
  102.6 4.0 %collective-permute-done.19.refs_1_ = bf16[192,384]{1,0:T(8,128)(2,1)S(1)} collective-permute-done((bf16[192,384]{1,0:T(8,128)(2,1)S(1)}, bf16[192,384]{1,0:T(8,128)(2,1)S(1)}, u32[]{:S(2)}, u32[]{:S(2)}) %collective-permute-start.19) | collective-permute-done | bytes 147488 | tf_op jit(solution)/shard_map/ppermute | solution.py:478
  106.6 2.2 %collective-permute-done.20.refs_2_ = bf16[192,384]{1,0:T(8,128)(2,1)S(1)} collective-permute-done((bf16[192,384]{1,0:T(8,128)(2,1)}, bf16[192,384]{1,0:T(8,128)(2,1)S(1)}, u32[]{:S(2)}, u32[]{:S(2)}) %collective-permute-start.20) | collective-permute-done | bytes 147488 | tf_op jit(solution)/shard_map/ppermute | solution.py:478
  108.8 0.0 collective-permute-done.21.refs_3_
  108.8 2.7 %output.1 = bf16[1,192,1536]{2,1,0:T(8,128)(2,1)} custom-call(s32[4]{0:T(128)S(1)} %pad_add_fusion.place_ref, bf16[4,2,384,768]{3,2,1,0:T(8,128)(2,1)S(1)} %get-tuple-element.90.weight, bf16[192,384]{1,0:T(8,128)(2,1)S(1)} %hold.3.refs_0_, bf16[192,384]{1,0:T(8,128)(2,1)S(1)} %collective-permute-done.19.refs_1_, ...), custom_call_target="tpu_custom_call" | custom-call | flops 1 | bytes 1 | tf_op jit(solution)/shard_map/output/pallas_call | solution.py:427
  (15 shorter events, 0.1 us)
Async XLA Ops:
  2.1 25.5 %collective-permute-start.4 = (bf16[240,1536]{1,0:T(8,128)(2,1)}, bf16[240,1536]{1,0:T(8,128)(2,1)}, u32[]{:S(2)}, u32[]{:S(2)}) collective-permute-start(bf16[240,1536]{1,0:T(8,128)(2,1)} %get-tuple-element.63), channel_id=1, source_target_pairs={{0,1},{1,3},{2,0},{3,2},{4,17},{5,19},{6,16},{7,18},{8,9},{9,11},{... | collective-permute-start | bytes 2211848 | tf_op jit(solution)/shard_map/ppermute | solution.py:478
  5.8 23.1 %collective-permute-start = (bf16[192,1536]{1,0:T(8,128)(2,1)}, bf16[192,1536]{1,0:T(8,128)(2,1)}, u32[]{:S(2)}, u32[]{:S(2)}) collective-permute-start(bf16[192,1536]{1,0:T(8,128)(2,1)} %bitcast.27), channel_id=1, source_target_pairs={{0,0},{1,1},{2,2},{3,3},{4,16},{5,17},{6,18},{7,19},{8,8},{9,9},{1... | collective-permute-start | bytes 1769480 | tf_op jit(solution)/shard_map/ppermute | solution.py:478
  9.1 14.8 %collective-permute-start.1 = (s32[7,12]{1,0:T(8,128)S(1)}, s32[7,12]{1,0:T(8,128)S(1)}, u32[]{:S(2)}, u32[]{:S(2)}) collective-permute-start(s32[7,12]{1,0:T(8,128)S(1)} %concatenate.3), channel_id=1, source_target_pairs={{0,0},{4,16},{8,8},{12,24},{16,4},{20,20},{24,12},{28,28},{1,1},{5... | collective-permute-start | bytes 1016 | tf_op jit(solution)/shard_map/ppermute | solution.py:508
  23.9 3.1 %copy-start.3 = (s32[7,12]{1,0:T(8,128)}, s32[7,12]{1,0:T(8,128)S(1)}, u32[]{:S(2)}) copy-start(s32[7,12]{1,0:T(8,128)S(1)} %collective-permute-done.1) | copy-start | bytes 1012
  23.9 5.0 %collective-permute-start.2 = (bf16[768,768]{1,0:T(8,128)(2,1)S(1)}, bf16[768,768]{1,0:T(8,128)(2,1)}, u32[]{:S(2)}, u32[]{:S(2)}) collective-permute-start(bf16[768,768]{1,0:T(8,128)(2,1)S(1)} %get-tuple-element.60.own_front), channel_id=1, source_target_pairs={{0,16},{16,0},{1,17},{17,1},{2,18},{18,2},{3,19},{19,3},{4,20},{20... | collective-permute-start | bytes 3538952 | tf_op jit(solution)/shard_map/ppermute | solution.py:510
  23.9 5.0 %collective-permute-start.3 = (bf16[768,768]{1,0:T(8,128)(2,1)S(1)}, bf16[768,768]{1,0:T(8,128)(2,1)S(1)}, u32[]{:S(2)}, u32[]{:S(2)}) collective-permute-start(bf16[768,768]{1,0:T(8,128)(2,1)S(1)} %get-tuple-element.61.own_back), channel_id=1, source_target_pairs={{0,16},{16,0},{1,17},{17,1},{2,18},{18,2},{3,19},{19,3},{4,20},{20... | collective-permute-start | bytes 3538952 | tf_op jit(solution)/shard_map/ppermute | solution.py:510
  27.6 21.7 %collective-permute-start.5 = (bf16[240,1536]{1,0:T(8,128)(2,1)}, bf16[240,1536]{1,0:T(8,128)(2,1)S(1)}, u32[]{:S(2)}, u32[]{:S(2)}) collective-permute-start(bf16[240,1536]{1,0:T(8,128)(2,1)} %collective-permute-done.4.refs_1_.first_ref), channel_id=1, source_target_pairs={{0,1},{1,3},{2,0},{3,2},{4,5},{5,7},{6,4},{7,6},{8,9},{9,11},{10,8... | collective-permute-start | bytes 2211848 | tf_op jit(solution)/shard_map/ppermute | solution.py:500
  28.9 9.3 %copy-start.5 = (bf16[96,768]{1,0:T(8,128)(2,1)S(1)}, bf16[96,768]{1,0:T(8,128)(2,1)}, u32[]{:S(2)}) copy-start(bf16[96,768]{1,0:T(8,128)(2,1)} %get-tuple-element.67) | copy-start | bytes 442372
  34.6 15.3 %collective-permute-start.11 = (bf16[384,768]{1,0:T(8,128)(2,1)}, bf16[384,768]{1,0:T(8,128)(2,1)S(1)}, u32[]{:S(2)}, u32[]{:S(2)}) collective-permute-start(bf16[384,768]{1,0:T(8,128)(2,1)} %get-tuple-element.73.refs_3_), channel_id=1, source_target_pairs={{0,16},{16,0},{1,17},{17,1},{2,18},{18,2},{3,19},{19,3},{4,20},{20... | collective-permute-start | bytes 1769480 | tf_op jit(solution)/shard_map/ppermute | solution.py:497
  35.0 14.9 %collective-permute-start.10 = (bf16[384,768]{1,0:T(8,128)(2,1)}, bf16[384,768]{1,0:T(8,128)(2,1)S(1)}, u32[]{:S(2)}, u32[]{:S(2)}) collective-permute-start(bf16[384,768]{1,0:T(8,128)(2,1)} %get-tuple-element.73.refs_3_), channel_id=1, source_target_pairs={{16,8},{20,12},{8,16},{12,20},{17,9},{21,13},{9,17},{13,21},{18,10... | collective-permute-start | bytes 1769480 | tf_op jit(solution)/shard_map/ppermute | solution.py:497
  38.2 11.1 %collective-permute-start.6 = (bf16[96,768]{1,0:T(8,128)(2,1)S(1)}, bf16[96,768]{1,0:T(8,128)(2,1)S(1)}, u32[]{:S(2)}, u32[]{:S(2)}) collective-permute-start(bf16[96,768]{1,0:T(8,128)(2,1)S(1)} %copy-done.5), channel_id=1, source_target_pairs={{0,2},{1,0},{2,3},{3,1},{4,18},{5,16},{6,19},{7,17},{8,10},{9,8},{... | collective-permute-start | bytes 442376 | tf_op jit(solution)/shard_map/ppermute | solution.py:478
  49.4 18.3 %collective-permute-start.7 = (bf16[192,1536]{1,0:T(8,128)(2,1)S(1)}, bf16[192,1536]{1,0:T(8,128)(2,1)S(1)}, u32[]{:S(2)}, u32[]{:S(2)}) collective-permute-start(bf16[192,1536]{1,0:T(8,128)(2,1)S(1)} %slice.11), channel_id=1, source_target_pairs={{0,1},{1,3},{2,0},{3,2},{4,5},{5,7},{6,4},{7,6},{8,9},{9,11},{10,8... | collective-permute-start | bytes 1769480 | tf_op jit(solution)/shard_map/ppermute | solution.py:500
  51.6 10.3 %collective-permute-start.15 = (bf16[144,1536]{1,0:T(8,128)(2,1)}, bf16[144,1536]{1,0:T(8,128)(2,1)S(1)}, u32[]{:S(2)}, u32[]{:S(2)}) collective-permute-start(bf16[144,1536]{1,0:T(8,128)(2,1)} %join.1.refs_12_), channel_id=1, source_target_pairs={{0,8},{4,12},{8,0},{12,4},{1,9},{5,13},{9,1},{13,5},{2,10},{6,14},... | collective-permute-start | bytes 1327112 | tf_op jit(solution)/shard_map/ppermute | solution.py:488
  52.8 9.9 %collective-permute-start.14 = (bf16[144,1536]{1,0:T(8,128)(2,1)}, bf16[144,1536]{1,0:T(8,128)(2,1)S(1)}, u32[]{:S(2)}, u32[]{:S(2)}) collective-permute-start(bf16[144,1536]{1,0:T(8,128)(2,1)} %join.1.refs_12_), channel_id=1, source_target_pairs={{0,4},{4,0},{8,12},{12,8},{1,5},{5,1},{9,13},{13,9},{2,6},{6,2},{1... | collective-permute-start | bytes 1327112 | tf_op jit(solution)/shard_map/ppermute | solution.py:488
  56.4 6.3 %collective-permute-start.9 = (bf16[192,768]{1,0:T(8,128)(2,1)}, bf16[192,768]{1,0:T(8,128)(2,1)S(1)}, u32[]{:S(2)}, u32[]{:S(2)}) collective-permute-start(bf16[192,768]{1,0:T(8,128)(2,1)} %get-tuple-element.70.refs_4_), channel_id=1, source_target_pairs={{0,16},{16,0},{1,17},{17,1},{2,18},{18,2},{3,19},{19,3},{4,20},{20... | collective-permute-start | bytes 884744 | tf_op jit(solution)/shard_map/ppermute | solution.py:497
  59.4 8.2 %collective-permute-start.8 = (bf16[192,768]{1,0:T(8,128)(2,1)}, bf16[192,768]{1,0:T(8,128)(2,1)S(1)}, u32[]{:S(2)}, u32[]{:S(2)}) collective-permute-start(bf16[192,768]{1,0:T(8,128)(2,1)} %get-tuple-element.70.refs_4_), channel_id=1, source_target_pairs={{16,8},{20,12},{8,16},{12,20},{17,9},{21,13},{9,17},{13,21},{18,10... | collective-permute-start | bytes 884744 | tf_op jit(solution)/shard_map/ppermute | solution.py:497
  62.7 16.7 %collective-permute-start.16 = (bf16[144,1536]{1,0:T(8,128)(2,1)S(1)}, bf16[144,1536]{1,0:T(8,128)(2,1)S(1)}, u32[]{:S(2)}, u32[]{:S(2)}) collective-permute-start(bf16[144,1536]{1,0:T(8,128)(2,1)S(1)} %collective-permute-done.15.refs_14_), channel_id=1, source_target_pairs={{0,4},{4,0},{8,12},{12,8},{1,5},{5,1},{9,13},{13,9},{2,6},{6,2},{1... | collective-permute-start | bytes 1327112 | tf_op jit(solution)/shard_map/ppermute | solution.py:490
  71.1 8.3 %collective-permute-start.13 = (bf16[192,768]{1,0:T(8,128)(2,1)}, bf16[192,768]{1,0:T(8,128)(2,1)S(1)}, u32[]{:S(2)}, u32[]{:S(2)}) collective-permute-start(bf16[192,768]{1,0:T(8,128)(2,1)} %get-tuple-element.74.refs_5_), channel_id=1, source_target_pairs={{16,8},{20,12},{8,16},{12,20},{17,9},{21,13},{9,17},{13,21},{18,10... | collective-permute-start | bytes 884744 | tf_op jit(solution)/shard_map/ppermute | solution.py:497
  74.2 5.2 %collective-permute-start.12 = (bf16[192,768]{1,0:T(8,128)(2,1)}, bf16[192,768]{1,0:T(8,128)(2,1)S(1)}, u32[]{:S(2)}, u32[]{:S(2)}) collective-permute-start(bf16[192,768]{1,0:T(8,128)(2,1)} %get-tuple-element.74.refs_5_), channel_id=1, source_target_pairs={{0,16},{16,0},{1,17},{17,1},{2,18},{18,2},{3,19},{19,3},{4,20},{20... | collective-permute-start | bytes 884744 | tf_op jit(solution)/shard_map/ppermute | solution.py:497
  79.4 3.8 %copy-start.2 = (s32[3]{0:T(128)S(1)}, s32[3]{0:T(128)}, u32[]{:S(2)}) copy-start(s32[3]{0:T(128)} %get-tuple-element.58.turn_ref) | copy-start | bytes 40
  79.4 3.8 %copy-start.4 = (s32[7,12]{1,0:T(8,128)S(1)}, s32[7,12]{1,0:T(8,128)}, u32[]{:S(2)}) copy-start(s32[7,12]{1,0:T(8,128)} %copy-done.3) | copy-start | bytes 1012
  83.1 7.1 %collective-permute-start.17 = (bf16[576,1536]{1,0:T(8,128)(2,1)}, bf16[576,1536]{1,0:T(8,128)(2,1)S(1)}, u32[]{:S(2)}, u32[]{:S(2)}) collective-permute-start(bf16[576,1536]{1,0:T(8,128)(2,1)} %get-tuple-element.89.refs_3_), channel_id=1, source_target_pairs={{0,16},{16,0},{1,17},{17,1},{2,18},{18,2},{3,19},{19,3},{4,20},{20... | collective-permute-start | bytes 5308424 | tf_op jit(solution)/shard_map/ppermute | solution.py:547
  83.2 7.0 %copy-start = (s32[6]{0:T(128)S(1)}, s32[6]{0:T(128)}, u32[]{:S(2)}) copy-start(s32[6]{0:T(128)} %stack.79.refs_0_) | copy-start | bytes 76
  83.2 7.0 %copy-start.1 = (s32[3]{0:T(128)S(1)}, s32[3]{0:T(128)}, u32[]{:S(2)}) copy-start(s32[3]{0:T(128)} %get-tuple-element.57.turn_ref) | copy-start | bytes 40
  87.8 9.8 %copy-start.6 = (bf16[192,384]{1,0:T(8,128)(2,1)S(1)}, bf16[192,384]{1,0:T(8,128)(2,1)}, u32[]{:S(2)}) copy-start(bf16[192,384]{1,0:T(8,128)(2,1)} %get-tuple-element.94) | copy-start | bytes 442372
  87.8 14.7 %collective-permute-start.18 = (bf16[192,384]{1,0:T(8,128)(2,1)}, bf16[192,384]{1,0:T(8,128)(2,1)S(1)}, u32[]{:S(2)}, u32[]{:S(2)}) collective-permute-start(bf16[192,384]{1,0:T(8,128)(2,1)} %get-tuple-element.91), channel_id=1, source_target_pairs={{0,2},{1,3},{2,0},{3,1},{4,18},{5,19},{6,16},{7,17},{8,10},{9,11},... | collective-permute-start | bytes 442376 | tf_op jit(solution)/shard_map/ppermute | solution.py:478
  97.6 9.0 %collective-permute-start.19 = (bf16[192,384]{1,0:T(8,128)(2,1)S(1)}, bf16[192,384]{1,0:T(8,128)(2,1)S(1)}, u32[]{:S(2)}, u32[]{:S(2)}) collective-permute-start(bf16[192,384]{1,0:T(8,128)(2,1)S(1)} %copy-done.6), channel_id=1, source_target_pairs={{0,3},{1,2},{2,1},{3,0},{4,19},{5,18},{6,17},{7,16},{8,11},{9,10},... | collective-permute-start | bytes 442376 | tf_op jit(solution)/shard_map/ppermute | solution.py:478
  99.6 9.2 %collective-permute-start.20 = (bf16[192,384]{1,0:T(8,128)(2,1)}, bf16[192,384]{1,0:T(8,128)(2,1)S(1)}, u32[]{:S(2)}, u32[]{:S(2)}) collective-permute-start(bf16[192,384]{1,0:T(8,128)(2,1)} %get-tuple-element.95), channel_id=1, source_target_pairs={{0,0},{1,1},{2,2},{3,3},{4,16},{5,17},{6,18},{7,19},{8,8},{9,9},{1... | collective-permute-start | bytes 442376 | tf_op jit(solution)/shard_map/ppermute | solution.py:478
  102.5 6.3 %collective-permute-start.21 = (bf16[192,384]{1,0:T(8,128)(2,1)}, bf16[192,384]{1,0:T(8,128)(2,1)S(1)}, u32[]{:S(2)}, u32[]{:S(2)}) collective-permute-start(bf16[192,384]{1,0:T(8,128)(2,1)} %get-tuple-element.96), channel_id=1, source_target_pairs={{0,1},{1,0},{2,3},{3,2},{4,17},{5,16},{6,19},{7,18},{8,9},{9,8},{1... | collective-permute-start | bytes 442376 | tf_op jit(solution)/shard_map/ppermute | solution.py:478

commit v11 on v9

--- a/solution.py
+++ b/solution.py
@@ -141,14 +141,19 @@
     query_ref, pair_ref, held, query_held, pair_held, sems = refs[blocks:]
     depth, width = own_front.shape[0], query_ref.shape[1]
     first = place_ref[0] == 0
-    loads = copy_all(
-        [(rows[i].at[pl.ds(0, count), :], held.at[pl.ds(i * count, count), :]) for i in range(blocks)], sems
-    )
+    loads = []
+    if blocks > 1:
+        loads = copy_all(
+            [(rows[i].at[pl.ds(0, count), :], held.at[pl.ds(i * count, count), :]) for i in range(blocks)], sems
+        )
     gain = gain_ref[...]
     mine, theirs = [], []
     for i in range(blocks):
-        loads[i].wait()
-        values = held[i * count:(i + 1) * count, :].astype(jnp.float32)
+        if blocks > 1:
+            loads[i].wait()
+            values = held[i * count:(i + 1) * count, :].astype(jnp.float32)
+        else:
+            values = rows[0][:count, :].astype(jnp.float32)
         center = values - jnp.mean(values, axis=-1, keepdims=True)
         spread = jnp.mean(center * center, axis=-1, keepdims=True)
         normalized = (center * lax.rsqrt(spread + epsilon) * gain).astype(jnp.bfloat16)
@@ -181,7 +186,7 @@
     return pl.pallas_call(
         functools.partial(project_kernel, blocks, count),
         out_shape=[pltpu.HBM((total, width), jnp.bfloat16), pltpu.HBM((total, 2 * width), jnp.bfloat16)],
-        in_specs=[SMEM] + [VMEM] * 5 + [HBM] * blocks,
+        in_specs=[SMEM] + [VMEM] * 5 + ([HBM] * blocks if blocks > 1 else [VMEM]),
         out_specs=[HBM, HBM],
         scratch_shapes=[
             pltpu.VMEM((total, depth), jnp.bfloat16),
@@ -530,13 +535,13 @@
 
     query_a, pair_a = project(core_at, [whole, first], count, width, gain, own, far, 1)
     link_a, chip_a = halos(pair_a)
-    second, link_a, chip_a = together(second, link_a, chip_a)
     third = ringed(second[:count])
+    piece, link_a, chip_a = together(piece, link_a, chip_a)
     query_b, pair_b = project(core_at, [second], count, width, gain, own, far, 1)
     shares = shared(join(count, first, second, piece), query_b)
     link_b, chip_b = halos(pair_b)
     third, link_b, chip_b = together(third, link_b, chip_b)
-    query_c, pair_c = project(core_at, [third], count, width, gain, own, far, 1 << 32)
+    query_c, pair_c = project(core_at, [third], count, width, gain, own, far, 1 << 30)
     link_c, chip_c = halos(pair_c)
     q_all, kv_all, vt_all, mine = window(
         place, groups, count, [query_a, query_b, query_c], [pair_a, pair_b, pair_c],

time: 109 us -> 110 us (level)
  starting transfers between devices: 37.4 us -> 39.4 us
  waiting for transfers between devices: 29.6 us -> 27.8 us
    ppermute x7, starting transfers between devices: 15.1 us -> 17.2 us  [moved(): return lax.ppermute(value, ('dp', 'seq', 'head'), pairs)]
    ppermute x1, waiting for transfers between devices: 1.12 us -> 0.01 us  [shared(): lax.ppermute(near[1], 'seq', [(s, s ^ 1) for s in range(seqs)])]
  transfers between devices with their start and end apart: 22 -> 22, of which waited for: 12 -> 11; matrix products, arithmetic and copies ran while one was open for 4% -> 4% of each run, Pallas kernels for 26% -> 26%
where the time goes in v11:
time: 110 us; the launch traced here: 109 us
  starting transfers between devices  39.4 us (36%)
  Pallas kernels  36.7 us (33%)
  waiting for transfers between devices  27.8 us (25%)
  local copies, waits for them, and re-layouts  3.37 us (3%)
    ppermute x7, starting transfers between devices, moved(): return lax.ppermute(value, ('dp', 'seq', 'head'), pairs)  17.2 us
    pallas_call x3, Pallas kernels, project(): pl.pallas_call(functools.partial(project_kernel, blocks, count), out_shap...  12.4 us
    pallas_call x2, Pallas kernels, attend(): pl.pallas_call(functools.partial(attend_kernel, groups, reach, block // 2...  12.3 us
    ppermute x7, waiting for transfers between devices, moved(): return lax.ppermute(value, ('dp', 'seq', 'head'), pairs)  9.99 us
    ppermute x3, starting transfers between devices, halos(): lax.ppermute(pair, ('dp', 'seq'), over_link)  8.92 us
    ppermute x3, waiting for transfers between devices, halos(): lax.ppermute(pair, ('dp', 'seq'), over_link)  8.62 us
    ppermute x2, starting transfers between devices, ringed(): return lax.ppermute(value, 'head', [(z, after[z]) for z in range(layers)])  6.12 us
    ppermute x2, waiting for transfers between devices, ringed(): return lax.ppermute(value, 'head', [(z, after[z]) for z in range(layers)])  5.22 us
  transfers between devices with their start and end apart: 22, of which 11 were waited for; matrix products, arithmetic and copies ran while one was open for 4% of the time, Pallas kernels for 26%

profile of v11, /device:TPU:1, one launch (start us, length us, event | category | flops | bytes accessed | tf_op | source)
XLA Modules:
  0.0 108.9 jit_solution(13661394495663103263)
XLA Ops:
  0.0 2.1 %pack.1 = (bf16[240,1536]{1,0:T(8,128)(2,1)}, bf16[96,768]{1,0:T(8,128)(2,1)}) custom-call(s32[1]{0:T(128)} %bitcast.9.place_ref, bf16[192,1536]{1,0:T(8,128)(2,1)} %bitcast.rows_ref, bf16[384,768]{1,0:T(8,128)(2,1)} %refs_1_.1), custom_call_target="tpu_custom_call" | custom-call | flops 1 | bytes 1 | tf_op jit(solution)/shard_map/pack/pallas_call | solution.py:69
  2.1 3.7 %collective-permute-start.5 = (bf16[240,1536]{1,0:T(8,128)(2,1)}, bf16[240,1536]{1,0:T(8,128)(2,1)}, u32[]{:S(2)}, u32[]{:S(2)}) collective-permute-start(bf16[240,1536]{1,0:T(8,128)(2,1)} %get-tuple-element.61), channel_id=1, source_target_pairs={{0,1},{1,3},{2,0},{3,2},{4,17},{5,19},{6,16},{7,18},{8,9},{9,11},{... | collective-permute-start | bytes 2211848 | tf_op jit(solution)/shard_map/ppermute | solution.py:483
  6.4 0.7 copy.13
  7.1 1.9 %collective-permute-start.1 = (s32[7,12]{1,0:T(8,128)S(1)}, s32[7,12]{1,0:T(8,128)S(1)}, u32[]{:S(2)}, u32[]{:S(2)}) collective-permute-start(s32[7,12]{1,0:T(8,128)S(1)} %concatenate.3), channel_id=1, source_target_pairs={{0,0},{4,16},{8,8},{12,24},{16,4},{20,20},{24,12},{28,28},{1,1},{5... | collective-permute-start | bytes 1016 | tf_op jit(solution)/shard_map/ppermute | solution.py:514
  9.0 1.6 %bundle.1 = (bf16[768,768]{1,0:T(8,128)(2,1)S(1)}, bf16[768,768]{1,0:T(8,128)(2,1)S(1)}) custom-call(bf16[768,384]{1,0:T(8,128)(2,1)} %query_ref.1, bf16[768,384]{1,0:T(8,128)(2,1)} %key_ref.1, bf16[768,384]{1,0:T(8,128)(2,1)} %value_ref.1, bf16[384,768]{1,0:T(8,128)(2,1)} %refs_1_.1), custom_call_target="tpu_custom_call" | custom-call | flops 1 | bytes 1 | tf_op jit(solution)/shard_map/bundle/pallas_call | solution.py:99
  10.7 1.8 %collective-permute-done.1 = s32[7,12]{1,0:T(8,128)S(1)} collective-permute-done((s32[7,12]{1,0:T(8,128)S(1)}, s32[7,12]{1,0:T(8,128)S(1)}, u32[]{:S(2)}, u32[]{:S(2)}) %collective-permute-start.1) | collective-permute-done | bytes 368 | tf_op jit(solution)/shard_map/ppermute | solution.py:514
  12.5 0.0 collective-permute-start.3
  12.5 0.5 collective-permute-start.4
  13.0 1.9 %collective-permute-start = (bf16[192,1536]{1,0:T(8,128)(2,1)}, bf16[192,1536]{1,0:T(8,128)(2,1)}, u32[]{:S(2)}, u32[]{:S(2)}) collective-permute-start(bf16[192,1536]{1,0:T(8,128)(2,1)} %bitcast.rows_ref), channel_id=1, source_target_pairs={{0,0},{1,1},{2,2},{3,3},{4,16},{5,17},{6,18},{7,19},{8,8},{9,9},{1... | collective-permute-start | bytes 1769480 | tf_op jit(solution)/shard_map/ppermute | solution.py:483
  14.9 2.6 %collective-permute-start.2 = (bf16[96,768]{1,0:T(8,128)(2,1)}, bf16[96,768]{1,0:T(8,128)(2,1)}, u32[]{:S(2)}, u32[]{:S(2)}) collective-permute-start(bf16[96,768]{1,0:T(8,128)(2,1)} %get-tuple-element.51), channel_id=1, source_target_pairs={{0,2},{1,0},{2,3},{3,1},{4,18},{5,16},{6,19},{7,17},{8,10},{9,8},{... | collective-permute-start | bytes 442376 | tf_op jit(solution)/shard_map/ppermute | solution.py:483
  17.5 0.1 pad_add_fusion.place_ref
  17.6 0.7 broadcast_in_dim.10.gain_ref
  18.3 0.7 stack.80.refs_0_
  18.9 0.7 add_add_fusion
  19.6 0.5 slice.9
  20.1 0.0 copy-done.3
  20.1 0.7 stack.77.place_ref
  20.8 2.7 %collective-permute-done.5.refs_1_.first_ref = bf16[240,1536]{1,0:T(8,128)(2,1)} collective-permute-done((bf16[240,1536]{1,0:T(8,128)(2,1)}, bf16[240,1536]{1,0:T(8,128)(2,1)}, u32[]{:S(2)}, u32[]{:S(2)}) %collective-permute-start.5) | collective-permute-done | bytes 737312 | tf_op jit(solution)/shard_map/ppermute | solution.py:483
  23.5 4.1 %collective-permute-start.6 = (bf16[240,1536]{1,0:T(8,128)(2,1)}, bf16[240,1536]{1,0:T(8,128)(2,1)S(1)}, u32[]{:S(2)}, u32[]{:S(2)}) collective-permute-start(bf16[240,1536]{1,0:T(8,128)(2,1)} %collective-permute-done.5.refs_1_.first_ref), channel_id=1, source_target_pairs={{0,1},{1,3},{2,0},{3,2},{4,5},{5,7},{6,4},{7,6},{8,9},{9,11},{10,8... | collective-permute-start | bytes 2211848 | tf_op jit(solution)/shard_map/ppermute | solution.py:505
  27.6 0.0 collective-permute-done.2.refs_0_
  27.6 1.7 %collective-permute-done.refs_0_ = bf16[192,1536]{1,0:T(8,128)(2,1)} collective-permute-done((bf16[192,1536]{1,0:T(8,128)(2,1)}, bf16[192,1536]{1,0:T(8,128)(2,1)}, u32[]{:S(2)}, u32[]{:S(2)}) %collective-permute-start) | collective-permute-done | bytes 589856 | tf_op jit(solution)/shard_map/ppermute | solution.py:483
  29.2 0.0 collective-permute-done.3.far_front
  29.2 0.0 collective-permute-done.4.far_back.refs_2_
  29.2 5.7 %project.3 = (bf16[384,384]{1,0:T(8,128)(2,1)}, bf16[384,768]{1,0:T(8,128)(2,1)}) custom-call(s32[1]{0:T(128)} %bitcast.1.place_ref, f32[1,1536]{1,0:T(1,128)S(1)} %broadcast_in_dim.10.gain_ref, bf16[768,768]{1,0:T(8,128)(2,1)S(1)} %get-tuple-element.58.own_front, bf16[768,768]{1,0:T(8,128)(2,1)S(1)} %get-tuple-element.59.own_back, ...), custom_call_target="tpu_custom_call" | custom-call | flops 1 | bytes 1 | tf_op jit(solution)/shard_map/project/pallas_call | solution.py:186
  34.9 0.1 collective-permute-start.11
  35.0 3.5 %collective-permute-start.10 = (bf16[384,768]{1,0:T(8,128)(2,1)}, bf16[384,768]{1,0:T(8,128)(2,1)S(1)}, u32[]{:S(2)}, u32[]{:S(2)}) collective-permute-start(bf16[384,768]{1,0:T(8,128)(2,1)} %get-tuple-element.67.refs_3_), channel_id=1, source_target_pairs={{16,8},{20,12},{8,16},{12,20},{17,9},{21,13},{9,17},{13,21},{18,10... | collective-permute-start | bytes 1769480 | tf_op jit(solution)/shard_map/ppermute | solution.py:502
  38.5 5.2 %collective-permute-done.6.refs_0_.second_ref = bf16[240,1536]{1,0:T(8,128)(2,1)S(1)} collective-permute-done((bf16[240,1536]{1,0:T(8,128)(2,1)}, bf16[240,1536]{1,0:T(8,128)(2,1)S(1)}, u32[]{:S(2)}, u32[]{:S(2)}) %collective-permute-start.6) | collective-permute-done | bytes 737312 | tf_op jit(solution)/shard_map/ppermute | solution.py:505
  43.8 2.1 %collective-permute-start.7 = (bf16[192,1536]{1,0:T(8,128)(2,1)S(1)}, bf16[192,1536]{1,0:T(8,128)(2,1)S(1)}, u32[]{:S(2)}, u32[]{:S(2)}) collective-permute-start(bf16[192,1536]{1,0:T(8,128)(2,1)S(1)} %slice.12), channel_id=1, source_target_pairs={{0,1},{1,3},{2,0},{3,2},{4,5},{5,7},{6,4},{7,6},{8,9},{9,11},{10,8... | collective-permute-start | bytes 1769480 | tf_op jit(solution)/shard_map/ppermute | solution.py:505
  45.9 0.0 collective-permute-done.11.refs_6_
  45.9 0.6 collective-permute-done.10.refs_9_
  46.4 1.9 %join.1.refs_12_ = bf16[144,1536]{1,0:T(8,128)(2,1)} custom-call(bf16[240,1536]{1,0:T(8,128)(2,1)} %collective-permute-done.5.refs_1_.first_ref, bf16[240,1536]{1,0:T(8,128)(2,1)S(1)} %collective-permute-done.6.refs_0_.second_ref, bf16[96,768]{1,0:T(8,128)(2,1)} %hold.2.piece_ref), custom_call_target="tpu_custom_call" | custom-call | flops 1 | bytes 1 | tf_op jit(solution)/shard_map/join/pallas_call | solution.py:127
  48.3 0.8 collective-permute-start.15
  49.1 0.0 collective-permute-start.14
  49.1 3.4 %project.4 = (bf16[192,384]{1,0:T(8,128)(2,1)}, bf16[192,768]{1,0:T(8,128)(2,1)}) custom-call(s32[1]{0:T(128)} %bitcast.1.place_ref, f32[1,1536]{1,0:T(1,128)S(1)} %broadcast_in_dim.10.gain_ref, bf16[768,768]{1,0:T(8,128)(2,1)S(1)} %get-tuple-element.58.own_front, bf16[768,768]{1,0:T(8,128)(2,1)S(1)} %get-tuple-element.59.own_back, ...), custom_call_target="tpu_custom_call" | custom-call | flops 1 | bytes 1 | tf_op jit(solution)/shard_map/project/pallas_call | solution.py:186
  52.5 2.4 %collective-permute-start.9 = (bf16[192,768]{1,0:T(8,128)(2,1)}, bf16[192,768]{1,0:T(8,128)(2,1)S(1)}, u32[]{:S(2)}, u32[]{:S(2)}) collective-permute-start(bf16[192,768]{1,0:T(8,128)(2,1)} %get-tuple-element.64.refs_4_), channel_id=1, source_target_pairs={{0,16},{16,0},{1,17},{17,1},{2,18},{18,2},{3,19},{19,3},{4,20},{20... | collective-permute-start | bytes 884744 | tf_op jit(solution)/shard_map/ppermute | solution.py:502
  54.9 2.0 %collective-permute-start.8 = (bf16[192,768]{1,0:T(8,128)(2,1)}, bf16[192,768]{1,0:T(8,128)(2,1)S(1)}, u32[]{:S(2)}, u32[]{:S(2)}) collective-permute-start(bf16[192,768]{1,0:T(8,128)(2,1)} %get-tuple-element.64.refs_4_), channel_id=1, source_target_pairs={{16,8},{20,12},{8,16},{12,20},{17,9},{21,13},{9,17},{13,21},{18,10... | collective-permute-start | bytes 884744 | tf_op jit(solution)/shard_map/ppermute | solution.py:502
  56.9 2.2 %collective-permute-done.15.refs_14_ = bf16[144,1536]{1,0:T(8,128)(2,1)S(1)} collective-permute-done((bf16[144,1536]{1,0:T(8,128)(2,1)}, bf16[144,1536]{1,0:T(8,128)(2,1)S(1)}, u32[]{:S(2)}, u32[]{:S(2)}) %collective-permute-start.15) | collective-permute-done | bytes 442400 | tf_op jit(solution)/shard_map/ppermute | solution.py:493
  59.1 0.0 collective-permute-done.14.refs_13_
  59.1 1.3 %collective-permute-start.16 = (bf16[144,1536]{1,0:T(8,128)(2,1)S(1)}, bf16[144,1536]{1,0:T(8,128)(2,1)S(1)}, u32[]{:S(2)}, u32[]{:S(2)}) collective-permute-start(bf16[144,1536]{1,0:T(8,128)(2,1)S(1)} %collective-permute-done.15.refs_14_), channel_id=1, source_target_pairs={{0,4},{4,0},{8,12},{12,8},{1,5},{5,1},{9,13},{13,9},{2,6},{6,2},{1... | collective-permute-start | bytes 1327112 | tf_op jit(solution)/shard_map/ppermute | solution.py:495
  60.4 0.0 collective-permute-done.9.refs_7_
  60.4 3.3 %collective-permute-done.8.refs_10_ = bf16[192,768]{1,0:T(8,128)(2,1)S(1)} collective-permute-done((bf16[192,768]{1,0:T(8,128)(2,1)}, bf16[192,768]{1,0:T(8,128)(2,1)S(1)}, u32[]{:S(2)}, u32[]{:S(2)}) %collective-permute-start.8) | collective-permute-done | bytes 294944 | tf_op jit(solution)/shard_map/ppermute | solution.py:502
  63.7 0.0 collective-permute-done.7.refs_0_
  63.7 3.4 %project.5 = (bf16[192,384]{1,0:T(8,128)(2,1)}, bf16[192,768]{1,0:T(8,128)(2,1)}) custom-call(s32[1]{0:T(128)} %bitcast.1.place_ref, f32[1,1536]{1,0:T(1,128)S(1)} %broadcast_in_dim.10.gain_ref, bf16[768,768]{1,0:T(8,128)(2,1)S(1)} %get-tuple-element.58.own_front, bf16[768,768]{1,0:T(8,128)(2,1)S(1)} %get-tuple-element.59.own_back, ...), custom_call_target="tpu_custom_call" | custom-call | flops 1073741824 | bytes 1 | tf_op jit(solution)/shard_map/project/pallas_call | solution.py:186
  67.0 3.4 %collective-permute-start.13 = (bf16[192,768]{1,0:T(8,128)(2,1)}, bf16[192,768]{1,0:T(8,128)(2,1)S(1)}, u32[]{:S(2)}, u32[]{:S(2)}) collective-permute-start(bf16[192,768]{1,0:T(8,128)(2,1)} %get-tuple-element.68.refs_5_), channel_id=1, source_target_pairs={{16,8},{20,12},{8,16},{12,20},{17,9},{21,13},{9,17},{13,21},{18,10... | collective-permute-start | bytes 884744 | tf_op jit(solution)/shard_map/ppermute | solution.py:502
  70.4 0.1 collective-permute-start.12
  70.5 4.8 %collective-permute-done.13.refs_11_ = bf16[192,768]{1,0:T(8,128)(2,1)S(1)} collective-permute-done((bf16[192,768]{1,0:T(8,128)(2,1)}, bf16[192,768]{1,0:T(8,128)(2,1)S(1)}, u32[]{:S(2)}, u32[]{:S(2)}) %collective-permute-start.13) | collective-permute-done | bytes 294944 | tf_op jit(solution)/shard_map/ppermute | solution.py:502
  75.3 0.0 collective-permute-done.12.refs_8_
  75.3 0.0 collective-permute-done.16.refs_15_
  75.3 3.7 %window.1 = (bf16[768,384]{1,0:T(8,128)(2,1)S(1)}, bf16[2304,768]{1,0:T(8,128)(2,1)S(1)}, bf16[3,18,128,128]{3,2,1,0:T(8,128)(2,1)S(1)}, bf16[576,1536]{1,0:T(8,128)(2,1)}) custom-call(s32[8]{0:T(128)S(1)} %stack.77.place_ref, bf16[384,384]{1,0:T(8,128)(2,1)} %get-tuple-element.62.refs_0_, bf16[192,384]{1,0:T(8,128)(2,1)} %get-tuple-element.63.refs_1_, ...), custom_call_target="tpu_custom_call" | custom-call | bytes 8257536 | tf_op jit(solution)/shard_map/window/pallas_call | solution.py:247
  79.0 0.1 collective-permute-start.17
  79.1 5.3 %attend.2 = (bf16[192,384]{1,0:T(8,128)(2,1)}, bf16[192,384]{1,0:T(8,128)(2,1)}) custom-call(s32[8]{0:T(128)S(1)} %stack.77.place_ref, s32[6,12]{1,0:T(8,128)S(1)} %bitcast.24, s32[3]{0:T(128)S(1)} %copy-done.2, bf16[768,384]{1,0:T(8,128)(2,1)S(1)} %get-tuple-element.81.q_all, bf16[2304,768]{1,0:T(8,128)(2,1)S(1)} %get-tuple-element.78.kv_all, ...), custom_call_target="tpu_custom_call" | custom-call | flops 17179869184 | bytes 1048576 | tf_op jit(solution)/shard_map/attend/pallas_call | solution.py:406
  84.5 1.3 %collective-permute-start.18 = (bf16[192,384]{1,0:T(8,128)(2,1)}, bf16[192,384]{1,0:T(8,128)(2,1)S(1)}, u32[]{:S(2)}, u32[]{:S(2)}) collective-permute-start(bf16[192,384]{1,0:T(8,128)(2,1)} %get-tuple-element.85), channel_id=1, source_target_pairs={{0,2},{1,3},{2,0},{3,1},{4,18},{5,19},{6,16},{7,17},{8,10},{9,11},... | collective-permute-start | bytes 442376 | tf_op jit(solution)/shard_map/ppermute | solution.py:483
  85.8 0.0 collective-permute-done.17.refs_4_
  85.8 0.0 copy-done.1
  85.8 6.9 %attend.3 = (bf16[192,384]{1,0:T(8,128)(2,1)}, bf16[192,384]{1,0:T(8,128)(2,1)}, bf16[4,2,384,768]{3,2,1,0:T(8,128)(2,1)S(1)}) custom-call(s32[8]{0:T(128)S(1)} %stack.77.place_ref, s32[6,12]{1,0:T(8,128)S(1)} %bitcast.25, s32[3]{0:T(128)S(1)} %copy-done.1, bf16[768,384]{1,0:T(8,128)(2,1)S(1)} %get-tuple-element.81.q_all, ...), custom_call_target="tpu_custom_call" | custom-call | flops 17179869184 | bytes 1048576 | tf_op jit(solution)/shard_map/attend/pallas_call | solution.py:406
  92.7 0.0 copy-done.5
  92.7 4.1 %collective-permute-start.19 = (bf16[192,384]{1,0:T(8,128)(2,1)S(1)}, bf16[192,384]{1,0:T(8,128)(2,1)S(1)}, u32[]{:S(2)}, u32[]{:S(2)}) collective-permute-start(bf16[192,384]{1,0:T(8,128)(2,1)S(1)} %copy-done.5), channel_id=1, source_target_pairs={{0,3},{1,2},{2,1},{3,0},{4,19},{5,18},{6,17},{7,16},{8,11},{9,10},... | collective-permute-start | bytes 442376 | tf_op jit(solution)/shard_map/ppermute | solution.py:483
  96.9 3.6 %collective-permute-start.20 = (bf16[192,384]{1,0:T(8,128)(2,1)}, bf16[192,384]{1,0:T(8,128)(2,1)S(1)}, u32[]{:S(2)}, u32[]{:S(2)}) collective-permute-start(bf16[192,384]{1,0:T(8,128)(2,1)} %get-tuple-element.89), channel_id=1, source_target_pairs={{0,0},{1,1},{2,2},{3,3},{4,16},{5,17},{6,18},{7,19},{8,8},{9,9},{1... | collective-permute-start | bytes 442376 | tf_op jit(solution)/shard_map/ppermute | solution.py:483
  100.4 0.1 collective-permute-start.21
  100.5 0.0 collective-permute-done.18.refs_0_
  100.5 0.9 collective-permute-done.19.refs_1_
  101.5 3.0 %collective-permute-done.20.refs_2_ = bf16[192,384]{1,0:T(8,128)(2,1)S(1)} collective-permute-done((bf16[192,384]{1,0:T(8,128)(2,1)}, bf16[192,384]{1,0:T(8,128)(2,1)S(1)}, u32[]{:S(2)}, u32[]{:S(2)}) %collective-permute-start.20) | collective-permute-done | bytes 147488 | tf_op jit(solution)/shard_map/ppermute | solution.py:483
  104.4 1.7 %collective-permute-done.21.refs_3_ = bf16[192,384]{1,0:T(8,128)(2,1)S(1)} collective-permute-done((bf16[192,384]{1,0:T(8,128)(2,1)}, bf16[192,384]{1,0:T(8,128)(2,1)S(1)}, u32[]{:S(2)}, u32[]{:S(2)}) %collective-permute-start.21) | collective-permute-done | bytes 147488 | tf_op jit(solution)/shard_map/ppermute | solution.py:483
  106.2 2.7 %output.1 = bf16[1,192,1536]{2,1,0:T(8,128)(2,1)} custom-call(s32[4]{0:T(128)S(1)} %pad_add_fusion.place_ref, bf16[4,2,384,768]{3,2,1,0:T(8,128)(2,1)S(1)} %get-tuple-element.84.weight, bf16[192,384]{1,0:T(8,128)(2,1)S(1)} %hold.3.refs_0_, bf16[192,384]{1,0:T(8,128)(2,1)S(1)} %collective-permute-done.19.refs_1_, ...), custom_call_target="tpu_custom_call" | custom-call | flops 1 | bytes 1 | tf_op jit(solution)/shard_map/output/pallas_call | solution.py:432
  (13 shorter events, 0.1 us)
Async XLA Ops:
  2.1 21.4 %collective-permute-start.5 = (bf16[240,1536]{1,0:T(8,128)(2,1)}, bf16[240,1536]{1,0:T(8,128)(2,1)}, u32[]{:S(2)}, u32[]{:S(2)}) collective-permute-start(bf16[240,1536]{1,0:T(8,128)(2,1)} %get-tuple-element.61), channel_id=1, source_target_pairs={{0,1},{1,3},{2,0},{3,2},{4,17},{5,19},{6,16},{7,18},{8,9},{9,11},{... | collective-permute-start | bytes 2211848 | tf_op jit(solution)/shard_map/ppermute | solution.py:483
  7.1 5.4 %collective-permute-start.1 = (s32[7,12]{1,0:T(8,128)S(1)}, s32[7,12]{1,0:T(8,128)S(1)}, u32[]{:S(2)}, u32[]{:S(2)}) collective-permute-start(s32[7,12]{1,0:T(8,128)S(1)} %concatenate.3), channel_id=1, source_target_pairs={{0,0},{4,16},{8,8},{12,24},{16,4},{20,20},{24,12},{28,28},{1,1},{5... | collective-permute-start | bytes 1016 | tf_op jit(solution)/shard_map/ppermute | solution.py:514
  12.5 7.6 %copy-start.3 = (s32[7,12]{1,0:T(8,128)}, s32[7,12]{1,0:T(8,128)S(1)}, u32[]{:S(2)}) copy-start(s32[7,12]{1,0:T(8,128)S(1)} %collective-permute-done.1) | copy-start | bytes 1012
  12.5 16.8 %collective-permute-start.3 = (bf16[768,768]{1,0:T(8,128)(2,1)S(1)}, bf16[768,768]{1,0:T(8,128)(2,1)}, u32[]{:S(2)}, u32[]{:S(2)}) collective-permute-start(bf16[768,768]{1,0:T(8,128)(2,1)S(1)} %get-tuple-element.58.own_front), channel_id=1, source_target_pairs={{0,16},{16,0},{1,17},{17,1},{2,18},{18,2},{3,19},{19,3},{4,20},{20... | collective-permute-start | bytes 3538952 | tf_op jit(solution)/shard_map/ppermute | solution.py:516
  12.5 16.8 %collective-permute-start.4 = (bf16[768,768]{1,0:T(8,128)(2,1)S(1)}, bf16[768,768]{1,0:T(8,128)(2,1)S(1)}, u32[]{:S(2)}, u32[]{:S(2)}) collective-permute-start(bf16[768,768]{1,0:T(8,128)(2,1)S(1)} %get-tuple-element.59.own_back), channel_id=1, source_target_pairs={{0,16},{16,0},{1,17},{17,1},{2,18},{18,2},{3,19},{19,3},{4,20},{20... | collective-permute-start | bytes 3538952 | tf_op jit(solution)/shard_map/ppermute | solution.py:516
  13.0 16.3 %collective-permute-start = (bf16[192,1536]{1,0:T(8,128)(2,1)}, bf16[192,1536]{1,0:T(8,128)(2,1)}, u32[]{:S(2)}, u32[]{:S(2)}) collective-permute-start(bf16[192,1536]{1,0:T(8,128)(2,1)} %bitcast.rows_ref), channel_id=1, source_target_pairs={{0,0},{1,1},{2,2},{3,3},{4,16},{5,17},{6,18},{7,19},{8,8},{9,9},{1... | collective-permute-start | bytes 1769480 | tf_op jit(solution)/shard_map/ppermute | solution.py:483
  14.9 12.6 %collective-permute-start.2 = (bf16[96,768]{1,0:T(8,128)(2,1)}, bf16[96,768]{1,0:T(8,128)(2,1)}, u32[]{:S(2)}, u32[]{:S(2)}) collective-permute-start(bf16[96,768]{1,0:T(8,128)(2,1)} %get-tuple-element.51), channel_id=1, source_target_pairs={{0,2},{1,0},{2,3},{3,1},{4,18},{5,16},{6,19},{7,17},{8,10},{9,8},{... | collective-permute-start | bytes 442376 | tf_op jit(solution)/shard_map/ppermute | solution.py:483
  23.5 20.3 %collective-permute-start.6 = (bf16[240,1536]{1,0:T(8,128)(2,1)}, bf16[240,1536]{1,0:T(8,128)(2,1)S(1)}, u32[]{:S(2)}, u32[]{:S(2)}) collective-permute-start(bf16[240,1536]{1,0:T(8,128)(2,1)} %collective-permute-done.5.refs_1_.first_ref), channel_id=1, source_target_pairs={{0,1},{1,3},{2,0},{3,2},{4,5},{5,7},{6,4},{7,6},{8,9},{9,11},{10,8... | collective-permute-start | bytes 2211848 | tf_op jit(solution)/shard_map/ppermute | solution.py:505
  34.9 10.9 %collective-permute-start.11 = (bf16[384,768]{1,0:T(8,128)(2,1)}, bf16[384,768]{1,0:T(8,128)(2,1)S(1)}, u32[]{:S(2)}, u32[]{:S(2)}) collective-permute-start(bf16[384,768]{1,0:T(8,128)(2,1)} %get-tuple-element.67.refs_3_), channel_id=1, source_target_pairs={{0,16},{16,0},{1,17},{17,1},{2,18},{18,2},{3,19},{19,3},{4,20},{20... | collective-permute-start | bytes 1769480 | tf_op jit(solution)/shard_map/ppermute | solution.py:502
  35.0 11.4 %collective-permute-start.10 = (bf16[384,768]{1,0:T(8,128)(2,1)}, bf16[384,768]{1,0:T(8,128)(2,1)S(1)}, u32[]{:S(2)}, u32[]{:S(2)}) collective-permute-start(bf16[384,768]{1,0:T(8,128)(2,1)} %get-tuple-element.67.refs_3_), channel_id=1, source_target_pairs={{16,8},{20,12},{8,16},{12,20},{17,9},{21,13},{9,17},{13,21},{18,10... | collective-permute-start | bytes 1769480 | tf_op jit(solution)/shard_map/ppermute | solution.py:502
  43.8 19.9 %collective-permute-start.7 = (bf16[192,1536]{1,0:T(8,128)(2,1)S(1)}, bf16[192,1536]{1,0:T(8,128)(2,1)S(1)}, u32[]{:S(2)}, u32[]{:S(2)}) collective-permute-start(bf16[192,1536]{1,0:T(8,128)(2,1)S(1)} %slice.12), channel_id=1, source_target_pairs={{0,1},{1,3},{2,0},{3,2},{4,5},{5,7},{6,4},{7,6},{8,9},{9,11},{10,8... | collective-permute-start | bytes 1769480 | tf_op jit(solution)/shard_map/ppermute | solution.py:505
  48.3 10.7 %collective-permute-start.15 = (bf16[144,1536]{1,0:T(8,128)(2,1)}, bf16[144,1536]{1,0:T(8,128)(2,1)S(1)}, u32[]{:S(2)}, u32[]{:S(2)}) collective-permute-start(bf16[144,1536]{1,0:T(8,128)(2,1)} %join.1.refs_12_), channel_id=1, source_target_pairs={{0,8},{4,12},{8,0},{12,4},{1,9},{5,13},{9,1},{13,5},{2,10},{6,14},... | collective-permute-start | bytes 1327112 | tf_op jit(solution)/shard_map/ppermute | solution.py:493
  49.1 10.0 %collective-permute-start.14 = (bf16[144,1536]{1,0:T(8,128)(2,1)}, bf16[144,1536]{1,0:T(8,128)(2,1)S(1)}, u32[]{:S(2)}, u32[]{:S(2)}) collective-permute-start(bf16[144,1536]{1,0:T(8,128)(2,1)} %join.1.refs_12_), channel_id=1, source_target_pairs={{0,4},{4,0},{8,12},{12,8},{1,5},{5,1},{9,13},{13,9},{2,6},{6,2},{1... | collective-permute-start | bytes 1327112 | tf_op jit(solution)/shard_map/ppermute | solution.py:493
  52.5 7.9 %collective-permute-start.9 = (bf16[192,768]{1,0:T(8,128)(2,1)}, bf16[192,768]{1,0:T(8,128)(2,1)S(1)}, u32[]{:S(2)}, u32[]{:S(2)}) collective-permute-start(bf16[192,768]{1,0:T(8,128)(2,1)} %get-tuple-element.64.refs_4_), channel_id=1, source_target_pairs={{0,16},{16,0},{1,17},{17,1},{2,18},{18,2},{3,19},{19,3},{4,20},{20... | collective-permute-start | bytes 884744 | tf_op jit(solution)/shard_map/ppermute | solution.py:502
  54.9 8.8 %collective-permute-start.8 = (bf16[192,768]{1,0:T(8,128)(2,1)}, bf16[192,768]{1,0:T(8,128)(2,1)S(1)}, u32[]{:S(2)}, u32[]{:S(2)}) collective-permute-start(bf16[192,768]{1,0:T(8,128)(2,1)} %get-tuple-element.64.refs_4_), channel_id=1, source_target_pairs={{16,8},{20,12},{8,16},{12,20},{17,9},{21,13},{9,17},{13,21},{18,10... | collective-permute-start | bytes 884744 | tf_op jit(solution)/shard_map/ppermute | solution.py:502
  59.1 16.2 %collective-permute-start.16 = (bf16[144,1536]{1,0:T(8,128)(2,1)S(1)}, bf16[144,1536]{1,0:T(8,128)(2,1)S(1)}, u32[]{:S(2)}, u32[]{:S(2)}) collective-permute-start(bf16[144,1536]{1,0:T(8,128)(2,1)S(1)} %collective-permute-done.15.refs_14_), channel_id=1, source_target_pairs={{0,4},{4,0},{8,12},{12,8},{1,5},{5,1},{9,13},{13,9},{2,6},{6,2},{1... | collective-permute-start | bytes 1327112 | tf_op jit(solution)/shard_map/ppermute | solution.py:495
  67.0 8.3 %collective-permute-start.13 = (bf16[192,768]{1,0:T(8,128)(2,1)}, bf16[192,768]{1,0:T(8,128)(2,1)S(1)}, u32[]{:S(2)}, u32[]{:S(2)}) collective-permute-start(bf16[192,768]{1,0:T(8,128)(2,1)} %get-tuple-element.68.refs_5_), channel_id=1, source_target_pairs={{16,8},{20,12},{8,16},{12,20},{17,9},{21,13},{9,17},{13,21},{18,10... | collective-permute-start | bytes 884744 | tf_op jit(solution)/shard_map/ppermute | solution.py:502
  70.4 4.9 %collective-permute-start.12 = (bf16[192,768]{1,0:T(8,128)(2,1)}, bf16[192,768]{1,0:T(8,128)(2,1)S(1)}, u32[]{:S(2)}, u32[]{:S(2)}) collective-permute-start(bf16[192,768]{1,0:T(8,128)(2,1)} %get-tuple-element.68.refs_5_), channel_id=1, source_target_pairs={{0,16},{16,0},{1,17},{17,1},{2,18},{18,2},{3,19},{19,3},{4,20},{20... | collective-permute-start | bytes 884744 | tf_op jit(solution)/shard_map/ppermute | solution.py:502
  75.3 3.8 %copy-start.2 = (s32[3]{0:T(128)S(1)}, s32[3]{0:T(128)}, u32[]{:S(2)}) copy-start(s32[3]{0:T(128)} %get-tuple-element.56.turn_ref) | copy-start | bytes 40
  75.3 3.8 %copy-start.4 = (s32[7,12]{1,0:T(8,128)S(1)}, s32[7,12]{1,0:T(8,128)}, u32[]{:S(2)}) copy-start(s32[7,12]{1,0:T(8,128)} %copy-done.3) | copy-start | bytes 1012
  79.0 6.7 %collective-permute-start.17 = (bf16[576,1536]{1,0:T(8,128)(2,1)}, bf16[576,1536]{1,0:T(8,128)(2,1)S(1)}, u32[]{:S(2)}, u32[]{:S(2)}) collective-permute-start(bf16[576,1536]{1,0:T(8,128)(2,1)} %get-tuple-element.83.refs_3_), channel_id=1, source_target_pairs={{0,16},{16,0},{1,17},{17,1},{2,18},{18,2},{3,19},{19,3},{4,20},{20... | collective-permute-start | bytes 5308424 | tf_op jit(solution)/shard_map/ppermute | solution.py:550
  79.1 6.6 %copy-start = (s32[6]{0:T(128)S(1)}, s32[6]{0:T(128)}, u32[]{:S(2)}) copy-start(s32[6]{0:T(128)} %stack.80.refs_0_) | copy-start | bytes 76
  79.1 6.6 %copy-start.1 = (s32[3]{0:T(128)S(1)}, s32[3]{0:T(128)}, u32[]{:S(2)}) copy-start(s32[3]{0:T(128)} %get-tuple-element.55.turn_ref) | copy-start | bytes 40
  84.5 8.2 %copy-start.5 = (bf16[192,384]{1,0:T(8,128)(2,1)S(1)}, bf16[192,384]{1,0:T(8,128)(2,1)}, u32[]{:S(2)}) copy-start(bf16[192,384]{1,0:T(8,128)(2,1)} %get-tuple-element.88) | copy-start | bytes 442372
  84.5 16.0 %collective-permute-start.18 = (bf16[192,384]{1,0:T(8,128)(2,1)}, bf16[192,384]{1,0:T(8,128)(2,1)S(1)}, u32[]{:S(2)}, u32[]{:S(2)}) collective-permute-start(bf16[192,384]{1,0:T(8,128)(2,1)} %get-tuple-element.85), channel_id=1, source_target_pairs={{0,2},{1,3},{2,0},{3,1},{4,18},{5,19},{6,16},{7,17},{8,10},{9,11},... | collective-permute-start | bytes 442376 | tf_op jit(solution)/shard_map/ppermute | solution.py:483
  92.7 8.7 %collective-permute-start.19 = (bf16[192,384]{1,0:T(8,128)(2,1)S(1)}, bf16[192,384]{1,0:T(8,128)(2,1)S(1)}, u32[]{:S(2)}, u32[]{:S(2)}) collective-permute-start(bf16[192,384]{1,0:T(8,128)(2,1)S(1)} %copy-done.5), channel_id=1, source_target_pairs={{0,3},{1,2},{2,1},{3,0},{4,19},{5,18},{6,17},{7,16},{8,11},{9,10},... | collective-permute-start | bytes 442376 | tf_op jit(solution)/shard_map/ppermute | solution.py:483
  96.9 7.6 %collective-permute-start.20 = (bf16[192,384]{1,0:T(8,128)(2,1)}, bf16[192,384]{1,0:T(8,128)(2,1)S(1)}, u32[]{:S(2)}, u32[]{:S(2)}) collective-permute-start(bf16[192,384]{1,0:T(8,128)(2,1)} %get-tuple-element.89), channel_id=1, source_target_pairs={{0,0},{1,1},{2,2},{3,3},{4,16},{5,17},{6,18},{7,19},{8,8},{9,9},{1... | collective-permute-start | bytes 442376 | tf_op jit(solution)/shard_map/ppermute | solution.py:483
  100.4 5.7 %collective-permute-start.21 = (bf16[192,384]{1,0:T(8,128)(2,1)}, bf16[192,384]{1,0:T(8,128)(2,1)S(1)}, u32[]{:S(2)}, u32[]{:S(2)}) collective-permute-start(bf16[192,384]{1,0:T(8,128)(2,1)} %get-tuple-element.90), channel_id=1, source_target_pairs={{0,1},{1,0},{2,3},{3,2},{4,17},{5,16},{6,19},{7,18},{8,9},{9,8},{1... | collective-permute-start | bytes 442376 | tf_op jit(solution)/shard_map/ppermute | solution.py:483

commit v12 on v11

--- a/solution.py
+++ b/solution.py
@@ -540,8 +540,7 @@
     query_b, pair_b = project(core_at, [second], count, width, gain, own, far, 1)
     shares = shared(join(count, first, second, piece), query_b)
     link_b, chip_b = halos(pair_b)
-    third, link_b, chip_b = together(third, link_b, chip_b)
-    query_c, pair_c = project(core_at, [third], count, width, gain, own, far, 1 << 30)
+    query_c, pair_c = project(core_at, [third], count, width, gain, own, far, 1 << 32)
     link_c, chip_c = halos(pair_c)
     q_all, kv_all, vt_all, mine = window(
         place, groups, count, [query_a, query_b, query_c], [pair_a, pair_b, pair_c],

time: 110 us -> 108 us (0.982)
  waiting for transfers between devices: 27.8 us -> 24.1 us
  starting transfers between devices: 39.4 us -> 42.6 us
  Pallas kernels: 36.7 us -> 35.2 us
    ppermute x3, starting transfers between devices: 8.92 us -> 13.1 us  [halos(): lax.ppermute(pair, ('dp', 'seq'), over_link)]
    ppermute x3, waiting for transfers between devices: 8.62 us -> 4.88 us  [halos(): lax.ppermute(pair, ('dp', 'seq'), over_link)]
    ppermute x3, starting transfers between devices: 2.54 us -> 0.21 us  [halos(): lax.ppermute(pair, 'dp', swap)]
    pallas_call x2, Pallas kernels: 12.3 us -> 10.7 us  [attend(): pl.pallas_call(functools.partial(attend_kernel, groups, reach, block // 2...]
    ppermute x7, starting transfers between devices: 17.2 us -> 18.7 us  [moved(): return lax.ppermute(value, ('dp', 'seq', 'head'), pairs)]
  transfers between devices with their start and end apart: 22 -> 22, of which waited for: 11 -> 10; matrix products, arithmetic and copies ran while one was open for 4% -> 4% of each run, Pallas kernels for 26% -> 25%
where the time goes in v12:
time: 108 us; the launch traced here: 107 us
  starting transfers between devices  42.6 us (39%)
  Pallas kernels  35.2 us (33%)
  waiting for transfers between devices  24.1 us (22%)
  local copies, waits for them, and re-layouts  3.37 us (3%)
    ppermute x7, starting transfers between devices, moved(): return lax.ppermute(value, ('dp', 'seq', 'head'), pairs)  18.7 us
    ppermute x3, starting transfers between devices, halos(): lax.ppermute(pair, ('dp', 'seq'), over_link)  13.1 us
    pallas_call x3, Pallas kernels, project(): pl.pallas_call(functools.partial(project_kernel, blocks, count), out_shap...  12.4 us
    pallas_call x2, Pallas kernels, attend(): pl.pallas_call(functools.partial(attend_kernel, groups, reach, block // 2...  10.7 us
    ppermute x7, waiting for transfers between devices, moved(): return lax.ppermute(value, ('dp', 'seq', 'head'), pairs)  9.99 us
    ppermute x2, starting transfers between devices, ringed(): return lax.ppermute(value, 'head', [(z, after[z]) for z in range(layers)])  6.12 us
    ppermute x2, waiting for transfers between devices, ringed(): return lax.ppermute(value, 'head', [(z, after[z]) for z in range(layers)])  5.22 us
    ppermute x3, waiting for transfers between devices, halos(): lax.ppermute(pair, ('dp', 'seq'), over_link)  4.88 us
  transfers between devices with their start and end apart: 22, of which 10 were waited for; matrix products, arithmetic and copies ran while one was open for 4% of the time, Pallas kernels for 25%

profile of v12, /device:TPU:1, one launch (start us, length us, event | category | flops | bytes accessed | tf_op | source)
XLA Modules:
  0.0 106.9 jit_solution(8417649577962759252)
XLA Ops:
  0.0 2.1 %pack.1 = (bf16[240,1536]{1,0:T(8,128)(2,1)}, bf16[96,768]{1,0:T(8,128)(2,1)}) custom-call(s32[1]{0:T(128)} %bitcast.9.place_ref, bf16[192,1536]{1,0:T(8,128)(2,1)} %bitcast.rows_ref, bf16[384,768]{1,0:T(8,128)(2,1)} %refs_1_.1), custom_call_target="tpu_custom_call" | custom-call | flops 1 | bytes 1 | tf_op jit(solution)/shard_map/pack/pallas_call | solution.py:69
  2.1 3.7 %collective-permute-start.5 = (bf16[240,1536]{1,0:T(8,128)(2,1)}, bf16[240,1536]{1,0:T(8,128)(2,1)}, u32[]{:S(2)}, u32[]{:S(2)}) collective-permute-start(bf16[240,1536]{1,0:T(8,128)(2,1)} %get-tuple-element.58), channel_id=1, source_target_pairs={{0,1},{1,3},{2,0},{3,2},{4,17},{5,19},{6,16},{7,18},{8,9},{9,11},{... | collective-permute-start | bytes 2211848 | tf_op jit(solution)/shard_map/ppermute | solution.py:483
  6.4 0.7 copy.13
  7.1 1.9 %collective-permute-start.1 = (s32[7,12]{1,0:T(8,128)S(1)}, s32[7,12]{1,0:T(8,128)S(1)}, u32[]{:S(2)}, u32[]{:S(2)}) collective-permute-start(s32[7,12]{1,0:T(8,128)S(1)} %concatenate.3), channel_id=1, source_target_pairs={{0,0},{4,16},{8,8},{12,24},{16,4},{20,20},{24,12},{28,28},{1,1},{5... | collective-permute-start | bytes 1016 | tf_op jit(solution)/shard_map/ppermute | solution.py:514
  9.0 1.6 %bundle.1 = (bf16[768,768]{1,0:T(8,128)(2,1)S(1)}, bf16[768,768]{1,0:T(8,128)(2,1)S(1)}) custom-call(bf16[768,384]{1,0:T(8,128)(2,1)} %query_ref.1, bf16[768,384]{1,0:T(8,128)(2,1)} %key_ref.1, bf16[768,384]{1,0:T(8,128)(2,1)} %value_ref.1, bf16[384,768]{1,0:T(8,128)(2,1)} %refs_1_.1), custom_call_target="tpu_custom_call" | custom-call | flops 1 | bytes 1 | tf_op jit(solution)/shard_map/bundle/pallas_call | solution.py:99
  10.7 1.8 %collective-permute-done.1 = s32[7,12]{1,0:T(8,128)S(1)} collective-permute-done((s32[7,12]{1,0:T(8,128)S(1)}, s32[7,12]{1,0:T(8,128)S(1)}, u32[]{:S(2)}, u32[]{:S(2)}) %collective-permute-start.1) | collective-permute-done | bytes 368 | tf_op jit(solution)/shard_map/ppermute | solution.py:514
  12.5 0.0 collective-permute-start.3
  12.5 0.5 collective-permute-start.4
  13.0 1.9 %collective-permute-start = (bf16[192,1536]{1,0:T(8,128)(2,1)}, bf16[192,1536]{1,0:T(8,128)(2,1)}, u32[]{:S(2)}, u32[]{:S(2)}) collective-permute-start(bf16[192,1536]{1,0:T(8,128)(2,1)} %bitcast.rows_ref), channel_id=1, source_target_pairs={{0,0},{1,1},{2,2},{3,3},{4,16},{5,17},{6,18},{7,19},{8,8},{9,9},{1... | collective-permute-start | bytes 1769480 | tf_op jit(solution)/shard_map/ppermute | solution.py:483
  14.9 2.6 %collective-permute-start.2 = (bf16[96,768]{1,0:T(8,128)(2,1)}, bf16[96,768]{1,0:T(8,128)(2,1)}, u32[]{:S(2)}, u32[]{:S(2)}) collective-permute-start(bf16[96,768]{1,0:T(8,128)(2,1)} %get-tuple-element.48), channel_id=1, source_target_pairs={{0,2},{1,0},{2,3},{3,1},{4,18},{5,16},{6,19},{7,17},{8,10},{9,8},{... | collective-permute-start | bytes 442376 | tf_op jit(solution)/shard_map/ppermute | solution.py:483
  17.5 0.1 pad_add_fusion.place_ref
  17.6 0.7 broadcast_in_dim.10.gain_ref
  18.3 0.7 stack.80.refs_0_
  18.9 0.7 add_add_fusion
  19.6 0.5 slice.9
  20.1 0.0 copy-done.3
  20.1 0.7 stack.77.place_ref
  20.8 2.7 %collective-permute-done.5.refs_1_.first_ref = bf16[240,1536]{1,0:T(8,128)(2,1)} collective-permute-done((bf16[240,1536]{1,0:T(8,128)(2,1)}, bf16[240,1536]{1,0:T(8,128)(2,1)}, u32[]{:S(2)}, u32[]{:S(2)}) %collective-permute-start.5) | collective-permute-done | bytes 737312 | tf_op jit(solution)/shard_map/ppermute | solution.py:483
  23.5 4.1 %collective-permute-start.6 = (bf16[240,1536]{1,0:T(8,128)(2,1)}, bf16[240,1536]{1,0:T(8,128)(2,1)S(1)}, u32[]{:S(2)}, u32[]{:S(2)}) collective-permute-start(bf16[240,1536]{1,0:T(8,128)(2,1)} %collective-permute-done.5.refs_1_.first_ref), channel_id=1, source_target_pairs={{0,1},{1,3},{2,0},{3,2},{4,5},{5,7},{6,4},{7,6},{8,9},{9,11},{10,8... | collective-permute-start | bytes 2211848 | tf_op jit(solution)/shard_map/ppermute | solution.py:505
  27.6 0.0 collective-permute-done.2.refs_0_
  27.6 1.7 %collective-permute-done.refs_0_ = bf16[192,1536]{1,0:T(8,128)(2,1)} collective-permute-done((bf16[192,1536]{1,0:T(8,128)(2,1)}, bf16[192,1536]{1,0:T(8,128)(2,1)}, u32[]{:S(2)}, u32[]{:S(2)}) %collective-permute-start) | collective-permute-done | bytes 589856 | tf_op jit(solution)/shard_map/ppermute | solution.py:483
  29.2 0.0 collective-permute-done.3.far_front
  29.2 0.0 collective-permute-done.4.far_back.refs_2_
  29.2 5.7 %project.3 = (bf16[384,384]{1,0:T(8,128)(2,1)}, bf16[384,768]{1,0:T(8,128)(2,1)}) custom-call(s32[1]{0:T(128)} %bitcast.1.place_ref, f32[1,1536]{1,0:T(1,128)S(1)} %broadcast_in_dim.10.gain_ref, bf16[768,768]{1,0:T(8,128)(2,1)S(1)} %get-tuple-element.55.own_front, bf16[768,768]{1,0:T(8,128)(2,1)S(1)} %get-tuple-element.56.own_back, ...), custom_call_target="tpu_custom_call" | custom-call | flops 1 | bytes 1 | tf_op jit(solution)/shard_map/project/pallas_call | solution.py:186
  34.9 0.1 collective-permute-start.9
  35.0 3.5 %collective-permute-start.8 = (bf16[384,768]{1,0:T(8,128)(2,1)}, bf16[384,768]{1,0:T(8,128)(2,1)S(1)}, u32[]{:S(2)}, u32[]{:S(2)}) collective-permute-start(bf16[384,768]{1,0:T(8,128)(2,1)} %get-tuple-element.62.refs_3_), channel_id=1, source_target_pairs={{16,8},{20,12},{8,16},{12,20},{17,9},{21,13},{9,17},{13,21},{18,10... | collective-permute-start | bytes 1769480 | tf_op jit(solution)/shard_map/ppermute | solution.py:502
  38.5 5.2 %collective-permute-done.6.refs_0_.second_ref = bf16[240,1536]{1,0:T(8,128)(2,1)S(1)} collective-permute-done((bf16[240,1536]{1,0:T(8,128)(2,1)}, bf16[240,1536]{1,0:T(8,128)(2,1)S(1)}, u32[]{:S(2)}, u32[]{:S(2)}) %collective-permute-start.6) | collective-permute-done | bytes 737312 | tf_op jit(solution)/shard_map/ppermute | solution.py:505
  43.8 2.1 %collective-permute-start.7 = (bf16[192,1536]{1,0:T(8,128)(2,1)S(1)}, bf16[192,1536]{1,0:T(8,128)(2,1)S(1)}, u32[]{:S(2)}, u32[]{:S(2)}) collective-permute-start(bf16[192,1536]{1,0:T(8,128)(2,1)S(1)} %slice.12), channel_id=1, source_target_pairs={{0,1},{1,3},{2,0},{3,2},{4,5},{5,7},{6,4},{7,6},{8,9},{9,11},{10,8... | collective-permute-start | bytes 1769480 | tf_op jit(solution)/shard_map/ppermute | solution.py:505
  45.9 0.0 collective-permute-done.9.refs_6_
  45.9 0.6 collective-permute-done.8.refs_9_
  46.4 1.9 %join.1.refs_12_ = bf16[144,1536]{1,0:T(8,128)(2,1)} custom-call(bf16[240,1536]{1,0:T(8,128)(2,1)} %collective-permute-done.5.refs_1_.first_ref, bf16[240,1536]{1,0:T(8,128)(2,1)S(1)} %collective-permute-done.6.refs_0_.second_ref, bf16[96,768]{1,0:T(8,128)(2,1)} %hold.2.piece_ref), custom_call_target="tpu_custom_call" | custom-call | flops 1 | bytes 1 | tf_op jit(solution)/shard_map/join/pallas_call | solution.py:127
  48.3 0.8 collective-permute-start.15
  49.1 0.0 collective-permute-start.14
  49.1 3.4 %project.4 = (bf16[192,384]{1,0:T(8,128)(2,1)}, bf16[192,768]{1,0:T(8,128)(2,1)}) custom-call(s32[1]{0:T(128)} %bitcast.1.place_ref, f32[1,1536]{1,0:T(1,128)S(1)} %broadcast_in_dim.10.gain_ref, bf16[768,768]{1,0:T(8,128)(2,1)S(1)} %get-tuple-element.55.own_front, bf16[768,768]{1,0:T(8,128)(2,1)S(1)} %get-tuple-element.56.own_back, ...), custom_call_target="tpu_custom_call" | custom-call | flops 1 | bytes 1 | tf_op jit(solution)/shard_map/project/pallas_call | solution.py:186
  52.5 4.3 %collective-permute-start.12 = (bf16[192,768]{1,0:T(8,128)(2,1)}, bf16[192,768]{1,0:T(8,128)(2,1)S(1)}, u32[]{:S(2)}, u32[]{:S(2)}) collective-permute-start(bf16[192,768]{1,0:T(8,128)(2,1)} %get-tuple-element.63.refs_4_), channel_id=1, source_target_pairs={{16,8},{20,12},{8,16},{12,20},{17,9},{21,13},{9,17},{13,21},{18,10... | collective-permute-start | bytes 884744 | tf_op jit(solution)/shard_map/ppermute | solution.py:502
  56.8 0.1 collective-permute-start.10
  56.9 2.2 %collective-permute-done.15.refs_14_ = bf16[144,1536]{1,0:T(8,128)(2,1)S(1)} collective-permute-done((bf16[144,1536]{1,0:T(8,128)(2,1)}, bf16[144,1536]{1,0:T(8,128)(2,1)S(1)}, u32[]{:S(2)}, u32[]{:S(2)}) %collective-permute-start.15) | collective-permute-done | bytes 442400 | tf_op jit(solution)/shard_map/ppermute | solution.py:493
  59.1 0.0 collective-permute-done.14.refs_13_
  59.1 1.3 %collective-permute-start.16 = (bf16[144,1536]{1,0:T(8,128)(2,1)S(1)}, bf16[144,1536]{1,0:T(8,128)(2,1)S(1)}, u32[]{:S(2)}, u32[]{:S(2)}) collective-permute-start(bf16[144,1536]{1,0:T(8,128)(2,1)S(1)} %collective-permute-done.15.refs_14_), channel_id=1, source_target_pairs={{0,4},{4,0},{8,12},{12,8},{1,5},{5,1},{9,13},{13,9},{2,6},{6,2},{1... | collective-permute-start | bytes 1327112 | tf_op jit(solution)/shard_map/ppermute | solution.py:495
  60.4 0.0 collective-permute-done.7.refs_0_
  60.4 3.4 %project.5 = (bf16[192,384]{1,0:T(8,128)(2,1)}, bf16[192,768]{1,0:T(8,128)(2,1)}) custom-call(s32[1]{0:T(128)} %bitcast.1.place_ref, f32[1,1536]{1,0:T(1,128)S(1)} %broadcast_in_dim.10.gain_ref, bf16[768,768]{1,0:T(8,128)(2,1)S(1)} %get-tuple-element.55.own_front, bf16[768,768]{1,0:T(8,128)(2,1)S(1)} %get-tuple-element.56.own_back, ...), custom_call_target="tpu_custom_call" | custom-call | flops 4294967296 | bytes 1 | tf_op jit(solution)/shard_map/project/pallas_call | solution.py:186
  63.8 5.2 %collective-permute-start.13 = (bf16[192,768]{1,0:T(8,128)(2,1)}, bf16[192,768]{1,0:T(8,128)(2,1)S(1)}, u32[]{:S(2)}, u32[]{:S(2)}) collective-permute-start(bf16[192,768]{1,0:T(8,128)(2,1)} %get-tuple-element.64.refs_5_), channel_id=1, source_target_pairs={{16,8},{20,12},{8,16},{12,20},{17,9},{21,13},{9,17},{13,21},{18,10... | collective-permute-start | bytes 884744 | tf_op jit(solution)/shard_map/ppermute | solution.py:502
  69.0 0.1 collective-permute-start.11
  69.0 0.0 collective-permute-done.12.refs_10_
  69.1 0.0 collective-permute-done.10.refs_7_
  69.1 4.3 %collective-permute-done.13.refs_11_ = bf16[192,768]{1,0:T(8,128)(2,1)S(1)} collective-permute-done((bf16[192,768]{1,0:T(8,128)(2,1)}, bf16[192,768]{1,0:T(8,128)(2,1)S(1)}, u32[]{:S(2)}, u32[]{:S(2)}) %collective-permute-start.13) | collective-permute-done | bytes 294944 | tf_op jit(solution)/shard_map/ppermute | solution.py:502
  73.4 0.0 collective-permute-done.11.refs_8_
  73.4 0.0 collective-permute-done.16.refs_15_
  73.4 0.0 copy-start.4
  73.4 3.7 %window.1 = (bf16[768,384]{1,0:T(8,128)(2,1)S(1)}, bf16[2304,768]{1,0:T(8,128)(2,1)S(1)}, bf16[3,18,128,128]{3,2,1,0:T(8,128)(2,1)S(1)}, bf16[576,1536]{1,0:T(8,128)(2,1)}) custom-call(s32[8]{0:T(128)S(1)} %stack.77.place_ref, bf16[384,384]{1,0:T(8,128)(2,1)} %get-tuple-element.59.refs_0_, bf16[192,384]{1,0:T(8,128)(2,1)} %get-tuple-element.60.refs_1_, ...), custom_call_target="tpu_custom_call" | custom-call | bytes 8257536 | tf_op jit(solution)/shard_map/window/pallas_call | solution.py:247
  77.1 0.1 collective-permute-start.17
  77.2 4.4 %attend.2 = (bf16[192,384]{1,0:T(8,128)(2,1)}, bf16[192,384]{1,0:T(8,128)(2,1)}) custom-call(s32[8]{0:T(128)S(1)} %stack.77.place_ref, s32[6,12]{1,0:T(8,128)S(1)} %bitcast.24, s32[3]{0:T(128)S(1)} %copy-done.2, bf16[768,384]{1,0:T(8,128)(2,1)S(1)} %get-tuple-element.75.q_all, bf16[2304,768]{1,0:T(8,128)(2,1)S(1)} %get-tuple-element.72.kv_all, ...), custom_call_target="tpu_custom_call" | custom-call | flops 17179869184 | bytes 1048576 | tf_op jit(solution)/shard_map/attend/pallas_call | solution.py:406
  81.6 3.2 %collective-permute-start.18 = (bf16[192,384]{1,0:T(8,128)(2,1)}, bf16[192,384]{1,0:T(8,128)(2,1)S(1)}, u32[]{:S(2)}, u32[]{:S(2)}) collective-permute-start(bf16[192,384]{1,0:T(8,128)(2,1)} %get-tuple-element.79), channel_id=1, source_target_pairs={{0,2},{1,3},{2,0},{3,1},{4,18},{5,19},{6,16},{7,17},{8,10},{9,11},... | collective-permute-start | bytes 442376 | tf_op jit(solution)/shard_map/ppermute | solution.py:483
  84.8 0.0 collective-permute-done.17.refs_4_
  84.8 0.0 copy-done
  84.8 6.4 %attend.3 = (bf16[192,384]{1,0:T(8,128)(2,1)}, bf16[192,384]{1,0:T(8,128)(2,1)}, bf16[4,2,384,768]{3,2,1,0:T(8,128)(2,1)S(1)}) custom-call(s32[8]{0:T(128)S(1)} %stack.77.place_ref, s32[6,12]{1,0:T(8,128)S(1)} %bitcast.25, s32[3]{0:T(128)S(1)} %copy-done.1, bf16[768,384]{1,0:T(8,128)(2,1)S(1)} %get-tuple-element.75.q_all, ...), custom_call_target="tpu_custom_call" | custom-call | flops 17179869184 | bytes 1048576 | tf_op jit(solution)/shard_map/attend/pallas_call | solution.py:406
  91.2 3.3 %collective-permute-start.19 = (bf16[192,384]{1,0:T(8,128)(2,1)S(1)}, bf16[192,384]{1,0:T(8,128)(2,1)S(1)}, u32[]{:S(2)}, u32[]{:S(2)}) collective-permute-start(bf16[192,384]{1,0:T(8,128)(2,1)S(1)} %copy-done.5), channel_id=1, source_target_pairs={{0,3},{1,2},{2,1},{3,0},{4,19},{5,18},{6,17},{7,16},{8,11},{9,10},... | collective-permute-start | bytes 442376 | tf_op jit(solution)/shard_map/ppermute | solution.py:483
  94.5 4.0 %collective-permute-start.20 = (bf16[192,384]{1,0:T(8,128)(2,1)}, bf16[192,384]{1,0:T(8,128)(2,1)S(1)}, u32[]{:S(2)}, u32[]{:S(2)}) collective-permute-start(bf16[192,384]{1,0:T(8,128)(2,1)} %get-tuple-element.83), channel_id=1, source_target_pairs={{0,0},{1,1},{2,2},{3,3},{4,16},{5,17},{6,18},{7,19},{8,8},{9,9},{1... | collective-permute-start | bytes 442376 | tf_op jit(solution)/shard_map/ppermute | solution.py:483
  98.5 0.1 collective-permute-start.21
  98.5 0.0 collective-permute-done.18.refs_0_
  98.6 1.5 %collective-permute-done.19.refs_1_ = bf16[192,384]{1,0:T(8,128)(2,1)S(1)} collective-permute-done((bf16[192,384]{1,0:T(8,128)(2,1)S(1)}, bf16[192,384]{1,0:T(8,128)(2,1)S(1)}, u32[]{:S(2)}, u32[]{:S(2)}) %collective-permute-start.19) | collective-permute-done | bytes 147488 | tf_op jit(solution)/shard_map/ppermute | solution.py:483
  100.1 1.8 %collective-permute-done.20.refs_2_ = bf16[192,384]{1,0:T(8,128)(2,1)S(1)} collective-permute-done((bf16[192,384]{1,0:T(8,128)(2,1)}, bf16[192,384]{1,0:T(8,128)(2,1)S(1)}, u32[]{:S(2)}, u32[]{:S(2)}) %collective-permute-start.20) | collective-permute-done | bytes 147488 | tf_op jit(solution)/shard_map/ppermute | solution.py:483
  101.9 2.3 %collective-permute-done.21.refs_3_ = bf16[192,384]{1,0:T(8,128)(2,1)S(1)} collective-permute-done((bf16[192,384]{1,0:T(8,128)(2,1)}, bf16[192,384]{1,0:T(8,128)(2,1)S(1)}, u32[]{:S(2)}, u32[]{:S(2)}) %collective-permute-start.21) | collective-permute-done | bytes 147488 | tf_op jit(solution)/shard_map/ppermute | solution.py:483
  104.2 2.7 %output.1 = bf16[1,192,1536]{2,1,0:T(8,128)(2,1)} custom-call(s32[4]{0:T(128)S(1)} %pad_add_fusion.place_ref, bf16[4,2,384,768]{3,2,1,0:T(8,128)(2,1)S(1)} %get-tuple-element.78.weight, bf16[192,384]{1,0:T(8,128)(2,1)S(1)} %hold.3.refs_0_, bf16[192,384]{1,0:T(8,128)(2,1)S(1)} %collective-permute-done.19.refs_1_, ...), custom_call_target="tpu_custom_call" | custom-call | flops 1 | bytes 1 | tf_op jit(solution)/shard_map/output/pallas_call | solution.py:432
  (13 shorter events, 0.1 us)
Async XLA Ops:
  2.1 21.4 %collective-permute-start.5 = (bf16[240,1536]{1,0:T(8,128)(2,1)}, bf16[240,1536]{1,0:T(8,128)(2,1)}, u32[]{:S(2)}, u32[]{:S(2)}) collective-permute-start(bf16[240,1536]{1,0:T(8,128)(2,1)} %get-tuple-element.58), channel_id=1, source_target_pairs={{0,1},{1,3},{2,0},{3,2},{4,17},{5,19},{6,16},{7,18},{8,9},{9,11},{... | collective-permute-start | bytes 2211848 | tf_op jit(solution)/shard_map/ppermute | solution.py:483
  7.1 5.4 %collective-permute-start.1 = (s32[7,12]{1,0:T(8,128)S(1)}, s32[7,12]{1,0:T(8,128)S(1)}, u32[]{:S(2)}, u32[]{:S(2)}) collective-permute-start(s32[7,12]{1,0:T(8,128)S(1)} %concatenate.3), channel_id=1, source_target_pairs={{0,0},{4,16},{8,8},{12,24},{16,4},{20,20},{24,12},{28,28},{1,1},{5... | collective-permute-start | bytes 1016 | tf_op jit(solution)/shard_map/ppermute | solution.py:514
  12.5 7.6 %copy-start.3 = (s32[7,12]{1,0:T(8,128)}, s32[7,12]{1,0:T(8,128)S(1)}, u32[]{:S(2)}) copy-start(s32[7,12]{1,0:T(8,128)S(1)} %collective-permute-done.1) | copy-start | bytes 1012
  12.5 16.8 %collective-permute-start.3 = (bf16[768,768]{1,0:T(8,128)(2,1)S(1)}, bf16[768,768]{1,0:T(8,128)(2,1)}, u32[]{:S(2)}, u32[]{:S(2)}) collective-permute-start(bf16[768,768]{1,0:T(8,128)(2,1)S(1)} %get-tuple-element.55.own_front), channel_id=1, source_target_pairs={{0,16},{16,0},{1,17},{17,1},{2,18},{18,2},{3,19},{19,3},{4,20},{20... | collective-permute-start | bytes 3538952 | tf_op jit(solution)/shard_map/ppermute | solution.py:516
  12.5 16.8 %collective-permute-start.4 = (bf16[768,768]{1,0:T(8,128)(2,1)S(1)}, bf16[768,768]{1,0:T(8,128)(2,1)S(1)}, u32[]{:S(2)}, u32[]{:S(2)}) collective-permute-start(bf16[768,768]{1,0:T(8,128)(2,1)S(1)} %get-tuple-element.56.own_back), channel_id=1, source_target_pairs={{0,16},{16,0},{1,17},{17,1},{2,18},{18,2},{3,19},{19,3},{4,20},{20... | collective-permute-start | bytes 3538952 | tf_op jit(solution)/shard_map/ppermute | solution.py:516
  13.0 16.3 %collective-permute-start = (bf16[192,1536]{1,0:T(8,128)(2,1)}, bf16[192,1536]{1,0:T(8,128)(2,1)}, u32[]{:S(2)}, u32[]{:S(2)}) collective-permute-start(bf16[192,1536]{1,0:T(8,128)(2,1)} %bitcast.rows_ref), channel_id=1, source_target_pairs={{0,0},{1,1},{2,2},{3,3},{4,16},{5,17},{6,18},{7,19},{8,8},{9,9},{1... | collective-permute-start | bytes 1769480 | tf_op jit(solution)/shard_map/ppermute | solution.py:483
  14.9 12.6 %collective-permute-start.2 = (bf16[96,768]{1,0:T(8,128)(2,1)}, bf16[96,768]{1,0:T(8,128)(2,1)}, u32[]{:S(2)}, u32[]{:S(2)}) collective-permute-start(bf16[96,768]{1,0:T(8,128)(2,1)} %get-tuple-element.48), channel_id=1, source_target_pairs={{0,2},{1,0},{2,3},{3,1},{4,18},{5,16},{6,19},{7,17},{8,10},{9,8},{... | collective-permute-start | bytes 442376 | tf_op jit(solution)/shard_map/ppermute | solution.py:483
  23.5 20.3 %collective-permute-start.6 = (bf16[240,1536]{1,0:T(8,128)(2,1)}, bf16[240,1536]{1,0:T(8,128)(2,1)S(1)}, u32[]{:S(2)}, u32[]{:S(2)}) collective-permute-start(bf16[240,1536]{1,0:T(8,128)(2,1)} %collective-permute-done.5.refs_1_.first_ref), channel_id=1, source_target_pairs={{0,1},{1,3},{2,0},{3,2},{4,5},{5,7},{6,4},{7,6},{8,9},{9,11},{10,8... | collective-permute-start | bytes 2211848 | tf_op jit(solution)/shard_map/ppermute | solution.py:505
  34.9 10.9 %collective-permute-start.9 = (bf16[384,768]{1,0:T(8,128)(2,1)}, bf16[384,768]{1,0:T(8,128)(2,1)S(1)}, u32[]{:S(2)}, u32[]{:S(2)}) collective-permute-start(bf16[384,768]{1,0:T(8,128)(2,1)} %get-tuple-element.62.refs_3_), channel_id=1, source_target_pairs={{0,16},{16,0},{1,17},{17,1},{2,18},{18,2},{3,19},{19,3},{4,20},{20... | collective-permute-start | bytes 1769480 | tf_op jit(solution)/shard_map/ppermute | solution.py:502
  35.0 11.4 %collective-permute-start.8 = (bf16[384,768]{1,0:T(8,128)(2,1)}, bf16[384,768]{1,0:T(8,128)(2,1)S(1)}, u32[]{:S(2)}, u32[]{:S(2)}) collective-permute-start(bf16[384,768]{1,0:T(8,128)(2,1)} %get-tuple-element.62.refs_3_), channel_id=1, source_target_pairs={{16,8},{20,12},{8,16},{12,20},{17,9},{21,13},{9,17},{13,21},{18,10... | collective-permute-start | bytes 1769480 | tf_op jit(solution)/shard_map/ppermute | solution.py:502
  43.8 16.6 %collective-permute-start.7 = (bf16[192,1536]{1,0:T(8,128)(2,1)S(1)}, bf16[192,1536]{1,0:T(8,128)(2,1)S(1)}, u32[]{:S(2)}, u32[]{:S(2)}) collective-permute-start(bf16[192,1536]{1,0:T(8,128)(2,1)S(1)} %slice.12), channel_id=1, source_target_pairs={{0,1},{1,3},{2,0},{3,2},{4,5},{5,7},{6,4},{7,6},{8,9},{9,11},{10,8... | collective-permute-start | bytes 1769480 | tf_op jit(solution)/shard_map/ppermute | solution.py:505
  48.3 10.7 %collective-permute-start.15 = (bf16[144,1536]{1,0:T(8,128)(2,1)}, bf16[144,1536]{1,0:T(8,128)(2,1)S(1)}, u32[]{:S(2)}, u32[]{:S(2)}) collective-permute-start(bf16[144,1536]{1,0:T(8,128)(2,1)} %join.1.refs_12_), channel_id=1, source_target_pairs={{0,8},{4,12},{8,0},{12,4},{1,9},{5,13},{9,1},{13,5},{2,10},{6,14},... | collective-permute-start | bytes 1327112 | tf_op jit(solution)/shard_map/ppermute | solution.py:493
  49.1 10.0 %collective-permute-start.14 = (bf16[144,1536]{1,0:T(8,128)(2,1)}, bf16[144,1536]{1,0:T(8,128)(2,1)S(1)}, u32[]{:S(2)}, u32[]{:S(2)}) collective-permute-start(bf16[144,1536]{1,0:T(8,128)(2,1)} %join.1.refs_12_), channel_id=1, source_target_pairs={{0,4},{4,0},{8,12},{12,8},{1,5},{5,1},{9,13},{13,9},{2,6},{6,2},{1... | collective-permute-start | bytes 1327112 | tf_op jit(solution)/shard_map/ppermute | solution.py:493
  52.5 16.6 %collective-permute-start.12 = (bf16[192,768]{1,0:T(8,128)(2,1)}, bf16[192,768]{1,0:T(8,128)(2,1)S(1)}, u32[]{:S(2)}, u32[]{:S(2)}) collective-permute-start(bf16[192,768]{1,0:T(8,128)(2,1)} %get-tuple-element.63.refs_4_), channel_id=1, source_target_pairs={{16,8},{20,12},{8,16},{12,20},{17,9},{21,13},{9,17},{13,21},{18,10... | collective-permute-start | bytes 884744 | tf_op jit(solution)/shard_map/ppermute | solution.py:502
  56.8 12.2 %collective-permute-start.10 = (bf16[192,768]{1,0:T(8,128)(2,1)}, bf16[192,768]{1,0:T(8,128)(2,1)S(1)}, u32[]{:S(2)}, u32[]{:S(2)}) collective-permute-start(bf16[192,768]{1,0:T(8,128)(2,1)} %get-tuple-element.63.refs_4_), channel_id=1, source_target_pairs={{0,16},{16,0},{1,17},{17,1},{2,18},{18,2},{3,19},{19,3},{4,20},{20... | collective-permute-start | bytes 884744 | tf_op jit(solution)/shard_map/ppermute | solution.py:502
  59.1 14.3 %collective-permute-start.16 = (bf16[144,1536]{1,0:T(8,128)(2,1)S(1)}, bf16[144,1536]{1,0:T(8,128)(2,1)S(1)}, u32[]{:S(2)}, u32[]{:S(2)}) collective-permute-start(bf16[144,1536]{1,0:T(8,128)(2,1)S(1)} %collective-permute-done.15.refs_14_), channel_id=1, source_target_pairs={{0,4},{4,0},{8,12},{12,8},{1,5},{5,1},{9,13},{13,9},{2,6},{6,2},{1... | collective-permute-start | bytes 1327112 | tf_op jit(solution)/shard_map/ppermute | solution.py:495
  63.8 9.6 %collective-permute-start.13 = (bf16[192,768]{1,0:T(8,128)(2,1)}, bf16[192,768]{1,0:T(8,128)(2,1)S(1)}, u32[]{:S(2)}, u32[]{:S(2)}) collective-permute-start(bf16[192,768]{1,0:T(8,128)(2,1)} %get-tuple-element.64.refs_5_), channel_id=1, source_target_pairs={{16,8},{20,12},{8,16},{12,20},{17,9},{21,13},{9,17},{13,21},{18,10... | collective-permute-start | bytes 884744 | tf_op jit(solution)/shard_map/ppermute | solution.py:502
  69.0 4.4 %collective-permute-start.11 = (bf16[192,768]{1,0:T(8,128)(2,1)}, bf16[192,768]{1,0:T(8,128)(2,1)S(1)}, u32[]{:S(2)}, u32[]{:S(2)}) collective-permute-start(bf16[192,768]{1,0:T(8,128)(2,1)} %get-tuple-element.64.refs_5_), channel_id=1, source_target_pairs={{0,16},{16,0},{1,17},{17,1},{2,18},{18,2},{3,19},{19,3},{4,20},{20... | collective-permute-start | bytes 884744 | tf_op jit(solution)/shard_map/ppermute | solution.py:502
  73.4 3.8 %copy-start.2 = (s32[3]{0:T(128)S(1)}, s32[3]{0:T(128)}, u32[]{:S(2)}) copy-start(s32[3]{0:T(128)} %get-tuple-element.53.turn_ref) | copy-start | bytes 40
  73.4 3.8 %copy-start.4 = (s32[7,12]{1,0:T(8,128)S(1)}, s32[7,12]{1,0:T(8,128)}, u32[]{:S(2)}) copy-start(s32[7,12]{1,0:T(8,128)} %copy-done.3) | copy-start | bytes 1012
  77.1 7.7 %collective-permute-start.17 = (bf16[576,1536]{1,0:T(8,128)(2,1)}, bf16[576,1536]{1,0:T(8,128)(2,1)S(1)}, u32[]{:S(2)}, u32[]{:S(2)}) collective-permute-start(bf16[576,1536]{1,0:T(8,128)(2,1)} %get-tuple-element.77.refs_3_), channel_id=1, source_target_pairs={{0,16},{16,0},{1,17},{17,1},{2,18},{18,2},{3,19},{19,3},{4,20},{20... | collective-permute-start | bytes 5308424 | tf_op jit(solution)/shard_map/ppermute | solution.py:549
  77.2 7.6 %copy-start = (s32[6]{0:T(128)S(1)}, s32[6]{0:T(128)}, u32[]{:S(2)}) copy-start(s32[6]{0:T(128)} %stack.80.refs_0_) | copy-start | bytes 76
  77.2 7.6 %copy-start.1 = (s32[3]{0:T(128)S(1)}, s32[3]{0:T(128)}, u32[]{:S(2)}) copy-start(s32[3]{0:T(128)} %get-tuple-element.52.turn_ref) | copy-start | bytes 40
  81.6 9.6 %copy-start.5 = (bf16[192,384]{1,0:T(8,128)(2,1)S(1)}, bf16[192,384]{1,0:T(8,128)(2,1)}, u32[]{:S(2)}) copy-start(bf16[192,384]{1,0:T(8,128)(2,1)} %get-tuple-element.82) | copy-start | bytes 442372
  81.6 16.9 %collective-permute-start.18 = (bf16[192,384]{1,0:T(8,128)(2,1)}, bf16[192,384]{1,0:T(8,128)(2,1)S(1)}, u32[]{:S(2)}, u32[]{:S(2)}) collective-permute-start(bf16[192,384]{1,0:T(8,128)(2,1)} %get-tuple-element.79), channel_id=1, source_target_pairs={{0,2},{1,3},{2,0},{3,1},{4,18},{5,19},{6,16},{7,17},{8,10},{9,11},... | collective-permute-start | bytes 442376 | tf_op jit(solution)/shard_map/ppermute | solution.py:483
  91.2 8.9 %collective-permute-start.19 = (bf16[192,384]{1,0:T(8,128)(2,1)S(1)}, bf16[192,384]{1,0:T(8,128)(2,1)S(1)}, u32[]{:S(2)}, u32[]{:S(2)}) collective-permute-start(bf16[192,384]{1,0:T(8,128)(2,1)S(1)} %copy-done.5), channel_id=1, source_target_pairs={{0,3},{1,2},{2,1},{3,0},{4,19},{5,18},{6,17},{7,16},{8,11},{9,10},... | collective-permute-start | bytes 442376 | tf_op jit(solution)/shard_map/ppermute | solution.py:483
  94.5 7.4 %collective-permute-start.20 = (bf16[192,384]{1,0:T(8,128)(2,1)}, bf16[192,384]{1,0:T(8,128)(2,1)S(1)}, u32[]{:S(2)}, u32[]{:S(2)}) collective-permute-start(bf16[192,384]{1,0:T(8,128)(2,1)} %get-tuple-element.83), channel_id=1, source_target_pairs={{0,0},{1,1},{2,2},{3,3},{4,16},{5,17},{6,18},{7,19},{8,8},{9,9},{1... | collective-permute-start | bytes 442376 | tf_op jit(solution)/shard_map/ppermute | solution.py:483
  98.5 5.7 %collective-permute-start.21 = (bf16[192,384]{1,0:T(8,128)(2,1)}, bf16[192,384]{1,0:T(8,128)(2,1)S(1)}, u32[]{:S(2)}, u32[]{:S(2)}) collective-permute-start(bf16[192,384]{1,0:T(8,128)(2,1)} %get-tuple-element.84), channel_id=1, source_target_pairs={{0,1},{1,0},{2,3},{3,2},{4,17},{5,16},{6,19},{7,18},{8,9},{9,8},{1... | collective-permute-start | bytes 442376 | tf_op jit(solution)/shard_map/ppermute | solution.py:483
